TPU v7x, 512 devices: a whole 4x8x8 slice. The times are simulated.
512 devices in a mesh: section: 32 (over y_lo, x, core), head: 16 (over y_hi, z).
Axes of the slice: x: 4, y: 8 (y_hi: 2, y_lo: 4; y = y_hi * 4 + y_lo), z: 8, core: 2. Of those that a mesh axis runs over, the one named last changes fastest.
Arguments:
- tokens: bfloat16 [16384, 2048], P('section', 'head'), may hold values from -6 to 6
- norm_gain: float32 [2048], replicated, may hold values from 0.1 to 1.9
- x_weight: bfloat16 [2048, 4096], P(None, 'head'), may hold values from -0.125 to 0.125
- gate_weight: bfloat16 [2048, 4096], P(None, 'head'), may hold values from -0.125 to 0.125
- dt_weight: bfloat16 [2048, 64], P(None, 'head'), may hold values from -0.125 to 0.125
- dt_bias: float32 [64], P('head'), may hold values from -3 to 1
- decay_rate: float32 [64], P('head'), may hold values from 1e-05 to 0.5
- skip_gain: float32 [64], P('head'), may hold values from 0.5 to 1.5
- bc_weight: bfloat16 [2048, 256], P('head'), may hold values from -0.125 to 0.125
- out_gain: float32 [4096], P('head'), may hold values from 0.1 to 1.9
- out_weight: bfloat16 [4096, 2048], P('head'), may hold values from -0.09375 to 0.09375
Outputs:
- mixed: float32 [16384, 2048], P('section', 'head')
All inputs are finite; a program needn't handle non-finite values.
Results may differ from a plain program's by a relative error of at most 0.0053.
Values may be sent and summed in bfloat16 or wider, within the bound.
No kernel may reach another device: no remote copies, remote signals or barrier semaphores. Data moves between devices by JAX's collectives and lax.ppermute only.
A program may use at most 64 MiB of HBM per device.

v0:
```python
import jax
import jax.numpy as jnp
from jax import lax
from jax.sharding import PartitionSpec as P

BLOCK = 256


eps = 1e-05
highest = lax.Precision.HIGHEST


def from_behind(block, axis, distance):
    devices = range(lax.axis_size(axis))
    route = [(i - distance, i) for i in devices if i - distance in devices]
    return lax.ppermute(block, axis, route)


def block_pass(state, pieces):
    inputs, writes, reads, step, decay = pieces
    cums = jnp.cumsum(decay, axis=0)
    cums_t = cums.T
    diff = cums_t[:, :, None] - cums_t[:, None, :]
    count = cums.shape[0]
    lower = lax.broadcasted_iota(jnp.int32, (count, count), 0) >= lax.broadcasted_iota(
        jnp.int32, (count, count), 1
    )
    weight = jnp.exp(jnp.where(lower[None, :, :], diff, -jnp.inf))
    scores = jnp.dot(reads, writes.T, precision=highest)
    mixing = weight * scores[None, :, :] * step.T[:, None, :]
    result = jnp.einsum("hts,shp->thp", mixing, inputs, precision=highest)
    carried = jnp.einsum("tn,hpn->thp", reads, state, precision=highest)
    result = result + jnp.exp(cums)[:, :, None] * carried
    tail = jnp.exp(cums[-1][None, :] - cums) * step
    fresh = jnp.einsum("sh,shp,sn->hpn", tail, inputs, writes, precision=highest)
    new_state = jnp.exp(cums[-1])[:, None, None] * state + fresh
    return (new_state, result)


def local(
    tokens,
    norm_gain,
    x_weight,
    gate_weight,
    dt_weight,
    dt_bias,
    decay_rate,
    skip_gain,
    bc_weight,
    out_gain,
    out_weight,
):
    rows, own_width = tokens.shape
    heads = decay_rate.shape[0]
    inner = x_weight.shape[1]
    size_p = inner // heads
    state_n = bc_weight.shape[1] // 2
    tok_real = tokens.astype(jnp.float32)
    offset = lax.axis_index("head") * own_width
    whole = lax.all_gather(tokens, "head", axis=1, tiled=True)
    whole_real = whole.astype(jnp.float32)
    scale = lax.rsqrt(jnp.mean(whole_real * whole_real, axis=-1, keepdims=True) + eps)
    normed = (whole_real * scale * norm_gain).astype(jnp.bfloat16)
    in_raw = jnp.dot(normed, x_weight, preferred_element_type=jnp.float32)
    gate = jnp.dot(normed, gate_weight, preferred_element_type=jnp.float32)
    step_raw = jnp.dot(normed, dt_weight, preferred_element_type=jnp.float32)
    own_normed = lax.dynamic_slice_in_dim(normed, offset, own_width, 1)
    both = lax.psum(jnp.dot(own_normed, bc_weight, preferred_element_type=jnp.float32), "head")
    writes = both[:, :state_n]
    reads = both[:, state_n:]
    inputs = jax.nn.silu(in_raw).reshape(rows, heads, size_p)
    step = jax.nn.softplus(step_raw + dt_bias)
    decay = -decay_rate * step
    blocks = rows // BLOCK
    pieces = (
        inputs.reshape(blocks, BLOCK, heads, size_p),
        writes.reshape(blocks, BLOCK, state_n),
        reads.reshape(blocks, BLOCK, state_n),
        step.reshape(blocks, BLOCK, heads),
        decay.reshape(blocks, BLOCK, heads),
    )
    zero_state = jnp.zeros((heads, size_p, state_n), jnp.float32)
    local_state, outs = lax.scan(block_pass, zero_state, pieces)
    running = jnp.cumsum(decay, axis=0)
    decay_total = jnp.exp(running[-1])[:, None, None]

    def chain_turn(turn, incoming):
        return from_behind(decay_total * incoming + local_state, "section", 1)

    state_in = lax.fori_loop(0, lax.axis_size("section") - 1, chain_turn, zero_state)
    carried = jnp.einsum("tn,hpn->thp", reads, state_in, precision=highest)
    result = outs.reshape(rows, heads, size_p) + jnp.exp(running)[:, :, None] * carried
    result = result + skip_gain[None, :, None] * inputs
    gated = result * jax.nn.silu(gate.reshape(rows, heads, size_p))
    gated = gated * lax.rsqrt(jnp.mean(gated * gated, axis=-1, keepdims=True) + eps)
    ynorm = (gated.reshape(rows, inner) * out_gain).astype(jnp.bfloat16)
    delta = lax.psum_scatter(
        lax.dot_general(
            out_weight, ynorm, (((0,), (1,)), ((), ())), preferred_element_type=jnp.float32
        ),
        "head",
        scatter_dimension=0,
        tiled=True,
    )
    return tok_real + delta.T


def solution(mesh):
    return jax.shard_map(
        local,
        mesh=mesh,
        in_specs=(
            P("section", "head"),
            P(),
            P(None, "head"),
            P(None, "head"),
            P(None, "head"),
            P("head"),
            P("head"),
            P("head"),
            P("head", None),
            P("head"),
            P("head", None),
        ),
        out_specs=P("section", "head"),
        check_vma=False,
    )
```

profile of v0, /device:TPU:8, one launch (start us, length us, event | category | flops | bytes accessed | tf_op | source)
XLA Modules:
  0.0 850.1 jit_solution(6856869700643997776)
XLA Ops:
  8.0 112.0 %all-gather.2.cloned.1.call-done = bf16[512,2048]{1,0:T(8,128)(2,1)} async-done(((bf16[512,128]{1,0:T(8,128)(2,1)}), bf16[512,2048]{1,0:T(8,128)(2,1)}) %all-gather.2.cloned.1.call-update) | async-done | bytes 2097168 | tf_op jit(solution)/shard_map/all_gather | solution.py:60
  134.5 182.8 %all-reduce.2.cloned.1.call-done = f32[512,256]{1,0:T(8,128)} async-done(((f32[512,256]{1,0:T(8,128)}), f32[512,256]{1,0:T(8,128)}) %all-reduce.2.cloned.1.call-update) | async-done | bytes 524304 | tf_op jit(solution)/shard_map/psum | solution.py:68
  318.3 21.2 %while.24 = (s32[]{:T(128)}, f32[4,64,128]{2,1,0:T(8,128)S(1)}, f32[2,256,4,64]{1,0,3,2:T(2,128)}, f32[2,256,4]{1,2,0:T(4,128)S(1)}, f32[2,256,4]{1,2,0:T(4,128)...) while((s32[]{:T(128)}, f32[4,64,128]{2,1,0:T(8,128)S(1)}, ...), condition=%wide.region_5.6_spmd.clone, body=%wide.region_2.5_spmd.clone.sunk | while | flops 504891392 | bytes 8734872 | solution.py:83
  341.2 262.9 %while.23 = (s32[]{:T(128)}, f32[4,64,128]{2,1,0:T(8,128)S(1)}, f32[4,1,1]{0,2,1:T(1,128)S(1)}, f32[4,64,128]{2,1,0:T(8,128)S(1)}, s32[]{:T(128)}) while((s32[]{:T(128)}, f32[4,64,128]{2,1,0:T(8,128)S(1)}, f32[4,1,1]{0,2,1:T(1,128)S(1)}, f32[4,64,128]{2,1,0:T(8,128)S(1)}, s32[]{:T(128)}) %tuple.68), condition=%wide.region_9.10_spmd, body=%wide.region_8.9_spmd.sunk | while | flops 65538 | bytes 917621 | solution.py:90
  343.2 6.5 collective-permute-done
  351.7 6.5 collective-permute-done
  360.1 6.5 collective-permute-done
  368.6 6.5 collective-permute-done
  385.6 6.5 collective-permute-done
  394.1 6.5 collective-permute-done
  411.0 6.5 collective-permute-done
  419.5 6.5 collective-permute-done
  436.5 6.5 collective-permute-done
  445.0 6.5 collective-permute-done
  470.4 6.5 collective-permute-done
  495.8 6.5 collective-permute-done
  521.3 6.5 collective-permute-done
  529.8 6.5 collective-permute-done
  546.7 6.5 collective-permute-done
  555.2 6.5 collective-permute-done
  572.2 6.5 collective-permute-done
  580.6 6.5 collective-permute-done
  597.6 6.5 collective-permute-done
  608.8 233.1 %reduce-scatter.2.cloned.1.call-done = f32[128,512]{0,1:T(8,128)} async-done(((f32[2048,512]{0,1:T(8,128)}), f32[128,512]{0,1:T(8,128)}) %reduce-scatter.2.cloned.1.call-update) | async-done | bytes 262160 | tf_op jit(solution)/shard_map/reduce_scatter | solution.py:97
  (181 shorter events, 185.5 us)
Async XLA Ops:
  6.5 113.4 %all-gather.2.cloned.1.call-start = ((), (), s32[]{:S(2)}) async-start(), calls=%async_computation.1 | async-start | bytes 2228224 | tf_op jit(solution)/shard_map/all_gather | solution.py:60
  7.3 310.0 %all-reduce.2.cloned.1.call-start = ((), (), s32[]{:S(2)}) async-start(), calls=%async_computation.2 | async-start | bytes 1048576 | tf_op jit(solution)/shard_map/psum | solution.py:68
  126.6 715.3 %reduce-scatter.2.cloned.1.call-start = ((), (), s32[]{:S(2)}) async-start(), calls=%async_computation.3 | async-start | bytes 4456448 | tf_op jit(solution)/shard_map/reduce_scatter | solution.py:97
  341.3 8.4 collective-permute-start
  358.2 8.4 collective-permute-start
  366.7 8.4 collective-permute-start
  383.7 8.4 collective-permute-start
  392.1 8.4 collective-permute-start
  400.6 8.4 collective-permute-start
  409.1 8.4 collective-permute-start
  417.6 8.4 collective-permute-start
  426.1 8.4 collective-permute-start
  434.5 8.4 collective-permute-start
  443.0 8.4 collective-permute-start
  451.5 8.4 collective-permute-start
  468.5 8.4 collective-permute-start
  476.9 8.4 collective-permute-start
  493.9 8.4 collective-permute-start
  502.4 8.4 collective-permute-start
  519.3 8.4 collective-permute-start
  527.8 8.4 collective-permute-start
  544.8 8.4 collective-permute-start
  553.3 8.4 collective-permute-start
  561.7 8.4 collective-permute-start
  (25 other events, 1841.3 us)
Sparse Core Ops, SparseCore 0:
  10.4 109.5 all-gather.1
  126.7 190.4 all-reduce.1
  608.9 232.9 reduce-scatter.1
where the time goes:
time: 851 us; the launch traced here: 850 us
  waiting for transfers between devices  729 us (86%)
  starting transfers between devices  59.6 us (7%)
  local copies, waits for them, and re-layouts  18.5 us (2%)
  matrix products  17 us (2%)
  between operations  13.3 us (2%)
  other arithmetic  12.2 us (1%)
    reduce_scatter x1, waiting for transfers between devices, local(): lax.psum_scatter(lax.dot_general(out_weight, ynorm, (((0,), (1,)), ((), (...  233 us
    ppermute x31, waiting for transfers between devices, from_behind(): return lax.ppermute(block, axis, route)  200 us
    psum x1, waiting for transfers between devices, local(): lax.psum(jnp.dot(own_normed, bc_weight, preferred_element_type=jnp.float3...  183 us
    all_gather x1, waiting for transfers between devices, local(): whole = lax.all_gather(tokens, 'head', axis=1, tiled=True)  112 us
    ppermute x31, starting transfers between devices, from_behind(): return lax.ppermute(block, axis, route)  59.5 us
  transfers between devices with their start and end apart: 34, of which 34 were waited for; matrix products, arithmetic and copies ran while one was open for 1% of the time, Pallas kernels for 0%

commit v1 on v0

--- a/solution.py
+++ b/solution.py
@@ -8,12 +8,6 @@
 
 eps = 1e-05
 highest = lax.Precision.HIGHEST
-
-
-def from_behind(block, axis, distance):
-    devices = range(lax.axis_size(axis))
-    route = [(i - distance, i) for i in devices if i - distance in devices]
-    return lax.ppermute(block, axis, route)
 
 
 def block_pass(state, pieces):
@@ -37,6 +31,30 @@
     return (new_state, result)
 
 
+def gather_head(block):
+    copies = jnp.broadcast_to(block[None], (lax.axis_size("head"),) + block.shape)
+    return lax.all_to_all(copies, "head", 0, 0)
+
+
+def incoming_state(local_state, log_decay):
+    sections = lax.axis_size("section")
+    heads, size_p, state_n = local_state.shape
+    lines = heads * size_p // sections
+    chunks = local_state.reshape(sections, lines, state_n)
+    extra = jnp.repeat(log_decay, sections // heads)[:, None, None]
+    extra = jnp.broadcast_to(extra, (sections, lines, state_n))
+    sent = lax.all_to_all(jnp.concatenate([chunks, extra], 1), "section", 0, 0)
+    got, logs = sent[:, :lines], sent[:, lines, 0]
+    until = jnp.cumsum(logs)
+    ahead = jnp.concatenate([jnp.zeros_like(until[:1]), until[:-1]])
+    place = jnp.arange(sections)
+    before = place[:, None] > place[None, :]
+    span = jnp.where(before, ahead[:, None] - until[None, :], -jnp.inf)
+    mixed = jnp.einsum("sr,rln->sln", jnp.exp(span), got, precision=highest)
+    back = lax.all_to_all(mixed, "section", 0, 0)
+    return back.reshape(heads, size_p, state_n)
+
+
 def local(
     tokens,
     norm_gain,
@@ -55,19 +73,20 @@
     inner = x_weight.shape[1]
     size_p = inner // heads
     state_n = bc_weight.shape[1] // 2
+    groups = lax.axis_size("head")
     tok_real = tokens.astype(jnp.float32)
-    offset = lax.axis_index("head") * own_width
-    whole = lax.all_gather(tokens, "head", axis=1, tiled=True)
-    whole_real = whole.astype(jnp.float32)
+    packed = jnp.concatenate([tokens, bc_weight[:, :state_n], bc_weight[:, state_n:]], 0)
+    whole = gather_head(packed)
+    write_weight = whole[:, rows : rows + own_width].reshape(groups * own_width, state_n)
+    read_weight = whole[:, rows + own_width :].reshape(groups * own_width, state_n)
+    whole_real = whole[:, :rows].transpose(1, 0, 2).reshape(rows, -1).astype(jnp.float32)
     scale = lax.rsqrt(jnp.mean(whole_real * whole_real, axis=-1, keepdims=True) + eps)
     normed = (whole_real * scale * norm_gain).astype(jnp.bfloat16)
     in_raw = jnp.dot(normed, x_weight, preferred_element_type=jnp.float32)
     gate = jnp.dot(normed, gate_weight, preferred_element_type=jnp.float32)
     step_raw = jnp.dot(normed, dt_weight, preferred_element_type=jnp.float32)
-    own_normed = lax.dynamic_slice_in_dim(normed, offset, own_width, 1)
-    both = lax.psum(jnp.dot(own_normed, bc_weight, preferred_element_type=jnp.float32), "head")
-    writes = both[:, :state_n]
-    reads = both[:, state_n:]
+    writes = jnp.dot(normed, write_weight, preferred_element_type=jnp.float32)
+    reads = jnp.dot(normed, read_weight, preferred_element_type=jnp.float32)
     inputs = jax.nn.silu(in_raw).reshape(rows, heads, size_p)
     step = jax.nn.softplus(step_raw + dt_bias)
     decay = -decay_rate * step
@@ -82,27 +101,17 @@
     zero_state = jnp.zeros((heads, size_p, state_n), jnp.float32)
     local_state, outs = lax.scan(block_pass, zero_state, pieces)
     running = jnp.cumsum(decay, axis=0)
-    decay_total = jnp.exp(running[-1])[:, None, None]
-
-    def chain_turn(turn, incoming):
-        return from_behind(decay_total * incoming + local_state, "section", 1)
-
-    state_in = lax.fori_loop(0, lax.axis_size("section") - 1, chain_turn, zero_state)
+    state_in = incoming_state(local_state, running[-1])
     carried = jnp.einsum("tn,hpn->thp", reads, state_in, precision=highest)
     result = outs.reshape(rows, heads, size_p) + jnp.exp(running)[:, :, None] * carried
     result = result + skip_gain[None, :, None] * inputs
     gated = result * jax.nn.silu(gate.reshape(rows, heads, size_p))
     gated = gated * lax.rsqrt(jnp.mean(gated * gated, axis=-1, keepdims=True) + eps)
     ynorm = (gated.reshape(rows, inner) * out_gain).astype(jnp.bfloat16)
-    delta = lax.psum_scatter(
-        lax.dot_general(
-            out_weight, ynorm, (((0,), (1,)), ((), ())), preferred_element_type=jnp.float32
-        ),
-        "head",
-        scatter_dimension=0,
-        tiled=True,
-    )
-    return tok_real + delta.T
+    shares = jnp.dot(ynorm, out_weight, preferred_element_type=jnp.float32)
+    shares = shares.astype(jnp.bfloat16).reshape(rows, groups, own_width).transpose(1, 0, 2)
+    shares = lax.all_to_all(shares, "head", 0, 0)
+    return tok_real + jnp.sum(shares.astype(jnp.float32), axis=0)
 
 
 def solution(mesh):

time: 851 us -> 291 us (0.34)
  waiting for transfers between devices: 729 us -> 91.6 us
  blocking collectives: 0 us -> 72.6 us
  local copies, waits for them, and re-layouts: 18.5 us -> 40.3 us
  starting transfers between devices: 59.6 us -> 44.6 us
  between operations: 13.3 us -> 0.32 us
    reduce_scatter x1 -> x0, waiting for transfers between devices: 233 us -> none  [local(): lax.psum_scatter(lax.dot_general(out_weight, ynorm, (((0,), (1,)), ((), (...]
    ppermute x31 -> x0, waiting for transfers between devices: 200 us -> none  [from_behind(): return lax.ppermute(block, axis, route)]
    psum x1 -> x0, waiting for transfers between devices: 183 us -> none  [local(): lax.psum(jnp.dot(own_normed, bc_weight, preferred_element_type=jnp.float3...]
    all_gather x1 -> x0, waiting for transfers between devices: 112 us -> none  [local(): whole = lax.all_gather(tokens, 'head', axis=1, tiled=True)]
    all_to_all x0 -> x3, waiting for transfers between devices: none -> 91.6 us  [the longest x1 83 us: gather_head(): return lax.all_to_all(copies, 'head', 0, 0)]
    all_to_all x0 -> x1, blocking collectives: none -> 72.6 us  [local(): shares = lax.all_to_all(shares, 'head', 0, 0)]
    ppermute x31 -> x0, starting transfers between devices: 59.5 us -> none  [from_behind(): return lax.ppermute(block, axis, route)]
    all_to_all x0 -> x3, starting transfers between devices: none -> 44.6 us  [the longest x1 24.8 us: incoming_state(): sent = lax.all_to_all(jnp.concatenate([chunks, extra], 1), 'section', 0, 0)]
  transfers between devices with their start and end apart: 34 -> 3, of which waited for: 34 -> 3; matrix products, arithmetic and copies ran while one was open for 1% -> 3% of each run, Pallas kernels for 0% -> 0%
where the time goes in v1:
time: 291 us; the launch traced here: 290 us
  waiting for transfers between devices  91.6 us (31%)
  blocking collectives  72.6 us (25%)
  starting transfers between devices  44.6 us (15%)
  local copies, waits for them, and re-layouts  40.3 us (14%)
  matrix products  20.7 us (7%)
  other arithmetic  19.9 us (7%)
    all_to_all x1, waiting for transfers between devices, gather_head(): return lax.all_to_all(copies, 'head', 0, 0)  83 us
    all_to_all x1, blocking collectives, local(): shares = lax.all_to_all(shares, 'head', 0, 0)  72.6 us
    all_to_all x1, starting transfers between devices, incoming_state(): sent = lax.all_to_all(jnp.concatenate([chunks, extra], 1), 'section', 0, 0)  24.8 us
    all_to_all x1, starting transfers between devices, gather_head(): return lax.all_to_all(copies, 'head', 0, 0)  15 us
    dynamic_update_slice x4, local copies, waits for them, and re-layouts, local(): local_state, outs = lax.scan(block_pass, zero_state, pieces)  7.87 us
  transfers between devices with their start and end apart: 3, of which 3 were waited for; matrix products, arithmetic and copies ran while one was open for 3% of the time, Pallas kernels for 0%

profile of v1, /device:TPU:8, one launch (start us, length us, event | category | flops | bytes accessed | tf_op | source)
XLA Modules:
  0.0 290.3 jit_solution(16980044908649136200)
XLA Ops:
  1.8 2.3 broadcast_in_dim.40
  4.1 15.0 %all-to-all-start = ((bf16[16,768,128]{2,1,0:T(8,128)(2,1)}), bf16[16,768,128]{2,1,0:T(8,128)(2,1)}, u32[]{:S(2)}, u32[]{:S(2)}) async-start(bf16[16,768,128]{2,1,0:T(8,128)(2,1)} %broadcast_in_dim.40), calls=%async_computation | async-start | bytes 6291456 | tf_op jit(solution)/shard_map/all_to_all | solution.py:36
  19.6 83.0 %all-to-all-done = bf16[16,768,128]{2,1,0:T(8,128)(2,1)} async-done(((bf16[16,768,128]{2,1,0:T(8,128)(2,1)}), bf16[16,768,128]{2,1,0:T(8,128)(2,1)}, u32[]{:S(2)}, u32[]{:S(2)}) %all-to-all-start) | async-done | bytes 3145760 | tf_op jit(solution)/shard_map/all_to_all | solution.py:36
  102.6 2.1 fusion.33
  104.7 2.3 fusion.38
  107.1 2.7 copy.85
  109.8 4.2 %convert_element_type.54 = bf16[2,256,2048]{2,1,0:T(8,128)(2,1)} reshape(bf16[512,16,128]{2,1,0:T(8,128)(2,1)} %copy.85) | data formatting | bytes 4194304 | tf_op jit(solution)/shard_map/convert_element_type | solution.py:84
  113.9 3.9 %convert_bitcast_fusion = f32[512,16,128]{2,0,1:T(8,128)} fusion(bf16[16,768,128]{2,1,0:T(8,128)(2,1)} %all-to-all-done), kind=kLoop, calls=%fused_computation.48 | loop fusion | flops 1048576 | bytes 6291456 | tf_op jit(solution)/shard_map/convert_element_type | solution.py:82
  117.9 5.3 %copy.84 = f32[512,16,128]{0,2,1:T(8,128)} copy(f32[512,16,128]{2,0,1:T(8,128)} %convert_bitcast_fusion) | data formatting | bytes 8388608 | tf_op jit(solution)/shard_map/convert_element_type | solution.py:82
  123.2 2.7 fusion.37
  128.9 2.2 reshape_reshape.3
  132.3 2.3 fusion.63
  135.6 2.5 fusion.43
  138.1 22.2 %while.13 = (s32[]{:T(128)}, f32[4,64,128]{2,1,0:T(8,128)S(1)}, f32[2,256,4,64]{1,0,3,2:T(2,128)}, f32[2,256,4]{1,2,0:T(4,128)S(1)}, f32[2,256,4]{1,2,0:T(4,128)...) while((s32[]{:T(128)}, f32[4,64,128]{2,1,0:T(8,128)S(1)}, ...), condition=%wide.region_4.5_spmd.clone, body=%wide.region_1.4_spmd.clone.sunk | while | flops 504891392 | bytes 9783468 | solution.py:102
  144.8 3.7 %dynamic_update_slice.6 = f32[2,256,4,64]{1,0,3,2:T(2,128)S(1)} dynamic-update-slice(f32[2,256,4,64]{1,0,3,2:T(2,128)S(1)} %copy-done.9, f32[1,256,4,64]{1,0,3,2:T(1,128)S(1)} %copy.146, s32[]{:T(128)} %get-tuple-element.216, s32[]{:T(128)} %constant.34.clone.1..sunk, s32[]{:T(128)} %constant.34.clone.1..sunk, s32[]{:T(128)} %constant.34.clone.1..sunk) | dynamic-update-slice | bytes 524292 | tf_op jit(solution)/shard_map/while/body/jit(dynamic_update_index_in_dim)/dynamic_update_slice | solution.py:102
  155.9 3.7 %dynamic_update_slice.6 = f32[2,256,4,64]{1,0,3,2:T(2,128)S(1)} dynamic-update-slice(f32[2,256,4,64]{1,0,3,2:T(2,128)S(1)} %copy-done.9, f32[1,256,4,64]{1,0,3,2:T(1,128)S(1)} %copy.146, s32[]{:T(128)} %get-tuple-element.216, s32[]{:T(128)} %constant.34.clone.1..sunk, s32[]{:T(128)} %constant.34.clone.1..sunk, s32[]{:T(128)} %constant.34.clone.1..sunk) | dynamic-update-slice | bytes 524292 | tf_op jit(solution)/shard_map/while/body/jit(dynamic_update_index_in_dim)/dynamic_update_slice | solution.py:102
  164.1 24.8 %all-to-all-start.1 = ((f32[32,16,128]{2,1,0:T(8,128)}), f32[32,16,128]{2,1,0:T(8,128)S(1)}, u32[]{:S(2)}, u32[]{:S(2)}) async-start(f32[32,16,128]{2,1,0:T(8,128)} %pad_maximum_fusion), calls=%async_computation.1 | async-start | bytes 524288 | tf_op jit(solution)/shard_map/all_to_all | solution.py:46
  188.9 2.3 copy.94
  191.2 2.6 copy.93
  193.8 5.2 %all-to-all-done.1 = f32[32,16,128]{2,1,0:T(8,128)S(1)} async-done(((f32[32,16,128]{2,1,0:T(8,128)}), f32[32,16,128]{2,1,0:T(8,128)S(1)}, u32[]{:S(2)}, u32[]{:S(2)}) %all-to-all-start.1) | async-done | bytes 262176 | tf_op jit(solution)/shard_map/all_to_all | solution.py:46
  200.4 4.9 %all-to-all-start.2 = ((f32[32,8,128]{2,1,0:T(8,128)}), f32[32,8,128]{2,1,0:T(8,128)S(1)}, u32[]{:S(2)}, u32[]{:S(2)}) async-start(f32[32,8,128]{2,1,0:T(8,128)} %copy.92), calls=%async_computation.2 | async-start | bytes 262144 | tf_op jit(solution)/shard_map/all_to_all | solution.py:54
  205.3 3.5 %fusion.64 = f32[512,4,64]{0,2,1:T(8,128)} fusion(bf16[512,2048,1]{0,1,2:T(8,128)(2,1)} %bitcast.169, bf16[4,64,2048]{2,1,0:T(8,128)(2,1)} %bitcast.171), kind=kOutput, calls=%fused_computation.107 | convolution fusion | flops 536870912 | bytes 3670016 | tf_op jit(solution)/shard_map/dot_general | solution.py:86
  209.2 3.5 %all-to-all-done.2 = f32[32,8,128]{2,1,0:T(8,128)S(1)} async-done(((f32[32,8,128]{2,1,0:T(8,128)}), f32[32,8,128]{2,1,0:T(8,128)S(1)}, u32[]{:S(2)}, u32[]{:S(2)}) %all-to-all-start.2) | async-done | bytes 131104 | tf_op jit(solution)/shard_map/all_to_all | solution.py:54
  216.0 72.6 %all_to_all.20 = bf16[16,512,128]{2,1,0:T(8,128)(2,1)S(1)} all-to-all(bf16[16,512,128]{2,1,0:T(8,128)(2,1)S(1)} %bitcast.166), channel_id=1, replica_groups=mesh['section'=32,'head'=16] {'head'}, dimensions={0} | all-to-all | bytes 4194304 | tf_op jit(solution)/shard_map/all_to_all | solution.py:113
  (125 shorter events, 32.8 us)
Async XLA Ops:
  0.0 214.7 %copy-start = (bf16[256,2048]{1,0:T(8,128)(2,1)S(1)}, bf16[256,2048]{1,0:T(8,128)(2,1)}, u32[]{:S(2)}) copy-start(bf16[256,2048]{1,0:T(8,128)(2,1)} %param.23) | copy-start | bytes 3145732
  4.1 15.0 %copy-start.18 = (f32[4]{0:T(128)S(1)}, f32[4]{0:T(128)}, u32[]{:S(2)}) copy-start(f32[4]{0:T(128)} %param.19) | copy-start | bytes 52
  4.1 98.5 %all-to-all-start = ((bf16[16,768,128]{2,1,0:T(8,128)(2,1)}), bf16[16,768,128]{2,1,0:T(8,128)(2,1)}, u32[]{:S(2)}, u32[]{:S(2)}) async-start(bf16[16,768,128]{2,1,0:T(8,128)(2,1)} %broadcast_in_dim.40), calls=%async_computation | async-start | bytes 6291456 | tf_op jit(solution)/shard_map/all_to_all | solution.py:36
  19.0 85.7 %copy-start.12 = (f32[2048]{0:T(1024)S(1)}, f32[2048]{0:T(1024)}, u32[]{:S(2)}) copy-start(f32[2048]{0:T(1024)} %param.14) | copy-start | bytes 24580
  107.0 28.6 %copy-start.1 = (bf16[512,16,128]{2,0,1:T(8,128)(2,1)}, bf16[512,16,128]{2,0,1:T(8,128)(2,1)S(1)}, u32[]{:S(2)}) copy-start(bf16[512,16,128]{2,0,1:T(8,128)(2,1)S(1)} %fusion.38) | copy-start | bytes 6291460
  123.2 4.1 %copy-start.17 = (bf16[2048,256]{1,0:T(8,128)(2,1)S(1)}, bf16[2048,256]{1,0:T(8,128)(2,1)}, u32[]{:S(2)}) copy-start(bf16[2048,256]{1,0:T(8,128)(2,1)} %param.15) | copy-start | bytes 3145732
  125.9 1.4 copy-start.3
  131.1 3.6 %copy-start.4 = (bf16[512,2048]{0,1:T(8,128)(2,1)S(1)}, bf16[512,2048]{0,1:T(8,128)(2,1)}, u32[]{:S(2)}) copy-start(bf16[512,2048]{0,1:T(8,128)(2,1)} %copy-done.3) | copy-start | bytes 6291460
  131.1 3.6 %copy-start.13 = (bf16[2048,4]{0,1:T(4,128)(2,1)S(1)}, bf16[2048,4]{0,1:T(4,128)(2,1)}, u32[]{:S(2)}) copy-start(bf16[2048,4]{0,1:T(4,128)(2,1)} %param.17) | copy-start | bytes 49156
  131.1 3.6 %copy-start.14 = (f32[4]{0:T(128)S(1)}, f32[4]{0:T(128)}, u32[]{:S(2)}) copy-start(f32[4]{0:T(128)} %neg.18) | copy-start | bytes 52
  131.1 3.6 %copy-start.15 = (f32[4]{0:T(128)S(1)}, f32[4]{0:T(128)}, u32[]{:S(2)}) copy-start(f32[4]{0:T(128)} %param.18) | copy-start | bytes 52
  138.1 6.0 %copy-start.5 = (f32[2,256,128]{2,1,0:T(8,128)S(1)}, f32[2,256,128]{2,1,0:T(8,128)}, u32[]{:S(2)}) copy-start(f32[2,256,128]{2,1,0:T(8,128)} %get-tuple-element.234) | copy-start | bytes 786436 | tf_op jit(solution)/shard_map/while
  139.7 5.0 %copy-start.9 = (f32[2,256,4,64]{1,0,3,2:T(2,128)S(1)}, f32[2,256,4,64]{1,0,3,2:T(2,128)}, u32[]{:S(2)}) copy-start(f32[2,256,4,64]{1,0,3,2:T(2,128)} %get-tuple-element.218) | copy-start | bytes 1572868 | tf_op jit(solution)/shard_map/while
  149.2 6.0 %copy-start.5 = (f32[2,256,128]{2,1,0:T(8,128)S(1)}, f32[2,256,128]{2,1,0:T(8,128)}, u32[]{:S(2)}) copy-start(f32[2,256,128]{2,1,0:T(8,128)} %get-tuple-element.234) | copy-start | bytes 786436 | tf_op jit(solution)/shard_map/while
  150.9 5.0 %copy-start.9 = (f32[2,256,4,64]{1,0,3,2:T(2,128)S(1)}, f32[2,256,4,64]{1,0,3,2:T(2,128)}, u32[]{:S(2)}) copy-start(f32[2,256,4,64]{1,0,3,2:T(2,128)} %get-tuple-element.218) | copy-start | bytes 1572868 | tf_op jit(solution)/shard_map/while
  160.3 30.8 %copy-start.2 = (bf16[512,16,128]{2,0,1:T(8,128)(2,1)S(1)}, bf16[512,16,128]{2,0,1:T(8,128)(2,1)}, u32[]{:S(2)}) copy-start(bf16[512,16,128]{2,0,1:T(8,128)(2,1)} %copy-done.1) | copy-start | bytes 6291460
  164.1 34.8 %all-to-all-start.1 = ((f32[32,16,128]{2,1,0:T(8,128)}), f32[32,16,128]{2,1,0:T(8,128)S(1)}, u32[]{:S(2)}, u32[]{:S(2)}) async-start(f32[32,16,128]{2,1,0:T(8,128)} %pad_maximum_fusion), calls=%async_computation.1 | async-start | bytes 524288 | tf_op jit(solution)/shard_map/all_to_all | solution.py:46
  200.4 12.3 %all-to-all-start.2 = ((f32[32,8,128]{2,1,0:T(8,128)}), f32[32,8,128]{2,1,0:T(8,128)S(1)}, u32[]{:S(2)}, u32[]{:S(2)}) async-start(f32[32,8,128]{2,1,0:T(8,128)} %copy.92), calls=%async_computation.2 | async-start | bytes 262144 | tf_op jit(solution)/shard_map/all_to_all | solution.py:54
  205.3 3.5 %copy-start.11 = (f32[2,256,4,64]{1,0,3,2:T(2,128)S(1)}, f32[2,256,4,64]{1,0,3,2:T(2,128)}, u32[]{:S(2)}) copy-start(f32[2,256,4,64]{1,0,3,2:T(2,128)} %get-tuple-element.48) | copy-start | bytes 1572868
  205.3 7.4 %copy-start.6 = (f32[2,256,128]{2,1,0:T(8,128)S(1)}, f32[2,256,128]{2,1,0:T(8,128)}, u32[]{:S(2)}) copy-start(f32[2,256,128]{2,1,0:T(8,128)} %get-tuple-element.240) | copy-start | bytes 786436
  205.3 7.4 %copy-start.8 = (f32[512,256]{0,1:T(8,128)S(1)}, f32[512,256]{0,1:T(8,128)}, u32[]{:S(2)}) copy-start(f32[512,256]{0,1:T(8,128)} %divide_multiply_fusion) | copy-start | bytes 1572868
  205.3 7.4 %copy-start.19 = (f32[4]{0:T(128)S(1)}, f32[4]{0:T(128)}, u32[]{:S(2)}) copy-start(f32[4]{0:T(128)} %param.20) | copy-start | bytes 52
  209.2 5.4 %copy-start.16 = (f32[256]{0:T(256)S(1)}, f32[256]{0:T(256)}, u32[]{:S(2)}) copy-start(f32[256]{0:T(256)} %param.22) | copy-start | bytes 3076
  288.7 0.9 copy-start.7
  (2 other events, 1.6 us)

commit v2 on v0

v2 whole, which is shorter than its diff:
```python
import functools

import jax
import jax.numpy as jnp
from jax import lax
from jax.experimental import pallas as pl
from jax.experimental.pallas import tpu as pltpu
from jax.sharding import PartitionSpec as P

eps = 1e-05
highest = lax.Precision.HIGHEST
RING = 8
SIDE = 2
f32 = jnp.float32
bf16 = jnp.bfloat16
VMEM_BYTES = 40 * 1024 * 1024


def dot(a, b, dims=((1,), (0,)), precision=None):
    return lax.dot_general(a, b, (dims, ((), ())), precision=precision, preferred_element_type=f32)


def silu(v):
    return v / (1.0 + jnp.exp(-v))


def softplus(v):
    return jnp.maximum(v, 0.0) + jnp.log1p(jnp.exp(-jnp.abs(v)))


def iota(shape, dim):
    return lax.broadcasted_iota(jnp.int32, shape, dim)


def spread(heads_on_lanes, width, size_p):
    lanes = heads_on_lanes.shape[1]
    pick = (iota((lanes, width), 1) // size_p == iota((lanes, width), 0)).astype(f32)
    return dot(heads_on_lanes, pick, precision=highest)


def column(row, rows, size_p, first):
    lanes = row.shape[1]
    mine = iota((rows, lanes), 1) == iota((rows, lanes), 0) // size_p + first
    return jnp.sum(jnp.where(mine, row, 0.0), axis=1, keepdims=True)


def log_rows(row):
    high = row.astype(bf16).astype(f32)
    low = row - high
    return jnp.concatenate([high, low, jnp.zeros((14, row.shape[1]), f32)], 0).astype(bf16)


def log_row(ref, half):
    tail = ref[half : half + 16].astype(f32)
    return tail[0:1] + tail[1:2]


def project_kernel(heads, size_p, place, *refs):
    blocks = refs[:RING]
    (gain, x_weight, dt_weight, bc_one, bc_two, small) = refs[RING : RING + 6]
    (normed, x_out, writes_out, reads_out, cums_out, step_out, mine, theirs, state) = refs[RING + 6 :]
    rows = normed.shape[0]
    own = blocks[0].shape[1]
    side, turn, core = place[0], place[1], place[2]

    def parts():
        for k in range(RING):
            for j in range(SIDE):
                head = lax.rem(side + j, SIDE) * RING + lax.rem(turn + k, RING)
                yield blocks[k][j * rows : (j + 1) * rows, :].astype(f32), head

    squares = jnp.zeros((rows, own), f32)
    for value, _ in parts():
        squares = squares + value * value
    mean = jnp.sum(squares, axis=1, keepdims=True) / (RING * SIDE * own)
    scale = lax.rsqrt(mean + eps)
    for value, head in parts():
        spot = pl.multiple_of(head * own, own)
        normed[:, pl.ds(spot, own)] = (value * scale * gain[pl.ds(head, 1), :]).astype(bf16)
    whole = normed[...]
    step = softplus(dot(whole, dt_weight[...]) + small[0:1, :])
    decay = -small[1:2, :] * step
    lower = (iota((rows, rows), 0) >= iota((rows, rows), 1)).astype(f32)
    cums = dot(lower, decay, precision=highest)
    one = dot(whole, bc_one[...])
    two = dot(whole, bc_two[...])
    writes = jnp.where(core == 0, one, two)
    reads = jnp.where(core == 0, two, one)
    x = silu(dot(whole, x_weight[...]))
    x_out[...] = x
    writes_out[...] = writes
    reads_out[...] = reads
    cums_out[...] = cums
    step_out[...] = step
    last = cums[rows - 1 : rows, :]
    tail = spread(jnp.exp(last - cums) * step, heads * size_p, size_p)
    state[...] = dot((x * tail).T, writes, precision=highest)
    half = heads * size_p // 2
    logs = log_rows(last)
    mine[0:half, :] = state[pl.ds(pl.multiple_of(core * half, half), half), :].astype(bf16)
    mine[half : half + 16, :] = logs
    theirs[0:half, :] = state[pl.ds(pl.multiple_of((1 - core) * half, half), half), :].astype(bf16)
    theirs[half : half + 16, :] = logs


def chip_kernel(size_p, place, mine, other, copies):
    half = mine.shape[0] - 16
    core = place[2]
    first = core * (half // size_p)
    early = core == 0
    log_mine, log_other = log_row(mine, half), log_row(other, half)
    value_mine, value_other = mine[0:half].astype(f32), other[0:half].astype(f32)
    log_late = jnp.where(early, log_other, log_mine)
    value_early = jnp.where(early, value_mine, value_other)
    value_late = jnp.where(early, value_other, value_mine)
    grown = jnp.exp(column(log_late, half, size_p, first)) * value_early + value_late
    value = grown.astype(bf16)
    logs = log_rows(log_mine + log_other)
    for i in range(copies.shape[0]):
        copies[i, 0:half, :] = value
        copies[i, half : half + 16, :] = logs


def prefix_kernel(size_p, place, gathered, mine, other, keep, send):
    half = mine.shape[0] - 16
    core, chip = place[2], place[3]
    first = core * (half // size_p)
    early = core == 0
    state = jnp.zeros((half, mine.shape[1]), f32)
    for i in range(gathered.shape[0] - 1):
        grow = jnp.exp(column(log_row(gathered.at[i], half), half, size_p, first))
        state = jnp.where(i < chip, grow * state + gathered[i, 0:half, :].astype(f32), state)
    log_early = jnp.where(early, log_row(mine, half), log_row(other, half))
    value_early = jnp.where(early, mine[0:half].astype(f32), other[0:half].astype(f32))
    later = jnp.exp(column(log_early, half, size_p, first)) * state + value_early
    keep[...] = jnp.where(early, state, later)
    send[...] = jnp.where(early, later, state).astype(bf16)


def scan_kernel(heads, size_p, block, normed, gate_weight, x_in, writes_in, reads_in, cums_in, step_in, small, result, opened):
    rows = x_in.shape[0]
    width = heads * size_p
    opened[...] = silu(dot(normed[...], gate_weight[...]))
    lower = iota((block, block), 0) >= iota((block, block), 1)
    skip = spread(small[0:8, :], width, size_p)[2:3]
    state = None
    base = None
    for b in range(rows // block):
        span = slice(b * block, (b + 1) * block)
        x, writes, reads = x_in[span, :], writes_in[span, :], reads_in[span, :]
        cums, step = cums_in[span, :], step_in[span, :]
        cums_t, step_t = cums.T, step.T
        scores = dot(reads, writes, ((1,), (1,)), highest)
        made = []
        for h in range(heads):
            gap = cums[:, h : h + 1] - cums_t[h : h + 1, :]
            mixing = jnp.exp(jnp.where(lower, gap, -jnp.inf)) * scores * step_t[h : h + 1, :]
            made.append(dot(mixing, x[:, h * size_p : (h + 1) * size_p], precision=highest))
        y = jnp.concatenate(made, axis=1) + skip * x
        if state is not None:
            carried = dot(reads, state, ((1,), (1,)), highest)
            y = y + spread(jnp.exp(cums - base), width, size_p) * carried
        result[span, :] = y
        if (b + 1) * block < rows:
            last = cums[block - 1 : block, :]
            tail = spread(jnp.exp(last - cums) * step, width, size_p)
            fresh = dot((x * tail).T, writes, precision=highest)
            if state is not None:
                grow = jnp.exp(column(last - base, width, size_p, 0))
                fresh = grow * state + fresh
            state, base = fresh, last


def finish_kernel(heads, size_p, place, result, opened, reads, cums, keep, other, out_gain, out_weight, *refs):
    shares, state = refs[:RING], refs[RING]
    rows, width = result.shape
    own = shares[0].shape[1]
    half = width // 2
    side, turn, core = place[0], place[1], place[2]
    state[pl.ds(pl.multiple_of(core * half, half), half), :] = keep[...]
    state[pl.ds(pl.multiple_of((1 - core) * half, half), half), :] = other[...].astype(f32)
    carried = dot(reads[...], state[...], ((1,), (1,)), highest)
    y = result[...] + spread(jnp.exp(cums[...]), width, size_p) * carried
    g = y * opened[...]
    same = (iota((width, width), 0) // size_p == iota((width, width), 1) // size_p).astype(f32)
    mean = dot(g * g, same, precision=highest) / size_p
    ynorm = (g * lax.rsqrt(mean + eps) * out_gain[...]).astype(bf16)
    for k in range(RING):
        for j in range(SIDE):
            head = lax.rem(side + j, SIDE) * RING + lax.rem(turn + k, RING)
            spot = pl.multiple_of(head * own, own)
            shares[k][j * rows : (j + 1) * rows, :] = dot(ynorm, out_weight[:, pl.ds(spot, own)]).astype(bf16)


def on_chip(kernel, outs, args, place=None, scratch=(), flops=0, transcendentals=0):
    specs = [pl.BlockSpec(memory_space=pltpu.VMEM)] * len(args)
    if place is not None:
        specs = [pl.BlockSpec(memory_space=pltpu.SMEM)] + specs
        args = [place] + list(args)
    moved = sum(a.size * a.dtype.itemsize for a in list(args) + list(outs))
    return pl.pallas_call(
        kernel,
        out_shape=outs,
        in_specs=specs,
        out_specs=[pl.BlockSpec(memory_space=pltpu.VMEM)] * len(outs),
        scratch_shapes=scratch,
        cost_estimate=pl.CostEstimate(flops=flops, bytes_accessed=moved, transcendentals=transcendentals),
        compiler_params=pltpu.CompilerParams(vmem_limit_bytes=VMEM_BYTES),
    )(*args)


def shape(dims, kind=f32):
    return jax.ShapeDtypeStruct(dims, kind)


def to_turn(block, step):
    route = [(i, i // RING * RING + (i + step) % RING) for i in range(SIDE * RING)]
    return lax.ppermute(block, "head", route)


def to_side(block):
    return lax.ppermute(block, "head", [(i, (i + RING) % (SIDE * RING)) for i in range(SIDE * RING)])


def to_core(block):
    return lax.ppermute(block, "section", [(i, i ^ 1) for i in range(lax.axis_size("section"))])


def gather_ring(block):
    found = {0: block}
    rows = block.shape[0] // 2
    for k in range(1, RING // 2):
        found[k] = to_turn(found[k - 1], -1)
        found[RING - k] = to_turn(found[(RING - k + 1) % RING], 1)
    k = RING // 2
    upper = to_turn(found[k - 1][:rows], -1)
    under = to_turn(found[k + 1][rows:], 1)
    found[k] = jnp.concatenate([upper, under], 0)
    return [found[k] for k in range(RING)]


def add(a, b):
    return (a.astype(f32) + b.astype(f32)).astype(bf16)


def reduce_ring(shares):
    rows = shares[0].shape[0] // 2
    far = RING // 2
    up = to_turn(shares[far][:rows], 1)
    down = to_turn(shares[far][rows:], -1)
    near, back = shares[far - 1], shares[far + 1]
    up = jnp.concatenate([add(up, near[:rows]), near[rows:]], 0)
    down = jnp.concatenate([back[:rows], add(down, back[rows:])], 0)
    for k in range(far - 2, 0, -1):
        up = add(to_turn(up, 1), shares[k])
        down = add(to_turn(down, -1), shares[RING - k])
    return shares[0].astype(f32) + to_turn(up, 1).astype(f32) + to_turn(down, -1).astype(f32)


def local(
    tokens,
    norm_gain,
    x_weight,
    gate_weight,
    dt_weight,
    dt_bias,
    decay_rate,
    skip_gain,
    bc_weight,
    out_gain,
    out_weight,
):
    rows, own = tokens.shape
    heads = decay_rate.shape[0]
    width = x_weight.shape[1]
    size_p = width // heads
    state_n = bc_weight.shape[1] // 2
    groups = lax.axis_size("head")
    sections = lax.axis_size("section")
    model = groups * own
    half = width // 2
    head, section = lax.axis_index("head"), lax.axis_index("section")
    core = section % 2
    place = jnp.stack([head // RING, head % RING, core, section // 2]).astype(jnp.int32)

    piece = lax.dynamic_slice_in_dim(bc_weight, core * state_n, state_n, 1)
    bc_one = lax.all_to_all(jnp.broadcast_to(piece[None], (groups, own, state_n)), "head", 0, 0)
    bc_one = bc_one.reshape(model, state_n)
    bc_two = to_core(bc_one)
    both = jnp.concatenate([tokens, to_side(tokens)], 0)
    blocks = gather_ring(both)

    small = jnp.zeros((8, 128), f32)
    small = small.at[0, :heads].set(dt_bias).at[1, :heads].set(decay_rate).at[2, :heads].set(skip_gain)
    dt_wide = jnp.pad(dt_weight, ((0, 0), (0, 128 - heads)))
    normed, x, writes, reads, cums, step, mine, theirs = on_chip(
        functools.partial(project_kernel, heads, size_p),
        [
            shape((rows, model), bf16),
            shape((rows, width)),
            shape((rows, state_n)),
            shape((rows, state_n)),
            shape((rows, 128)),
            shape((rows, 128)),
            shape((half + 16, state_n), bf16),
            shape((half + 16, state_n), bf16),
        ],
        [*blocks, norm_gain.reshape(groups, own), x_weight, dt_wide, bc_one, bc_two, small],
        place,
        [pltpu.VMEM((width, state_n), f32)],
        flops=2 * rows * model * (width + 3 * 128),
    )
    result, opened = on_chip(
        functools.partial(scan_kernel, heads, size_p, 256),
        [shape((rows, width)), shape((rows, width))],
        [normed, gate_weight, x, writes, reads, cums, step, small],
        flops=2 * rows * model * width + 12 * rows * 256 * (width + 3 * state_n),
        transcendentals=heads * rows * 256,
    )
    other = to_core(theirs)
    copies = on_chip(
        functools.partial(chip_kernel, size_p),
        [shape((sections // 2, half + 16, state_n), bf16)],
        [mine, other],
        place,
    )[0]
    chips = [list(range(c, sections, 2)) for c in range(2)]
    gathered = lax.all_to_all(copies, "section", 0, 0, axis_index_groups=chips)
    keep, send = on_chip(
        functools.partial(prefix_kernel, size_p),
        [shape((half, state_n)), shape((half, state_n), bf16)],
        [gathered, mine, other],
        place,
    )
    rest = to_core(send)
    shares = on_chip(
        functools.partial(finish_kernel, heads, size_p),
        [shape((SIDE * rows, own), bf16)] * RING,
        [result, opened, reads, cums, keep, rest, out_gain.reshape(1, width), out_weight],
        place,
        [pltpu.VMEM((width, state_n), f32)],
        flops=2 * rows * model * width,
    )
    summed = reduce_ring(shares)
    return tokens.astype(f32) + summed[:rows] + to_side(summed[rows:].astype(bf16)).astype(f32)


def solution(mesh):
    return jax.shard_map(
        local,
        mesh=mesh,
        in_specs=(
            P("section", "head"),
            P(),
            P(None, "head"),
            P(None, "head"),
            P(None, "head"),
            P("head"),
            P("head"),
            P("head"),
            P("head", None),
            P("head"),
            P("head", None),
        ),
        out_specs=P("section", "head"),
        check_vma=False,
    )
```

time: 851 us -> 190 us (0.22)
  waiting for transfers between devices: 729 us -> 49.6 us
  starting transfers between devices: 59.6 us -> 89 us
  blocking collectives: 0 us -> 23.5 us
  Pallas kernels: 0 us -> 17.5 us
  matrix products: 17 us -> 0 us
  between operations: 13.3 us -> 0.57 us
  local copies, waits for them, and re-layouts: 18.5 us -> 6.67 us
  other arithmetic: 12.2 us -> 2.33 us
    reduce_scatter x1 -> x0, waiting for transfers between devices: 233 us -> none  [local(): lax.psum_scatter(lax.dot_general(out_weight, ynorm, (((0,), (1,)), ((), (...]
    psum x1 -> x0, waiting for transfers between devices: 183 us -> none  [local(): lax.psum(jnp.dot(own_normed, bc_weight, preferred_element_type=jnp.float3...]
    ppermute x31 -> x21, waiting for transfers between devices: 200 us -> 49.6 us  [the longest x2 24.4 us: to_side(): lax.ppermute(block, 'head', [(i, (i + RING) % (SIDE * RING)) for i in ran...]
    all_gather x1 -> x0, waiting for transfers between devices: 112 us -> none  [local(): whole = lax.all_gather(tokens, 'head', axis=1, tiled=True)]
    all_to_all x0 -> x1, blocking collectives: none -> 23.5 us  [local(): gathered = lax.all_to_all(copies, 'section', 0, 0, axis_index_groups=chips)]
    pallas_call x0 -> x5, Pallas kernels: none -> 17.5 us  [on_chip(): pl.pallas_call(kernel, out_shape=outs, in_specs=specs, out_specs=[pl.Bloc...]
    dot_general x14 -> x0, matrix products: 17 us -> none  [the longest x1 2.87 us: local(): in_raw = jnp.dot(normed, x_weight, preferred_element_type=jnp.float32)]
    all_to_all x0 -> x1, starting transfers between devices: none -> 14.9 us  [local(): lax.all_to_all(jnp.broadcast_to(piece[None], (groups, own, state_n)), 'he...]
  transfers between devices with their start and end apart: 34 -> 22, of which waited for: 34 -> 12; matrix products, arithmetic and copies ran while one was open for 1% -> 3% of each run, Pallas kernels for 0% -> 2%
where the time goes in v2:
time: 190 us; the launch traced here: 189 us
  starting transfers between devices  89 us (47%)
  waiting for transfers between devices  49.6 us (26%)
  blocking collectives  23.5 us (12%)
  Pallas kernels  17.5 us (9%)
  local copies, waits for them, and re-layouts  6.67 us (4%)
  other arithmetic  2.33 us (1%)
    ppermute x16, starting transfers between devices, to_turn(): return lax.ppermute(block, 'head', route)  58.4 us
    ppermute x2, waiting for transfers between devices, to_side(): lax.ppermute(block, 'head', [(i, (i + RING) % (SIDE * RING)) for i in ran...  24.4 us
    ppermute x16, waiting for transfers between devices, to_turn(): return lax.ppermute(block, 'head', route)  24 us
    all_to_all x1, blocking collectives, local(): gathered = lax.all_to_all(copies, 'section', 0, 0, axis_index_groups=chips)  23.5 us
    pallas_call x5, Pallas kernels, on_chip(): pl.pallas_call(kernel, out_shape=outs, in_specs=specs, out_specs=[pl.Bloc...  17.5 us
    all_to_all x1, starting transfers between devices, local(): lax.all_to_all(jnp.broadcast_to(piece[None], (groups, own, state_n)), 'he...  14.9 us
    ppermute x2, starting transfers between devices, to_side(): lax.ppermute(block, 'head', [(i, (i + RING) % (SIDE * RING)) for i in ran...  9.66 us
    ppermute x3, starting transfers between devices, to_core(): lax.ppermute(block, 'section', [(i, i ^ 1) for i in range(lax.axis_size('...  6.07 us
  transfers between devices with their start and end apart: 22, of which 12 were waited for; matrix products, arithmetic and copies ran while one was open for 3% of the time, Pallas kernels for 2%

profile of v2, /device:TPU:8, one launch (start us, length us, event | category | flops | bytes accessed | tf_op | source)
XLA Modules:
  0.0 189.1 jit_solution(2803538126260962283)
XLA Ops:
  1.7 14.9 %all-to-all-start = ((bf16[16,128,128]{2,1,0:T(8,128)(2,1)}), bf16[16,128,128]{2,1,0:T(8,128)(2,1)S(1)}, u32[]{:S(2)}, u32[]{:S(2)}) async-start(bf16[16,128,128]{2,1,0:T(8,128)(2,1)} %broadcast_in_dim.2), calls=%async_computation | async-start | bytes 1048576 | tf_op jit(solution)/shard_map/all_to_all | solution.py:287
  16.7 7.7 %collective-permute-start = (bf16[512,128]{1,0:T(8,128)(2,1)}, bf16[512,128]{1,0:T(8,128)(2,1)S(1)}, u32[]{:S(2)}, u32[]{:S(2)}) collective-permute-start(bf16[512,128]{1,0:T(8,128)(2,1)} %param.17), channel_id=1, source_target_pairs={{0,8},{1,9},{2,10},{3,11},{4,12},{5,13},{6,14},{7,15},{8,0},{9,1},... | collective-permute-start | bytes 393224 | tf_op jit(solution)/shard_map/ppermute | solution.py:222
  25.3 14.1 %collective-permute-done = bf16[512,128]{1,0:T(8,128)(2,1)S(1)} collective-permute-done((bf16[512,128]{1,0:T(8,128)(2,1)}, bf16[512,128]{1,0:T(8,128)(2,1)S(1)}, u32[]{:S(2)}, u32[]{:S(2)}) %collective-permute-start) | collective-permute-done | bytes 131104 | tf_op jit(solution)/shard_map/ppermute | solution.py:222
  39.5 3.6 %collective-permute-start.5 = (bf16[1024,128]{1,0:T(8,128)(2,1)S(1)}, bf16[1024,128]{1,0:T(8,128)(2,1)S(1)}, u32[]{:S(2)}, u32[]{:S(2)}) collective-permute-start(bf16[1024,128]{1,0:T(8,128)(2,1)S(1)} %constant_dynamic-update-slice_fusion.refs_0_), channel_id=1, source_target_pairs={{0,1},{1,2},{2,3},{3,4},{4,5},{5,6},{6,7},{7,0},{8,9},{9,10},{10,1... | collective-permute-start | bytes 786440 | tf_op jit(solution)/shard_map/ppermute | solution.py:218
  43.1 3.5 %collective-permute-start.1 = (bf16[1024,128]{1,0:T(8,128)(2,1)S(1)}, bf16[1024,128]{1,0:T(8,128)(2,1)S(1)}, u32[]{:S(2)}, u32[]{:S(2)}) collective-permute-start(bf16[1024,128]{1,0:T(8,128)(2,1)S(1)} %constant_dynamic-update-slice_fusion.refs_0_), channel_id=1, source_target_pairs={{0,7},{1,0},{2,1},{3,2},{4,3},{5,4},{6,5},{7,6},{8,15},{9,8},{10,9... | collective-permute-start | bytes 786440 | tf_op jit(solution)/shard_map/ppermute | solution.py:218
  46.6 4.0 %collective-permute-done.5.refs_7_ = bf16[1024,128]{1,0:T(8,128)(2,1)S(1)} collective-permute-done((bf16[1024,128]{1,0:T(8,128)(2,1)S(1)}, bf16[1024,128]{1,0:T(8,128)(2,1)S(1)}, u32[]{:S(2)}, u32[]{:S(2)}) %collective-permute-start.5) | collective-permute-done | bytes 262176 | tf_op jit(solution)/shard_map/ppermute | solution.py:218
  50.6 2.4 %collective-permute-start.6 = (bf16[1024,128]{1,0:T(8,128)(2,1)S(1)}, bf16[1024,128]{1,0:T(8,128)(2,1)}, u32[]{:S(2)}, u32[]{:S(2)}) collective-permute-start(bf16[1024,128]{1,0:T(8,128)(2,1)S(1)} %collective-permute-done.5.refs_7_), channel_id=1, source_target_pairs={{0,1},{1,2},{2,3},{3,4},{4,5},{5,6},{6,7},{7,0},{8,9},{9,10},{10,1... | collective-permute-start | bytes 786440 | tf_op jit(solution)/shard_map/ppermute | solution.py:218
  53.0 4.7 %collective-permute-start.2 = (bf16[1024,128]{1,0:T(8,128)(2,1)S(1)}, bf16[1024,128]{1,0:T(8,128)(2,1)}, u32[]{:S(2)}, u32[]{:S(2)}) collective-permute-start(bf16[1024,128]{1,0:T(8,128)(2,1)S(1)} %collective-permute-done.1.refs_1_), channel_id=1, source_target_pairs={{0,7},{1,0},{2,1},{3,2},{4,3},{5,4},{6,5},{7,6},{8,15},{9,8},{10,9... | collective-permute-start | bytes 786440 | tf_op jit(solution)/shard_map/ppermute | solution.py:218
  62.8 5.1 %collective-permute-start.3 = (bf16[1024,128]{1,0:T(8,128)(2,1)}, bf16[1024,128]{1,0:T(8,128)(2,1)S(1)}, u32[]{:S(2)}, u32[]{:S(2)}) collective-permute-start(bf16[1024,128]{1,0:T(8,128)(2,1)} %collective-permute-done.2.refs_2_), channel_id=1, source_target_pairs={{0,7},{1,0},{2,1},{3,2},{4,3},{5,4},{6,5},{7,6},{8,15},{9,8},{10,9... | collective-permute-start | bytes 786440 | tf_op jit(solution)/shard_map/ppermute | solution.py:218
  68.0 3.7 %collective-permute-done.7.refs_5_ = bf16[1024,128]{1,0:T(8,128)(2,1)S(1)} collective-permute-done((bf16[1024,128]{1,0:T(8,128)(2,1)}, bf16[1024,128]{1,0:T(8,128)(2,1)S(1)}, u32[]{:S(2)}, u32[]{:S(2)}) %collective-permute-start.7) | collective-permute-done | bytes 262176 | tf_op jit(solution)/shard_map/ppermute | solution.py:218
  74.9 5.1 %collective-permute-start.4 = (bf16[512,128]{1,0:T(8,128)(2,1)}, bf16[512,128]{1,0:T(8,128)(2,1)}, u32[]{:S(2)}, u32[]{:S(2)}) collective-permute-start(bf16[512,128]{1,0:T(8,128)(2,1)} %slice.95), channel_id=1, source_target_pairs={{0,7},{1,0},{2,1},{3,2},{4,3},{5,4},{6,5},{7,6},{8,15},{9,8},{10,9... | collective-permute-start | bytes 393224 | tf_op jit(solution)/shard_map/ppermute | solution.py:218
  83.9 8.0 %shard_map.109 = (bf16[512,2048]{1,0:T(8,128)(2,1)S(1)}, f32[512,256]{1,0:T(8,128)S(1)}, f32[512,128]{1,0:T(8,128)S(1)}, f32[512,128]{1,0:T(8,128)S(1)}, f32[512...) custom-call(s32[4]{0:T(128)S(1)} %pad_add_fusion.place, ...), custom_call_target="tpu_custom_call" | custom-call | flops 1342177280 | bytes 8474640 | tf_op jit(solution)/shard_map/pallas_call | solution.py:201
  95.8 23.5 %all_to_all.10.gathered = bf16[16,144,128]{2,1,0:T(8,128)(2,1)S(1)} all-to-all(bf16[16,144,128]{2,1,0:T(8,128)(2,1)S(1)} %shard_map.111), channel_id=1, replica_groups={{0,32,64,96,128,160,192,224,256,288,320,352,384,416,448,480},{16,48,80,..., dimensions={0} | all-to-all | bytes 1179648 | tf_op jit(solution)/shard_map/all_to_all | solution.py:328
  120.2 2.1 %collective-permute-start.11 = (bf16[128,128]{1,0:T(8,128)(2,1)S(1)}, bf16[128,128]{1,0:T(8,128)(2,1)S(1)}, u32[]{:S(2)}, u32[]{:S(2)}) collective-permute-start(bf16[128,128]{1,0:T(8,128)(2,1)S(1)} %get-tuple-element.72), channel_id=1, source_target_pairs={{0,16},{16,0},{32,48},{48,32},{64,80},{80,64},{96,112},{112,96},{1... | collective-permute-start | bytes 98312 | tf_op jit(solution)/shard_map/ppermute | solution.py:226
  122.4 4.1 %shard_map.110 = (f32[512,256]{1,0:T(8,128)S(1)}, f32[512,256]{1,0:T(8,128)S(1)}) custom-call(bf16[512,2048]{1,0:T(8,128)(2,1)S(1)} %get-tuple-element.61.normed, bf16[2048,256]{1,0:T(8,128)(2,1)S(1)} %copy-done.4, f32[512,256]{1,0:T(8,128)S(1)} %get-tuple-element.62.x_in, f32[512,128]{1,0:T(8,128)S(1)} %get-tuple-element.63.writes_in, ...), custom_call_target="tpu_custom_call" | custom-call | flops 1543503872 | bytes 5771264 | tf_op jit(solution)/shard_map/pallas_call | solution.py:201
  126.5 3.9 %shard_map.113 = (bf16[1024,128]{1,0:T(8,128)(2,1)S(1)}, bf16[1024,128]{1,0:T(8,128)(2,1)S(1)}, bf16[1024,128]{1,0:T(8,128)(2,1)S(1)}, bf16[1024,128]{1,0:T(8,12...) custom-call(s32[4]{0:T(128)S(1)} %pad_add_fusion.place, ...), custom_call_target="tpu_custom_call" | custom-call | flops 536870912 | bytes 4817936 | tf_op jit(solution)/shard_map/pallas_call | solution.py:201
  130.4 5.6 %collective-permute-start.16 = (bf16[512,128]{1,0:T(8,128)(2,1)S(1)}, bf16[512,128]{1,0:T(8,128)(2,1)S(1)}, u32[]{:S(2)}, u32[]{:S(2)}) collective-permute-start(bf16[512,128]{1,0:T(8,128)(2,1)S(1)} %get-tuple-element.82), channel_id=1, source_target_pairs={{0,7},{1,0},{2,1},{3,2},{4,3},{5,4},{6,5},{7,6},{8,15},{9,8},{10,9... | collective-permute-start | bytes 393224 | tf_op jit(solution)/shard_map/ppermute | solution.py:218
  139.4 5.6 %collective-permute-start.17 = (bf16[1024,128]{1,0:T(8,128)(2,1)S(1)}, bf16[1024,128]{1,0:T(8,128)(2,1)S(1)}, u32[]{:S(2)}, u32[]{:S(2)}) collective-permute-start(bf16[1024,128]{1,0:T(8,128)(2,1)S(1)} %pad_maximum_fusion.2), channel_id=1, source_target_pairs={{0,7},{1,0},{2,1},{3,2},{4,3},{5,4},{6,5},{7,6},{8,15},{9,8},{10,9... | collective-permute-start | bytes 786440 | tf_op jit(solution)/shard_map/ppermute | solution.py:218
  147.0 3.4 %collective-permute-done.17 = bf16[1024,128]{1,0:T(8,128)(2,1)S(1)} collective-permute-done((bf16[1024,128]{1,0:T(8,128)(2,1)S(1)}, bf16[1024,128]{1,0:T(8,128)(2,1)S(1)}, u32[]{:S(2)}, u32[]{:S(2)}) %collective-permute-start.17) | collective-permute-done | bytes 262176 | tf_op jit(solution)/shard_map/ppermute | solution.py:218
  150.5 5.7 %collective-permute-start.18 = (bf16[1024,128]{1,0:T(8,128)(2,1)S(1)}, bf16[1024,128]{1,0:T(8,128)(2,1)S(1)}, u32[]{:S(2)}, u32[]{:S(2)}) collective-permute-start(bf16[1024,128]{1,0:T(8,128)(2,1)S(1)} %add_convert_fusion.1), channel_id=1, source_target_pairs={{0,7},{1,0},{2,1},{3,2},{4,3},{5,4},{6,5},{7,6},{8,15},{9,8},{10,9... | collective-permute-start | bytes 786440 | tf_op jit(solution)/shard_map/ppermute | solution.py:218
  158.3 2.5 %collective-permute-done.18 = bf16[1024,128]{1,0:T(8,128)(2,1)S(1)} collective-permute-done((bf16[1024,128]{1,0:T(8,128)(2,1)S(1)}, bf16[1024,128]{1,0:T(8,128)(2,1)S(1)}, u32[]{:S(2)}, u32[]{:S(2)}) %collective-permute-start.18) | collective-permute-done | bytes 262176 | tf_op jit(solution)/shard_map/ppermute | solution.py:218
  160.9 5.6 %collective-permute-start.19 = (bf16[1024,128]{1,0:T(8,128)(2,1)S(1)}, bf16[1024,128]{1,0:T(8,128)(2,1)S(1)}, u32[]{:S(2)}, u32[]{:S(2)}) collective-permute-start(bf16[1024,128]{1,0:T(8,128)(2,1)S(1)} %add_convert_fusion), channel_id=1, source_target_pairs={{0,7},{1,0},{2,1},{3,2},{4,3},{5,4},{6,5},{7,6},{8,15},{9,8},{10,9... | collective-permute-start | bytes 786440 | tf_op jit(solution)/shard_map/ppermute | solution.py:218
  170.4 5.7 %collective-permute-done.15 = bf16[1024,128]{1,0:T(8,128)(2,1)S(1)} collective-permute-done((bf16[1024,128]{1,0:T(8,128)(2,1)S(1)}, bf16[1024,128]{1,0:T(8,128)(2,1)S(1)}, u32[]{:S(2)}, u32[]{:S(2)}) %collective-permute-start.15) | collective-permute-done | bytes 262176 | tf_op jit(solution)/shard_map/ppermute | solution.py:218
  178.1 10.2 %collective-permute-done.20 = bf16[512,128]{1,0:T(8,128)(2,1)S(1)} collective-permute-done((bf16[512,128]{1,0:T(8,128)(2,1)S(1)}, bf16[512,128]{1,0:T(8,128)(2,1)S(1)}, u32[]{:S(2)}, u32[]{:S(2)}) %collective-permute-start.20) | collective-permute-done | bytes 131104 | tf_op jit(solution)/shard_map/ppermute | solution.py:222
  (75 shorter events, 33.8 us)
Async XLA Ops:
  1.7 82.1 %copy-start.3 = (bf16[2048,256]{1,0:T(8,128)(2,1)S(1)}, bf16[2048,256]{1,0:T(8,128)(2,1)}, u32[]{:S(2)}) copy-start(bf16[2048,256]{1,0:T(8,128)(2,1)} %refs_9_.1) | copy-start | bytes 3145732
  1.7 82.1 %copy-start.5 = (f32[2048]{0:T(1024)S(1)}, f32[2048]{0:T(1024)}, u32[]{:S(2)}) copy-start(f32[2048]{0:T(1024)} %param.18) | copy-start | bytes 24580
  1.7 55.9 %all-to-all-start = ((bf16[16,128,128]{2,1,0:T(8,128)(2,1)}), bf16[16,128,128]{2,1,0:T(8,128)(2,1)S(1)}, u32[]{:S(2)}, u32[]{:S(2)}) async-start(bf16[16,128,128]{2,1,0:T(8,128)(2,1)} %broadcast_in_dim.2), calls=%async_computation | async-start | bytes 1048576 | tf_op jit(solution)/shard_map/all_to_all | solution.py:287
  16.7 22.8 %collective-permute-start = (bf16[512,128]{1,0:T(8,128)(2,1)}, bf16[512,128]{1,0:T(8,128)(2,1)S(1)}, u32[]{:S(2)}, u32[]{:S(2)}) collective-permute-start(bf16[512,128]{1,0:T(8,128)(2,1)} %param.17), channel_id=1, source_target_pairs={{0,8},{1,9},{2,10},{3,11},{4,12},{5,13},{6,14},{7,15},{8,0},{9,1},... | collective-permute-start | bytes 393224 | tf_op jit(solution)/shard_map/ppermute | solution.py:222
  39.5 11.1 %collective-permute-start.5 = (bf16[1024,128]{1,0:T(8,128)(2,1)S(1)}, bf16[1024,128]{1,0:T(8,128)(2,1)S(1)}, u32[]{:S(2)}, u32[]{:S(2)}) collective-permute-start(bf16[1024,128]{1,0:T(8,128)(2,1)S(1)} %constant_dynamic-update-slice_fusion.refs_0_), channel_id=1, source_target_pairs={{0,1},{1,2},{2,3},{3,4},{4,5},{5,6},{6,7},{7,0},{8,9},{9,10},{10,1... | collective-permute-start | bytes 786440 | tf_op jit(solution)/shard_map/ppermute | solution.py:218
  43.1 9.9 %collective-permute-start.1 = (bf16[1024,128]{1,0:T(8,128)(2,1)S(1)}, bf16[1024,128]{1,0:T(8,128)(2,1)S(1)}, u32[]{:S(2)}, u32[]{:S(2)}) collective-permute-start(bf16[1024,128]{1,0:T(8,128)(2,1)S(1)} %constant_dynamic-update-slice_fusion.refs_0_), channel_id=1, source_target_pairs={{0,7},{1,0},{2,1},{3,2},{4,3},{5,4},{6,5},{7,6},{8,15},{9,8},{10,9... | collective-permute-start | bytes 786440 | tf_op jit(solution)/shard_map/ppermute | solution.py:218
  50.6 10.3 %collective-permute-start.6 = (bf16[1024,128]{1,0:T(8,128)(2,1)S(1)}, bf16[1024,128]{1,0:T(8,128)(2,1)}, u32[]{:S(2)}, u32[]{:S(2)}) collective-permute-start(bf16[1024,128]{1,0:T(8,128)(2,1)S(1)} %collective-permute-done.5.refs_7_), channel_id=1, source_target_pairs={{0,1},{1,2},{2,3},{3,4},{4,5},{5,6},{6,7},{7,0},{8,9},{9,10},{10,1... | collective-permute-start | bytes 786440 | tf_op jit(solution)/shard_map/ppermute | solution.py:218
  53.0 9.8 %collective-permute-start.2 = (bf16[1024,128]{1,0:T(8,128)(2,1)S(1)}, bf16[1024,128]{1,0:T(8,128)(2,1)}, u32[]{:S(2)}, u32[]{:S(2)}) collective-permute-start(bf16[1024,128]{1,0:T(8,128)(2,1)S(1)} %collective-permute-done.1.refs_1_), channel_id=1, source_target_pairs={{0,7},{1,0},{2,1},{3,2},{4,3},{5,4},{6,5},{7,6},{8,15},{9,8},{10,9... | collective-permute-start | bytes 786440 | tf_op jit(solution)/shard_map/ppermute | solution.py:218
  57.7 26.2 %collective-permute-start.9 = (bf16[2048,128]{1,0:T(8,128)(2,1)S(1)}, bf16[2048,128]{1,0:T(8,128)(2,1)S(1)}, u32[]{:S(2)}, u32[]{:S(2)}) collective-permute-start(bf16[2048,128]{1,0:T(8,128)(2,1)S(1)} %bitcast.10), channel_id=1, source_target_pairs={{0,16},{16,0},{32,48},{48,32},{64,80},{80,64},{96,112},{112,96},{1... | collective-permute-start | bytes 1572872 | tf_op jit(solution)/shard_map/ppermute | solution.py:226
  60.9 10.7 %collective-permute-start.7 = (bf16[1024,128]{1,0:T(8,128)(2,1)}, bf16[1024,128]{1,0:T(8,128)(2,1)S(1)}, u32[]{:S(2)}, u32[]{:S(2)}) collective-permute-start(bf16[1024,128]{1,0:T(8,128)(2,1)} %collective-permute-done.6.refs_6_), channel_id=1, source_target_pairs={{0,1},{1,2},{2,3},{3,4},{4,5},{5,6},{6,7},{7,0},{8,9},{9,10},{10,1... | collective-permute-start | bytes 786440 | tf_op jit(solution)/shard_map/ppermute | solution.py:218
  62.8 11.4 %collective-permute-start.3 = (bf16[1024,128]{1,0:T(8,128)(2,1)}, bf16[1024,128]{1,0:T(8,128)(2,1)S(1)}, u32[]{:S(2)}, u32[]{:S(2)}) collective-permute-start(bf16[1024,128]{1,0:T(8,128)(2,1)} %collective-permute-done.2.refs_2_), channel_id=1, source_target_pairs={{0,7},{1,0},{2,1},{3,2},{4,3},{5,4},{6,5},{7,6},{8,15},{9,8},{10,9... | collective-permute-start | bytes 786440 | tf_op jit(solution)/shard_map/ppermute | solution.py:218
  72.3 10.5 %collective-permute-start.8 = (bf16[512,128]{1,0:T(8,128)(2,1)}, bf16[512,128]{1,0:T(8,128)(2,1)}, u32[]{:S(2)}, u32[]{:S(2)}) collective-permute-start(bf16[512,128]{1,0:T(8,128)(2,1)} %slice.96), channel_id=1, source_target_pairs={{0,1},{1,2},{2,3},{3,4},{4,5},{5,6},{6,7},{7,0},{8,9},{9,10},{10,1... | collective-permute-start | bytes 393224 | tf_op jit(solution)/shard_map/ppermute | solution.py:218
  74.9 7.9 %collective-permute-start.4 = (bf16[512,128]{1,0:T(8,128)(2,1)}, bf16[512,128]{1,0:T(8,128)(2,1)}, u32[]{:S(2)}, u32[]{:S(2)}) collective-permute-start(bf16[512,128]{1,0:T(8,128)(2,1)} %slice.95), channel_id=1, source_target_pairs={{0,7},{1,0},{2,1},{3,2},{4,3},{5,4},{6,5},{7,6},{8,15},{9,8},{10,9... | collective-permute-start | bytes 393224 | tf_op jit(solution)/shard_map/ppermute | solution.py:218
  91.9 3.2 %collective-permute-start.10 = (bf16[144,128]{1,0:T(8,128)(2,1)S(1)}, bf16[144,128]{1,0:T(8,128)(2,1)S(1)}, u32[]{:S(2)}, u32[]{:S(2)}) collective-permute-start(bf16[144,128]{1,0:T(8,128)(2,1)S(1)} %get-tuple-element.70), channel_id=1, source_target_pairs={{0,16},{16,0},{32,48},{48,32},{64,80},{80,64},{96,112},{112,96},{1... | collective-permute-start | bytes 110600 | tf_op jit(solution)/shard_map/ppermute | solution.py:226
  120.2 6.2 %collective-permute-start.11 = (bf16[128,128]{1,0:T(8,128)(2,1)S(1)}, bf16[128,128]{1,0:T(8,128)(2,1)S(1)}, u32[]{:S(2)}, u32[]{:S(2)}) collective-permute-start(bf16[128,128]{1,0:T(8,128)(2,1)S(1)} %get-tuple-element.72), channel_id=1, source_target_pairs={{0,16},{16,0},{32,48},{48,32},{64,80},{80,64},{96,112},{112,96},{1... | collective-permute-start | bytes 98312 | tf_op jit(solution)/shard_map/ppermute | solution.py:226
  130.4 9.0 %collective-permute-start.16 = (bf16[512,128]{1,0:T(8,128)(2,1)S(1)}, bf16[512,128]{1,0:T(8,128)(2,1)S(1)}, u32[]{:S(2)}, u32[]{:S(2)}) collective-permute-start(bf16[512,128]{1,0:T(8,128)(2,1)S(1)} %get-tuple-element.82), channel_id=1, source_target_pairs={{0,7},{1,0},{2,1},{3,2},{4,3},{5,4},{6,5},{7,6},{8,15},{9,8},{10,9... | collective-permute-start | bytes 393224 | tf_op jit(solution)/shard_map/ppermute | solution.py:218
  136.0 9.0 %collective-permute-start.12 = (bf16[512,128]{1,0:T(8,128)(2,1)S(1)}, bf16[512,128]{1,0:T(8,128)(2,1)S(1)}, u32[]{:S(2)}, u32[]{:S(2)}) collective-permute-start(bf16[512,128]{1,0:T(8,128)(2,1)S(1)} %get-tuple-element.81), channel_id=1, source_target_pairs={{0,1},{1,2},{2,3},{3,4},{4,5},{5,6},{6,7},{7,0},{8,9},{9,10},{10,1... | collective-permute-start | bytes 393224 | tf_op jit(solution)/shard_map/ppermute | solution.py:218
  139.4 11.0 %collective-permute-start.17 = (bf16[1024,128]{1,0:T(8,128)(2,1)S(1)}, bf16[1024,128]{1,0:T(8,128)(2,1)S(1)}, u32[]{:S(2)}, u32[]{:S(2)}) collective-permute-start(bf16[1024,128]{1,0:T(8,128)(2,1)S(1)} %pad_maximum_fusion.2), channel_id=1, source_target_pairs={{0,7},{1,0},{2,1},{3,2},{4,3},{5,4},{6,5},{7,6},{8,15},{9,8},{10,9... | collective-permute-start | bytes 786440 | tf_op jit(solution)/shard_map/ppermute | solution.py:218
  145.1 11.2 %collective-permute-start.13 = (bf16[1024,128]{1,0:T(8,128)(2,1)S(1)}, bf16[1024,128]{1,0:T(8,128)(2,1)S(1)}, u32[]{:S(2)}, u32[]{:S(2)}) collective-permute-start(bf16[1024,128]{1,0:T(8,128)(2,1)S(1)} %pad_maximum_fusion.1), channel_id=1, source_target_pairs={{0,1},{1,2},{2,3},{3,4},{4,5},{5,6},{6,7},{7,0},{8,9},{9,10},{10,1... | collective-permute-start | bytes 786440 | tf_op jit(solution)/shard_map/ppermute | solution.py:218
  150.5 10.3 %collective-permute-start.18 = (bf16[1024,128]{1,0:T(8,128)(2,1)S(1)}, bf16[1024,128]{1,0:T(8,128)(2,1)S(1)}, u32[]{:S(2)}, u32[]{:S(2)}) collective-permute-start(bf16[1024,128]{1,0:T(8,128)(2,1)S(1)} %add_convert_fusion.1), channel_id=1, source_target_pairs={{0,7},{1,0},{2,1},{3,2},{4,3},{5,4},{6,5},{7,6},{8,15},{9,8},{10,9... | collective-permute-start | bytes 786440 | tf_op jit(solution)/shard_map/ppermute | solution.py:218
  156.4 10.1 %collective-permute-start.14 = (bf16[1024,128]{1,0:T(8,128)(2,1)S(1)}, bf16[1024,128]{1,0:T(8,128)(2,1)S(1)}, u32[]{:S(2)}, u32[]{:S(2)}) collective-permute-start(bf16[1024,128]{1,0:T(8,128)(2,1)S(1)} %add_convert_fusion.3), channel_id=1, source_target_pairs={{0,1},{1,2},{2,3},{3,4},{4,5},{5,6},{6,7},{7,0},{8,9},{9,10},{10,1... | collective-permute-start | bytes 786440 | tf_op jit(solution)/shard_map/ppermute | solution.py:218
  160.9 9.5 %collective-permute-start.19 = (bf16[1024,128]{1,0:T(8,128)(2,1)S(1)}, bf16[1024,128]{1,0:T(8,128)(2,1)S(1)}, u32[]{:S(2)}, u32[]{:S(2)}) collective-permute-start(bf16[1024,128]{1,0:T(8,128)(2,1)S(1)} %add_convert_fusion), channel_id=1, source_target_pairs={{0,7},{1,0},{2,1},{3,2},{4,3},{5,4},{6,5},{7,6},{8,15},{9,8},{10,9... | collective-permute-start | bytes 786440 | tf_op jit(solution)/shard_map/ppermute | solution.py:218
  166.6 9.5 %collective-permute-start.15 = (bf16[1024,128]{1,0:T(8,128)(2,1)S(1)}, bf16[1024,128]{1,0:T(8,128)(2,1)S(1)}, u32[]{:S(2)}, u32[]{:S(2)}) collective-permute-start(bf16[1024,128]{1,0:T(8,128)(2,1)S(1)} %add_convert_fusion.2), channel_id=1, source_target_pairs={{0,1},{1,2},{2,3},{3,4},{4,5},{5,6},{6,7},{7,0},{8,9},{9,10},{10,1... | collective-permute-start | bytes 786440 | tf_op jit(solution)/shard_map/ppermute | solution.py:218
  176.2 12.2 %collective-permute-start.20 = (bf16[512,128]{1,0:T(8,128)(2,1)S(1)}, bf16[512,128]{1,0:T(8,128)(2,1)S(1)}, u32[]{:S(2)}, u32[]{:S(2)}) collective-permute-start(bf16[512,128]{1,0:T(8,128)(2,1)S(1)} %slice.105), channel_id=1, source_target_pairs={{0,8},{1,9},{2,10},{3,11},{4,12},{5,13},{6,14},{7,15},{8,0},{9,1},... | collective-permute-start | bytes 393224 | tf_op jit(solution)/shard_map/ppermute | solution.py:222
  (9 other events, 401.1 us)

commit v3 on v2

--- a/solution.py
+++ b/solution.py
@@ -32,10 +32,42 @@
     return lax.broadcasted_iota(jnp.int32, shape, dim)
 
 
+def split(v):
+    high = v.astype(bf16)
+    return high, (v - high.astype(f32)).astype(bf16)
+
+
+def dot_pair(a, exact, dims=((1,), (0,))):
+    high, low = split(a)
+    return dot(high, exact, dims) + dot(low, exact, dims)
+
+
+def dot_three(a, b, dims=((1,), (0,))):
+    a_high, a_low = split(a)
+    b_high, b_low = split(b)
+    return dot(a_high, b_high, dims) + (dot(a_high, b_low, dims) + dot(a_low, b_high, dims))
+
+
+def running_sum(v):
+    rows = v.shape[0]
+    lower = (iota((rows, rows), 0) >= iota((rows, rows), 1)).astype(bf16)
+    high, rest = split(v)
+    left = v - high.astype(f32)
+    middle = rest
+    low = (left - middle.astype(f32)).astype(bf16)
+    return dot(lower, high) + (dot(lower, middle) + dot(lower, low))
+
+
 def spread(heads_on_lanes, width, size_p):
     lanes = heads_on_lanes.shape[1]
-    pick = (iota((lanes, width), 1) // size_p == iota((lanes, width), 0)).astype(f32)
-    return dot(heads_on_lanes, pick, precision=highest)
+    pick = (iota((lanes, width), 1) // size_p == iota((lanes, width), 0)).astype(bf16)
+    return dot_pair(heads_on_lanes, pick)
+
+
+def lanes_of(row, scratch):
+    scratch[...] = jnp.zeros_like(scratch)
+    scratch[0:1, 0 : row.shape[1]] = row[...]
+    return scratch[0:1, :]
 
 
 def column(row, rows, size_p, first):
@@ -55,48 +87,58 @@
     return tail[0:1] + tail[1:2]
 
 
-def project_kernel(heads, size_p, place, *refs):
+def norm_kernel(rows, place, *refs):
     blocks = refs[:RING]
-    (gain, x_weight, dt_weight, bc_one, bc_two, small) = refs[RING : RING + 6]
-    (normed, x_out, writes_out, reads_out, cums_out, step_out, mine, theirs, state) = refs[RING + 6 :]
-    rows = normed.shape[0]
+    gain, normed, bc_half = refs[RING:]
     own = blocks[0].shape[1]
-    side, turn, core = place[0], place[1], place[2]
+    side, turn = place[0], place[1]
+    piece = blocks[0].shape[0] // SIDE
 
     def parts():
         for k in range(RING):
             for j in range(SIDE):
                 head = lax.rem(side + j, SIDE) * RING + lax.rem(turn + k, RING)
-                yield blocks[k][j * rows : (j + 1) * rows, :].astype(f32), head
+                yield blocks[k], j * piece, head
 
     squares = jnp.zeros((rows, own), f32)
-    for value, _ in parts():
+    for block, at, _ in parts():
+        value = block[at : at + rows, :].astype(f32)
         squares = squares + value * value
     mean = jnp.sum(squares, axis=1, keepdims=True) / (RING * SIDE * own)
     scale = lax.rsqrt(mean + eps)
-    for value, head in parts():
+    for block, at, head in parts():
+        value = block[at : at + rows, :].astype(f32)
         spot = pl.multiple_of(head * own, own)
         normed[:, pl.ds(spot, own)] = (value * scale * gain[pl.ds(head, 1), :]).astype(bf16)
+        bc_half[pl.ds(spot, own), :] = block[at + rows : at + piece, :]
+
+
+def project_kernel(heads, size_p, normed, x_weight, dt_weight, bias, rate, x_out, tail_out, cums_out, step_out, wide, line):
+    rows = normed.shape[0]
+    wide[...] = jnp.zeros_like(wide)
+    wide[0:heads, :] = dt_weight[...]
     whole = normed[...]
-    step = softplus(dot(whole, dt_weight[...]) + small[0:1, :])
-    decay = -small[1:2, :] * step
-    lower = (iota((rows, rows), 0) >= iota((rows, rows), 1)).astype(f32)
-    cums = dot(lower, decay, precision=highest)
-    one = dot(whole, bc_one[...])
-    two = dot(whole, bc_two[...])
-    writes = jnp.where(core == 0, one, two)
-    reads = jnp.where(core == 0, two, one)
+    step = softplus(dot(whole, wide[...], ((1,), (1,))) + lanes_of(bias, line))
+    decay = -lanes_of(rate, line) * step
+    cums = running_sum(decay)
     x = silu(dot(whole, x_weight[...]))
+    last = cums[rows - 1 : rows, :]
+    tail = spread(jnp.exp(last - cums) * step, heads * size_p, size_p)
     x_out[...] = x
-    writes_out[...] = writes
-    reads_out[...] = reads
+    tail_out[...] = x * tail
     cums_out[...] = cums
     step_out[...] = step
-    last = cums[rows - 1 : rows, :]
-    tail = spread(jnp.exp(last - cums) * step, heads * size_p, size_p)
-    state[...] = dot((x * tail).T, writes, precision=highest)
-    half = heads * size_p // 2
-    logs = log_rows(last)
+
+
+def state_kernel(place, normed, tailed, bc_one, bc_two, cums, writes_out, mine, theirs, state):
+    core = place[2]
+    rows, width = tailed.shape
+    weight = jnp.where(core == 0, bc_one[...], bc_two[...])
+    writes = dot(normed[...], weight)
+    writes_out[...] = writes
+    state[...] = dot_three(tailed[...].T, writes)
+    half = width // 2
+    logs = log_rows(cums[rows - 1 : rows, :])
     mine[0:half, :] = state[pl.ds(pl.multiple_of(core * half, half), half), :].astype(bf16)
     mine[half : half + 16, :] = logs
     theirs[0:half, :] = state[pl.ds(pl.multiple_of((1 - core) * half, half), half), :].astype(bf16)
@@ -121,7 +163,7 @@
         copies[i, half : half + 16, :] = logs
 
 
-def prefix_kernel(size_p, place, gathered, mine, other, keep, send):
+def prefix_kernel(size_p, place, gathered, mine, other, after, keep, send):
     half = mine.shape[0] - 16
     core, chip = place[2], place[3]
     first = core * (half // size_p)
@@ -137,37 +179,39 @@
     send[...] = jnp.where(early, later, state).astype(bf16)
 
 
-def scan_kernel(heads, size_p, block, normed, gate_weight, x_in, writes_in, reads_in, cums_in, step_in, small, result, opened):
+def scan_kernel(heads, size_p, block, place, normed, gate_weight, bc_one, bc_two, x_in, writes_in, cums_in, step_in, gain, *refs):
+    result, opened, reads_out, line = refs
     rows = x_in.shape[0]
     width = heads * size_p
+    weight = jnp.where(place[2] == 0, bc_two[...], bc_one[...])
+    reads_out[...] = dot(normed[...], weight)
     opened[...] = silu(dot(normed[...], gate_weight[...]))
     lower = iota((block, block), 0) >= iota((block, block), 1)
-    skip = spread(small[0:8, :], width, size_p)[2:3]
+    skip = spread(lanes_of(gain, line) + jnp.zeros((8, line.shape[1]), f32), width, size_p)[0:1]
     state = None
     base = None
     for b in range(rows // block):
         span = slice(b * block, (b + 1) * block)
-        x, writes, reads = x_in[span, :], writes_in[span, :], reads_in[span, :]
+        x, writes, reads = x_in[span, :], writes_in[span, :], reads_out[span, :]
         cums, step = cums_in[span, :], step_in[span, :]
         cums_t, step_t = cums.T, step.T
-        scores = dot(reads, writes, ((1,), (1,)), highest)
+        scores = dot_three(reads, writes, ((1,), (1,)))
         made = []
         for h in range(heads):
             gap = cums[:, h : h + 1] - cums_t[h : h + 1, :]
             mixing = jnp.exp(jnp.where(lower, gap, -jnp.inf)) * scores * step_t[h : h + 1, :]
-            made.append(dot(mixing, x[:, h * size_p : (h + 1) * size_p], precision=highest))
+            made.append(dot_three(mixing, x[:, h * size_p : (h + 1) * size_p]))
         y = jnp.concatenate(made, axis=1) + skip * x
         if state is not None:
-            carried = dot(reads, state, ((1,), (1,)), highest)
+            carried = dot_three(reads, state, ((1,), (1,)))
             y = y + spread(jnp.exp(cums - base), width, size_p) * carried
         result[span, :] = y
         if (b + 1) * block < rows:
             last = cums[block - 1 : block, :]
             tail = spread(jnp.exp(last - cums) * step, width, size_p)
-            fresh = dot((x * tail).T, writes, precision=highest)
+            fresh = dot_three((x * tail).T, writes)
             if state is not None:
-                grow = jnp.exp(column(last - base, width, size_p, 0))
-                fresh = grow * state + fresh
+                fresh = jnp.exp(column(last - base, width, size_p, 0)) * state + fresh
             state, base = fresh, last
 
 
@@ -179,11 +223,11 @@
     side, turn, core = place[0], place[1], place[2]
     state[pl.ds(pl.multiple_of(core * half, half), half), :] = keep[...]
     state[pl.ds(pl.multiple_of((1 - core) * half, half), half), :] = other[...].astype(f32)
-    carried = dot(reads[...], state[...], ((1,), (1,)), highest)
+    carried = dot_pair(reads[...], state[...].astype(bf16), ((1,), (1,)))
     y = result[...] + spread(jnp.exp(cums[...]), width, size_p) * carried
     g = y * opened[...]
-    same = (iota((width, width), 0) // size_p == iota((width, width), 1) // size_p).astype(f32)
-    mean = dot(g * g, same, precision=highest) / size_p
+    same = (iota((width, width), 0) // size_p == iota((width, width), 1) // size_p).astype(bf16)
+    mean = dot_pair(g * g, same) / size_p
     ynorm = (g * lax.rsqrt(mean + eps) * out_gain[...]).astype(bf16)
     for k in range(RING):
         for j in range(SIDE):
@@ -192,8 +236,8 @@
             shares[k][j * rows : (j + 1) * rows, :] = dot(ynorm, out_weight[:, pl.ds(spot, own)]).astype(bf16)
 
 
-def on_chip(kernel, outs, args, place=None, scratch=(), flops=0, transcendentals=0):
-    specs = [pl.BlockSpec(memory_space=pltpu.VMEM)] * len(args)
+def on_chip(kernel, outs, args, place=None, scratch=(), flops=0, transcendentals=0, whole=()):
+    specs = [pl.BlockSpec(memory_space=pl.ANY if i in whole else pltpu.VMEM) for i in range(len(args))]
     if place is not None:
         specs = [pl.BlockSpec(memory_space=pltpu.SMEM)] + specs
         args = [place] + list(args)
@@ -228,14 +272,10 @@
 
 def gather_ring(block):
     found = {0: block}
-    rows = block.shape[0] // 2
     for k in range(1, RING // 2):
         found[k] = to_turn(found[k - 1], -1)
         found[RING - k] = to_turn(found[(RING - k + 1) % RING], 1)
-    k = RING // 2
-    upper = to_turn(found[k - 1][:rows], -1)
-    under = to_turn(found[k + 1][rows:], 1)
-    found[k] = jnp.concatenate([upper, under], 0)
+    found[RING // 2] = to_turn(found[RING // 2 - 1], -1)
     return [found[k] for k in range(RING)]
 
 
@@ -244,17 +284,14 @@
 
 
 def reduce_ring(shares):
-    rows = shares[0].shape[0] // 2
     far = RING // 2
-    up = to_turn(shares[far][:rows], 1)
-    down = to_turn(shares[far][rows:], -1)
-    near, back = shares[far - 1], shares[far + 1]
-    up = jnp.concatenate([add(up, near[:rows]), near[rows:]], 0)
-    down = jnp.concatenate([back[:rows], add(down, back[rows:])], 0)
-    for k in range(far - 2, 0, -1):
-        up = add(to_turn(up, 1), shares[k])
-        down = add(to_turn(down, -1), shares[RING - k])
-    return shares[0].astype(f32) + to_turn(up, 1).astype(f32) + to_turn(down, -1).astype(f32)
+    up = to_turn(shares[far], 1)
+    down = None
+    for k in range(far - 1, 0, -1):
+        back = shares[RING - k]
+        up = to_turn(add(up, shares[k]), 1)
+        down = to_turn(back if down is None else add(down, back), -1)
+    return shares[0].astype(f32) + up.astype(f32) + down.astype(f32)
 
 
 def local(
@@ -284,37 +321,37 @@
     place = jnp.stack([head // RING, head % RING, core, section // 2]).astype(jnp.int32)
 
     piece = lax.dynamic_slice_in_dim(bc_weight, core * state_n, state_n, 1)
-    bc_one = lax.all_to_all(jnp.broadcast_to(piece[None], (groups, own, state_n)), "head", 0, 0)
-    bc_one = bc_one.reshape(model, state_n)
+    packed = jnp.concatenate([tokens, piece], 0)
+    blocks = gather_ring(jnp.concatenate([packed, to_side(packed)], 0))
+    normed, bc_one = on_chip(
+        functools.partial(norm_kernel, rows),
+        [shape((rows, model), bf16), shape((model, state_n), bf16)],
+        [*blocks, norm_gain.reshape(groups, own)],
+        place,
+    )
     bc_two = to_core(bc_one)
-    both = jnp.concatenate([tokens, to_side(tokens)], 0)
-    blocks = gather_ring(both)
-
-    small = jnp.zeros((8, 128), f32)
-    small = small.at[0, :heads].set(dt_bias).at[1, :heads].set(decay_rate).at[2, :heads].set(skip_gain)
-    dt_wide = jnp.pad(dt_weight, ((0, 0), (0, 128 - heads)))
-    normed, x, writes, reads, cums, step, mine, theirs = on_chip(
+    x, tailed, cums, step = on_chip(
         functools.partial(project_kernel, heads, size_p),
-        [
-            shape((rows, model), bf16),
-            shape((rows, width)),
-            shape((rows, state_n)),
-            shape((rows, state_n)),
-            shape((rows, 128)),
-            shape((rows, 128)),
-            shape((half + 16, state_n), bf16),
-            shape((half + 16, state_n), bf16),
-        ],
-        [*blocks, norm_gain.reshape(groups, own), x_weight, dt_wide, bc_one, bc_two, small],
+        [shape((rows, width)), shape((rows, width)), shape((rows, 128)), shape((rows, 128))],
+        [normed, x_weight, dt_weight.T, dt_bias.reshape(1, heads), decay_rate.reshape(1, heads)],
+        scratch=[pltpu.VMEM((128, model), bf16), pltpu.VMEM((8, 128), f32)],
+        flops=2 * rows * model * (width + 128),
+    )
+    writes, mine, theirs = on_chip(
+        state_kernel,
+        [shape((rows, state_n)), shape((half + 16, state_n), bf16), shape((half + 16, state_n), bf16)],
+        [normed, tailed, bc_one, bc_two, cums],
         place,
         [pltpu.VMEM((width, state_n), f32)],
-        flops=2 * rows * model * (width + 3 * 128),
-    )
-    result, opened = on_chip(
+        flops=2 * rows * model * state_n,
+    )
+    result, opened, reads = on_chip(
         functools.partial(scan_kernel, heads, size_p, 256),
-        [shape((rows, width)), shape((rows, width))],
-        [normed, gate_weight, x, writes, reads, cums, step, small],
-        flops=2 * rows * model * width + 12 * rows * 256 * (width + 3 * state_n),
+        [shape((rows, width)), shape((rows, width)), shape((rows, state_n))],
+        [normed, gate_weight, bc_one, bc_two, x, writes, cums, step, skip_gain.reshape(1, heads)],
+        place,
+        [pltpu.VMEM((8, 128), f32)],
+        flops=2 * rows * model * (width + state_n) + 12 * rows * 256 * (width + 3 * state_n),
         transcendentals=heads * rows * 256,
     )
     other = to_core(theirs)
@@ -329,8 +366,9 @@
     keep, send = on_chip(
         functools.partial(prefix_kernel, size_p),
         [shape((half, state_n)), shape((half, state_n), bf16)],
-        [gathered, mine, other],
-        place,
+        [gathered, mine, other, result],
+        place,
+        whole=(3,),
     )
     rest = to_core(send)
     shares = on_chip(

time: 190 us -> 185 us (0.974)
  the two profiles are of different devices: /device:TPU:8 before, /device:TPU:16 now
where the time goes in v3:
time: 185 us; the launch traced here: 183 us
  starting transfers between devices  83.2 us (45%)
  waiting for transfers between devices  51.5 us (28%)
  local copies, waits for them, and re-layouts  28.8 us (16%)
  Pallas kernels  16 us (9%)
  other arithmetic  3.12 us (2%)
    ppermute x14, starting transfers between devices, to_turn(): return lax.ppermute(block, 'head', route)  58.9 us
    ppermute x14, waiting for transfers between devices, to_turn(): return lax.ppermute(block, 'head', route)  31.6 us
    unnamed x92, local copies, waits for them, and re-layouts  28.8 us
    pallas_call x7, Pallas kernels, on_chip(): pl.pallas_call(kernel, out_shape=outs, in_specs=specs, out_specs=[pl.Bloc...  16 us
    ppermute x2, waiting for transfers between devices, to_side(): lax.ppermute(block, 'head', [(i, (i + RING) % (SIDE * RING)) for i in ran...  14.3 us
    ppermute x2, starting transfers between devices, to_side(): lax.ppermute(block, 'head', [(i, (i + RING) % (SIDE * RING)) for i in ran...  11.4 us
    all_to_all x1, starting transfers between devices, local(): gathered = lax.all_to_all(copies, 'section', 0, 0, axis_index_groups=chips)  6.67 us
    ppermute x3, starting transfers between devices, to_core(): lax.ppermute(block, 'section', [(i, i ^ 1) for i in range(lax.axis_size('...  6.23 us
  transfers between devices with their start and end apart: 20, of which 13 were waited for; matrix products, arithmetic and copies ran while one was open for 0% of the time, Pallas kernels for 4%

profile of v3, /device:TPU:16, one launch (start us, length us, event | category | flops | bytes accessed | tf_op | source)
XLA Modules:
  0.0 183.1 jit_solution(13790981153154313082)
XLA Ops:
  1.8 5.9 %collective-permute-start = (bf16[640,128]{1,0:T(8,128)(2,1)S(1)}, bf16[640,128]{1,0:T(8,128)(2,1)S(1)}, u32[]{:S(2)}, u32[]{:S(2)}) collective-permute-start(bf16[640,128]{1,0:T(8,128)(2,1)S(1)} %pad_maximum_fusion.1), channel_id=1, source_target_pairs={{0,8},{1,9},{2,10},{3,11},{4,12},{5,13},{6,14},{7,15},{8,0},{9,1},... | collective-permute-start | bytes 491528 | tf_op jit(solution)/shard_map/ppermute | solution.py:266
  7.7 7.6 %collective-permute-done = bf16[640,128]{1,0:T(8,128)(2,1)S(1)} collective-permute-done((bf16[640,128]{1,0:T(8,128)(2,1)S(1)}, bf16[640,128]{1,0:T(8,128)(2,1)S(1)}, u32[]{:S(2)}, u32[]{:S(2)}) %collective-permute-start) | collective-permute-done | bytes 163872 | tf_op jit(solution)/shard_map/ppermute | solution.py:266
  16.2 12.7 %collective-permute-start.1 = (bf16[1280,128]{1,0:T(8,128)(2,1)S(1)}, bf16[1280,128]{1,0:T(8,128)(2,1)S(1)}, u32[]{:S(2)}, u32[]{:S(2)}) collective-permute-start(bf16[1280,128]{1,0:T(8,128)(2,1)S(1)} %pad_maximum_fusion.refs_0_), channel_id=1, source_target_pairs={{0,7},{1,0},{2,1},{3,2},{4,3},{5,4},{6,5},{7,6},{8,15},{9,8},{10,9... | collective-permute-start | bytes 983048 | tf_op jit(solution)/shard_map/ppermute | solution.py:262
  30.9 5.1 %collective-permute-done.1.refs_1_ = bf16[1280,128]{1,0:T(8,128)(2,1)S(1)} collective-permute-done((bf16[1280,128]{1,0:T(8,128)(2,1)S(1)}, bf16[1280,128]{1,0:T(8,128)(2,1)S(1)}, u32[]{:S(2)}, u32[]{:S(2)}) %collective-permute-start.1) | collective-permute-done | bytes 327712 | tf_op jit(solution)/shard_map/ppermute | solution.py:262
  36.0 5.6 %collective-permute-start.2 = (bf16[1280,128]{1,0:T(8,128)(2,1)S(1)}, bf16[1280,128]{1,0:T(8,128)(2,1)S(1)}, u32[]{:S(2)}, u32[]{:S(2)}) collective-permute-start(bf16[1280,128]{1,0:T(8,128)(2,1)S(1)} %collective-permute-done.1.refs_1_), channel_id=1, source_target_pairs={{0,7},{1,0},{2,1},{3,2},{4,3},{5,4},{6,5},{7,6},{8,15},{9,8},{10,9... | collective-permute-start | bytes 983048 | tf_op jit(solution)/shard_map/ppermute | solution.py:262
  45.0 2.8 %collective-permute-done.2.refs_2_ = bf16[1280,128]{1,0:T(8,128)(2,1)S(1)} collective-permute-done((bf16[1280,128]{1,0:T(8,128)(2,1)S(1)}, bf16[1280,128]{1,0:T(8,128)(2,1)S(1)}, u32[]{:S(2)}, u32[]{:S(2)}) %collective-permute-start.2) | collective-permute-done | bytes 327712 | tf_op jit(solution)/shard_map/ppermute | solution.py:262
  47.7 5.6 %collective-permute-start.3 = (bf16[1280,128]{1,0:T(8,128)(2,1)S(1)}, bf16[1280,128]{1,0:T(8,128)(2,1)S(1)}, u32[]{:S(2)}, u32[]{:S(2)}) collective-permute-start(bf16[1280,128]{1,0:T(8,128)(2,1)S(1)} %collective-permute-done.2.refs_2_), channel_id=1, source_target_pairs={{0,7},{1,0},{2,1},{3,2},{4,3},{5,4},{6,5},{7,6},{8,15},{9,8},{10,9... | collective-permute-start | bytes 983048 | tf_op jit(solution)/shard_map/ppermute | solution.py:262
  58.6 5.6 %collective-permute-start.4 = (bf16[1280,128]{1,0:T(8,128)(2,1)S(1)}, bf16[1280,128]{1,0:T(8,128)(2,1)S(1)}, u32[]{:S(2)}, u32[]{:S(2)}) collective-permute-start(bf16[1280,128]{1,0:T(8,128)(2,1)S(1)} %collective-permute-done.3.refs_3_), channel_id=1, source_target_pairs={{0,7},{1,0},{2,1},{3,2},{4,3},{5,4},{6,5},{7,6},{8,15},{9,8},{10,9... | collective-permute-start | bytes 983048 | tf_op jit(solution)/shard_map/ppermute | solution.py:262
  65.7 3.0 %collective-permute-done.4.refs_4_ = bf16[1280,128]{1,0:T(8,128)(2,1)S(1)} collective-permute-done((bf16[1280,128]{1,0:T(8,128)(2,1)S(1)}, bf16[1280,128]{1,0:T(8,128)(2,1)S(1)}, u32[]{:S(2)}, u32[]{:S(2)}) %collective-permute-start.4) | collective-permute-done | bytes 327712 | tf_op jit(solution)/shard_map/ppermute | solution.py:262
  81.0 3.1 %shard_map.110 = (f32[512,256]{1,0:T(8,128)S(1)}, f32[512,256]{1,0:T(8,128)S(1)}, f32[512,128]{1,0:T(8,128)S(1)}, f32[512,128]{1,0:T(8,128)S(1)}) custom-call(bf16[512,2048]{1,0:T(8,128)(2,1)S(1)} %get-tuple-element.27.normed, bf16[2048,256]{1,0:T(8,128)(2,1)S(1)} %copy-done.1, bf16[4,2048]{1,0:T(4,128)(2,1)S(1)} %bitcast.10, f32[1,4]{1,0:T(1,128)S(1)} %bitcast.13, ...), custom_call_target="tpu_custom_call" | custom-call | flops 805306368 | bytes 4735008 | tf_op jit(solution)/shard_map/pallas_call | solution.py:245
  86.8 2.4 %collective-permute-start.9 = (bf16[144,128]{1,0:T(8,128)(2,1)S(1)}, bf16[144,128]{1,0:T(8,128)(2,1)S(1)}, u32[]{:S(2)}, u32[]{:S(2)}) collective-permute-start(bf16[144,128]{1,0:T(8,128)(2,1)S(1)} %get-tuple-element.38), channel_id=1, source_target_pairs={{0,16},{16,0},{32,48},{48,32},{64,80},{80,64},{96,112},{112,96},{1... | collective-permute-start | bytes 110600 | tf_op jit(solution)/shard_map/ppermute | solution.py:270
  92.8 6.7 %all-to-all-start = ((bf16[16,144,128]{2,1,0:T(8,128)(2,1)}), bf16[16,144,128]{2,1,0:T(8,128)(2,1)S(1)}, u32[]{:S(2)}, u32[]{:S(2)}) async-start(bf16[16,144,128]{2,1,0:T(8,128)(2,1)} %shard_map.113), calls=%async_computation | async-start | bytes 1179648 | tf_op jit(solution)/shard_map/all_to_all | solution.py:365
  106.7 4.1 %shard_map.112 = (f32[512,256]{1,0:T(8,128)S(1)}, f32[512,256]{1,0:T(8,128)S(1)}, f32[512,128]{1,0:T(8,128)S(1)}) custom-call(s32[4]{0:T(128)S(1)} %pad_add_fusion.place, bf16[512,2048]{1,0:T(8,128)(2,1)S(1)} %get-tuple-element.27.normed, bf16[2048,256]{1,0:T(8,128)(2,1)S(1)} %copy-done.37, bf16[2048,128]{1,0:T(8,128)(2,1)S(1)} %copy-done.7, ...), custom_call_target="tpu_custom_call" | custom-call | flops 1811939328 | bytes 6815776 | tf_op jit(solution)/shard_map/pallas_call | solution.py:245
  112.3 3.6 %all-to-all-done.gathered = bf16[16,144,128]{2,1,0:T(8,128)(2,1)S(1)} async-done(((bf16[16,144,128]{2,1,0:T(8,128)(2,1)}), bf16[16,144,128]{2,1,0:T(8,128)(2,1)S(1)}, u32[]{:S(2)}, u32[]{:S(2)}) %all-to-all-start) | async-done | bytes 589856 | tf_op jit(solution)/shard_map/all_to_all | solution.py:365
  124.7 2.5 %shard_map.115 = (bf16[1024,128]{1,0:T(8,128)(2,1)S(1)}, bf16[1024,128]{1,0:T(8,128)(2,1)S(1)}, bf16[1024,128]{1,0:T(8,128)(2,1)S(1)}, bf16[1024,128]{1,0:T(8,12...) custom-call(s32[4]{0:T(128)S(1)} %pad_add_fusion.place, ...), custom_call_target="tpu_custom_call" | custom-call | flops 536870912 | bytes 4817936 | tf_op jit(solution)/shard_map/pallas_call | solution.py:245
  129.1 5.6 %collective-permute-start.15 = (bf16[1024,128]{1,0:T(8,128)(2,1)S(1)}, bf16[1024,128]{1,0:T(8,128)(2,1)S(1)}, u32[]{:S(2)}, u32[]{:S(2)}) collective-permute-start(bf16[1024,128]{1,0:T(8,128)(2,1)S(1)} %get-tuple-element.46), channel_id=1, source_target_pairs={{0,7},{1,0},{2,1},{3,2},{4,3},{5,4},{6,5},{7,6},{8,15},{9,8},{10,9... | collective-permute-start | bytes 786440 | tf_op jit(solution)/shard_map/ppermute | solution.py:262
  134.7 4.7 %collective-permute-done.11 = bf16[1024,128]{1,0:T(8,128)(2,1)S(1)} collective-permute-done((bf16[1024,128]{1,0:T(8,128)(2,1)S(1)}, bf16[1024,128]{1,0:T(8,128)(2,1)S(1)}, u32[]{:S(2)}, u32[]{:S(2)}) %collective-permute-start.11) | collective-permute-done | bytes 262176 | tf_op jit(solution)/shard_map/ppermute | solution.py:262
  141.5 5.3 %collective-permute-start.16 = (bf16[1024,128]{1,0:T(8,128)(2,1)S(1)}, bf16[1024,128]{1,0:T(8,128)(2,1)S(1)}, u32[]{:S(2)}, u32[]{:S(2)}) collective-permute-start(bf16[1024,128]{1,0:T(8,128)(2,1)S(1)} %add_convert_fusion.1), channel_id=1, source_target_pairs={{0,7},{1,0},{2,1},{3,2},{4,3},{5,4},{6,5},{7,6},{8,15},{9,8},{10,9... | collective-permute-start | bytes 786440 | tf_op jit(solution)/shard_map/ppermute | solution.py:262
  146.7 3.7 %collective-permute-done.12 = bf16[1024,128]{1,0:T(8,128)(2,1)S(1)} collective-permute-done((bf16[1024,128]{1,0:T(8,128)(2,1)S(1)}, bf16[1024,128]{1,0:T(8,128)(2,1)S(1)}, u32[]{:S(2)}, u32[]{:S(2)}) %collective-permute-start.12) | collective-permute-done | bytes 262176 | tf_op jit(solution)/shard_map/ppermute | solution.py:262
  152.5 5.1 %collective-permute-start.17 = (bf16[1024,128]{1,0:T(8,128)(2,1)S(1)}, bf16[1024,128]{1,0:T(8,128)(2,1)S(1)}, u32[]{:S(2)}, u32[]{:S(2)}) collective-permute-start(bf16[1024,128]{1,0:T(8,128)(2,1)S(1)} %add_convert_fusion), channel_id=1, source_target_pairs={{0,7},{1,0},{2,1},{3,2},{4,3},{5,4},{6,5},{7,6},{8,15},{9,8},{10,9... | collective-permute-start | bytes 786440 | tf_op jit(solution)/shard_map/ppermute | solution.py:262
  157.6 2.9 %collective-permute-done.13 = bf16[1024,128]{1,0:T(8,128)(2,1)S(1)} collective-permute-done((bf16[1024,128]{1,0:T(8,128)(2,1)S(1)}, bf16[1024,128]{1,0:T(8,128)(2,1)S(1)}, u32[]{:S(2)}, u32[]{:S(2)}) %collective-permute-start.13) | collective-permute-done | bytes 262176 | tf_op jit(solution)/shard_map/ppermute | solution.py:262
  162.6 7.5 %collective-permute-done.14 = bf16[1024,128]{1,0:T(8,128)(2,1)S(1)} collective-permute-done((bf16[1024,128]{1,0:T(8,128)(2,1)S(1)}, bf16[1024,128]{1,0:T(8,128)(2,1)S(1)}, u32[]{:S(2)}, u32[]{:S(2)}) %collective-permute-start.14) | collective-permute-done | bytes 262176 | tf_op jit(solution)/shard_map/ppermute | solution.py:262
  170.2 5.5 %collective-permute-start.18 = (bf16[512,128]{1,0:T(8,128)(2,1)S(1)}, bf16[512,128]{1,0:T(8,128)(2,1)S(1)}, u32[]{:S(2)}, u32[]{:S(2)}) collective-permute-start(bf16[512,128]{1,0:T(8,128)(2,1)S(1)} %slice.15), channel_id=1, source_target_pairs={{0,8},{1,9},{2,10},{3,11},{4,12},{5,13},{6,14},{7,15},{8,0},{9,1},... | collective-permute-start | bytes 393224 | tf_op jit(solution)/shard_map/ppermute | solution.py:266
  175.7 6.7 %collective-permute-done.18 = bf16[512,128]{1,0:T(8,128)(2,1)S(1)} collective-permute-done((bf16[512,128]{1,0:T(8,128)(2,1)S(1)}, bf16[512,128]{1,0:T(8,128)(2,1)S(1)}, u32[]{:S(2)}, u32[]{:S(2)}) %collective-permute-start.18) | collective-permute-done | bytes 131104 | tf_op jit(solution)/shard_map/ppermute | solution.py:266
  (127 shorter events, 59.4 us)
Async XLA Ops:
  0.0 81.0 %copy-start.36 = (f32[4]{0:T(128)S(1)}, f32[4]{0:T(128)}, u32[]{:S(2)}) copy-start(f32[4]{0:T(128)} %param.17) | copy-start | bytes 52
  0.0 81.0 %copy-start.35 = (f32[4]{0:T(128)S(1)}, f32[4]{0:T(128)}, u32[]{:S(2)}) copy-start(f32[4]{0:T(128)} %param.16) | copy-start | bytes 52
  0.0 81.0 %copy-start.1 = (bf16[2048,256]{1,0:T(8,128)(2,1)S(1)}, bf16[2048,256]{1,0:T(8,128)(2,1)}, u32[]{:S(2)}) copy-start(bf16[2048,256]{1,0:T(8,128)(2,1)} %x_weight.1) | copy-start | bytes 3145732
  1.8 13.6 %collective-permute-start = (bf16[640,128]{1,0:T(8,128)(2,1)S(1)}, bf16[640,128]{1,0:T(8,128)(2,1)S(1)}, u32[]{:S(2)}, u32[]{:S(2)}) collective-permute-start(bf16[640,128]{1,0:T(8,128)(2,1)S(1)} %pad_maximum_fusion.1), channel_id=1, source_target_pairs={{0,8},{1,9},{2,10},{3,11},{4,12},{5,13},{6,14},{7,15},{8,0},{9,1},... | collective-permute-start | bytes 491528 | tf_op jit(solution)/shard_map/ppermute | solution.py:266
  16.2 19.7 %collective-permute-start.1 = (bf16[1280,128]{1,0:T(8,128)(2,1)S(1)}, bf16[1280,128]{1,0:T(8,128)(2,1)S(1)}, u32[]{:S(2)}, u32[]{:S(2)}) collective-permute-start(bf16[1280,128]{1,0:T(8,128)(2,1)S(1)} %pad_maximum_fusion.refs_0_), channel_id=1, source_target_pairs={{0,7},{1,0},{2,1},{3,2},{4,3},{5,4},{6,5},{7,6},{8,15},{9,8},{10,9... | collective-permute-start | bytes 983048 | tf_op jit(solution)/shard_map/ppermute | solution.py:262
  29.0 13.4 %collective-permute-start.5 = (bf16[1280,128]{1,0:T(8,128)(2,1)S(1)}, bf16[1280,128]{1,0:T(8,128)(2,1)S(1)}, u32[]{:S(2)}, u32[]{:S(2)}) collective-permute-start(bf16[1280,128]{1,0:T(8,128)(2,1)S(1)} %pad_maximum_fusion.refs_0_), channel_id=1, source_target_pairs={{0,1},{1,2},{2,3},{3,4},{4,5},{5,6},{6,7},{7,0},{8,9},{9,10},{10,1... | collective-permute-start | bytes 983048 | tf_op jit(solution)/shard_map/ppermute | solution.py:262
  36.0 11.8 %collective-permute-start.2 = (bf16[1280,128]{1,0:T(8,128)(2,1)S(1)}, bf16[1280,128]{1,0:T(8,128)(2,1)S(1)}, u32[]{:S(2)}, u32[]{:S(2)}) collective-permute-start(bf16[1280,128]{1,0:T(8,128)(2,1)S(1)} %collective-permute-done.1.refs_1_), channel_id=1, source_target_pairs={{0,7},{1,0},{2,1},{3,2},{4,3},{5,4},{6,5},{7,6},{8,15},{9,8},{10,9... | collective-permute-start | bytes 983048 | tf_op jit(solution)/shard_map/ppermute | solution.py:262
  42.3 11.7 %collective-permute-start.6 = (bf16[1280,128]{1,0:T(8,128)(2,1)S(1)}, bf16[1280,128]{1,0:T(8,128)(2,1)S(1)}, u32[]{:S(2)}, u32[]{:S(2)}) collective-permute-start(bf16[1280,128]{1,0:T(8,128)(2,1)S(1)} %collective-permute-done.5.refs_7_), channel_id=1, source_target_pairs={{0,1},{1,2},{2,3},{3,4},{4,5},{5,6},{6,7},{7,0},{8,9},{9,10},{10,1... | collective-permute-start | bytes 983048 | tf_op jit(solution)/shard_map/ppermute | solution.py:262
  47.7 10.8 %collective-permute-start.3 = (bf16[1280,128]{1,0:T(8,128)(2,1)S(1)}, bf16[1280,128]{1,0:T(8,128)(2,1)S(1)}, u32[]{:S(2)}, u32[]{:S(2)}) collective-permute-start(bf16[1280,128]{1,0:T(8,128)(2,1)S(1)} %collective-permute-done.2.refs_2_), channel_id=1, source_target_pairs={{0,7},{1,0},{2,1},{3,2},{4,3},{5,4},{6,5},{7,6},{8,15},{9,8},{10,9... | collective-permute-start | bytes 983048 | tf_op jit(solution)/shard_map/ppermute | solution.py:262
  54.1 10.9 %collective-permute-start.7 = (bf16[1280,128]{1,0:T(8,128)(2,1)S(1)}, bf16[1280,128]{1,0:T(8,128)(2,1)S(1)}, u32[]{:S(2)}, u32[]{:S(2)}) collective-permute-start(bf16[1280,128]{1,0:T(8,128)(2,1)S(1)} %collective-permute-done.6.refs_6_), channel_id=1, source_target_pairs={{0,1},{1,2},{2,3},{3,4},{4,5},{5,6},{6,7},{7,0},{8,9},{9,10},{10,1... | collective-permute-start | bytes 983048 | tf_op jit(solution)/shard_map/ppermute | solution.py:262
  58.6 10.2 %collective-permute-start.4 = (bf16[1280,128]{1,0:T(8,128)(2,1)S(1)}, bf16[1280,128]{1,0:T(8,128)(2,1)S(1)}, u32[]{:S(2)}, u32[]{:S(2)}) collective-permute-start(bf16[1280,128]{1,0:T(8,128)(2,1)S(1)} %collective-permute-done.3.refs_3_), channel_id=1, source_target_pairs={{0,7},{1,0},{2,1},{3,2},{4,3},{5,4},{6,5},{7,6},{8,15},{9,8},{10,9... | collective-permute-start | bytes 983048 | tf_op jit(solution)/shard_map/ppermute | solution.py:262
  79.0 5.1 %collective-permute-start.8 = (bf16[2048,128]{1,0:T(8,128)(2,1)S(1)}, bf16[2048,128]{1,0:T(8,128)(2,1)S(1)}, u32[]{:S(2)}, u32[]{:S(2)}) collective-permute-start(bf16[2048,128]{1,0:T(8,128)(2,1)S(1)} %get-tuple-element.28.bc_one), channel_id=1, source_target_pairs={{0,16},{16,0},{32,48},{48,32},{64,80},{80,64},{96,112},{112,96},{1... | collective-permute-start | bytes 1572872 | tf_op jit(solution)/shard_map/ppermute | solution.py:270
  86.8 3.2 %collective-permute-start.9 = (bf16[144,128]{1,0:T(8,128)(2,1)S(1)}, bf16[144,128]{1,0:T(8,128)(2,1)S(1)}, u32[]{:S(2)}, u32[]{:S(2)}) collective-permute-start(bf16[144,128]{1,0:T(8,128)(2,1)S(1)} %get-tuple-element.38), channel_id=1, source_target_pairs={{0,16},{16,0},{32,48},{48,32},{64,80},{80,64},{96,112},{112,96},{1... | collective-permute-start | bytes 110600 | tf_op jit(solution)/shard_map/ppermute | solution.py:270
  92.8 23.1 %all-to-all-start = ((bf16[16,144,128]{2,1,0:T(8,128)(2,1)}), bf16[16,144,128]{2,1,0:T(8,128)(2,1)S(1)}, u32[]{:S(2)}, u32[]{:S(2)}) async-start(bf16[16,144,128]{2,1,0:T(8,128)(2,1)} %shard_map.113), calls=%async_computation | async-start | bytes 1179648 | tf_op jit(solution)/shard_map/all_to_all | solution.py:365
  118.3 3.1 %collective-permute-start.10 = (bf16[128,128]{1,0:T(8,128)(2,1)S(1)}, bf16[128,128]{1,0:T(8,128)(2,1)S(1)}, u32[]{:S(2)}, u32[]{:S(2)}) collective-permute-start(bf16[128,128]{1,0:T(8,128)(2,1)S(1)} %get-tuple-element.40), channel_id=1, source_target_pairs={{0,16},{16,0},{32,48},{48,32},{64,80},{80,64},{96,112},{112,96},{1... | collective-permute-start | bytes 98312 | tf_op jit(solution)/shard_map/ppermute | solution.py:270
  127.1 12.2 %collective-permute-start.11 = (bf16[1024,128]{1,0:T(8,128)(2,1)S(1)}, bf16[1024,128]{1,0:T(8,128)(2,1)S(1)}, u32[]{:S(2)}, u32[]{:S(2)}) collective-permute-start(bf16[1024,128]{1,0:T(8,128)(2,1)S(1)} %get-tuple-element.42), channel_id=1, source_target_pairs={{0,1},{1,2},{2,3},{3,4},{4,5},{5,6},{6,7},{7,0},{8,9},{9,10},{10,1... | collective-permute-start | bytes 786440 | tf_op jit(solution)/shard_map/ppermute | solution.py:262
  129.1 12.3 %collective-permute-start.15 = (bf16[1024,128]{1,0:T(8,128)(2,1)S(1)}, bf16[1024,128]{1,0:T(8,128)(2,1)S(1)}, u32[]{:S(2)}, u32[]{:S(2)}) collective-permute-start(bf16[1024,128]{1,0:T(8,128)(2,1)S(1)} %get-tuple-element.46), channel_id=1, source_target_pairs={{0,7},{1,0},{2,1},{3,2},{4,3},{5,4},{6,5},{7,6},{8,15},{9,8},{10,9... | collective-permute-start | bytes 786440 | tf_op jit(solution)/shard_map/ppermute | solution.py:262
  139.4 11.0 %collective-permute-start.12 = (bf16[1024,128]{1,0:T(8,128)(2,1)S(1)}, bf16[1024,128]{1,0:T(8,128)(2,1)S(1)}, u32[]{:S(2)}, u32[]{:S(2)}) collective-permute-start(bf16[1024,128]{1,0:T(8,128)(2,1)S(1)} %add_convert_fusion.4), channel_id=1, source_target_pairs={{0,1},{1,2},{2,3},{3,4},{4,5},{5,6},{6,7},{7,0},{8,9},{9,10},{10,1... | collective-permute-start | bytes 786440 | tf_op jit(solution)/shard_map/ppermute | solution.py:262
  141.4 40.9 %copy-start.45 = (bf16[512,128]{1,0:T(8,128)(2,1)S(1)}, bf16[512,128]{1,0:T(8,128)(2,1)}, u32[]{:S(2)}) copy-start(bf16[512,128]{1,0:T(8,128)(2,1)} %param.11) | copy-start | bytes 393220
  141.5 11.0 %collective-permute-start.16 = (bf16[1024,128]{1,0:T(8,128)(2,1)S(1)}, bf16[1024,128]{1,0:T(8,128)(2,1)S(1)}, u32[]{:S(2)}, u32[]{:S(2)}) collective-permute-start(bf16[1024,128]{1,0:T(8,128)(2,1)S(1)} %add_convert_fusion.1), channel_id=1, source_target_pairs={{0,7},{1,0},{2,1},{3,2},{4,3},{5,4},{6,5},{7,6},{8,15},{9,8},{10,9... | collective-permute-start | bytes 786440 | tf_op jit(solution)/shard_map/ppermute | solution.py:262
  150.5 10.1 %collective-permute-start.13 = (bf16[1024,128]{1,0:T(8,128)(2,1)S(1)}, bf16[1024,128]{1,0:T(8,128)(2,1)S(1)}, u32[]{:S(2)}, u32[]{:S(2)}) collective-permute-start(bf16[1024,128]{1,0:T(8,128)(2,1)S(1)} %add_convert_fusion.3), channel_id=1, source_target_pairs={{0,1},{1,2},{2,3},{3,4},{4,5},{5,6},{6,7},{7,0},{8,9},{9,10},{10,1... | collective-permute-start | bytes 786440 | tf_op jit(solution)/shard_map/ppermute | solution.py:262
  152.5 10.1 %collective-permute-start.17 = (bf16[1024,128]{1,0:T(8,128)(2,1)S(1)}, bf16[1024,128]{1,0:T(8,128)(2,1)S(1)}, u32[]{:S(2)}, u32[]{:S(2)}) collective-permute-start(bf16[1024,128]{1,0:T(8,128)(2,1)S(1)} %add_convert_fusion), channel_id=1, source_target_pairs={{0,7},{1,0},{2,1},{3,2},{4,3},{5,4},{6,5},{7,6},{8,15},{9,8},{10,9... | collective-permute-start | bytes 786440 | tf_op jit(solution)/shard_map/ppermute | solution.py:262
  160.6 9.5 %collective-permute-start.14 = (bf16[1024,128]{1,0:T(8,128)(2,1)S(1)}, bf16[1024,128]{1,0:T(8,128)(2,1)S(1)}, u32[]{:S(2)}, u32[]{:S(2)}) collective-permute-start(bf16[1024,128]{1,0:T(8,128)(2,1)S(1)} %add_convert_fusion.2), channel_id=1, source_target_pairs={{0,1},{1,2},{2,3},{3,4},{4,5},{5,6},{6,7},{7,0},{8,9},{9,10},{10,1... | collective-permute-start | bytes 786440 | tf_op jit(solution)/shard_map/ppermute | solution.py:262
  170.2 12.2 %collective-permute-start.18 = (bf16[512,128]{1,0:T(8,128)(2,1)S(1)}, bf16[512,128]{1,0:T(8,128)(2,1)S(1)}, u32[]{:S(2)}, u32[]{:S(2)}) collective-permute-start(bf16[512,128]{1,0:T(8,128)(2,1)S(1)} %slice.15), channel_id=1, source_target_pairs={{0,8},{1,9},{2,10},{3,11},{4,12},{5,13},{6,14},{7,15},{8,0},{9,1},... | collective-permute-start | bytes 393224 | tf_op jit(solution)/shard_map/ppermute | solution.py:266
  (42 other events, 106.8 us)

commit v4 on v3

--- a/solution.py
+++ b/solution.py
@@ -11,9 +11,10 @@
 highest = lax.Precision.HIGHEST
 RING = 8
 SIDE = 2
+ROW = 8
 f32 = jnp.float32
 bf16 = jnp.bfloat16
-VMEM_BYTES = 40 * 1024 * 1024
+VMEM_BYTES = 24 * 1024 * 1024
 
 
 def dot(a, b, dims=((1,), (0,)), precision=None):
@@ -130,7 +131,7 @@
     step_out[...] = step
 
 
-def state_kernel(place, normed, tailed, bc_one, bc_two, cums, writes_out, mine, theirs, state):
+def state_kernel(place, normed, tailed, bc_one, bc_two, cums, writes_out, slots, state):
     core = place[2]
     rows, width = tailed.shape
     weight = jnp.where(core == 0, bc_one[...], bc_two[...])
@@ -139,44 +140,47 @@
     state[...] = dot_three(tailed[...].T, writes)
     half = width // 2
     logs = log_rows(cums[rows - 1 : rows, :])
-    mine[0:half, :] = state[pl.ds(pl.multiple_of(core * half, half), half), :].astype(bf16)
-    mine[half : half + 16, :] = logs
-    theirs[0:half, :] = state[pl.ds(pl.multiple_of((1 - core) * half, half), half), :].astype(bf16)
-    theirs[half : half + 16, :] = logs
-
-
-def chip_kernel(size_p, place, mine, other, copies):
-    half = mine.shape[0] - 16
-    core = place[2]
+    for i in range(slots.shape[0]):
+        at = i % 2 * half
+        slots[i, 0:half, :] = state[at : at + half, :].astype(bf16)
+        slots[i, half : half + 16, :] = logs
+
+
+def row_kernel(size_p, place, gathered, copies, own_out, pair_out, logs_out):
+    half = gathered.shape[1] - 16
+    core, spot = place[2], place[3]
     first = core * (half // size_p)
-    early = core == 0
-    log_mine, log_other = log_row(mine, half), log_row(other, half)
-    value_mine, value_other = mine[0:half].astype(f32), other[0:half].astype(f32)
-    log_late = jnp.where(early, log_other, log_mine)
-    value_early = jnp.where(early, value_mine, value_other)
-    value_late = jnp.where(early, value_other, value_mine)
-    grown = jnp.exp(column(log_late, half, size_p, first)) * value_early + value_late
-    value = grown.astype(bf16)
-    logs = log_rows(log_mine + log_other)
+    pair = spot + 1 - 2 * core
+    state = jnp.zeros((half, gathered.shape[2]), f32)
+    log = jnp.zeros((1, gathered.shape[2]), f32)
+    own, other, own_log, other_log = state, state, log, log
+    for i in range(gathered.shape[0]):
+        own, own_log = jnp.where(i == spot, state, own), jnp.where(i == spot, log, own_log)
+        other, other_log = jnp.where(i == pair, state, other), jnp.where(i == pair, log, other_log)
+        here = log_row(gathered.at[i], half)
+        state = jnp.exp(column(here, half, size_p, first)) * state + gathered[i, 0:half, :].astype(f32)
+        log = log + here
+    own_out[...] = own
+    pair_out[...] = other
+    logs_out[0:1, :] = own_log
+    logs_out[1:2, :] = other_log
+    value, logs = state.astype(bf16), log_rows(log)
     for i in range(copies.shape[0]):
         copies[i, 0:half, :] = value
         copies[i, half : half + 16, :] = logs
 
 
-def prefix_kernel(size_p, place, gathered, mine, other, after, keep, send):
-    half = mine.shape[0] - 16
-    core, chip = place[2], place[3]
+def prefix_kernel(size_p, place, gathered, own, pair, logs, keep, send):
+    half = own.shape[0]
+    core, row = place[2], place[4]
     first = core * (half // size_p)
-    early = core == 0
-    state = jnp.zeros((half, mine.shape[1]), f32)
+    state = jnp.zeros((half, own.shape[1]), f32)
     for i in range(gathered.shape[0] - 1):
         grow = jnp.exp(column(log_row(gathered.at[i], half), half, size_p, first))
-        state = jnp.where(i < chip, grow * state + gathered[i, 0:half, :].astype(f32), state)
-    log_early = jnp.where(early, log_row(mine, half), log_row(other, half))
-    value_early = jnp.where(early, mine[0:half].astype(f32), other[0:half].astype(f32))
-    later = jnp.exp(column(log_early, half, size_p, first)) * state + value_early
-    keep[...] = jnp.where(early, state, later)
-    send[...] = jnp.where(early, later, state).astype(bf16)
+        state = jnp.where(i < row, grow * state + gathered[i, 0:half, :].astype(f32), state)
+    keep[...] = jnp.exp(column(logs[0:1, :], half, size_p, first)) * state + own[...]
+    later = jnp.exp(column(logs[1:2, :], half, size_p, first)) * state + pair[...]
+    send[...] = later.astype(bf16)
 
 
 def scan_kernel(heads, size_p, block, place, normed, gate_weight, bc_one, bc_two, x_in, writes_in, cums_in, step_in, gain, *refs):
@@ -200,7 +204,7 @@
         for h in range(heads):
             gap = cums[:, h : h + 1] - cums_t[h : h + 1, :]
             mixing = jnp.exp(jnp.where(lower, gap, -jnp.inf)) * scores * step_t[h : h + 1, :]
-            made.append(dot_three(mixing, x[:, h * size_p : (h + 1) * size_p]))
+            made.append(dot(mixing.astype(bf16), x[:, h * size_p : (h + 1) * size_p].astype(bf16)))
         y = jnp.concatenate(made, axis=1) + skip * x
         if state is not None:
             carried = dot_three(reads, state, ((1,), (1,)))
@@ -318,7 +322,7 @@
     half = width // 2
     head, section = lax.axis_index("head"), lax.axis_index("section")
     core = section % 2
-    place = jnp.stack([head // RING, head % RING, core, section // 2]).astype(jnp.int32)
+    place = jnp.stack([head // RING, head % RING, core, section % ROW, section // ROW]).astype(jnp.int32)
 
     piece = lax.dynamic_slice_in_dim(bc_weight, core * state_n, state_n, 1)
     packed = jnp.concatenate([tokens, piece], 0)
@@ -337,9 +341,9 @@
         scratch=[pltpu.VMEM((128, model), bf16), pltpu.VMEM((8, 128), f32)],
         flops=2 * rows * model * (width + 128),
     )
-    writes, mine, theirs = on_chip(
+    writes, slots = on_chip(
         state_kernel,
-        [shape((rows, state_n)), shape((half + 16, state_n), bf16), shape((half + 16, state_n), bf16)],
+        [shape((rows, state_n)), shape((ROW, half + 16, state_n), bf16)],
         [normed, tailed, bc_one, bc_two, cums],
         place,
         [pltpu.VMEM((width, state_n), f32)],
@@ -354,21 +358,20 @@
         flops=2 * rows * model * (width + state_n) + 12 * rows * 256 * (width + 3 * state_n),
         transcendentals=heads * rows * 256,
     )
-    other = to_core(theirs)
-    copies = on_chip(
-        functools.partial(chip_kernel, size_p),
-        [shape((sections // 2, half + 16, state_n), bf16)],
-        [mine, other],
-        place,
-    )[0]
-    chips = [list(range(c, sections, 2)) for c in range(2)]
-    gathered = lax.all_to_all(copies, "section", 0, 0, axis_index_groups=chips)
+    lines = sections // ROW
+    by_row = [list(range(r * ROW, (r + 1) * ROW)) for r in range(lines)]
+    by_spot = [list(range(p, sections, ROW)) for p in range(ROW)]
+    copies, enter_own, enter_pair, logs = on_chip(
+        functools.partial(row_kernel, size_p),
+        [shape((lines, half + 16, state_n), bf16), shape((half, state_n)), shape((half, state_n)), shape((8, state_n))],
+        [lax.all_to_all(slots, "section", 0, 0, axis_index_groups=by_row)],
+        place,
+    )
     keep, send = on_chip(
         functools.partial(prefix_kernel, size_p),
         [shape((half, state_n)), shape((half, state_n), bf16)],
-        [gathered, mine, other, result],
-        place,
-        whole=(3,),
+        [lax.all_to_all(copies, "section", 0, 0, axis_index_groups=by_spot), enter_own, enter_pair, logs],
+        place,
     )
     rest = to_core(send)
     shares = on_chip(

time: 185 us -> 167 us (0.903)
  the two profiles are of different devices: /device:TPU:16 before, /device:TPU:8 now
where the time goes in v4:
time: 167 us; the launch traced here: 166 us
  starting transfers between devices  73.5 us (44%)
  waiting for transfers between devices  46.9 us (28%)
  blocking collectives  25.5 us (15%)
  Pallas kernels  14.8 us (9%)
  other arithmetic  3.03 us (2%)
    ppermute x14, starting transfers between devices, to_turn(): return lax.ppermute(block, 'head', route)  57.3 us
    ppermute x14, waiting for transfers between devices, to_turn(): return lax.ppermute(block, 'head', route)  33.6 us
    pallas_call x7, Pallas kernels, on_chip(): pl.pallas_call(kernel, out_shape=outs, in_specs=specs, out_specs=[pl.Bloc...  14.8 us
    all_to_all x1, blocking collectives, local(): lax.all_to_all(copies, 'section', 0, 0, axis_index_groups=by_spot)  13.4 us
    ppermute x2, waiting for transfers between devices, to_side(): lax.ppermute(block, 'head', [(i, (i + RING) % (SIDE * RING)) for i in ran...  13.3 us
    ppermute x2, starting transfers between devices, to_side(): lax.ppermute(block, 'head', [(i, (i + RING) % (SIDE * RING)) for i in ran...  12.4 us
    all_to_all x1, blocking collectives, local(): lax.all_to_all(slots, 'section', 0, 0, axis_index_groups=by_row)  12.1 us
    ppermute x2, starting transfers between devices, to_core(): lax.ppermute(block, 'section', [(i, i ^ 1) for i in range(lax.axis_size('...  3.84 us
  transfers between devices with their start and end apart: 18, of which 10 were waited for; matrix products, arithmetic and copies ran while one was open for 0% of the time, Pallas kernels for 4%

profile of v4, /device:TPU:8, one launch (start us, length us, event | category | flops | bytes accessed | tf_op | source)
XLA Modules:
  0.0 165.8 jit_solution(12146639873028032574)
XLA Ops:
  1.8 6.8 %collective-permute-start = (bf16[640,128]{1,0:T(8,128)(2,1)S(1)}, bf16[640,128]{1,0:T(8,128)(2,1)S(1)}, u32[]{:S(2)}, u32[]{:S(2)}) collective-permute-start(bf16[640,128]{1,0:T(8,128)(2,1)S(1)} %pad_maximum_fusion.1), channel_id=1, source_target_pairs={{0,8},{1,9},{2,10},{3,11},{4,12},{5,13},{6,14},{7,15},{8,0},{9,1},... | collective-permute-start | bytes 491528 | tf_op jit(solution)/shard_map/ppermute | solution.py:270
  8.6 7.6 %collective-permute-done = bf16[640,128]{1,0:T(8,128)(2,1)S(1)} collective-permute-done((bf16[640,128]{1,0:T(8,128)(2,1)S(1)}, bf16[640,128]{1,0:T(8,128)(2,1)S(1)}, u32[]{:S(2)}, u32[]{:S(2)}) %collective-permute-start) | collective-permute-done | bytes 163872 | tf_op jit(solution)/shard_map/ppermute | solution.py:270
  17.1 10.9 %collective-permute-start.1 = (bf16[1280,128]{1,0:T(8,128)(2,1)S(1)}, bf16[1280,128]{1,0:T(8,128)(2,1)S(1)}, u32[]{:S(2)}, u32[]{:S(2)}) collective-permute-start(bf16[1280,128]{1,0:T(8,128)(2,1)S(1)} %pad_maximum_fusion.refs_0_), channel_id=1, source_target_pairs={{0,7},{1,0},{2,1},{3,2},{4,3},{5,4},{6,5},{7,6},{8,15},{9,8},{10,9... | collective-permute-start | bytes 983048 | tf_op jit(solution)/shard_map/ppermute | solution.py:266
  30.0 3.9 %collective-permute-done.1.refs_1_ = bf16[1280,128]{1,0:T(8,128)(2,1)S(1)} collective-permute-done((bf16[1280,128]{1,0:T(8,128)(2,1)S(1)}, bf16[1280,128]{1,0:T(8,128)(2,1)S(1)}, u32[]{:S(2)}, u32[]{:S(2)}) %collective-permute-start.1) | collective-permute-done | bytes 327712 | tf_op jit(solution)/shard_map/ppermute | solution.py:266
  33.9 5.6 %collective-permute-start.2 = (bf16[1280,128]{1,0:T(8,128)(2,1)S(1)}, bf16[1280,128]{1,0:T(8,128)(2,1)S(1)}, u32[]{:S(2)}, u32[]{:S(2)}) collective-permute-start(bf16[1280,128]{1,0:T(8,128)(2,1)S(1)} %collective-permute-done.1.refs_1_), channel_id=1, source_target_pairs={{0,7},{1,0},{2,1},{3,2},{4,3},{5,4},{6,5},{7,6},{8,15},{9,8},{10,9... | collective-permute-start | bytes 983048 | tf_op jit(solution)/shard_map/ppermute | solution.py:266
  41.4 2.9 %collective-permute-done.2.refs_2_ = bf16[1280,128]{1,0:T(8,128)(2,1)S(1)} collective-permute-done((bf16[1280,128]{1,0:T(8,128)(2,1)S(1)}, bf16[1280,128]{1,0:T(8,128)(2,1)S(1)}, u32[]{:S(2)}, u32[]{:S(2)}) %collective-permute-start.2) | collective-permute-done | bytes 327712 | tf_op jit(solution)/shard_map/ppermute | solution.py:266
  44.4 5.6 %collective-permute-start.3 = (bf16[1280,128]{1,0:T(8,128)(2,1)S(1)}, bf16[1280,128]{1,0:T(8,128)(2,1)S(1)}, u32[]{:S(2)}, u32[]{:S(2)}) collective-permute-start(bf16[1280,128]{1,0:T(8,128)(2,1)S(1)} %collective-permute-done.2.refs_2_), channel_id=1, source_target_pairs={{0,7},{1,0},{2,1},{3,2},{4,3},{5,4},{6,5},{7,6},{8,15},{9,8},{10,9... | collective-permute-start | bytes 983048 | tf_op jit(solution)/shard_map/ppermute | solution.py:266
  51.9 2.6 %collective-permute-done.3.refs_3_ = bf16[1280,128]{1,0:T(8,128)(2,1)S(1)} collective-permute-done((bf16[1280,128]{1,0:T(8,128)(2,1)S(1)}, bf16[1280,128]{1,0:T(8,128)(2,1)S(1)}, u32[]{:S(2)}, u32[]{:S(2)}) %collective-permute-start.3) | collective-permute-done | bytes 327712 | tf_op jit(solution)/shard_map/ppermute | solution.py:266
  54.6 5.6 %collective-permute-start.4 = (bf16[1280,128]{1,0:T(8,128)(2,1)S(1)}, bf16[1280,128]{1,0:T(8,128)(2,1)}, u32[]{:S(2)}, u32[]{:S(2)}) collective-permute-start(bf16[1280,128]{1,0:T(8,128)(2,1)S(1)} %collective-permute-done.3.refs_3_), channel_id=1, source_target_pairs={{0,7},{1,0},{2,1},{3,2},{4,3},{5,4},{6,5},{7,6},{8,15},{9,8},{10,9... | collective-permute-start | bytes 983048 | tf_op jit(solution)/shard_map/ppermute | solution.py:266
  60.3 4.4 %collective-permute-done.4.refs_4_ = bf16[1280,128]{1,0:T(8,128)(2,1)} collective-permute-done((bf16[1280,128]{1,0:T(8,128)(2,1)S(1)}, bf16[1280,128]{1,0:T(8,128)(2,1)}, u32[]{:S(2)}, u32[]{:S(2)}) %collective-permute-start.4) | collective-permute-done | bytes 327712 | tf_op jit(solution)/shard_map/ppermute | solution.py:266
  69.8 3.1 %shard_map.110 = (f32[512,256]{1,0:T(8,128)S(1)}, f32[512,256]{1,0:T(8,128)S(1)}, f32[512,128]{1,0:T(8,128)S(1)}, f32[512,128]{1,0:T(8,128)S(1)}) custom-call(bf16[512,2048]{1,0:T(8,128)(2,1)S(1)} %get-tuple-element.30.normed, bf16[2048,256]{1,0:T(8,128)(2,1)S(1)} %copy-done.1, bf16[4,2048]{1,0:T(4,128)(2,1)S(1)} %bitcast.11, f32[1,4]{1,0:T(1,128)S(1)} %bitcast.14, ...), custom_call_target="tpu_custom_call" | custom-call | flops 805306368 | bytes 4735008 | tf_op jit(solution)/shard_map/pallas_call | solution.py:249
  74.8 12.1 %all_to_all.10.gathered = bf16[8,144,128]{2,1,0:T(8,128)(2,1)S(1)} all-to-all(bf16[8,144,128]{2,1,0:T(8,128)(2,1)S(1)} %get-tuple-element.40), channel_id=1, replica_groups={{0,16,32,48,64,80,96,112},{128,144,160,176,192,208,224,240},{256,272,28..., dimensions={0} | all-to-all | bytes 589824 | tf_op jit(solution)/shard_map/all_to_all | solution.py:367
  87.7 13.4 %all_to_all.11.gathered = bf16[4,144,128]{2,1,0:T(8,128)(2,1)S(1)} all-to-all(bf16[4,144,128]{2,1,0:T(8,128)(2,1)S(1)} %get-tuple-element.41), channel_id=1, replica_groups={{0,128,256,384},{16,144,272,400},{32,160,288,416},{48,176,304,432},{64,..., dimensions={0} | all-to-all | bytes 294912 | tf_op jit(solution)/shard_map/all_to_all | solution.py:373
  103.8 3.4 %shard_map.112 = (f32[512,256]{1,0:T(8,128)S(1)}, f32[512,256]{1,0:T(8,128)S(1)}, f32[512,128]{1,0:T(8,128)S(1)}) custom-call(s32[5]{0:T(128)S(1)} %stack.23.place, bf16[512,2048]{1,0:T(8,128)(2,1)S(1)} %get-tuple-element.30.normed, bf16[2048,256]{1,0:T(8,128)(2,1)S(1)} %copy-done.8, bf16[2048,128]{1,0:T(8,128)(2,1)S(1)} %get-tuple-element.31.bc_one, ...), custom_call_target="tpu_custom_call" | custom-call | flops 1811939328 | bytes 6815780 | tf_op jit(solution)/shard_map/pallas_call | solution.py:249
  107.3 2.5 %shard_map.115 = (bf16[1024,128]{1,0:T(8,128)(2,1)S(1)}, bf16[1024,128]{1,0:T(8,128)(2,1)S(1)}, bf16[1024,128]{1,0:T(8,128)(2,1)S(1)}, bf16[1024,128]{1,0:T(8,12...) custom-call(s32[5]{0:T(128)S(1)} %stack.23.place, ...), custom_call_target="tpu_custom_call" | custom-call | flops 536870912 | bytes 4817940 | tf_op jit(solution)/shard_map/pallas_call | solution.py:249
  111.7 5.7 %collective-permute-start.14 = (bf16[1024,128]{1,0:T(8,128)(2,1)S(1)}, bf16[1024,128]{1,0:T(8,128)(2,1)S(1)}, u32[]{:S(2)}, u32[]{:S(2)}) collective-permute-start(bf16[1024,128]{1,0:T(8,128)(2,1)S(1)} %get-tuple-element.52), channel_id=1, source_target_pairs={{0,7},{1,0},{2,1},{3,2},{4,3},{5,4},{6,5},{7,6},{8,15},{9,8},{10,9... | collective-permute-start | bytes 786440 | tf_op jit(solution)/shard_map/ppermute | solution.py:266
  117.4 5.0 %collective-permute-done.10 = bf16[1024,128]{1,0:T(8,128)(2,1)S(1)} collective-permute-done((bf16[1024,128]{1,0:T(8,128)(2,1)S(1)}, bf16[1024,128]{1,0:T(8,128)(2,1)S(1)}, u32[]{:S(2)}, u32[]{:S(2)}) %collective-permute-start.10) | collective-permute-done | bytes 262176 | tf_op jit(solution)/shard_map/ppermute | solution.py:266
  124.6 5.3 %collective-permute-start.15 = (bf16[1024,128]{1,0:T(8,128)(2,1)S(1)}, bf16[1024,128]{1,0:T(8,128)(2,1)S(1)}, u32[]{:S(2)}, u32[]{:S(2)}) collective-permute-start(bf16[1024,128]{1,0:T(8,128)(2,1)S(1)} %add_convert_fusion.1), channel_id=1, source_target_pairs={{0,7},{1,0},{2,1},{3,2},{4,3},{5,4},{6,5},{7,6},{8,15},{9,8},{10,9... | collective-permute-start | bytes 786440 | tf_op jit(solution)/shard_map/ppermute | solution.py:266
  129.8 3.9 %collective-permute-done.11 = bf16[1024,128]{1,0:T(8,128)(2,1)S(1)} collective-permute-done((bf16[1024,128]{1,0:T(8,128)(2,1)S(1)}, bf16[1024,128]{1,0:T(8,128)(2,1)S(1)}, u32[]{:S(2)}, u32[]{:S(2)}) %collective-permute-start.11) | collective-permute-done | bytes 262176 | tf_op jit(solution)/shard_map/ppermute | solution.py:266
  135.8 5.1 %collective-permute-start.16 = (bf16[1024,128]{1,0:T(8,128)(2,1)S(1)}, bf16[1024,128]{1,0:T(8,128)(2,1)S(1)}, u32[]{:S(2)}, u32[]{:S(2)}) collective-permute-start(bf16[1024,128]{1,0:T(8,128)(2,1)S(1)} %add_convert_fusion), channel_id=1, source_target_pairs={{0,7},{1,0},{2,1},{3,2},{4,3},{5,4},{6,5},{7,6},{8,15},{9,8},{10,9... | collective-permute-start | bytes 786440 | tf_op jit(solution)/shard_map/ppermute | solution.py:266
  141.0 3.2 %collective-permute-done.12 = bf16[1024,128]{1,0:T(8,128)(2,1)S(1)} collective-permute-done((bf16[1024,128]{1,0:T(8,128)(2,1)S(1)}, bf16[1024,128]{1,0:T(8,128)(2,1)S(1)}, u32[]{:S(2)}, u32[]{:S(2)}) %collective-permute-start.12) | collective-permute-done | bytes 262176 | tf_op jit(solution)/shard_map/ppermute | solution.py:266
  146.2 7.5 %collective-permute-done.13 = bf16[1024,128]{1,0:T(8,128)(2,1)S(1)} collective-permute-done((bf16[1024,128]{1,0:T(8,128)(2,1)S(1)}, bf16[1024,128]{1,0:T(8,128)(2,1)S(1)}, u32[]{:S(2)}, u32[]{:S(2)}) %collective-permute-start.13) | collective-permute-done | bytes 262176 | tf_op jit(solution)/shard_map/ppermute | solution.py:266
  153.9 5.5 %collective-permute-start.17 = (bf16[512,128]{1,0:T(8,128)(2,1)S(1)}, bf16[512,128]{1,0:T(8,128)(2,1)S(1)}, u32[]{:S(2)}, u32[]{:S(2)}) collective-permute-start(bf16[512,128]{1,0:T(8,128)(2,1)S(1)} %slice.15), channel_id=1, source_target_pairs={{0,8},{1,9},{2,10},{3,11},{4,12},{5,13},{6,14},{7,15},{8,0},{9,1},... | collective-permute-start | bytes 393224 | tf_op jit(solution)/shard_map/ppermute | solution.py:270
  159.4 5.7 %collective-permute-done.17 = bf16[512,128]{1,0:T(8,128)(2,1)S(1)} collective-permute-done((bf16[512,128]{1,0:T(8,128)(2,1)S(1)}, bf16[512,128]{1,0:T(8,128)(2,1)S(1)}, u32[]{:S(2)}, u32[]{:S(2)}) %collective-permute-start.17) | collective-permute-done | bytes 131104 | tf_op jit(solution)/shard_map/ppermute | solution.py:270
  (55 shorter events, 27.8 us)
Async XLA Ops:
  0.0 69.8 %copy-start.3 = (bf16[2048,4]{0,1:T(4,128)(2,1)S(1)}, bf16[2048,4]{0,1:T(4,128)(2,1)}, u32[]{:S(2)}) copy-start(bf16[2048,4]{0,1:T(4,128)(2,1)} %param.15) | copy-start | bytes 49156
  0.0 69.8 %copy-start.6 = (f32[4]{0:T(128)S(1)}, f32[4]{0:T(128)}, u32[]{:S(2)}) copy-start(f32[4]{0:T(128)} %param.16) | copy-start | bytes 52
  0.0 69.8 %copy-start.7 = (f32[4]{0:T(128)S(1)}, f32[4]{0:T(128)}, u32[]{:S(2)}) copy-start(f32[4]{0:T(128)} %param.17) | copy-start | bytes 52
  0.0 69.8 %copy-start.1 = (bf16[2048,256]{1,0:T(8,128)(2,1)S(1)}, bf16[2048,256]{1,0:T(8,128)(2,1)}, u32[]{:S(2)}) copy-start(bf16[2048,256]{1,0:T(8,128)(2,1)} %x_weight.1) | copy-start | bytes 3145732
  1.8 14.5 %collective-permute-start = (bf16[640,128]{1,0:T(8,128)(2,1)S(1)}, bf16[640,128]{1,0:T(8,128)(2,1)S(1)}, u32[]{:S(2)}, u32[]{:S(2)}) collective-permute-start(bf16[640,128]{1,0:T(8,128)(2,1)S(1)} %pad_maximum_fusion.1), channel_id=1, source_target_pairs={{0,8},{1,9},{2,10},{3,11},{4,12},{5,13},{6,14},{7,15},{8,0},{9,1},... | collective-permute-start | bytes 491528 | tf_op jit(solution)/shard_map/ppermute | solution.py:270
  17.1 16.8 %collective-permute-start.1 = (bf16[1280,128]{1,0:T(8,128)(2,1)S(1)}, bf16[1280,128]{1,0:T(8,128)(2,1)S(1)}, u32[]{:S(2)}, u32[]{:S(2)}) collective-permute-start(bf16[1280,128]{1,0:T(8,128)(2,1)S(1)} %pad_maximum_fusion.refs_0_), channel_id=1, source_target_pairs={{0,7},{1,0},{2,1},{3,2},{4,3},{5,4},{6,5},{7,6},{8,15},{9,8},{10,9... | collective-permute-start | bytes 983048 | tf_op jit(solution)/shard_map/ppermute | solution.py:266
  28.1 11.4 %collective-permute-start.5 = (bf16[1280,128]{1,0:T(8,128)(2,1)S(1)}, bf16[1280,128]{1,0:T(8,128)(2,1)S(1)}, u32[]{:S(2)}, u32[]{:S(2)}) collective-permute-start(bf16[1280,128]{1,0:T(8,128)(2,1)S(1)} %pad_maximum_fusion.refs_0_), channel_id=1, source_target_pairs={{0,1},{1,2},{2,3},{3,4},{4,5},{5,6},{6,7},{7,0},{8,9},{9,10},{10,1... | collective-permute-start | bytes 983048 | tf_op jit(solution)/shard_map/ppermute | solution.py:266
  33.9 10.5 %collective-permute-start.2 = (bf16[1280,128]{1,0:T(8,128)(2,1)S(1)}, bf16[1280,128]{1,0:T(8,128)(2,1)S(1)}, u32[]{:S(2)}, u32[]{:S(2)}) collective-permute-start(bf16[1280,128]{1,0:T(8,128)(2,1)S(1)} %collective-permute-done.1.refs_1_), channel_id=1, source_target_pairs={{0,7},{1,0},{2,1},{3,2},{4,3},{5,4},{6,5},{7,6},{8,15},{9,8},{10,9... | collective-permute-start | bytes 983048 | tf_op jit(solution)/shard_map/ppermute | solution.py:266
  39.5 10.5 %collective-permute-start.6 = (bf16[1280,128]{1,0:T(8,128)(2,1)S(1)}, bf16[1280,128]{1,0:T(8,128)(2,1)S(1)}, u32[]{:S(2)}, u32[]{:S(2)}) collective-permute-start(bf16[1280,128]{1,0:T(8,128)(2,1)S(1)} %collective-permute-done.5.refs_7_), channel_id=1, source_target_pairs={{0,1},{1,2},{2,3},{3,4},{4,5},{5,6},{6,7},{7,0},{8,9},{9,10},{10,1... | collective-permute-start | bytes 983048 | tf_op jit(solution)/shard_map/ppermute | solution.py:266
  44.4 10.2 %collective-permute-start.3 = (bf16[1280,128]{1,0:T(8,128)(2,1)S(1)}, bf16[1280,128]{1,0:T(8,128)(2,1)S(1)}, u32[]{:S(2)}, u32[]{:S(2)}) collective-permute-start(bf16[1280,128]{1,0:T(8,128)(2,1)S(1)} %collective-permute-done.2.refs_2_), channel_id=1, source_target_pairs={{0,7},{1,0},{2,1},{3,2},{4,3},{5,4},{6,5},{7,6},{8,15},{9,8},{10,9... | collective-permute-start | bytes 983048 | tf_op jit(solution)/shard_map/ppermute | solution.py:266
  50.0 10.3 %collective-permute-start.7 = (bf16[1280,128]{1,0:T(8,128)(2,1)S(1)}, bf16[1280,128]{1,0:T(8,128)(2,1)S(1)}, u32[]{:S(2)}, u32[]{:S(2)}) collective-permute-start(bf16[1280,128]{1,0:T(8,128)(2,1)S(1)} %collective-permute-done.6.refs_6_), channel_id=1, source_target_pairs={{0,1},{1,2},{2,3},{3,4},{4,5},{5,6},{6,7},{7,0},{8,9},{9,10},{10,1... | collective-permute-start | bytes 983048 | tf_op jit(solution)/shard_map/ppermute | solution.py:266
  54.6 10.2 %collective-permute-start.4 = (bf16[1280,128]{1,0:T(8,128)(2,1)S(1)}, bf16[1280,128]{1,0:T(8,128)(2,1)}, u32[]{:S(2)}, u32[]{:S(2)}) collective-permute-start(bf16[1280,128]{1,0:T(8,128)(2,1)S(1)} %collective-permute-done.3.refs_3_), channel_id=1, source_target_pairs={{0,7},{1,0},{2,1},{3,2},{4,3},{5,4},{6,5},{7,6},{8,15},{9,8},{10,9... | collective-permute-start | bytes 983048 | tf_op jit(solution)/shard_map/ppermute | solution.py:266
  67.9 5.0 %collective-permute-start.8 = (bf16[2048,128]{1,0:T(8,128)(2,1)S(1)}, bf16[2048,128]{1,0:T(8,128)(2,1)S(1)}, u32[]{:S(2)}, u32[]{:S(2)}) collective-permute-start(bf16[2048,128]{1,0:T(8,128)(2,1)S(1)} %get-tuple-element.31.bc_one), channel_id=1, source_target_pairs={{0,16},{16,0},{32,48},{48,32},{64,80},{80,64},{96,112},{112,96},{1... | collective-permute-start | bytes 1572872 | tf_op jit(solution)/shard_map/ppermute | solution.py:274
  72.9 30.9 %copy-start.8 = (bf16[2048,256]{1,0:T(8,128)(2,1)S(1)}, bf16[2048,256]{1,0:T(8,128)(2,1)}, u32[]{:S(2)}) copy-start(bf16[2048,256]{1,0:T(8,128)(2,1)} %gate_weight.1) | copy-start | bytes 3145732
  101.9 5.4 %collective-permute-start.9 = (bf16[128,128]{1,0:T(8,128)(2,1)S(1)}, bf16[128,128]{1,0:T(8,128)(2,1)S(1)}, u32[]{:S(2)}, u32[]{:S(2)}) collective-permute-start(bf16[128,128]{1,0:T(8,128)(2,1)S(1)} %get-tuple-element.46), channel_id=1, source_target_pairs={{0,16},{16,0},{32,48},{48,32},{64,80},{80,64},{96,112},{112,96},{1... | collective-permute-start | bytes 98312 | tf_op jit(solution)/shard_map/ppermute | solution.py:274
  109.8 12.7 %collective-permute-start.10 = (bf16[1024,128]{1,0:T(8,128)(2,1)S(1)}, bf16[1024,128]{1,0:T(8,128)(2,1)S(1)}, u32[]{:S(2)}, u32[]{:S(2)}) collective-permute-start(bf16[1024,128]{1,0:T(8,128)(2,1)S(1)} %get-tuple-element.48), channel_id=1, source_target_pairs={{0,1},{1,2},{2,3},{3,4},{4,5},{5,6},{6,7},{7,0},{8,9},{9,10},{10,1... | collective-permute-start | bytes 786440 | tf_op jit(solution)/shard_map/ppermute | solution.py:266
  111.7 12.7 %collective-permute-start.14 = (bf16[1024,128]{1,0:T(8,128)(2,1)S(1)}, bf16[1024,128]{1,0:T(8,128)(2,1)S(1)}, u32[]{:S(2)}, u32[]{:S(2)}) collective-permute-start(bf16[1024,128]{1,0:T(8,128)(2,1)S(1)} %get-tuple-element.52), channel_id=1, source_target_pairs={{0,7},{1,0},{2,1},{3,2},{4,3},{5,4},{6,5},{7,6},{8,15},{9,8},{10,9... | collective-permute-start | bytes 786440 | tf_op jit(solution)/shard_map/ppermute | solution.py:266
  122.5 11.2 %collective-permute-start.11 = (bf16[1024,128]{1,0:T(8,128)(2,1)S(1)}, bf16[1024,128]{1,0:T(8,128)(2,1)S(1)}, u32[]{:S(2)}, u32[]{:S(2)}) collective-permute-start(bf16[1024,128]{1,0:T(8,128)(2,1)S(1)} %add_convert_fusion.4), channel_id=1, source_target_pairs={{0,1},{1,2},{2,3},{3,4},{4,5},{5,6},{6,7},{7,0},{8,9},{9,10},{10,1... | collective-permute-start | bytes 786440 | tf_op jit(solution)/shard_map/ppermute | solution.py:266
  124.5 40.5 %copy-start.10 = (bf16[512,128]{1,0:T(8,128)(2,1)S(1)}, bf16[512,128]{1,0:T(8,128)(2,1)}, u32[]{:S(2)}) copy-start(bf16[512,128]{1,0:T(8,128)(2,1)} %param.11) | copy-start | bytes 393220
  124.6 11.2 %collective-permute-start.15 = (bf16[1024,128]{1,0:T(8,128)(2,1)S(1)}, bf16[1024,128]{1,0:T(8,128)(2,1)S(1)}, u32[]{:S(2)}, u32[]{:S(2)}) collective-permute-start(bf16[1024,128]{1,0:T(8,128)(2,1)S(1)} %add_convert_fusion.1), channel_id=1, source_target_pairs={{0,7},{1,0},{2,1},{3,2},{4,3},{5,4},{6,5},{7,6},{8,15},{9,8},{10,9... | collective-permute-start | bytes 786440 | tf_op jit(solution)/shard_map/ppermute | solution.py:266
  133.8 10.4 %collective-permute-start.12 = (bf16[1024,128]{1,0:T(8,128)(2,1)S(1)}, bf16[1024,128]{1,0:T(8,128)(2,1)S(1)}, u32[]{:S(2)}, u32[]{:S(2)}) collective-permute-start(bf16[1024,128]{1,0:T(8,128)(2,1)S(1)} %add_convert_fusion.3), channel_id=1, source_target_pairs={{0,1},{1,2},{2,3},{3,4},{4,5},{5,6},{6,7},{7,0},{8,9},{9,10},{10,1... | collective-permute-start | bytes 786440 | tf_op jit(solution)/shard_map/ppermute | solution.py:266
  135.8 10.3 %collective-permute-start.16 = (bf16[1024,128]{1,0:T(8,128)(2,1)S(1)}, bf16[1024,128]{1,0:T(8,128)(2,1)S(1)}, u32[]{:S(2)}, u32[]{:S(2)}) collective-permute-start(bf16[1024,128]{1,0:T(8,128)(2,1)S(1)} %add_convert_fusion), channel_id=1, source_target_pairs={{0,7},{1,0},{2,1},{3,2},{4,3},{5,4},{6,5},{7,6},{8,15},{9,8},{10,9... | collective-permute-start | bytes 786440 | tf_op jit(solution)/shard_map/ppermute | solution.py:266
  144.3 9.5 %collective-permute-start.13 = (bf16[1024,128]{1,0:T(8,128)(2,1)S(1)}, bf16[1024,128]{1,0:T(8,128)(2,1)S(1)}, u32[]{:S(2)}, u32[]{:S(2)}) collective-permute-start(bf16[1024,128]{1,0:T(8,128)(2,1)S(1)} %add_convert_fusion.2), channel_id=1, source_target_pairs={{0,1},{1,2},{2,3},{3,4},{4,5},{5,6},{6,7},{7,0},{8,9},{9,10},{10,1... | collective-permute-start | bytes 786440 | tf_op jit(solution)/shard_map/ppermute | solution.py:266
  153.9 11.2 %collective-permute-start.17 = (bf16[512,128]{1,0:T(8,128)(2,1)S(1)}, bf16[512,128]{1,0:T(8,128)(2,1)S(1)}, u32[]{:S(2)}, u32[]{:S(2)}) collective-permute-start(bf16[512,128]{1,0:T(8,128)(2,1)S(1)} %slice.15), channel_id=1, source_target_pairs={{0,8},{1,9},{2,10},{3,11},{4,12},{5,13},{6,14},{7,15},{8,0},{9,1},... | collective-permute-start | bytes 393224 | tf_op jit(solution)/shard_map/ppermute | solution.py:270
  (5 other events, 39.4 us)

commit v5 on v4

v5 whole, which is shorter than its diff:
```python
import functools

import jax
import jax.numpy as jnp
from jax import lax
from jax.experimental import pallas as pl
from jax.experimental.pallas import tpu as pltpu
from jax.sharding import PartitionSpec as P

eps = 1e-05
RING = 8
SIDE = 2
ROW = 8
HEADS = 16
f32 = jnp.float32
bf16 = jnp.bfloat16
VMEM_BYTES = 24 * 1024 * 1024


def dot(a, b, dims=((1,), (0,))):
    return lax.dot_general(a, b, (dims, ((), ())), preferred_element_type=f32)


def silu(v):
    return v / (1.0 + jnp.exp(-v))


def softplus(v):
    return jnp.maximum(v, 0.0) + jnp.log1p(jnp.exp(-jnp.abs(v)))


def iota(shape, dim):
    return lax.broadcasted_iota(jnp.int32, shape, dim)


def split(v):
    high = v.astype(bf16)
    return high, (v - high.astype(f32)).astype(bf16)


def dot_pair(a, exact, dims=((1,), (0,))):
    high, low = split(a)
    return dot(high, exact, dims) + dot(low, exact, dims)


def dot_three(a, b, dims=((1,), (0,))):
    a_high, a_low = split(a)
    b_high, b_low = split(b)
    return dot(a_high, b_high, dims) + (dot(a_high, b_low, dims) + dot(a_low, b_high, dims))


def running_sum(v):
    count = v.shape[1]
    upper = (iota((count, count), 0) <= iota((count, count), 1)).astype(bf16)
    high, middle = split(v)
    low = (v - high.astype(f32) - middle.astype(f32)).astype(bf16)
    return dot(high, upper) + (dot(middle, upper) + dot(low, upper))


def owners(width, size_p):
    return iota((HEADS, width), 1) // size_p == iota((HEADS, width), 0)


def spread(heads_on_lanes, width, size_p):
    return dot_pair(heads_on_lanes, owners(width, size_p).astype(bf16))


def spread_row(heads_on_rows, width, size_p):
    return jnp.sum(jnp.where(owners(width, size_p), heads_on_rows, 0.0), axis=0, keepdims=True)


def stood(row, scratch):
    scratch[...] = jnp.zeros_like(scratch)
    scratch[0:1, 0 : row.shape[1]] = row[...]
    square = iota((HEADS, HEADS), 0) == iota((HEADS, HEADS), 1)
    return jnp.sum(jnp.where(square, scratch[0:1, 0:HEADS], 0.0), axis=1, keepdims=True)


def log_rows(row):
    high = row.astype(bf16).astype(f32)
    low = row - high
    return jnp.concatenate([high, low, jnp.zeros((14, row.shape[1]), f32)], 0).astype(bf16)


def log_row(block):
    tail = block[block.shape[0] - 16 :].astype(f32)
    return tail[0:1] + tail[1:2]


def front_kernel(rows, heads, size_p, place, *refs):
    blocks = refs[:RING]
    (gain, x_weight, dt_weight, bias, rate) = refs[RING : RING + 5]
    (normed, x_out, both_out, cums_out, step_out, slots, bc, wide, line) = refs[RING + 5 :]
    own = blocks[0].shape[1]
    side, turn = place[0], place[1]
    piece = blocks[0].shape[0] // SIDE
    width = heads * size_p
    state_n = own

    def parts():
        for k in range(RING):
            for j in range(SIDE):
                head = lax.rem(side + j, SIDE) * RING + lax.rem(turn + k, RING)
                yield blocks[k], j * piece, head

    squares = jnp.zeros((rows, own), f32)
    for block, at, _ in parts():
        value = block[at : at + rows, :].astype(f32)
        squares = squares + value * value
    mean = jnp.sum(squares, axis=1, keepdims=True) / (RING * SIDE * own)
    scale = lax.rsqrt(mean + eps)
    for block, at, head in parts():
        value = block[at : at + rows, :].astype(f32)
        spot = pl.multiple_of(head * own, own)
        normed[:, pl.ds(spot, own)] = (value * scale * gain[pl.ds(head, 1), :]).astype(bf16)
        bc[pl.ds(spot, own), 0:state_n] = block[at + rows : at + rows + own, :]
        bc[pl.ds(spot, own), state_n : 2 * state_n] = block[at + rows + own : at + piece, :]
    wide[...] = jnp.zeros_like(wide)
    wide[0:heads, :] = dt_weight[...]
    whole = normed[...]
    raw = dot(whole, wide[...], ((1,), (1,))).T[0:HEADS, :]
    step = softplus(raw + stood(bias, line))
    decay = -stood(rate, line) * step
    cums = running_sum(decay)
    last = cums[:, rows - 1 : rows]
    tail = (jnp.exp(last - cums) * step).T
    x = silu(dot(whole, x_weight[...]))
    both = dot(whole, bc[...])
    state = dot_three(both[:, 0:state_n].T, x * spread(tail, width, size_p)).astype(bf16)
    logs = log_rows(spread_row(last, width, size_p))
    half = width // 2
    for i in range(slots.shape[0]):
        at = i % 2 * half
        slots[i, 0:state_n, :] = state[:, at : at + half]
        slots[i, state_n : state_n + 16, :] = logs[:, at : at + half]
    x_out[...] = x
    both_out[...] = both
    cums_out[...] = cums
    step_out[...] = step


def row_kernel(place, gathered, copies, own_out, pair_out, logs_out):
    state_n, half = gathered.shape[1] - 16, gathered.shape[2]
    core, spot = place[2], place[3]
    pair = spot + 1 - 2 * core
    state = jnp.zeros((state_n, half), f32)
    log = jnp.zeros((1, half), f32)
    own, other, own_log, other_log = state, state, log, log
    for i in range(gathered.shape[0]):
        own, own_log = jnp.where(i == spot, state, own), jnp.where(i == spot, log, own_log)
        other, other_log = jnp.where(i == pair, state, other), jnp.where(i == pair, log, other_log)
        here = log_row(gathered[i])
        state = jnp.exp(here) * state + gathered[i, 0:state_n, :].astype(f32)
        log = log + here
    own_out[...] = own
    pair_out[...] = other
    logs_out[0:1, :] = own_log
    logs_out[1:2, :] = other_log
    value, logs = state.astype(bf16), log_rows(log)
    for i in range(copies.shape[0]):
        copies[i, 0:state_n, :] = value
        copies[i, state_n : state_n + 16, :] = logs


def prefix_kernel(place, gathered, own, pair, logs, keep, send):
    state_n = own.shape[0]
    row = place[4]
    state = jnp.zeros(own.shape, f32)
    for i in range(gathered.shape[0] - 1):
        passed = jnp.exp(log_row(gathered[i])) * state + gathered[i, 0:state_n, :].astype(f32)
        state = jnp.where(i < row, passed, state)
    keep[...] = (jnp.exp(logs[0:1, :]) * state + own[...]).astype(bf16)
    send[...] = (jnp.exp(logs[1:2, :]) * state + pair[...]).astype(bf16)


def scan_kernel(heads, size_p, block, normed, gate_weight, x_in, both_in, cums_in, step_in, gain, result, opened, line):
    rows, width = x_in.shape
    state_n = both_in.shape[1] // 2
    opened[...] = silu(dot(normed[...], gate_weight[...]))
    lower = iota((block, block), 0) >= iota((block, block), 1)
    skip = spread_row(stood(gain, line), width, size_p)
    state = None
    base = None
    for b in range(rows // block):
        span = slice(b * block, (b + 1) * block)
        x, writes, reads = x_in[span, :], both_in[span, 0:state_n], both_in[span, state_n:]
        cums_t, step_t = cums_in[:, span], step_in[:, span]
        cums = cums_t.T
        scores = dot_three(reads, writes, ((1,), (1,)))
        made = []
        for h in range(heads):
            gap = cums[:, h : h + 1] - cums_t[h : h + 1, :]
            mixing = jnp.exp(jnp.where(lower, gap, -jnp.inf)) * scores * step_t[h : h + 1, :]
            made.append(dot(mixing.astype(bf16), x[:, h * size_p : (h + 1) * size_p].astype(bf16)))
        y = jnp.concatenate(made, axis=1) + skip * x
        if state is not None:
            y = y + spread(jnp.exp(cums_t - base).T, width, size_p) * dot_three(reads, state)
        result[span, :] = y
        if (b + 1) * block < rows:
            last = cums_t[:, block - 1 : block]
            tail = (jnp.exp(last - cums_t) * step_t).T
            fresh = dot_three(writes.T, x * spread(tail, width, size_p))
            if state is not None:
                fresh = jnp.exp(spread_row(last - base, width, size_p)) * state + fresh
            state, base = fresh, last


def share(ynorm, out_weight, place, k, out):
    rows, own = ynorm.shape[0], out.shape[1]
    for j in range(SIDE):
        head = lax.rem(place[0] + j, SIDE) * RING + lax.rem(place[1] + k, RING)
        spot = pl.multiple_of(head * own, own)
        out[j * rows : (j + 1) * rows, :] = dot(ynorm, out_weight[:, pl.ds(spot, own)]).astype(bf16)


def finish_kernel(size_p, ks, place, result, opened, both, cums, keep, other, out_gain, out_weight, ynorm_out, *shares):
    rows, width = result.shape
    state_n = both.shape[1] // 2
    first = place[2] == 0
    left, right = jnp.where(first, keep[...], other[...]), jnp.where(first, other[...], keep[...])
    state = jnp.concatenate([left, right], axis=1)
    carried = dot_pair(both[:, state_n:], state)
    y = result[...] + spread(jnp.exp(cums[...]).T, width, size_p) * carried
    g = y * opened[...]
    same = (iota((width, width), 0) // size_p == iota((width, width), 1) // size_p).astype(bf16)
    mean = dot_pair(g * g, same) / size_p
    ynorm = (g * lax.rsqrt(mean + eps) * out_gain[...]).astype(bf16)
    ynorm_out[...] = ynorm
    for k, out in zip(ks, shares):
        share(ynorm, out_weight, place, k, out)


def share_kernel(ks, place, ynorm, out_weight, *shares):
    for k, out in zip(ks, shares):
        share(ynorm[...], out_weight, place, k, out)


def on_chip(kernel, outs, args, place=None, scratch=(), flops=0, transcendentals=0, whole=()):
    specs = [pl.BlockSpec(memory_space=pl.ANY if i in whole else pltpu.VMEM) for i in range(len(args))]
    if place is not None:
        specs = [pl.BlockSpec(memory_space=pltpu.SMEM)] + specs
        args = [place] + list(args)
    moved = sum(a.size * a.dtype.itemsize for a in list(args) + list(outs))
    return pl.pallas_call(
        kernel,
        out_shape=outs,
        in_specs=specs,
        out_specs=[pl.BlockSpec(memory_space=pltpu.VMEM)] * len(outs),
        scratch_shapes=scratch,
        cost_estimate=pl.CostEstimate(flops=flops, bytes_accessed=moved, transcendentals=transcendentals),
        compiler_params=pltpu.CompilerParams(vmem_limit_bytes=VMEM_BYTES),
    )(*args)


def shape(dims, kind=f32):
    return jax.ShapeDtypeStruct(dims, kind)


def to_turn(block, step):
    route = [(i, i // RING * RING + (i + step) % RING) for i in range(SIDE * RING)]
    return lax.ppermute(block, "head", route)


def to_side(block):
    return lax.ppermute(block, "head", [(i, (i + RING) % (SIDE * RING)) for i in range(SIDE * RING)])


def to_core(block):
    return lax.ppermute(block, "section", [(i, i ^ 1) for i in range(lax.axis_size("section"))])


def gather_ring(block):
    found = {0: block}
    for k in range(1, RING // 2):
        found[k] = to_turn(found[k - 1], -1)
        found[RING - k] = to_turn(found[(RING - k + 1) % RING], 1)
    found[RING // 2] = to_turn(found[RING // 2 - 1], -1)
    return [found[k] for k in range(RING)]


def add(a, b):
    return (a.astype(f32) + b.astype(f32)).astype(bf16)


def reduce_ring(shares):
    far = RING // 2
    up = to_turn(shares[far], 1)
    down = None
    for k in range(far - 1, 0, -1):
        back = shares[RING - k]
        up = to_turn(add(up, shares[k]), 1)
        down = to_turn(back if down is None else add(down, back), -1)
    return shares[0].astype(f32) + up.astype(f32) + down.astype(f32)


def local(
    tokens,
    norm_gain,
    x_weight,
    gate_weight,
    dt_weight,
    dt_bias,
    decay_rate,
    skip_gain,
    bc_weight,
    out_gain,
    out_weight,
):
    rows, own = tokens.shape
    heads = decay_rate.shape[0]
    width = x_weight.shape[1]
    size_p = width // heads
    state_n = bc_weight.shape[1] // 2
    groups = lax.axis_size("head")
    sections = lax.axis_size("section")
    model = groups * own
    half = width // 2
    head, section = lax.axis_index("head"), lax.axis_index("section")
    place = jnp.stack([head // RING, head % RING, section % 2, section % ROW, section // ROW]).astype(jnp.int32)

    bc = jnp.concatenate([bc_weight[:, :state_n], bc_weight[:, state_n:]], 0)
    blocks = gather_ring(jnp.concatenate([tokens, bc, to_side(tokens), to_side(bc)], 0))
    normed, x, both, cums, step, slots = on_chip(
        functools.partial(front_kernel, rows, heads, size_p),
        [
            shape((rows, model), bf16),
            shape((rows, width)),
            shape((rows, 2 * state_n)),
            shape((HEADS, rows)),
            shape((HEADS, rows)),
            shape((ROW, state_n + 16, half), bf16),
        ],
        [
            *blocks,
            norm_gain.reshape(groups, own),
            x_weight,
            dt_weight.T,
            dt_bias.reshape(1, heads),
            decay_rate.reshape(1, heads),
        ],
        place,
        [pltpu.VMEM((model, 2 * state_n), bf16), pltpu.VMEM((128, model), bf16), pltpu.VMEM((8, 128), f32)],
        flops=2 * rows * model * (width + 2 * state_n + 128),
    )
    result, opened = on_chip(
        functools.partial(scan_kernel, heads, size_p, 256),
        [shape((rows, width)), shape((rows, width))],
        [normed, gate_weight, x, both, cums, step, skip_gain.reshape(1, heads)],
        scratch=[pltpu.VMEM((8, 128), f32)],
        flops=2 * rows * model * width + 12 * rows * 256 * (width + 3 * state_n),
        transcendentals=heads * rows * 256,
    )
    lines = sections // ROW
    by_row = [list(range(r * ROW, (r + 1) * ROW)) for r in range(lines)]
    by_spot = [list(range(p, sections, ROW)) for p in range(ROW)]
    copies, enter_own, enter_pair, logs = on_chip(
        row_kernel,
        [shape((lines, state_n + 16, half), bf16), shape((state_n, half)), shape((state_n, half)), shape((8, half))],
        [lax.all_to_all(slots, "section", 0, 0, axis_index_groups=by_row)],
        place,
    )
    keep, send = on_chip(
        prefix_kernel,
        [shape((state_n, half), bf16), shape((state_n, half), bf16)],
        [lax.all_to_all(copies, "section", 0, 0, axis_index_groups=by_spot), enter_own, enter_pair, logs],
        place,
    )
    rest = to_core(send)
    soon, later = (RING // 2, RING // 2 + 1), tuple(k for k in range(RING) if k // 2 != RING // 4)
    ynorm, *early = on_chip(
        functools.partial(finish_kernel, size_p, soon),
        [shape((rows, width), bf16)] + [shape((SIDE * rows, own), bf16)] * len(soon),
        [result, opened, both, cums, keep, rest, out_gain.reshape(1, width), out_weight],
        place,
        flops=2 * rows * width * (2 * SIDE * own + 4 * width),
    )
    late = on_chip(
        functools.partial(share_kernel, later),
        [shape((SIDE * rows, own), bf16)] * len(later),
        [ynorm, out_weight],
        place,
        flops=2 * rows * width * len(later) * SIDE * own,
    )
    made = dict(zip(soon + later, [*early, *late]))
    shares = [made[k] for k in range(RING)]
    summed = reduce_ring(shares)
    return tokens.astype(f32) + summed[:rows] + to_side(summed[rows:].astype(bf16)).astype(f32)


def solution(mesh):
    return jax.shard_map(
        local,
        mesh=mesh,
        in_specs=(
            P("section", "head"),
            P(),
            P(None, "head"),
            P(None, "head"),
            P(None, "head"),
            P("head"),
            P("head"),
            P("head"),
            P("head", None),
            P("head"),
            P("head", None),
        ),
        out_specs=P("section", "head"),
        check_vma=False,
    )
```

time: 167 us -> 170 us (1.018)
  the two profiles are of different devices: /device:TPU:8 before, /device:TPU:2 now
where the time goes in v5:
time: 170 us; the launch traced here: 169 us
  starting transfers between devices  72.3 us (43%)
  waiting for transfers between devices  56 us (33%)
  blocking collectives  20.3 us (12%)
  Pallas kernels  11.8 us (7%)
  local copies, waits for them, and re-layouts  6.6 us (4%)
    ppermute x14, starting transfers between devices, to_turn(): return lax.ppermute(block, 'head', route)  57.2 us
    ppermute x14, waiting for transfers between devices, to_turn(): return lax.ppermute(block, 'head', route)  40.1 us
    ppermute x3, waiting for transfers between devices, to_side(): lax.ppermute(block, 'head', [(i, (i + RING) % (SIDE * RING)) for i in ran...  16 us
    ppermute x3, starting transfers between devices, to_side(): lax.ppermute(block, 'head', [(i, (i + RING) % (SIDE * RING)) for i in ran...  13.2 us
    pallas_call x6, Pallas kernels, on_chip(): pl.pallas_call(kernel, out_shape=outs, in_specs=specs, out_specs=[pl.Bloc...  11.8 us
    all_to_all x1, blocking collectives, local(): lax.all_to_all(slots, 'section', 0, 0, axis_index_groups=by_row)  11.1 us
    all_to_all x1, blocking collectives, local(): lax.all_to_all(copies, 'section', 0, 0, axis_index_groups=by_spot)  9.22 us
    unnamed x23, local copies, waits for them, and re-layouts  5.69 us
  transfers between devices with their start and end apart: 18, of which 10 were waited for; matrix products, arithmetic and copies ran while one was open for 2% of the time, Pallas kernels for 2%

profile of v5, /device:TPU:2, one launch (start us, length us, event | category | flops | bytes accessed | tf_op | source)
XLA Modules:
  0.0 168.6 jit_solution(15285910460879299176)
XLA Ops:
  0.0 7.7 %collective-permute-start = (bf16[512,128]{1,0:T(8,128)(2,1)}, bf16[512,128]{1,0:T(8,128)(2,1)S(1)}, u32[]{:S(2)}, u32[]{:S(2)}) collective-permute-start(bf16[512,128]{1,0:T(8,128)(2,1)} %param.11), channel_id=1, source_target_pairs={{0,8},{1,9},{2,10},{3,11},{4,12},{5,13},{6,14},{7,15},{8,0},{9,1},... | collective-permute-start | bytes 393224 | tf_op jit(solution)/shard_map/ppermute | solution.py:265
  9.5 2.0 %collective-permute-start.1 = (bf16[256,128]{1,0:T(8,128)(2,1)S(1)}, bf16[256,128]{1,0:T(8,128)(2,1)S(1)}, u32[]{:S(2)}, u32[]{:S(2)}) collective-permute-start(bf16[256,128]{1,0:T(8,128)(2,1)S(1)} %pad_maximum_fusion), channel_id=1, source_target_pairs={{0,8},{1,9},{2,10},{3,11},{4,12},{5,13},{6,14},{7,15},{8,0},{9,1},... | collective-permute-start | bytes 196616 | tf_op jit(solution)/shard_map/ppermute | solution.py:265
  12.3 8.0 %collective-permute-done.1 = bf16[256,128]{1,0:T(8,128)(2,1)S(1)} collective-permute-done((bf16[256,128]{1,0:T(8,128)(2,1)S(1)}, bf16[256,128]{1,0:T(8,128)(2,1)S(1)}, u32[]{:S(2)}, u32[]{:S(2)}) %collective-permute-start.1) | collective-permute-done | bytes 65568 | tf_op jit(solution)/shard_map/ppermute | solution.py:265
  20.3 10.9 %collective-permute-start.2 = (bf16[1536,128]{1,0:T(8,128)(2,1)S(1)}, bf16[1536,128]{1,0:T(8,128)(2,1)S(1)}, u32[]{:S(2)}, u32[]{:S(2)}) collective-permute-start(bf16[1536,128]{1,0:T(8,128)(2,1)S(1)} %constant_dynamic-update-slice_fusion.refs_0_), channel_id=1, source_target_pairs={{0,7},{1,0},{2,1},{3,2},{4,3},{5,4},{6,5},{7,6},{8,15},{9,8},{10,9... | collective-permute-start | bytes 1179656 | tf_op jit(solution)/shard_map/ppermute | solution.py:261
  33.2 6.4 %collective-permute-done.2.refs_1_ = bf16[1536,128]{1,0:T(8,128)(2,1)S(1)} collective-permute-done((bf16[1536,128]{1,0:T(8,128)(2,1)S(1)}, bf16[1536,128]{1,0:T(8,128)(2,1)S(1)}, u32[]{:S(2)}, u32[]{:S(2)}) %collective-permute-start.2) | collective-permute-done | bytes 393248 | tf_op jit(solution)/shard_map/ppermute | solution.py:261
  39.6 5.6 %collective-permute-start.3 = (bf16[1536,128]{1,0:T(8,128)(2,1)S(1)}, bf16[1536,128]{1,0:T(8,128)(2,1)S(1)}, u32[]{:S(2)}, u32[]{:S(2)}) collective-permute-start(bf16[1536,128]{1,0:T(8,128)(2,1)S(1)} %collective-permute-done.2.refs_1_), channel_id=1, source_target_pairs={{0,7},{1,0},{2,1},{3,2},{4,3},{5,4},{6,5},{7,6},{8,15},{9,8},{10,9... | collective-permute-start | bytes 1179656 | tf_op jit(solution)/shard_map/ppermute | solution.py:261
  47.2 5.5 %collective-permute-done.3.refs_2_ = bf16[1536,128]{1,0:T(8,128)(2,1)S(1)} collective-permute-done((bf16[1536,128]{1,0:T(8,128)(2,1)S(1)}, bf16[1536,128]{1,0:T(8,128)(2,1)S(1)}, u32[]{:S(2)}, u32[]{:S(2)}) %collective-permute-start.3) | collective-permute-done | bytes 393248 | tf_op jit(solution)/shard_map/ppermute | solution.py:261
  52.6 5.6 %collective-permute-start.4 = (bf16[1536,128]{1,0:T(8,128)(2,1)S(1)}, bf16[1536,128]{1,0:T(8,128)(2,1)S(1)}, u32[]{:S(2)}, u32[]{:S(2)}) collective-permute-start(bf16[1536,128]{1,0:T(8,128)(2,1)S(1)} %collective-permute-done.3.refs_2_), channel_id=1, source_target_pairs={{0,7},{1,0},{2,1},{3,2},{4,3},{5,4},{6,5},{7,6},{8,15},{9,8},{10,9... | collective-permute-start | bytes 1179656 | tf_op jit(solution)/shard_map/ppermute | solution.py:261
  60.2 4.6 %collective-permute-done.4.refs_3_ = bf16[1536,128]{1,0:T(8,128)(2,1)S(1)} collective-permute-done((bf16[1536,128]{1,0:T(8,128)(2,1)S(1)}, bf16[1536,128]{1,0:T(8,128)(2,1)S(1)}, u32[]{:S(2)}, u32[]{:S(2)}) %collective-permute-start.4) | collective-permute-done | bytes 393248 | tf_op jit(solution)/shard_map/ppermute | solution.py:261
  64.8 5.6 %collective-permute-start.5 = (bf16[1536,128]{1,0:T(8,128)(2,1)S(1)}, bf16[1536,128]{1,0:T(8,128)(2,1)S(1)}, u32[]{:S(2)}, u32[]{:S(2)}) collective-permute-start(bf16[1536,128]{1,0:T(8,128)(2,1)S(1)} %collective-permute-done.4.refs_3_), channel_id=1, source_target_pairs={{0,7},{1,0},{2,1},{3,2},{4,3},{5,4},{6,5},{7,6},{8,15},{9,8},{10,9... | collective-permute-start | bytes 1179656 | tf_op jit(solution)/shard_map/ppermute | solution.py:261
  70.5 5.5 %collective-permute-done.5.refs_4_ = bf16[1536,128]{1,0:T(8,128)(2,1)S(1)} collective-permute-done((bf16[1536,128]{1,0:T(8,128)(2,1)S(1)}, bf16[1536,128]{1,0:T(8,128)(2,1)S(1)}, u32[]{:S(2)}, u32[]{:S(2)}) %collective-permute-start.5) | collective-permute-done | bytes 393248 | tf_op jit(solution)/shard_map/ppermute | solution.py:261
  79.9 5.3 %shard_map.109 = (bf16[512,2048]{1,0:T(8,128)(2,1)S(1)}, f32[512,256]{1,0:T(8,128)S(1)}, f32[512,256]{1,0:T(8,128)S(1)}, f32[16,512]{1,0:T(8,128)S(1)}, f32[16,5...) custom-call(s32[5]{0:T(128)S(1)} %stack.23.place, bf16[1536,128]{1,0:T(8,128)(2,1)S(1)} %constant_dynamic-update-slice_fusion.refs_0_, ...), custom_call_target="tpu_custom_call" | custom-call | flops 1342177280 | bytes 7725108 | tf_op jit(solution)/shard_map/pallas_call | solution.py:244
  85.2 11.1 %all_to_all.10.gathered = bf16[8,144,128]{2,1,0:T(8,128)(2,1)S(1)} all-to-all(bf16[8,144,128]{2,1,0:T(8,128)(2,1)S(1)} %get-tuple-element.35), channel_id=1, replica_groups={{0,16,32,48,64,80,96,112},{128,144,160,176,192,208,224,240},{256,272,28..., dimensions={0} | all-to-all | bytes 589824 | tf_op jit(solution)/shard_map/all_to_all | solution.py:359
  96.9 9.2 %all_to_all.11.gathered = bf16[4,144,128]{2,1,0:T(8,128)(2,1)S(1)} all-to-all(bf16[4,144,128]{2,1,0:T(8,128)(2,1)S(1)} %get-tuple-element.36), channel_id=1, replica_groups={{0,128,256,384},{16,144,272,400},{32,160,288,416},{48,176,304,432},{64,..., dimensions={0} | all-to-all | bytes 294912 | tf_op jit(solution)/shard_map/all_to_all | solution.py:365
  108.7 2.0 %shard_map.110 = (f32[512,256]{1,0:T(8,128)S(1)}, f32[512,256]{1,0:T(8,128)S(1)}) custom-call(bf16[512,2048]{1,0:T(8,128)(2,1)S(1)} %get-tuple-element.28.normed, bf16[2048,256]{1,0:T(8,128)(2,1)S(1)} %copy-done.3, f32[512,256]{1,0:T(8,128)S(1)} %get-tuple-element.29.x_in, f32[512,256]{1,0:T(8,128)S(1)} %get-tuple-element.30.both_in.both, ...), custom_call_target="tpu_custom_call" | custom-call | flops 1543503872 | bytes 5308432 | tf_op jit(solution)/shard_map/pallas_call | solution.py:244
  114.4 5.6 %collective-permute-start.14 = (bf16[1024,128]{1,0:T(8,128)(2,1)S(1)}, bf16[1024,128]{1,0:T(8,128)(2,1)S(1)}, u32[]{:S(2)}, u32[]{:S(2)}) collective-permute-start(bf16[1024,128]{1,0:T(8,128)(2,1)S(1)} %get-tuple-element.48), channel_id=1, source_target_pairs={{0,7},{1,0},{2,1},{3,2},{4,3},{5,4},{6,5},{7,6},{8,15},{9,8},{10,9... | collective-permute-start | bytes 786440 | tf_op jit(solution)/shard_map/ppermute | solution.py:261
  121.5 3.5 %collective-permute-done.10 = bf16[1024,128]{1,0:T(8,128)(2,1)S(1)} collective-permute-done((bf16[1024,128]{1,0:T(8,128)(2,1)S(1)}, bf16[1024,128]{1,0:T(8,128)(2,1)S(1)}, u32[]{:S(2)}, u32[]{:S(2)}) %collective-permute-start.10) | collective-permute-done | bytes 262176 | tf_op jit(solution)/shard_map/ppermute | solution.py:261
  127.1 5.3 %collective-permute-start.15 = (bf16[1024,128]{1,0:T(8,128)(2,1)S(1)}, bf16[1024,128]{1,0:T(8,128)(2,1)S(1)}, u32[]{:S(2)}, u32[]{:S(2)}) collective-permute-start(bf16[1024,128]{1,0:T(8,128)(2,1)S(1)} %add_convert_fusion.1), channel_id=1, source_target_pairs={{0,7},{1,0},{2,1},{3,2},{4,3},{5,4},{6,5},{7,6},{8,15},{9,8},{10,9... | collective-permute-start | bytes 786440 | tf_op jit(solution)/shard_map/ppermute | solution.py:261
  132.4 3.9 %collective-permute-done.11 = bf16[1024,128]{1,0:T(8,128)(2,1)S(1)} collective-permute-done((bf16[1024,128]{1,0:T(8,128)(2,1)S(1)}, bf16[1024,128]{1,0:T(8,128)(2,1)S(1)}, u32[]{:S(2)}, u32[]{:S(2)}) %collective-permute-start.11) | collective-permute-done | bytes 262176 | tf_op jit(solution)/shard_map/ppermute | solution.py:261
  138.4 5.1 %collective-permute-start.16 = (bf16[1024,128]{1,0:T(8,128)(2,1)S(1)}, bf16[1024,128]{1,0:T(8,128)(2,1)S(1)}, u32[]{:S(2)}, u32[]{:S(2)}) collective-permute-start(bf16[1024,128]{1,0:T(8,128)(2,1)S(1)} %add_convert_fusion), channel_id=1, source_target_pairs={{0,7},{1,0},{2,1},{3,2},{4,3},{5,4},{6,5},{7,6},{8,15},{9,8},{10,9... | collective-permute-start | bytes 786440 | tf_op jit(solution)/shard_map/ppermute | solution.py:261
  143.5 3.2 %collective-permute-done.12 = bf16[1024,128]{1,0:T(8,128)(2,1)S(1)} collective-permute-done((bf16[1024,128]{1,0:T(8,128)(2,1)S(1)}, bf16[1024,128]{1,0:T(8,128)(2,1)S(1)}, u32[]{:S(2)}, u32[]{:S(2)}) %collective-permute-start.12) | collective-permute-done | bytes 262176 | tf_op jit(solution)/shard_map/ppermute | solution.py:261
  148.8 7.5 %collective-permute-done.13 = bf16[1024,128]{1,0:T(8,128)(2,1)S(1)} collective-permute-done((bf16[1024,128]{1,0:T(8,128)(2,1)S(1)}, bf16[1024,128]{1,0:T(8,128)(2,1)S(1)}, u32[]{:S(2)}, u32[]{:S(2)}) %collective-permute-start.13) | collective-permute-done | bytes 262176 | tf_op jit(solution)/shard_map/ppermute | solution.py:261
  156.4 3.5 %collective-permute-start.17 = (bf16[512,128]{1,0:T(8,128)(2,1)S(1)}, bf16[512,128]{1,0:T(8,128)(2,1)S(1)}, u32[]{:S(2)}, u32[]{:S(2)}) collective-permute-start(bf16[512,128]{1,0:T(8,128)(2,1)S(1)} %slice.25), channel_id=1, source_target_pairs={{0,8},{1,9},{2,10},{3,11},{4,12},{5,13},{6,14},{7,15},{8,0},{9,1},... | collective-permute-start | bytes 393224 | tf_op jit(solution)/shard_map/ppermute | solution.py:265
  159.9 7.9 %collective-permute-done.17 = bf16[512,128]{1,0:T(8,128)(2,1)S(1)} collective-permute-done((bf16[512,128]{1,0:T(8,128)(2,1)S(1)}, bf16[512,128]{1,0:T(8,128)(2,1)S(1)}, u32[]{:S(2)}, u32[]{:S(2)}) %collective-permute-start.17) | collective-permute-done | bytes 131104 | tf_op jit(solution)/shard_map/ppermute | solution.py:265
  (55 shorter events, 27.7 us)
Async XLA Ops:
  0.0 12.3 %collective-permute-start = (bf16[512,128]{1,0:T(8,128)(2,1)}, bf16[512,128]{1,0:T(8,128)(2,1)S(1)}, u32[]{:S(2)}, u32[]{:S(2)}) collective-permute-start(bf16[512,128]{1,0:T(8,128)(2,1)} %param.11), channel_id=1, source_target_pairs={{0,8},{1,9},{2,10},{3,11},{4,12},{5,13},{6,14},{7,15},{8,0},{9,1},... | collective-permute-start | bytes 393224 | tf_op jit(solution)/shard_map/ppermute | solution.py:265
  9.5 10.9 %collective-permute-start.1 = (bf16[256,128]{1,0:T(8,128)(2,1)S(1)}, bf16[256,128]{1,0:T(8,128)(2,1)S(1)}, u32[]{:S(2)}, u32[]{:S(2)}) collective-permute-start(bf16[256,128]{1,0:T(8,128)(2,1)S(1)} %pad_maximum_fusion), channel_id=1, source_target_pairs={{0,8},{1,9},{2,10},{3,11},{4,12},{5,13},{6,14},{7,15},{8,0},{9,1},... | collective-permute-start | bytes 196616 | tf_op jit(solution)/shard_map/ppermute | solution.py:265
  20.3 19.3 %collective-permute-start.2 = (bf16[1536,128]{1,0:T(8,128)(2,1)S(1)}, bf16[1536,128]{1,0:T(8,128)(2,1)S(1)}, u32[]{:S(2)}, u32[]{:S(2)}) collective-permute-start(bf16[1536,128]{1,0:T(8,128)(2,1)S(1)} %constant_dynamic-update-slice_fusion.refs_0_), channel_id=1, source_target_pairs={{0,7},{1,0},{2,1},{3,2},{4,3},{5,4},{6,5},{7,6},{8,15},{9,8},{10,9... | collective-permute-start | bytes 1179656 | tf_op jit(solution)/shard_map/ppermute | solution.py:261
  31.3 13.9 %collective-permute-start.6 = (bf16[1536,128]{1,0:T(8,128)(2,1)S(1)}, bf16[1536,128]{1,0:T(8,128)(2,1)S(1)}, u32[]{:S(2)}, u32[]{:S(2)}) collective-permute-start(bf16[1536,128]{1,0:T(8,128)(2,1)S(1)} %constant_dynamic-update-slice_fusion.refs_0_), channel_id=1, source_target_pairs={{0,1},{1,2},{2,3},{3,4},{4,5},{5,6},{6,7},{7,0},{8,9},{9,10},{10,1... | collective-permute-start | bytes 1179656 | tf_op jit(solution)/shard_map/ppermute | solution.py:261
  39.6 13.0 %collective-permute-start.3 = (bf16[1536,128]{1,0:T(8,128)(2,1)S(1)}, bf16[1536,128]{1,0:T(8,128)(2,1)S(1)}, u32[]{:S(2)}, u32[]{:S(2)}) collective-permute-start(bf16[1536,128]{1,0:T(8,128)(2,1)S(1)} %collective-permute-done.2.refs_1_), channel_id=1, source_target_pairs={{0,7},{1,0},{2,1},{3,2},{4,3},{5,4},{6,5},{7,6},{8,15},{9,8},{10,9... | collective-permute-start | bytes 1179656 | tf_op jit(solution)/shard_map/ppermute | solution.py:261
  45.2 13.0 %collective-permute-start.7 = (bf16[1536,128]{1,0:T(8,128)(2,1)S(1)}, bf16[1536,128]{1,0:T(8,128)(2,1)S(1)}, u32[]{:S(2)}, u32[]{:S(2)}) collective-permute-start(bf16[1536,128]{1,0:T(8,128)(2,1)S(1)} %collective-permute-done.6.refs_7_), channel_id=1, source_target_pairs={{0,1},{1,2},{2,3},{3,4},{4,5},{5,6},{6,7},{7,0},{8,9},{9,10},{10,1... | collective-permute-start | bytes 1179656 | tf_op jit(solution)/shard_map/ppermute | solution.py:261
  52.6 12.1 %collective-permute-start.4 = (bf16[1536,128]{1,0:T(8,128)(2,1)S(1)}, bf16[1536,128]{1,0:T(8,128)(2,1)S(1)}, u32[]{:S(2)}, u32[]{:S(2)}) collective-permute-start(bf16[1536,128]{1,0:T(8,128)(2,1)S(1)} %collective-permute-done.3.refs_2_), channel_id=1, source_target_pairs={{0,7},{1,0},{2,1},{3,2},{4,3},{5,4},{6,5},{7,6},{8,15},{9,8},{10,9... | collective-permute-start | bytes 1179656 | tf_op jit(solution)/shard_map/ppermute | solution.py:261
  58.3 12.2 %collective-permute-start.8 = (bf16[1536,128]{1,0:T(8,128)(2,1)S(1)}, bf16[1536,128]{1,0:T(8,128)(2,1)S(1)}, u32[]{:S(2)}, u32[]{:S(2)}) collective-permute-start(bf16[1536,128]{1,0:T(8,128)(2,1)S(1)} %collective-permute-done.7.refs_6_), channel_id=1, source_target_pairs={{0,1},{1,2},{2,3},{3,4},{4,5},{5,6},{6,7},{7,0},{8,9},{9,10},{10,1... | collective-permute-start | bytes 1179656 | tf_op jit(solution)/shard_map/ppermute | solution.py:261
  64.8 11.2 %collective-permute-start.5 = (bf16[1536,128]{1,0:T(8,128)(2,1)S(1)}, bf16[1536,128]{1,0:T(8,128)(2,1)S(1)}, u32[]{:S(2)}, u32[]{:S(2)}) collective-permute-start(bf16[1536,128]{1,0:T(8,128)(2,1)S(1)} %collective-permute-done.4.refs_3_), channel_id=1, source_target_pairs={{0,7},{1,0},{2,1},{3,2},{4,3},{5,4},{6,5},{7,6},{8,15},{9,8},{10,9... | collective-permute-start | bytes 1179656 | tf_op jit(solution)/shard_map/ppermute | solution.py:261
  75.9 1.2 copy-start.2
  79.9 28.8 %copy-start.3 = (bf16[2048,256]{1,0:T(8,128)(2,1)S(1)}, bf16[2048,256]{1,0:T(8,128)(2,1)}, u32[]{:S(2)}) copy-start(bf16[2048,256]{1,0:T(8,128)(2,1)} %gate_weight.1) | copy-start | bytes 3145732
  79.9 28.8 %copy-start.8 = (f32[4]{0:T(128)S(1)}, f32[4]{0:T(128)}, u32[]{:S(2)}) copy-start(f32[4]{0:T(128)} %param.18) | copy-start | bytes 52
  106.8 4.0 %collective-permute-start.9 = (bf16[128,128]{1,0:T(8,128)(2,1)S(1)}, bf16[128,128]{1,0:T(8,128)(2,1)S(1)}, u32[]{:S(2)}, u32[]{:S(2)}) collective-permute-start(bf16[128,128]{1,0:T(8,128)(2,1)S(1)} %get-tuple-element.41), channel_id=1, source_target_pairs={{0,16},{16,0},{32,48},{48,32},{64,80},{80,64},{96,112},{112,96},{1... | collective-permute-start | bytes 98312 | tf_op jit(solution)/shard_map/ppermute | solution.py:269
  108.7 2.0 %copy-start = (bf16[256,2048]{1,0:T(8,128)(2,1)S(1)}, bf16[256,2048]{1,0:T(8,128)(2,1)}, u32[]{:S(2)}) copy-start(bf16[256,2048]{1,0:T(8,128)(2,1)} %out_weight.3) | copy-start | bytes 3145732
  108.7 2.0 %copy-start.1 = (f32[256]{0:T(256)S(1)}, f32[256]{0:T(256)}, u32[]{:S(2)}) copy-start(f32[256]{0:T(256)} %param.20) | copy-start | bytes 3076
  112.4 12.6 %collective-permute-start.10 = (bf16[1024,128]{1,0:T(8,128)(2,1)S(1)}, bf16[1024,128]{1,0:T(8,128)(2,1)S(1)}, u32[]{:S(2)}, u32[]{:S(2)}) collective-permute-start(bf16[1024,128]{1,0:T(8,128)(2,1)S(1)} %get-tuple-element.44), channel_id=1, source_target_pairs={{0,1},{1,2},{2,3},{3,4},{4,5},{5,6},{6,7},{7,0},{8,9},{9,10},{10,1... | collective-permute-start | bytes 786440 | tf_op jit(solution)/shard_map/ppermute | solution.py:261
  114.4 12.6 %collective-permute-start.14 = (bf16[1024,128]{1,0:T(8,128)(2,1)S(1)}, bf16[1024,128]{1,0:T(8,128)(2,1)S(1)}, u32[]{:S(2)}, u32[]{:S(2)}) collective-permute-start(bf16[1024,128]{1,0:T(8,128)(2,1)S(1)} %get-tuple-element.48), channel_id=1, source_target_pairs={{0,7},{1,0},{2,1},{3,2},{4,3},{5,4},{6,5},{7,6},{8,15},{9,8},{10,9... | collective-permute-start | bytes 786440 | tf_op jit(solution)/shard_map/ppermute | solution.py:261
  125.1 11.2 %collective-permute-start.11 = (bf16[1024,128]{1,0:T(8,128)(2,1)S(1)}, bf16[1024,128]{1,0:T(8,128)(2,1)S(1)}, u32[]{:S(2)}, u32[]{:S(2)}) collective-permute-start(bf16[1024,128]{1,0:T(8,128)(2,1)S(1)} %add_convert_fusion.4), channel_id=1, source_target_pairs={{0,1},{1,2},{2,3},{3,4},{4,5},{5,6},{6,7},{7,0},{8,9},{9,10},{10,1... | collective-permute-start | bytes 786440 | tf_op jit(solution)/shard_map/ppermute | solution.py:261
  127.1 40.7 %copy-start.9 = (bf16[512,128]{1,0:T(8,128)(2,1)S(1)}, bf16[512,128]{1,0:T(8,128)(2,1)}, u32[]{:S(2)}) copy-start(bf16[512,128]{1,0:T(8,128)(2,1)} %param.11) | copy-start | bytes 393220
  127.1 11.2 %collective-permute-start.15 = (bf16[1024,128]{1,0:T(8,128)(2,1)S(1)}, bf16[1024,128]{1,0:T(8,128)(2,1)S(1)}, u32[]{:S(2)}, u32[]{:S(2)}) collective-permute-start(bf16[1024,128]{1,0:T(8,128)(2,1)S(1)} %add_convert_fusion.1), channel_id=1, source_target_pairs={{0,7},{1,0},{2,1},{3,2},{4,3},{5,4},{6,5},{7,6},{8,15},{9,8},{10,9... | collective-permute-start | bytes 786440 | tf_op jit(solution)/shard_map/ppermute | solution.py:261
  136.4 10.4 %collective-permute-start.12 = (bf16[1024,128]{1,0:T(8,128)(2,1)S(1)}, bf16[1024,128]{1,0:T(8,128)(2,1)S(1)}, u32[]{:S(2)}, u32[]{:S(2)}) collective-permute-start(bf16[1024,128]{1,0:T(8,128)(2,1)S(1)} %add_convert_fusion.3), channel_id=1, source_target_pairs={{0,1},{1,2},{2,3},{3,4},{4,5},{5,6},{6,7},{7,0},{8,9},{9,10},{10,1... | collective-permute-start | bytes 786440 | tf_op jit(solution)/shard_map/ppermute | solution.py:261
  138.4 10.4 %collective-permute-start.16 = (bf16[1024,128]{1,0:T(8,128)(2,1)S(1)}, bf16[1024,128]{1,0:T(8,128)(2,1)S(1)}, u32[]{:S(2)}, u32[]{:S(2)}) collective-permute-start(bf16[1024,128]{1,0:T(8,128)(2,1)S(1)} %add_convert_fusion), channel_id=1, source_target_pairs={{0,7},{1,0},{2,1},{3,2},{4,3},{5,4},{6,5},{7,6},{8,15},{9,8},{10,9... | collective-permute-start | bytes 786440 | tf_op jit(solution)/shard_map/ppermute | solution.py:261
  146.8 9.5 %collective-permute-start.13 = (bf16[1024,128]{1,0:T(8,128)(2,1)S(1)}, bf16[1024,128]{1,0:T(8,128)(2,1)S(1)}, u32[]{:S(2)}, u32[]{:S(2)}) collective-permute-start(bf16[1024,128]{1,0:T(8,128)(2,1)S(1)} %add_convert_fusion.2), channel_id=1, source_target_pairs={{0,1},{1,2},{2,3},{3,4},{4,5},{5,6},{6,7},{7,0},{8,9},{9,10},{10,1... | collective-permute-start | bytes 786440 | tf_op jit(solution)/shard_map/ppermute | solution.py:261
  156.4 11.4 %collective-permute-start.17 = (bf16[512,128]{1,0:T(8,128)(2,1)S(1)}, bf16[512,128]{1,0:T(8,128)(2,1)S(1)}, u32[]{:S(2)}, u32[]{:S(2)}) collective-permute-start(bf16[512,128]{1,0:T(8,128)(2,1)S(1)} %slice.25), channel_id=1, source_target_pairs={{0,8},{1,9},{2,10},{3,11},{4,12},{5,13},{6,14},{7,15},{8,0},{9,1},... | collective-permute-start | bytes 393224 | tf_op jit(solution)/shard_map/ppermute | solution.py:265
  (4 other events, 2.7 us)

commit v6 on v5

--- a/solution.py
+++ b/solution.py
@@ -69,11 +69,9 @@
     return jnp.sum(jnp.where(owners(width, size_p), heads_on_rows, 0.0), axis=0, keepdims=True)
 
 
-def stood(row, scratch):
-    scratch[...] = jnp.zeros_like(scratch)
-    scratch[0:1, 0 : row.shape[1]] = row[...]
+def stood(row):
     square = iota((HEADS, HEADS), 0) == iota((HEADS, HEADS), 1)
-    return jnp.sum(jnp.where(square, scratch[0:1, 0:HEADS], 0.0), axis=1, keepdims=True)
+    return jnp.sum(jnp.where(square, row, 0.0), axis=1, keepdims=True)
 
 
 def log_rows(row):
@@ -87,15 +85,12 @@
     return tail[0:1] + tail[1:2]
 
 
-def front_kernel(rows, heads, size_p, place, *refs):
+def norm_kernel(rows, place, *refs):
     blocks = refs[:RING]
-    (gain, x_weight, dt_weight, bias, rate) = refs[RING : RING + 5]
-    (normed, x_out, both_out, cums_out, step_out, slots, bc, wide, line) = refs[RING + 5 :]
+    small, normed, bc_half = refs[RING:]
     own = blocks[0].shape[1]
     side, turn = place[0], place[1]
     piece = blocks[0].shape[0] // SIDE
-    width = heads * size_p
-    state_n = own
 
     def parts():
         for k in range(RING):
@@ -112,31 +107,41 @@
     for block, at, head in parts():
         value = block[at : at + rows, :].astype(f32)
         spot = pl.multiple_of(head * own, own)
-        normed[:, pl.ds(spot, own)] = (value * scale * gain[pl.ds(head, 1), :]).astype(bf16)
-        bc[pl.ds(spot, own), 0:state_n] = block[at + rows : at + rows + own, :]
-        bc[pl.ds(spot, own), state_n : 2 * state_n] = block[at + rows + own : at + piece, :]
-    wide[...] = jnp.zeros_like(wide)
-    wide[0:heads, :] = dt_weight[...]
+        normed[:, pl.ds(spot, own)] = (value * scale * small[pl.ds(head + 8, 1), :]).astype(bf16)
+        bc_half[pl.ds(spot, own), :] = block[at + rows : at + piece, :]
+
+
+def project_kernel(heads, size_p, normed, x_weight, dt_weight, small, x_out, tailed_out, cums_out, step_out):
+    rows = normed.shape[0]
+    width = heads * size_p
     whole = normed[...]
-    raw = dot(whole, wide[...], ((1,), (1,))).T[0:HEADS, :]
-    step = softplus(raw + stood(bias, line))
-    decay = -stood(rate, line) * step
+    raw = dot(whole, dt_weight[...], ((1,), (1,))).T[0:HEADS, :]
+    step = softplus(raw + stood(small[0:1, 0:HEADS]))
+    decay = -stood(small[1:2, 0:HEADS]) * step
     cums = running_sum(decay)
-    last = cums[:, rows - 1 : rows]
-    tail = (jnp.exp(last - cums) * step).T
+    tail = (jnp.exp(cums[:, rows - 1 : rows] - cums) * step).T
     x = silu(dot(whole, x_weight[...]))
-    both = dot(whole, bc[...])
-    state = dot_three(both[:, 0:state_n].T, x * spread(tail, width, size_p)).astype(bf16)
-    logs = log_rows(spread_row(last, width, size_p))
+    x_out[...] = x
+    tailed_out[...] = x * spread(tail, width, size_p)
+    cums_out[...] = cums
+    step_out[...] = step
+
+
+def state_kernel(size_p, place, normed, tailed, bc_mine, bc_other, cums, both_out, slots):
+    rows, width = tailed.shape
+    state_n = bc_mine.shape[1]
     half = width // 2
+    first = place[2] == 0
+    one, two = dot(normed[...], bc_mine[...]), dot(normed[...], bc_other[...])
+    writes, reads = jnp.where(first, one, two), jnp.where(first, two, one)
+    both_out[:, 0:state_n] = writes
+    both_out[:, state_n:] = reads
+    state = dot_three(writes.T, tailed[...]).astype(bf16)
+    logs = log_rows(spread_row(cums[:, rows - 1 : rows], width, size_p))
     for i in range(slots.shape[0]):
         at = i % 2 * half
         slots[i, 0:state_n, :] = state[:, at : at + half]
         slots[i, state_n : state_n + 16, :] = logs[:, at : at + half]
-    x_out[...] = x
-    both_out[...] = both
-    cums_out[...] = cums
-    step_out[...] = step
 
 
 def row_kernel(place, gathered, copies, own_out, pair_out, logs_out):
@@ -173,12 +178,12 @@
     send[...] = (jnp.exp(logs[1:2, :]) * state + pair[...]).astype(bf16)
 
 
-def scan_kernel(heads, size_p, block, normed, gate_weight, x_in, both_in, cums_in, step_in, gain, result, opened, line):
+def scan_kernel(heads, size_p, block, normed, gate_weight, x_in, both_in, cums_in, step_in, small, result, opened):
     rows, width = x_in.shape
     state_n = both_in.shape[1] // 2
     opened[...] = silu(dot(normed[...], gate_weight[...]))
     lower = iota((block, block), 0) >= iota((block, block), 1)
-    skip = spread_row(stood(gain, line), width, size_p)
+    skip = spread_row(stood(small[2:3, 0:HEADS]), width, size_p)
     state = None
     base = None
     for b in range(rows // block):
@@ -235,8 +240,8 @@
         share(ynorm[...], out_weight, place, k, out)
 
 
-def on_chip(kernel, outs, args, place=None, scratch=(), flops=0, transcendentals=0, whole=()):
-    specs = [pl.BlockSpec(memory_space=pl.ANY if i in whole else pltpu.VMEM) for i in range(len(args))]
+def on_chip(kernel, outs, args, place=None, scratch=(), flops=0, transcendentals=0):
+    specs = [pl.BlockSpec(memory_space=pltpu.VMEM)] * len(args)
     if place is not None:
         specs = [pl.BlockSpec(memory_space=pltpu.SMEM)] + specs
         args = [place] + list(args)
@@ -318,35 +323,38 @@
     head, section = lax.axis_index("head"), lax.axis_index("section")
     place = jnp.stack([head // RING, head % RING, section % 2, section % ROW, section // ROW]).astype(jnp.int32)
 
-    bc = jnp.concatenate([bc_weight[:, :state_n], bc_weight[:, state_n:]], 0)
-    blocks = gather_ring(jnp.concatenate([tokens, bc, to_side(tokens), to_side(bc)], 0))
-    normed, x, both, cums, step, slots = on_chip(
-        functools.partial(front_kernel, rows, heads, size_p),
-        [
-            shape((rows, model), bf16),
-            shape((rows, width)),
-            shape((rows, 2 * state_n)),
-            shape((HEADS, rows)),
-            shape((HEADS, rows)),
-            shape((ROW, state_n + 16, half), bf16),
-        ],
-        [
-            *blocks,
-            norm_gain.reshape(groups, own),
-            x_weight,
-            dt_weight.T,
-            dt_bias.reshape(1, heads),
-            decay_rate.reshape(1, heads),
-        ],
-        place,
-        [pltpu.VMEM((model, 2 * state_n), bf16), pltpu.VMEM((128, model), bf16), pltpu.VMEM((8, 128), f32)],
-        flops=2 * rows * model * (width + 2 * state_n + 128),
+    piece = lax.dynamic_slice_in_dim(bc_weight, section % 2 * state_n, state_n, 1)
+    packed = jnp.concatenate([tokens, piece], 0)
+    far = RING // 2
+    blocks = gather_ring(jnp.concatenate([packed, to_side(packed)], 0))
+    dt_wide = jnp.pad(dt_weight.T, ((0, 128 - heads), (0, 0)))
+    small = jnp.zeros((8 + groups, own), f32)
+    small = small.at[0, :heads].set(dt_bias).at[1, :heads].set(decay_rate).at[2, :heads].set(skip_gain)
+    small = small.at[8:].set(norm_gain.reshape(groups, own))
+    normed, bc_mine = on_chip(
+        functools.partial(norm_kernel, rows),
+        [shape((rows, model), bf16), shape((model, state_n), bf16)],
+        [*blocks, small],
+        place,
+    )
+    bc_other = to_core(bc_mine)
+    x, tailed, cums, step = on_chip(
+        functools.partial(project_kernel, heads, size_p),
+        [shape((rows, width)), shape((rows, width)), shape((HEADS, rows)), shape((HEADS, rows))],
+        [normed, x_weight, dt_wide, small],
+        flops=2 * rows * model * (width + 128),
+    )
+    both, slots = on_chip(
+        functools.partial(state_kernel, size_p),
+        [shape((rows, 2 * state_n)), shape((ROW, state_n + 16, half), bf16)],
+        [normed, tailed, bc_mine, bc_other, cums],
+        place,
+        flops=2 * rows * model * 2 * state_n,
     )
     result, opened = on_chip(
         functools.partial(scan_kernel, heads, size_p, 256),
         [shape((rows, width)), shape((rows, width))],
-        [normed, gate_weight, x, both, cums, step, skip_gain.reshape(1, heads)],
-        scratch=[pltpu.VMEM((8, 128), f32)],
+        [normed, gate_weight, x, both, cums, step, small],
         flops=2 * rows * model * width + 12 * rows * 256 * (width + 3 * state_n),
         transcendentals=heads * rows * 256,
     )
@@ -366,7 +374,7 @@
         place,
     )
     rest = to_core(send)
-    soon, later = (RING // 2, RING // 2 + 1), tuple(k for k in range(RING) if k // 2 != RING // 4)
+    soon, later = (far, far + 1), tuple(k for k in range(RING) if k // 2 != RING // 4)
     ynorm, *early = on_chip(
         functools.partial(finish_kernel, size_p, soon),
         [shape((rows, width), bf16)] + [shape((SIDE * rows, own), bf16)] * len(soon),

time: 170 us -> 164 us (0.965)
  the two profiles are of different devices: /device:TPU:2 before, /device:TPU:8 now
where the time goes in v6:
time: 164 us; the launch traced here: 163 us
  starting transfers between devices  73.4 us (45%)
  waiting for transfers between devices  42.6 us (26%)
  blocking collectives  25.5 us (16%)
  Pallas kernels  13.9 us (8%)
  local copies, waits for them, and re-layouts  3.91 us (2%)
  other arithmetic  3.12 us (2%)
    ppermute x14, starting transfers between devices, to_turn(): return lax.ppermute(block, 'head', route)  57.3 us
    ppermute x14, waiting for transfers between devices, to_turn(): return lax.ppermute(block, 'head', route)  29.2 us
    pallas_call x8, Pallas kernels, on_chip(): pl.pallas_call(kernel, out_shape=outs, in_specs=specs, out_specs=[pl.Bloc...  13.9 us
    all_to_all x1, blocking collectives, local(): lax.all_to_all(copies, 'section', 0, 0, axis_index_groups=by_spot)  13.4 us
    ppermute x2, waiting for transfers between devices, to_side(): lax.ppermute(block, 'head', [(i, (i + RING) % (SIDE * RING)) for i in ran...  13.4 us
    ppermute x2, starting transfers between devices, to_side(): lax.ppermute(block, 'head', [(i, (i + RING) % (SIDE * RING)) for i in ran...  12.3 us
    all_to_all x1, blocking collectives, local(): lax.all_to_all(slots, 'section', 0, 0, axis_index_groups=by_row)  12.1 us
    ppermute x2, starting transfers between devices, to_core(): lax.ppermute(block, 'section', [(i, i ^ 1) for i in range(lax.axis_size('...  3.84 us
  transfers between devices with their start and end apart: 18, of which 10 were waited for; matrix products, arithmetic and copies ran while one was open for 2% of the time, Pallas kernels for 4%

profile of v6, /device:TPU:8, one launch (start us, length us, event | category | flops | bytes accessed | tf_op | source)
XLA Modules:
  0.0 162.9 jit_solution(1020179549097038554)
XLA Ops:
  1.9 6.8 %collective-permute-start = (bf16[640,128]{1,0:T(8,128)(2,1)S(1)}, bf16[640,128]{1,0:T(8,128)(2,1)S(1)}, u32[]{:S(2)}, u32[]{:S(2)}) collective-permute-start(bf16[640,128]{1,0:T(8,128)(2,1)S(1)} %pad_maximum_fusion.1), channel_id=1, source_target_pairs={{0,8},{1,9},{2,10},{3,11},{4,12},{5,13},{6,14},{7,15},{8,0},{9,1},... | collective-permute-start | bytes 491528 | tf_op jit(solution)/shard_map/ppermute | solution.py:270
  8.7 7.6 %collective-permute-done = bf16[640,128]{1,0:T(8,128)(2,1)S(1)} collective-permute-done((bf16[640,128]{1,0:T(8,128)(2,1)S(1)}, bf16[640,128]{1,0:T(8,128)(2,1)S(1)}, u32[]{:S(2)}, u32[]{:S(2)}) %collective-permute-start) | collective-permute-done | bytes 163872 | tf_op jit(solution)/shard_map/ppermute | solution.py:270
  17.2 10.9 %collective-permute-start.1 = (bf16[1280,128]{1,0:T(8,128)(2,1)S(1)}, bf16[1280,128]{1,0:T(8,128)(2,1)S(1)}, u32[]{:S(2)}, u32[]{:S(2)}) collective-permute-start(bf16[1280,128]{1,0:T(8,128)(2,1)S(1)} %pad_maximum_fusion.refs_0_), channel_id=1, source_target_pairs={{0,7},{1,0},{2,1},{3,2},{4,3},{5,4},{6,5},{7,6},{8,15},{9,8},{10,9... | collective-permute-start | bytes 983048 | tf_op jit(solution)/shard_map/ppermute | solution.py:266
  30.1 3.9 %collective-permute-done.1.refs_1_ = bf16[1280,128]{1,0:T(8,128)(2,1)S(1)} collective-permute-done((bf16[1280,128]{1,0:T(8,128)(2,1)S(1)}, bf16[1280,128]{1,0:T(8,128)(2,1)S(1)}, u32[]{:S(2)}, u32[]{:S(2)}) %collective-permute-start.1) | collective-permute-done | bytes 327712 | tf_op jit(solution)/shard_map/ppermute | solution.py:266
  34.0 5.6 %collective-permute-start.2 = (bf16[1280,128]{1,0:T(8,128)(2,1)S(1)}, bf16[1280,128]{1,0:T(8,128)(2,1)S(1)}, u32[]{:S(2)}, u32[]{:S(2)}) collective-permute-start(bf16[1280,128]{1,0:T(8,128)(2,1)S(1)} %collective-permute-done.1.refs_1_), channel_id=1, source_target_pairs={{0,7},{1,0},{2,1},{3,2},{4,3},{5,4},{6,5},{7,6},{8,15},{9,8},{10,9... | collective-permute-start | bytes 983048 | tf_op jit(solution)/shard_map/ppermute | solution.py:266
  41.5 2.9 %collective-permute-done.2.refs_2_ = bf16[1280,128]{1,0:T(8,128)(2,1)S(1)} collective-permute-done((bf16[1280,128]{1,0:T(8,128)(2,1)S(1)}, bf16[1280,128]{1,0:T(8,128)(2,1)S(1)}, u32[]{:S(2)}, u32[]{:S(2)}) %collective-permute-start.2) | collective-permute-done | bytes 327712 | tf_op jit(solution)/shard_map/ppermute | solution.py:266
  44.5 5.6 %collective-permute-start.3 = (bf16[1280,128]{1,0:T(8,128)(2,1)S(1)}, bf16[1280,128]{1,0:T(8,128)(2,1)S(1)}, u32[]{:S(2)}, u32[]{:S(2)}) collective-permute-start(bf16[1280,128]{1,0:T(8,128)(2,1)S(1)} %collective-permute-done.2.refs_2_), channel_id=1, source_target_pairs={{0,7},{1,0},{2,1},{3,2},{4,3},{5,4},{6,5},{7,6},{8,15},{9,8},{10,9... | collective-permute-start | bytes 983048 | tf_op jit(solution)/shard_map/ppermute | solution.py:266
  52.0 2.6 %collective-permute-done.3.refs_3_ = bf16[1280,128]{1,0:T(8,128)(2,1)S(1)} collective-permute-done((bf16[1280,128]{1,0:T(8,128)(2,1)S(1)}, bf16[1280,128]{1,0:T(8,128)(2,1)S(1)}, u32[]{:S(2)}, u32[]{:S(2)}) %collective-permute-start.3) | collective-permute-done | bytes 327712 | tf_op jit(solution)/shard_map/ppermute | solution.py:266
  54.6 5.6 %collective-permute-start.4 = (bf16[1280,128]{1,0:T(8,128)(2,1)S(1)}, bf16[1280,128]{1,0:T(8,128)(2,1)}, u32[]{:S(2)}, u32[]{:S(2)}) collective-permute-start(bf16[1280,128]{1,0:T(8,128)(2,1)S(1)} %collective-permute-done.3.refs_3_), channel_id=1, source_target_pairs={{0,7},{1,0},{2,1},{3,2},{4,3},{5,4},{6,5},{7,6},{8,15},{9,8},{10,9... | collective-permute-start | bytes 983048 | tf_op jit(solution)/shard_map/ppermute | solution.py:266
  64.8 2.4 %shard_map.109 = (bf16[512,2048]{1,0:T(8,128)(2,1)S(1)}, bf16[2048,128]{1,0:T(8,128)(2,1)S(1)}) custom-call(s32[5]{0:T(128)S(1)} %stack.23.place, bf16[1280,128]{1,0:T(8,128)(2,1)S(1)} %pad_maximum_fusion.refs_0_, bf16[1280,128]{1,0:T(8,128)(2,1)S(1)} %collective-permute-done.1.refs_1_, bf16[1280,128]{1,0:T(8,128)(2,1)S(1)} %collective-permute-done.2.refs_2_, ...), custom_call_target="tpu_custom_call" | custom-call | bytes 5255188 | tf_op jit(solution)/shard_map/pallas_call | solution.py:249
  69.3 2.8 %shard_map.110 = (f32[512,256]{1,0:T(8,128)S(1)}, f32[512,256]{1,0:T(8,128)S(1)}, f32[16,512]{1,0:T(8,128)S(1)}, f32[16,512]{1,0:T(8,128)S(1)}) custom-call(bf16[512,2048]{1,0:T(8,128)(2,1)S(1)} %get-tuple-element.78.normed, bf16[2048,256]{1,0:T(8,128)(2,1)S(1)} %copy-done.2, bf16[128,2048]{1,0:T(8,128)(2,1)S(1)} %pad.17.dt_weight, ...), custom_call_target="tpu_custom_call" | custom-call | flops 805306368 | bytes 4796416 | tf_op jit(solution)/shard_map/pallas_call | solution.py:249
  72.1 2.2 %shard_map.111 = (f32[512,256]{1,0:T(8,128)S(1)}, bf16[8,144,128]{2,1,0:T(8,128)(2,1)S(1)}) custom-call(s32[5]{0:T(128)S(1)} %stack.23.place, bf16[512,2048]{1,0:T(8,128)(2,1)S(1)} %get-tuple-element.78.normed, f32[512,256]{1,0:T(8,128)S(1)} %get-tuple-element.80.tailed, bf16[2048,128]{1,0:T(8,128)(2,1)S(1)} %get-tuple-element.81.bc_mine, ...), custom_call_target="tpu_custom_call" | custom-call | flops 536870912 | bytes 4522004 | tf_op jit(solution)/shard_map/pallas_call | solution.py:249
  74.3 12.1 %all_to_all.10.gathered = bf16[8,144,128]{2,1,0:T(8,128)(2,1)S(1)} all-to-all(bf16[8,144,128]{2,1,0:T(8,128)(2,1)S(1)} %get-tuple-element.87), channel_id=1, replica_groups={{0,16,32,48,64,80,96,112},{128,144,160,176,192,208,224,240},{256,272,28..., dimensions={0} | all-to-all | bytes 589824 | tf_op jit(solution)/shard_map/all_to_all | solution.py:367
  87.1 13.4 %all_to_all.11.gathered = bf16[4,144,128]{2,1,0:T(8,128)(2,1)S(1)} all-to-all(bf16[4,144,128]{2,1,0:T(8,128)(2,1)S(1)} %get-tuple-element.88), channel_id=1, replica_groups={{0,128,256,384},{16,144,272,400},{32,160,288,416},{48,176,304,432},{64,..., dimensions={0} | all-to-all | bytes 294912 | tf_op jit(solution)/shard_map/all_to_all | solution.py:373
  103.1 2.0 %shard_map.112 = (f32[512,256]{1,0:T(8,128)S(1)}, f32[512,256]{1,0:T(8,128)S(1)}) custom-call(bf16[512,2048]{1,0:T(8,128)(2,1)S(1)} %get-tuple-element.78.normed, bf16[2048,256]{1,0:T(8,128)(2,1)S(1)} %copy-done.4, f32[512,256]{1,0:T(8,128)S(1)} %get-tuple-element.79.x_in, f32[512,256]{1,0:T(8,128)S(1)} %get-tuple-element.83.both_in.both, ...), custom_call_target="tpu_custom_call" | custom-call | flops 1543503872 | bytes 5320704 | tf_op jit(solution)/shard_map/pallas_call | solution.py:249
  108.7 5.7 %collective-permute-start.14 = (bf16[1024,128]{1,0:T(8,128)(2,1)S(1)}, bf16[1024,128]{1,0:T(8,128)(2,1)S(1)}, u32[]{:S(2)}, u32[]{:S(2)}) collective-permute-start(bf16[1024,128]{1,0:T(8,128)(2,1)S(1)} %get-tuple-element.100), channel_id=1, source_target_pairs={{0,7},{1,0},{2,1},{3,2},{4,3},{5,4},{6,5},{7,6},{8,15},{9,8},{10,9... | collective-permute-start | bytes 786440 | tf_op jit(solution)/shard_map/ppermute | solution.py:266
  116.0 3.5 %collective-permute-done.10 = bf16[1024,128]{1,0:T(8,128)(2,1)S(1)} collective-permute-done((bf16[1024,128]{1,0:T(8,128)(2,1)S(1)}, bf16[1024,128]{1,0:T(8,128)(2,1)S(1)}, u32[]{:S(2)}, u32[]{:S(2)}) %collective-permute-start.10) | collective-permute-done | bytes 262176 | tf_op jit(solution)/shard_map/ppermute | solution.py:266
  121.5 5.3 %collective-permute-start.15 = (bf16[1024,128]{1,0:T(8,128)(2,1)S(1)}, bf16[1024,128]{1,0:T(8,128)(2,1)S(1)}, u32[]{:S(2)}, u32[]{:S(2)}) collective-permute-start(bf16[1024,128]{1,0:T(8,128)(2,1)S(1)} %add_convert_fusion.1), channel_id=1, source_target_pairs={{0,7},{1,0},{2,1},{3,2},{4,3},{5,4},{6,5},{7,6},{8,15},{9,8},{10,9... | collective-permute-start | bytes 786440 | tf_op jit(solution)/shard_map/ppermute | solution.py:266
  126.8 3.9 %collective-permute-done.11 = bf16[1024,128]{1,0:T(8,128)(2,1)S(1)} collective-permute-done((bf16[1024,128]{1,0:T(8,128)(2,1)S(1)}, bf16[1024,128]{1,0:T(8,128)(2,1)S(1)}, u32[]{:S(2)}, u32[]{:S(2)}) %collective-permute-start.11) | collective-permute-done | bytes 262176 | tf_op jit(solution)/shard_map/ppermute | solution.py:266
  132.9 5.1 %collective-permute-start.16 = (bf16[1024,128]{1,0:T(8,128)(2,1)S(1)}, bf16[1024,128]{1,0:T(8,128)(2,1)S(1)}, u32[]{:S(2)}, u32[]{:S(2)}) collective-permute-start(bf16[1024,128]{1,0:T(8,128)(2,1)S(1)} %add_convert_fusion), channel_id=1, source_target_pairs={{0,7},{1,0},{2,1},{3,2},{4,3},{5,4},{6,5},{7,6},{8,15},{9,8},{10,9... | collective-permute-start | bytes 786440 | tf_op jit(solution)/shard_map/ppermute | solution.py:266
  138.0 3.2 %collective-permute-done.12 = bf16[1024,128]{1,0:T(8,128)(2,1)S(1)} collective-permute-done((bf16[1024,128]{1,0:T(8,128)(2,1)S(1)}, bf16[1024,128]{1,0:T(8,128)(2,1)S(1)}, u32[]{:S(2)}, u32[]{:S(2)}) %collective-permute-start.12) | collective-permute-done | bytes 262176 | tf_op jit(solution)/shard_map/ppermute | solution.py:266
  143.2 7.5 %collective-permute-done.13 = bf16[1024,128]{1,0:T(8,128)(2,1)S(1)} collective-permute-done((bf16[1024,128]{1,0:T(8,128)(2,1)S(1)}, bf16[1024,128]{1,0:T(8,128)(2,1)S(1)}, u32[]{:S(2)}, u32[]{:S(2)}) %collective-permute-start.13) | collective-permute-done | bytes 262176 | tf_op jit(solution)/shard_map/ppermute | solution.py:266
  150.9 5.5 %collective-permute-start.17 = (bf16[512,128]{1,0:T(8,128)(2,1)S(1)}, bf16[512,128]{1,0:T(8,128)(2,1)S(1)}, u32[]{:S(2)}, u32[]{:S(2)}) collective-permute-start(bf16[512,128]{1,0:T(8,128)(2,1)S(1)} %slice.86), channel_id=1, source_target_pairs={{0,8},{1,9},{2,10},{3,11},{4,12},{5,13},{6,14},{7,15},{8,0},{9,1},... | collective-permute-start | bytes 393224 | tf_op jit(solution)/shard_map/ppermute | solution.py:270
  156.4 5.8 %collective-permute-done.17 = bf16[512,128]{1,0:T(8,128)(2,1)S(1)} collective-permute-done((bf16[512,128]{1,0:T(8,128)(2,1)S(1)}, bf16[512,128]{1,0:T(8,128)(2,1)S(1)}, u32[]{:S(2)}, u32[]{:S(2)}) %collective-permute-start.17) | collective-permute-done | bytes 131104 | tf_op jit(solution)/shard_map/ppermute | solution.py:270
  (53 shorter events, 30.4 us)
Async XLA Ops:
  0.0 69.2 %copy-start.6 = (bf16[2048,4]{0,1:T(4,128)(2,1)S(1)}, bf16[2048,4]{0,1:T(4,128)(2,1)}, u32[]{:S(2)}) copy-start(bf16[2048,4]{0,1:T(4,128)(2,1)} %param.23) | copy-start | bytes 49156
  0.8 68.4 %copy-start.2 = (bf16[2048,256]{1,0:T(8,128)(2,1)S(1)}, bf16[2048,256]{1,0:T(8,128)(2,1)}, u32[]{:S(2)}) copy-start(bf16[2048,256]{1,0:T(8,128)(2,1)} %x_weight.1) | copy-start | bytes 3145732
  1.9 14.5 %collective-permute-start = (bf16[640,128]{1,0:T(8,128)(2,1)S(1)}, bf16[640,128]{1,0:T(8,128)(2,1)S(1)}, u32[]{:S(2)}, u32[]{:S(2)}) collective-permute-start(bf16[640,128]{1,0:T(8,128)(2,1)S(1)} %pad_maximum_fusion.1), channel_id=1, source_target_pairs={{0,8},{1,9},{2,10},{3,11},{4,12},{5,13},{6,14},{7,15},{8,0},{9,1},... | collective-permute-start | bytes 491528 | tf_op jit(solution)/shard_map/ppermute | solution.py:270
  17.2 16.8 %collective-permute-start.1 = (bf16[1280,128]{1,0:T(8,128)(2,1)S(1)}, bf16[1280,128]{1,0:T(8,128)(2,1)S(1)}, u32[]{:S(2)}, u32[]{:S(2)}) collective-permute-start(bf16[1280,128]{1,0:T(8,128)(2,1)S(1)} %pad_maximum_fusion.refs_0_), channel_id=1, source_target_pairs={{0,7},{1,0},{2,1},{3,2},{4,3},{5,4},{6,5},{7,6},{8,15},{9,8},{10,9... | collective-permute-start | bytes 983048 | tf_op jit(solution)/shard_map/ppermute | solution.py:266
  28.2 11.4 %collective-permute-start.5 = (bf16[1280,128]{1,0:T(8,128)(2,1)S(1)}, bf16[1280,128]{1,0:T(8,128)(2,1)S(1)}, u32[]{:S(2)}, u32[]{:S(2)}) collective-permute-start(bf16[1280,128]{1,0:T(8,128)(2,1)S(1)} %pad_maximum_fusion.refs_0_), channel_id=1, source_target_pairs={{0,1},{1,2},{2,3},{3,4},{4,5},{5,6},{6,7},{7,0},{8,9},{9,10},{10,1... | collective-permute-start | bytes 983048 | tf_op jit(solution)/shard_map/ppermute | solution.py:266
  34.0 10.5 %collective-permute-start.2 = (bf16[1280,128]{1,0:T(8,128)(2,1)S(1)}, bf16[1280,128]{1,0:T(8,128)(2,1)S(1)}, u32[]{:S(2)}, u32[]{:S(2)}) collective-permute-start(bf16[1280,128]{1,0:T(8,128)(2,1)S(1)} %collective-permute-done.1.refs_1_), channel_id=1, source_target_pairs={{0,7},{1,0},{2,1},{3,2},{4,3},{5,4},{6,5},{7,6},{8,15},{9,8},{10,9... | collective-permute-start | bytes 983048 | tf_op jit(solution)/shard_map/ppermute | solution.py:266
  39.6 10.5 %collective-permute-start.6 = (bf16[1280,128]{1,0:T(8,128)(2,1)S(1)}, bf16[1280,128]{1,0:T(8,128)(2,1)S(1)}, u32[]{:S(2)}, u32[]{:S(2)}) collective-permute-start(bf16[1280,128]{1,0:T(8,128)(2,1)S(1)} %collective-permute-done.5.refs_7_), channel_id=1, source_target_pairs={{0,1},{1,2},{2,3},{3,4},{4,5},{5,6},{6,7},{7,0},{8,9},{9,10},{10,1... | collective-permute-start | bytes 983048 | tf_op jit(solution)/shard_map/ppermute | solution.py:266
  44.5 10.2 %collective-permute-start.3 = (bf16[1280,128]{1,0:T(8,128)(2,1)S(1)}, bf16[1280,128]{1,0:T(8,128)(2,1)S(1)}, u32[]{:S(2)}, u32[]{:S(2)}) collective-permute-start(bf16[1280,128]{1,0:T(8,128)(2,1)S(1)} %collective-permute-done.2.refs_2_), channel_id=1, source_target_pairs={{0,7},{1,0},{2,1},{3,2},{4,3},{5,4},{6,5},{7,6},{8,15},{9,8},{10,9... | collective-permute-start | bytes 983048 | tf_op jit(solution)/shard_map/ppermute | solution.py:266
  50.1 13.2 %collective-permute-start.7 = (bf16[1280,128]{1,0:T(8,128)(2,1)S(1)}, bf16[1280,128]{1,0:T(8,128)(2,1)S(1)}, u32[]{:S(2)}, u32[]{:S(2)}) collective-permute-start(bf16[1280,128]{1,0:T(8,128)(2,1)S(1)} %collective-permute-done.6.refs_6_), channel_id=1, source_target_pairs={{0,1},{1,2},{2,3},{3,4},{4,5},{5,6},{6,7},{7,0},{8,9},{9,10},{10,1... | collective-permute-start | bytes 983048 | tf_op jit(solution)/shard_map/ppermute | solution.py:266
  54.6 10.2 %collective-permute-start.4 = (bf16[1280,128]{1,0:T(8,128)(2,1)S(1)}, bf16[1280,128]{1,0:T(8,128)(2,1)}, u32[]{:S(2)}, u32[]{:S(2)}) collective-permute-start(bf16[1280,128]{1,0:T(8,128)(2,1)S(1)} %collective-permute-done.3.refs_3_), channel_id=1, source_target_pairs={{0,7},{1,0},{2,1},{3,2},{4,3},{5,4},{6,5},{7,6},{8,15},{9,8},{10,9... | collective-permute-start | bytes 983048 | tf_op jit(solution)/shard_map/ppermute | solution.py:266
  67.3 4.8 %collective-permute-start.8 = (bf16[2048,128]{1,0:T(8,128)(2,1)S(1)}, bf16[2048,128]{1,0:T(8,128)(2,1)S(1)}, u32[]{:S(2)}, u32[]{:S(2)}) collective-permute-start(bf16[2048,128]{1,0:T(8,128)(2,1)S(1)} %get-tuple-element.81.bc_mine), channel_id=1, source_target_pairs={{0,16},{16,0},{32,48},{48,32},{64,80},{80,64},{96,112},{112,96},{1... | collective-permute-start | bytes 1572872 | tf_op jit(solution)/shard_map/ppermute | solution.py:274
  72.1 31.0 %copy-start.4 = (bf16[2048,256]{1,0:T(8,128)(2,1)S(1)}, bf16[2048,256]{1,0:T(8,128)(2,1)}, u32[]{:S(2)}) copy-start(bf16[2048,256]{1,0:T(8,128)(2,1)} %gate_weight.1) | copy-start | bytes 3145732
  101.1 3.9 %collective-permute-start.9 = (bf16[128,128]{1,0:T(8,128)(2,1)S(1)}, bf16[128,128]{1,0:T(8,128)(2,1)S(1)}, u32[]{:S(2)}, u32[]{:S(2)}) collective-permute-start(bf16[128,128]{1,0:T(8,128)(2,1)S(1)} %get-tuple-element.93), channel_id=1, source_target_pairs={{0,16},{16,0},{32,48},{48,32},{64,80},{80,64},{96,112},{112,96},{1... | collective-permute-start | bytes 98312 | tf_op jit(solution)/shard_map/ppermute | solution.py:274
  103.0 2.0 %copy-start.1 = (bf16[256,2048]{1,0:T(8,128)(2,1)S(1)}, bf16[256,2048]{1,0:T(8,128)(2,1)}, u32[]{:S(2)}) copy-start(bf16[256,2048]{1,0:T(8,128)(2,1)} %out_weight.3) | copy-start | bytes 3145732
  103.0 2.0 %copy-start.3 = (f32[256]{0:T(256)S(1)}, f32[256]{0:T(256)}, u32[]{:S(2)}) copy-start(f32[256]{0:T(256)} %param.28) | copy-start | bytes 3076
  106.8 12.7 %collective-permute-start.10 = (bf16[1024,128]{1,0:T(8,128)(2,1)S(1)}, bf16[1024,128]{1,0:T(8,128)(2,1)S(1)}, u32[]{:S(2)}, u32[]{:S(2)}) collective-permute-start(bf16[1024,128]{1,0:T(8,128)(2,1)S(1)} %get-tuple-element.96), channel_id=1, source_target_pairs={{0,1},{1,2},{2,3},{3,4},{4,5},{5,6},{6,7},{7,0},{8,9},{9,10},{10,1... | collective-permute-start | bytes 786440 | tf_op jit(solution)/shard_map/ppermute | solution.py:266
  108.7 12.8 %collective-permute-start.14 = (bf16[1024,128]{1,0:T(8,128)(2,1)S(1)}, bf16[1024,128]{1,0:T(8,128)(2,1)S(1)}, u32[]{:S(2)}, u32[]{:S(2)}) collective-permute-start(bf16[1024,128]{1,0:T(8,128)(2,1)S(1)} %get-tuple-element.100), channel_id=1, source_target_pairs={{0,7},{1,0},{2,1},{3,2},{4,3},{5,4},{6,5},{7,6},{8,15},{9,8},{10,9... | collective-permute-start | bytes 786440 | tf_op jit(solution)/shard_map/ppermute | solution.py:266
  119.5 11.2 %collective-permute-start.11 = (bf16[1024,128]{1,0:T(8,128)(2,1)S(1)}, bf16[1024,128]{1,0:T(8,128)(2,1)S(1)}, u32[]{:S(2)}, u32[]{:S(2)}) collective-permute-start(bf16[1024,128]{1,0:T(8,128)(2,1)S(1)} %add_convert_fusion.4), channel_id=1, source_target_pairs={{0,1},{1,2},{2,3},{3,4},{4,5},{5,6},{6,7},{7,0},{8,9},{9,10},{10,1... | collective-permute-start | bytes 786440 | tf_op jit(solution)/shard_map/ppermute | solution.py:266
  121.5 40.6 %copy-start.5 = (bf16[512,128]{1,0:T(8,128)(2,1)S(1)}, bf16[512,128]{1,0:T(8,128)(2,1)}, u32[]{:S(2)}) copy-start(bf16[512,128]{1,0:T(8,128)(2,1)} %param.19) | copy-start | bytes 393220
  121.5 11.2 %collective-permute-start.15 = (bf16[1024,128]{1,0:T(8,128)(2,1)S(1)}, bf16[1024,128]{1,0:T(8,128)(2,1)S(1)}, u32[]{:S(2)}, u32[]{:S(2)}) collective-permute-start(bf16[1024,128]{1,0:T(8,128)(2,1)S(1)} %add_convert_fusion.1), channel_id=1, source_target_pairs={{0,7},{1,0},{2,1},{3,2},{4,3},{5,4},{6,5},{7,6},{8,15},{9,8},{10,9... | collective-permute-start | bytes 786440 | tf_op jit(solution)/shard_map/ppermute | solution.py:266
  130.8 10.4 %collective-permute-start.12 = (bf16[1024,128]{1,0:T(8,128)(2,1)S(1)}, bf16[1024,128]{1,0:T(8,128)(2,1)S(1)}, u32[]{:S(2)}, u32[]{:S(2)}) collective-permute-start(bf16[1024,128]{1,0:T(8,128)(2,1)S(1)} %add_convert_fusion.3), channel_id=1, source_target_pairs={{0,1},{1,2},{2,3},{3,4},{4,5},{5,6},{6,7},{7,0},{8,9},{9,10},{10,1... | collective-permute-start | bytes 786440 | tf_op jit(solution)/shard_map/ppermute | solution.py:266
  132.9 10.4 %collective-permute-start.16 = (bf16[1024,128]{1,0:T(8,128)(2,1)S(1)}, bf16[1024,128]{1,0:T(8,128)(2,1)S(1)}, u32[]{:S(2)}, u32[]{:S(2)}) collective-permute-start(bf16[1024,128]{1,0:T(8,128)(2,1)S(1)} %add_convert_fusion), channel_id=1, source_target_pairs={{0,7},{1,0},{2,1},{3,2},{4,3},{5,4},{6,5},{7,6},{8,15},{9,8},{10,9... | collective-permute-start | bytes 786440 | tf_op jit(solution)/shard_map/ppermute | solution.py:266
  141.3 9.5 %collective-permute-start.13 = (bf16[1024,128]{1,0:T(8,128)(2,1)S(1)}, bf16[1024,128]{1,0:T(8,128)(2,1)S(1)}, u32[]{:S(2)}, u32[]{:S(2)}) collective-permute-start(bf16[1024,128]{1,0:T(8,128)(2,1)S(1)} %add_convert_fusion.2), channel_id=1, source_target_pairs={{0,1},{1,2},{2,3},{3,4},{4,5},{5,6},{6,7},{7,0},{8,9},{9,10},{10,1... | collective-permute-start | bytes 786440 | tf_op jit(solution)/shard_map/ppermute | solution.py:266
  150.9 11.3 %collective-permute-start.17 = (bf16[512,128]{1,0:T(8,128)(2,1)S(1)}, bf16[512,128]{1,0:T(8,128)(2,1)S(1)}, u32[]{:S(2)}, u32[]{:S(2)}) collective-permute-start(bf16[512,128]{1,0:T(8,128)(2,1)S(1)} %slice.86), channel_id=1, source_target_pairs={{0,8},{1,9},{2,10},{3,11},{4,12},{5,13},{6,14},{7,15},{8,0},{9,1},... | collective-permute-start | bytes 393224 | tf_op jit(solution)/shard_map/ppermute | solution.py:270
  (1 other events, 0.8 us)

commit v7 on v6

--- a/solution.py
+++ b/solution.py
@@ -85,9 +85,29 @@
     return tail[0:1] + tail[1:2]
 
 
+def square_sum(rows, *blocks):
+    value = jnp.zeros((rows, blocks[0].shape[1]), f32)
+    for block in blocks:
+        for j in range(SIDE):
+            at = j * block.shape[0] // SIDE
+            part = block[at : at + rows, :].astype(f32)
+            value = value + part * part
+    return value
+
+
+def square_kernel(rows, *refs):
+    refs[-1][...] = square_sum(rows, *refs[:-1])
+
+
+def join_kernel(one, two, out):
+    rows = one.shape[0]
+    out[0:rows, :] = one[...]
+    out[rows : 2 * rows, :] = two[...]
+
+
 def norm_kernel(rows, place, *refs):
     blocks = refs[:RING]
-    small, normed, bc_half = refs[RING:]
+    early, small, normed, bc_half = refs[RING:]
     own = blocks[0].shape[1]
     side, turn = place[0], place[1]
     piece = blocks[0].shape[0] // SIDE
@@ -98,10 +118,7 @@
                 head = lax.rem(side + j, SIDE) * RING + lax.rem(turn + k, RING)
                 yield blocks[k], j * piece, head
 
-    squares = jnp.zeros((rows, own), f32)
-    for block, at, _ in parts():
-        value = block[at : at + rows, :].astype(f32)
-        squares = squares + value * value
+    squares = early[...] + square_sum(rows, blocks[RING // 2])
     mean = jnp.sum(squares, axis=1, keepdims=True) / (RING * SIDE * own)
     scale = lax.rsqrt(mean + eps)
     for block, at, head in parts():
@@ -144,7 +161,7 @@
         slots[i, state_n : state_n + 16, :] = logs[:, at : at + half]
 
 
-def row_kernel(place, gathered, copies, own_out, pair_out, logs_out):
+def row_kernel(place, gathered, row_out, own_out, pair_out, logs_out):
     state_n, half = gathered.shape[1] - 16, gathered.shape[2]
     core, spot = place[2], place[3]
     pair = spot + 1 - 2 * core
@@ -161,26 +178,24 @@
     pair_out[...] = other
     logs_out[0:1, :] = own_log
     logs_out[1:2, :] = other_log
-    value, logs = state.astype(bf16), log_rows(log)
-    for i in range(copies.shape[0]):
-        copies[i, 0:state_n, :] = value
-        copies[i, state_n : state_n + 16, :] = logs
-
-
-def prefix_kernel(place, gathered, own, pair, logs, keep, send):
+    row_out[0:state_n, :] = state.astype(bf16)
+    row_out[state_n : state_n + 16, :] = log_rows(log)
+
+
+def prefix_kernel(own, pair, logs, after, *refs):
+    totals, (keep, send) = refs[:-2], refs[-2:]
     state_n = own.shape[0]
-    row = place[4]
     state = jnp.zeros(own.shape, f32)
-    for i in range(gathered.shape[0] - 1):
-        passed = jnp.exp(log_row(gathered[i])) * state + gathered[i, 0:state_n, :].astype(f32)
-        state = jnp.where(i < row, passed, state)
+    for row in reversed(totals):
+        state = jnp.exp(log_row(row[...])) * state + row[0:state_n, :].astype(f32)
     keep[...] = (jnp.exp(logs[0:1, :]) * state + own[...]).astype(bf16)
     send[...] = (jnp.exp(logs[1:2, :]) * state + pair[...]).astype(bf16)
 
 
-def scan_kernel(heads, size_p, block, normed, gate_weight, x_in, both_in, cums_in, step_in, small, result, opened):
+def scan_kernel(heads, size_p, block, normed, gate_weight, x_in, both_in, cums_in, step_in, small, after, result, opened, done):
     rows, width = x_in.shape
     state_n = both_in.shape[1] // 2
+    done[...] = jnp.zeros_like(done)
     opened[...] = silu(dot(normed[...], gate_weight[...]))
     lower = iota((block, block), 0) >= iota((block, block), 1)
     skip = spread_row(stood(small[2:3, 0:HEADS]), width, size_p)
@@ -274,6 +289,11 @@
     return lax.ppermute(block, "section", [(i, i ^ 1) for i in range(lax.axis_size("section"))])
 
 
+def to_row(block, count):
+    sections, ahead = lax.axis_size("section"), count * ROW
+    return lax.ppermute(block, "section", [(i, i + ahead) for i in range(sections - ahead)])
+
+
 def gather_ring(block):
     found = {0: block}
     for k in range(1, RING // 2):
@@ -326,7 +346,13 @@
     piece = lax.dynamic_slice_in_dim(bc_weight, section % 2 * state_n, state_n, 1)
     packed = jnp.concatenate([tokens, piece], 0)
     far = RING // 2
-    blocks = gather_ring(jnp.concatenate([packed, to_side(packed)], 0))
+    joined = on_chip(join_kernel, [shape((SIDE * (rows + own), own), bf16)], [packed, to_side(packed)])[0]
+    blocks = gather_ring(joined)
+    early = on_chip(
+        functools.partial(square_kernel, rows),
+        [shape((rows, own))],
+        [blocks[k] for k in range(RING) if k != far],
+    )[0]
     dt_wide = jnp.pad(dt_weight.T, ((0, 128 - heads), (0, 0)))
     small = jnp.zeros((8 + groups, own), f32)
     small = small.at[0, :heads].set(dt_bias).at[1, :heads].set(decay_rate).at[2, :heads].set(skip_gain)
@@ -334,7 +360,7 @@
     normed, bc_mine = on_chip(
         functools.partial(norm_kernel, rows),
         [shape((rows, model), bf16), shape((model, state_n), bf16)],
-        [*blocks, small],
+        [*blocks, early, small],
         place,
     )
     bc_other = to_core(bc_mine)
@@ -351,27 +377,26 @@
         place,
         flops=2 * rows * model * 2 * state_n,
     )
-    result, opened = on_chip(
+    lines = sections // ROW
+    by_row = [list(range(r * ROW, (r + 1) * ROW)) for r in range(lines)]
+    row_total, enter_own, enter_pair, logs = on_chip(
+        row_kernel,
+        [shape((state_n + 16, half), bf16), shape((state_n, half)), shape((state_n, half)), shape((8, half))],
+        [lax.all_to_all(slots, "section", 0, 0, axis_index_groups=by_row)],
+        place,
+    )
+    above = [to_row(row_total, k) for k in range(1, lines)]
+    result, opened, done = on_chip(
         functools.partial(scan_kernel, heads, size_p, 256),
-        [shape((rows, width)), shape((rows, width))],
-        [normed, gate_weight, x, both, cums, step, small],
+        [shape((rows, width)), shape((rows, width)), shape((8, 128))],
+        [normed, gate_weight, x, both, cums, step, small, logs],
         flops=2 * rows * model * width + 12 * rows * 256 * (width + 3 * state_n),
         transcendentals=heads * rows * 256,
-    )
-    lines = sections // ROW
-    by_row = [list(range(r * ROW, (r + 1) * ROW)) for r in range(lines)]
-    by_spot = [list(range(p, sections, ROW)) for p in range(ROW)]
-    copies, enter_own, enter_pair, logs = on_chip(
-        row_kernel,
-        [shape((lines, state_n + 16, half), bf16), shape((state_n, half)), shape((state_n, half)), shape((8, half))],
-        [lax.all_to_all(slots, "section", 0, 0, axis_index_groups=by_row)],
-        place,
     )
     keep, send = on_chip(
         prefix_kernel,
         [shape((state_n, half), bf16), shape((state_n, half), bf16)],
-        [lax.all_to_all(copies, "section", 0, 0, axis_index_groups=by_spot), enter_own, enter_pair, logs],
-        place,
+        [enter_own, enter_pair, logs, done, *above],
     )
     rest = to_core(send)
     soon, later = (far, far + 1), tuple(k for k in range(RING) if k // 2 != RING // 4)

time: 164 us -> 160 us (0.976)
  the two profiles are of different devices: /device:TPU:8 before, /device:TPU:40 now
where the time goes in v7:
time: 160 us; the launch traced here: 159 us
  starting transfers between devices  74.6 us (47%)
  waiting for transfers between devices  52.4 us (33%)
  Pallas kernels  13.1 us (8%)
  blocking collectives  12.1 us (8%)
  local copies, waits for them, and re-layouts  3.92 us (2%)
  other arithmetic  2.1 us (1%)
    ppermute x14, starting transfers between devices, to_turn(): return lax.ppermute(block, 'head', route)  57.1 us
    ppermute x14, waiting for transfers between devices, to_turn(): return lax.ppermute(block, 'head', route)  28.8 us
    ppermute x2, waiting for transfers between devices, to_side(): lax.ppermute(block, 'head', [(i, (i + RING) % (SIDE * RING)) for i in ran...  20.6 us
    pallas_call x10, Pallas kernels, on_chip(): pl.pallas_call(kernel, out_shape=outs, in_specs=specs, out_specs=[pl.Bloc...  13.1 us
    all_to_all x1, blocking collectives, local(): lax.all_to_all(slots, 'section', 0, 0, axis_index_groups=by_row)  12.1 us
    ppermute x3, starting transfers between devices, to_row(): lax.ppermute(block, 'section', [(i, i + ahead) for i in range(sections -...  8.3 us
    ppermute x2, starting transfers between devices, to_side(): lax.ppermute(block, 'head', [(i, (i + RING) % (SIDE * RING)) for i in ran...  5.37 us
    ppermute x2, starting transfers between devices, to_core(): lax.ppermute(block, 'section', [(i, i ^ 1) for i in range(lax.axis_size('...  3.84 us
  transfers between devices with their start and end apart: 21, of which 12 were waited for; matrix products, arithmetic and copies ran while one was open for 2% of the time, Pallas kernels for 4%

profile of v7, /device:TPU:40, one launch (start us, length us, event | category | flops | bytes accessed | tf_op | source)
XLA Modules:
  0.0 158.7 jit_solution(5971786361337948870)
XLA Ops:
  1.8 2.9 %collective-permute-start = (bf16[640,128]{1,0:T(8,128)(2,1)S(1)}, bf16[640,128]{1,0:T(8,128)(2,1)S(1)}, u32[]{:S(2)}, u32[]{:S(2)}) collective-permute-start(bf16[640,128]{1,0:T(8,128)(2,1)S(1)} %pad_maximum_fusion.one), channel_id=1, source_target_pairs={{0,8},{1,9},{2,10},{3,11},{4,12},{5,13},{6,14},{7,15},{8,0},{9,1},... | collective-permute-start | bytes 491528 | tf_op jit(solution)/shard_map/ppermute | solution.py:285
  4.7 11.7 %collective-permute-done.two = bf16[640,128]{1,0:T(8,128)(2,1)S(1)} collective-permute-done((bf16[640,128]{1,0:T(8,128)(2,1)S(1)}, bf16[640,128]{1,0:T(8,128)(2,1)S(1)}, u32[]{:S(2)}, u32[]{:S(2)}) %collective-permute-start) | collective-permute-done | bytes 163872 | tf_op jit(solution)/shard_map/ppermute | solution.py:285
  16.4 10.9 %collective-permute-start.1 = (bf16[1280,128]{1,0:T(8,128)(2,1)S(1)}, bf16[1280,128]{1,0:T(8,128)(2,1)S(1)}, u32[]{:S(2)}, u32[]{:S(2)}) collective-permute-start(bf16[1280,128]{1,0:T(8,128)(2,1)S(1)} %shard_map.109.refs_0_), channel_id=1, source_target_pairs={{0,7},{1,0},{2,1},{3,2},{4,3},{5,4},{6,5},{7,6},{8,15},{9,8},{10,9... | collective-permute-start | bytes 983048 | tf_op jit(solution)/shard_map/ppermute | solution.py:281
  29.3 4.3 %collective-permute-done.1.refs_1_ = bf16[1280,128]{1,0:T(8,128)(2,1)S(1)} collective-permute-done((bf16[1280,128]{1,0:T(8,128)(2,1)S(1)}, bf16[1280,128]{1,0:T(8,128)(2,1)S(1)}, u32[]{:S(2)}, u32[]{:S(2)}) %collective-permute-start.1) | collective-permute-done | bytes 327712 | tf_op jit(solution)/shard_map/ppermute | solution.py:281
  33.6 5.6 %collective-permute-start.2 = (bf16[1280,128]{1,0:T(8,128)(2,1)S(1)}, bf16[1280,128]{1,0:T(8,128)(2,1)S(1)}, u32[]{:S(2)}, u32[]{:S(2)}) collective-permute-start(bf16[1280,128]{1,0:T(8,128)(2,1)S(1)} %collective-permute-done.1.refs_1_), channel_id=1, source_target_pairs={{0,7},{1,0},{2,1},{3,2},{4,3},{5,4},{6,5},{7,6},{8,15},{9,8},{10,9... | collective-permute-start | bytes 983048 | tf_op jit(solution)/shard_map/ppermute | solution.py:281
  41.2 3.4 %collective-permute-done.2.refs_2_ = bf16[1280,128]{1,0:T(8,128)(2,1)S(1)} collective-permute-done((bf16[1280,128]{1,0:T(8,128)(2,1)S(1)}, bf16[1280,128]{1,0:T(8,128)(2,1)S(1)}, u32[]{:S(2)}, u32[]{:S(2)}) %collective-permute-start.2) | collective-permute-done | bytes 327712 | tf_op jit(solution)/shard_map/ppermute | solution.py:281
  44.6 5.6 %collective-permute-start.3 = (bf16[1280,128]{1,0:T(8,128)(2,1)S(1)}, bf16[1280,128]{1,0:T(8,128)(2,1)S(1)}, u32[]{:S(2)}, u32[]{:S(2)}) collective-permute-start(bf16[1280,128]{1,0:T(8,128)(2,1)S(1)} %collective-permute-done.2.refs_2_), channel_id=1, source_target_pairs={{0,7},{1,0},{2,1},{3,2},{4,3},{5,4},{6,5},{7,6},{8,15},{9,8},{10,9... | collective-permute-start | bytes 983048 | tf_op jit(solution)/shard_map/ppermute | solution.py:281
  52.1 2.6 %collective-permute-done.3.refs_3_ = bf16[1280,128]{1,0:T(8,128)(2,1)S(1)} collective-permute-done((bf16[1280,128]{1,0:T(8,128)(2,1)S(1)}, bf16[1280,128]{1,0:T(8,128)(2,1)S(1)}, u32[]{:S(2)}, u32[]{:S(2)}) %collective-permute-start.3) | collective-permute-done | bytes 327712 | tf_op jit(solution)/shard_map/ppermute | solution.py:281
  54.8 5.6 %collective-permute-start.4 = (bf16[1280,128]{1,0:T(8,128)(2,1)S(1)}, bf16[1280,128]{1,0:T(8,128)(2,1)S(1)}, u32[]{:S(2)}, u32[]{:S(2)}) collective-permute-start(bf16[1280,128]{1,0:T(8,128)(2,1)S(1)} %collective-permute-done.3.refs_3_), channel_id=1, source_target_pairs={{0,7},{1,0},{2,1},{3,2},{4,3},{5,4},{6,5},{7,6},{8,15},{9,8},{10,9... | collective-permute-start | bytes 983048 | tf_op jit(solution)/shard_map/ppermute | solution.py:281
  66.7 1.9 %collective-permute-start.8 = (bf16[2048,128]{1,0:T(8,128)(2,1)S(1)}, bf16[2048,128]{1,0:T(8,128)(2,1)S(1)}, u32[]{:S(2)}, u32[]{:S(2)}) collective-permute-start(bf16[2048,128]{1,0:T(8,128)(2,1)S(1)} %get-tuple-element.82.bc_mine), channel_id=1, source_target_pairs={{0,16},{16,0},{32,48},{48,32},{64,80},{80,64},{96,112},{112,96},{1... | collective-permute-start | bytes 1572872 | tf_op jit(solution)/shard_map/ppermute | solution.py:289
  68.7 2.8 %shard_map.112 = (f32[512,256]{1,0:T(8,128)S(1)}, f32[512,256]{1,0:T(8,128)S(1)}, f32[16,512]{1,0:T(8,128)S(1)}, f32[16,512]{1,0:T(8,128)S(1)}) custom-call(bf16[512,2048]{1,0:T(8,128)(2,1)S(1)} %get-tuple-element.79.normed, bf16[2048,256]{1,0:T(8,128)(2,1)S(1)} %copy-done.2, bf16[128,2048]{1,0:T(8,128)(2,1)S(1)} %pad.17.dt_weight, ...), custom_call_target="tpu_custom_call" | custom-call | flops 805306368 | bytes 4796416 | tf_op jit(solution)/shard_map/pallas_call | solution.py:264
  71.5 2.2 %shard_map.113 = (f32[512,256]{1,0:T(8,128)S(1)}, bf16[8,144,128]{2,1,0:T(8,128)(2,1)S(1)}) custom-call(s32[5]{0:T(128)S(1)} %stack.23.place, bf16[512,2048]{1,0:T(8,128)(2,1)S(1)} %get-tuple-element.79.normed, f32[512,256]{1,0:T(8,128)S(1)} %get-tuple-element.81.tailed, bf16[2048,128]{1,0:T(8,128)(2,1)S(1)} %get-tuple-element.82.bc_mine, ...), custom_call_target="tpu_custom_call" | custom-call | flops 536870912 | bytes 4522004 | tf_op jit(solution)/shard_map/pallas_call | solution.py:264
  73.7 12.1 %all_to_all.5.gathered = bf16[8,144,128]{2,1,0:T(8,128)(2,1)S(1)} all-to-all(bf16[8,144,128]{2,1,0:T(8,128)(2,1)S(1)} %get-tuple-element.86), channel_id=1, replica_groups={{0,16,32,48,64,80,96,112},{128,144,160,176,192,208,224,240},{256,272,28..., dimensions={0} | all-to-all | bytes 589824 | tf_op jit(solution)/shard_map/all_to_all | solution.py:385
  87.2 5.7 %collective-permute-start.10 = (bf16[144,128]{1,0:T(8,128)(2,1)S(1)}, bf16[144,128]{1,0:T(8,128)(2,1)S(1)}, u32[]{:S(2)}, u32[]{:S(2)}) collective-permute-start(bf16[144,128]{1,0:T(8,128)(2,1)S(1)} %get-tuple-element.93), channel_id=1, source_target_pairs={{0,256},{16,272},{32,288},{48,304},{64,320},{80,336},{96,352},{112... | collective-permute-start | bytes 110600 | tf_op jit(solution)/shard_map/ppermute | solution.py:294
  94.8 2.0 %shard_map.115 = (f32[512,256]{1,0:T(8,128)S(1)}, f32[512,256]{1,0:T(8,128)S(1)}, f32[8,128]{1,0:T(8,128)S(1)}) custom-call(bf16[512,2048]{1,0:T(8,128)(2,1)S(1)} %get-tuple-element.79.normed, bf16[2048,256]{1,0:T(8,128)(2,1)S(1)} %copy-done.4, f32[512,256]{1,0:T(8,128)S(1)} %get-tuple-element.80.x_in, f32[512,256]{1,0:T(8,128)S(1)} %get-tuple-element.84.both_in.both, ...), custom_call_target="tpu_custom_call" | custom-call | flops 1543503872 | bytes 5328896 | tf_op jit(solution)/shard_map/pallas_call | solution.py:264
  105.5 5.6 %collective-permute-start.17 = (bf16[1024,128]{1,0:T(8,128)(2,1)S(1)}, bf16[1024,128]{1,0:T(8,128)(2,1)S(1)}, u32[]{:S(2)}, u32[]{:S(2)}) collective-permute-start(bf16[1024,128]{1,0:T(8,128)(2,1)S(1)} %get-tuple-element.102), channel_id=1, source_target_pairs={{0,7},{1,0},{2,1},{3,2},{4,3},{5,4},{6,5},{7,6},{8,15},{9,8},{10,9... | collective-permute-start | bytes 786440 | tf_op jit(solution)/shard_map/ppermute | solution.py:281
  112.7 3.1 %collective-permute-done.13 = bf16[1024,128]{1,0:T(8,128)(2,1)S(1)} collective-permute-done((bf16[1024,128]{1,0:T(8,128)(2,1)S(1)}, bf16[1024,128]{1,0:T(8,128)(2,1)S(1)}, u32[]{:S(2)}, u32[]{:S(2)}) %collective-permute-start.13) | collective-permute-done | bytes 262176 | tf_op jit(solution)/shard_map/ppermute | solution.py:281
  117.9 5.3 %collective-permute-start.18 = (bf16[1024,128]{1,0:T(8,128)(2,1)S(1)}, bf16[1024,128]{1,0:T(8,128)(2,1)S(1)}, u32[]{:S(2)}, u32[]{:S(2)}) collective-permute-start(bf16[1024,128]{1,0:T(8,128)(2,1)S(1)} %add_convert_fusion.1), channel_id=1, source_target_pairs={{0,7},{1,0},{2,1},{3,2},{4,3},{5,4},{6,5},{7,6},{8,15},{9,8},{10,9... | collective-permute-start | bytes 786440 | tf_op jit(solution)/shard_map/ppermute | solution.py:281
  123.2 3.7 %collective-permute-done.14 = bf16[1024,128]{1,0:T(8,128)(2,1)S(1)} collective-permute-done((bf16[1024,128]{1,0:T(8,128)(2,1)S(1)}, bf16[1024,128]{1,0:T(8,128)(2,1)S(1)}, u32[]{:S(2)}, u32[]{:S(2)}) %collective-permute-start.14) | collective-permute-done | bytes 262176 | tf_op jit(solution)/shard_map/ppermute | solution.py:281
  128.9 5.1 %collective-permute-start.19 = (bf16[1024,128]{1,0:T(8,128)(2,1)S(1)}, bf16[1024,128]{1,0:T(8,128)(2,1)S(1)}, u32[]{:S(2)}, u32[]{:S(2)}) collective-permute-start(bf16[1024,128]{1,0:T(8,128)(2,1)S(1)} %add_convert_fusion), channel_id=1, source_target_pairs={{0,7},{1,0},{2,1},{3,2},{4,3},{5,4},{6,5},{7,6},{8,15},{9,8},{10,9... | collective-permute-start | bytes 786440 | tf_op jit(solution)/shard_map/ppermute | solution.py:281
  134.1 2.9 %collective-permute-done.15 = bf16[1024,128]{1,0:T(8,128)(2,1)S(1)} collective-permute-done((bf16[1024,128]{1,0:T(8,128)(2,1)S(1)}, bf16[1024,128]{1,0:T(8,128)(2,1)S(1)}, u32[]{:S(2)}, u32[]{:S(2)}) %collective-permute-start.15) | collective-permute-done | bytes 262176 | tf_op jit(solution)/shard_map/ppermute | solution.py:281
  139.0 7.5 %collective-permute-done.16 = bf16[1024,128]{1,0:T(8,128)(2,1)S(1)} collective-permute-done((bf16[1024,128]{1,0:T(8,128)(2,1)S(1)}, bf16[1024,128]{1,0:T(8,128)(2,1)S(1)}, u32[]{:S(2)}, u32[]{:S(2)}) %collective-permute-start.16) | collective-permute-done | bytes 262176 | tf_op jit(solution)/shard_map/ppermute | solution.py:281
  146.6 2.5 %collective-permute-start.20 = (bf16[512,128]{1,0:T(8,128)(2,1)S(1)}, bf16[512,128]{1,0:T(8,128)(2,1)S(1)}, u32[]{:S(2)}, u32[]{:S(2)}) collective-permute-start(bf16[512,128]{1,0:T(8,128)(2,1)S(1)} %slice.86), channel_id=1, source_target_pairs={{0,8},{1,9},{2,10},{3,11},{4,12},{5,13},{6,14},{7,15},{8,0},{9,1},... | collective-permute-start | bytes 393224 | tf_op jit(solution)/shard_map/ppermute | solution.py:285
  149.1 8.9 %collective-permute-done.20 = bf16[512,128]{1,0:T(8,128)(2,1)S(1)} collective-permute-done((bf16[512,128]{1,0:T(8,128)(2,1)S(1)}, bf16[512,128]{1,0:T(8,128)(2,1)S(1)}, u32[]{:S(2)}, u32[]{:S(2)}) %collective-permute-start.20) | collective-permute-done | bytes 131104 | tf_op jit(solution)/shard_map/ppermute | solution.py:285
  (59 shorter events, 34.3 us)
Async XLA Ops:
  1.8 14.6 %collective-permute-start = (bf16[640,128]{1,0:T(8,128)(2,1)S(1)}, bf16[640,128]{1,0:T(8,128)(2,1)S(1)}, u32[]{:S(2)}, u32[]{:S(2)}) collective-permute-start(bf16[640,128]{1,0:T(8,128)(2,1)S(1)} %pad_maximum_fusion.one), channel_id=1, source_target_pairs={{0,8},{1,9},{2,10},{3,11},{4,12},{5,13},{6,14},{7,15},{8,0},{9,1},... | collective-permute-start | bytes 491528 | tf_op jit(solution)/shard_map/ppermute | solution.py:285
  16.4 17.2 %collective-permute-start.1 = (bf16[1280,128]{1,0:T(8,128)(2,1)S(1)}, bf16[1280,128]{1,0:T(8,128)(2,1)S(1)}, u32[]{:S(2)}, u32[]{:S(2)}) collective-permute-start(bf16[1280,128]{1,0:T(8,128)(2,1)S(1)} %shard_map.109.refs_0_), channel_id=1, source_target_pairs={{0,7},{1,0},{2,1},{3,2},{4,3},{5,4},{6,5},{7,6},{8,15},{9,8},{10,9... | collective-permute-start | bytes 983048 | tf_op jit(solution)/shard_map/ppermute | solution.py:281
  27.4 11.9 %collective-permute-start.5 = (bf16[1280,128]{1,0:T(8,128)(2,1)S(1)}, bf16[1280,128]{1,0:T(8,128)(2,1)S(1)}, u32[]{:S(2)}, u32[]{:S(2)}) collective-permute-start(bf16[1280,128]{1,0:T(8,128)(2,1)S(1)} %shard_map.109.refs_0_), channel_id=1, source_target_pairs={{0,1},{1,2},{2,3},{3,4},{4,5},{5,6},{6,7},{7,0},{8,9},{9,10},{10,1... | collective-permute-start | bytes 983048 | tf_op jit(solution)/shard_map/ppermute | solution.py:281
  33.6 10.9 %collective-permute-start.2 = (bf16[1280,128]{1,0:T(8,128)(2,1)S(1)}, bf16[1280,128]{1,0:T(8,128)(2,1)S(1)}, u32[]{:S(2)}, u32[]{:S(2)}) collective-permute-start(bf16[1280,128]{1,0:T(8,128)(2,1)S(1)} %collective-permute-done.1.refs_1_), channel_id=1, source_target_pairs={{0,7},{1,0},{2,1},{3,2},{4,3},{5,4},{6,5},{7,6},{8,15},{9,8},{10,9... | collective-permute-start | bytes 983048 | tf_op jit(solution)/shard_map/ppermute | solution.py:281
  39.2 10.9 %collective-permute-start.6 = (bf16[1280,128]{1,0:T(8,128)(2,1)S(1)}, bf16[1280,128]{1,0:T(8,128)(2,1)S(1)}, u32[]{:S(2)}, u32[]{:S(2)}) collective-permute-start(bf16[1280,128]{1,0:T(8,128)(2,1)S(1)} %collective-permute-done.5.refs_6_.refs_7_), channel_id=1, source_target_pairs={{0,1},{1,2},{2,3},{3,4},{4,5},{5,6},{6,7},{7,0},{8,9},{9,10},{10,1... | collective-permute-start | bytes 983048 | tf_op jit(solution)/shard_map/ppermute | solution.py:281
  44.6 10.2 %collective-permute-start.3 = (bf16[1280,128]{1,0:T(8,128)(2,1)S(1)}, bf16[1280,128]{1,0:T(8,128)(2,1)S(1)}, u32[]{:S(2)}, u32[]{:S(2)}) collective-permute-start(bf16[1280,128]{1,0:T(8,128)(2,1)S(1)} %collective-permute-done.2.refs_2_), channel_id=1, source_target_pairs={{0,7},{1,0},{2,1},{3,2},{4,3},{5,4},{6,5},{7,6},{8,15},{9,8},{10,9... | collective-permute-start | bytes 983048 | tf_op jit(solution)/shard_map/ppermute | solution.py:281
  50.2 13.2 %collective-permute-start.7 = (bf16[1280,128]{1,0:T(8,128)(2,1)S(1)}, bf16[1280,128]{1,0:T(8,128)(2,1)S(1)}, u32[]{:S(2)}, u32[]{:S(2)}) collective-permute-start(bf16[1280,128]{1,0:T(8,128)(2,1)S(1)} %collective-permute-done.6.refs_5_.refs_6_), channel_id=1, source_target_pairs={{0,1},{1,2},{2,3},{3,4},{4,5},{5,6},{6,7},{7,0},{8,9},{9,10},{10,1... | collective-permute-start | bytes 983048 | tf_op jit(solution)/shard_map/ppermute | solution.py:281
  54.8 10.2 %collective-permute-start.4 = (bf16[1280,128]{1,0:T(8,128)(2,1)S(1)}, bf16[1280,128]{1,0:T(8,128)(2,1)S(1)}, u32[]{:S(2)}, u32[]{:S(2)}) collective-permute-start(bf16[1280,128]{1,0:T(8,128)(2,1)S(1)} %collective-permute-done.3.refs_3_), channel_id=1, source_target_pairs={{0,7},{1,0},{2,1},{3,2},{4,3},{5,4},{6,5},{7,6},{8,15},{9,8},{10,9... | collective-permute-start | bytes 983048 | tf_op jit(solution)/shard_map/ppermute | solution.py:281
  66.7 4.8 %collective-permute-start.8 = (bf16[2048,128]{1,0:T(8,128)(2,1)S(1)}, bf16[2048,128]{1,0:T(8,128)(2,1)S(1)}, u32[]{:S(2)}, u32[]{:S(2)}) collective-permute-start(bf16[2048,128]{1,0:T(8,128)(2,1)S(1)} %get-tuple-element.82.bc_mine), channel_id=1, source_target_pairs={{0,16},{16,0},{32,48},{48,32},{64,80},{80,64},{96,112},{112,96},{1... | collective-permute-start | bytes 1572872 | tf_op jit(solution)/shard_map/ppermute | solution.py:289
  71.5 23.3 %copy-start.4 = (bf16[2048,256]{1,0:T(8,128)(2,1)S(1)}, bf16[2048,256]{1,0:T(8,128)(2,1)}, u32[]{:S(2)}) copy-start(bf16[2048,256]{1,0:T(8,128)(2,1)} %gate_weight.1) | copy-start | bytes 3145732
  86.5 10.3 %collective-permute-start.11 = (bf16[144,128]{1,0:T(8,128)(2,1)S(1)}, bf16[144,128]{1,0:T(8,128)(2,1)S(1)}, u32[]{:S(2)}, u32[]{:S(2)}) collective-permute-start(bf16[144,128]{1,0:T(8,128)(2,1)S(1)} %get-tuple-element.93), channel_id=1, source_target_pairs={{0,384},{16,400},{32,416},{48,432},{64,448},{80,464},{96,480},{112... | collective-permute-start | bytes 110600 | tf_op jit(solution)/shard_map/ppermute | solution.py:294
  87.2 9.7 %collective-permute-start.10 = (bf16[144,128]{1,0:T(8,128)(2,1)S(1)}, bf16[144,128]{1,0:T(8,128)(2,1)S(1)}, u32[]{:S(2)}, u32[]{:S(2)}) collective-permute-start(bf16[144,128]{1,0:T(8,128)(2,1)S(1)} %get-tuple-element.93), channel_id=1, source_target_pairs={{0,256},{16,272},{32,288},{48,304},{64,320},{80,336},{96,352},{112... | collective-permute-start | bytes 110600 | tf_op jit(solution)/shard_map/ppermute | solution.py:294
  92.9 5.9 %collective-permute-start.9 = (bf16[144,128]{1,0:T(8,128)(2,1)S(1)}, bf16[144,128]{1,0:T(8,128)(2,1)S(1)}, u32[]{:S(2)}, u32[]{:S(2)}) collective-permute-start(bf16[144,128]{1,0:T(8,128)(2,1)S(1)} %get-tuple-element.93), channel_id=1, source_target_pairs={{0,128},{16,144},{32,160},{48,176},{64,192},{80,208},{96,224},{112... | collective-permute-start | bytes 110600 | tf_op jit(solution)/shard_map/ppermute | solution.py:294
  94.8 7.1 %copy-start.1 = (bf16[256,2048]{1,0:T(8,128)(2,1)S(1)}, bf16[256,2048]{1,0:T(8,128)(2,1)}, u32[]{:S(2)}) copy-start(bf16[256,2048]{1,0:T(8,128)(2,1)} %out_weight.3) | copy-start | bytes 3145732
  98.8 3.1 %collective-permute-start.12 = (bf16[128,128]{1,0:T(8,128)(2,1)S(1)}, bf16[128,128]{1,0:T(8,128)(2,1)S(1)}, u32[]{:S(2)}, u32[]{:S(2)}) collective-permute-start(bf16[128,128]{1,0:T(8,128)(2,1)S(1)} %get-tuple-element.95), channel_id=1, source_target_pairs={{0,16},{16,0},{32,48},{48,32},{64,80},{80,64},{96,112},{112,96},{1... | collective-permute-start | bytes 98312 | tf_op jit(solution)/shard_map/ppermute | solution.py:289
  103.6 12.2 %collective-permute-start.13 = (bf16[1024,128]{1,0:T(8,128)(2,1)S(1)}, bf16[1024,128]{1,0:T(8,128)(2,1)S(1)}, u32[]{:S(2)}, u32[]{:S(2)}) collective-permute-start(bf16[1024,128]{1,0:T(8,128)(2,1)S(1)} %get-tuple-element.98), channel_id=1, source_target_pairs={{0,1},{1,2},{2,3},{3,4},{4,5},{5,6},{6,7},{7,0},{8,9},{9,10},{10,1... | collective-permute-start | bytes 786440 | tf_op jit(solution)/shard_map/ppermute | solution.py:281
  105.5 12.3 %collective-permute-start.17 = (bf16[1024,128]{1,0:T(8,128)(2,1)S(1)}, bf16[1024,128]{1,0:T(8,128)(2,1)S(1)}, u32[]{:S(2)}, u32[]{:S(2)}) collective-permute-start(bf16[1024,128]{1,0:T(8,128)(2,1)S(1)} %get-tuple-element.102), channel_id=1, source_target_pairs={{0,7},{1,0},{2,1},{3,2},{4,3},{5,4},{6,5},{7,6},{8,15},{9,8},{10,9... | collective-permute-start | bytes 786440 | tf_op jit(solution)/shard_map/ppermute | solution.py:281
  115.9 11.0 %collective-permute-start.14 = (bf16[1024,128]{1,0:T(8,128)(2,1)S(1)}, bf16[1024,128]{1,0:T(8,128)(2,1)S(1)}, u32[]{:S(2)}, u32[]{:S(2)}) collective-permute-start(bf16[1024,128]{1,0:T(8,128)(2,1)S(1)} %add_convert_fusion.4), channel_id=1, source_target_pairs={{0,1},{1,2},{2,3},{3,4},{4,5},{5,6},{6,7},{7,0},{8,9},{9,10},{10,1... | collective-permute-start | bytes 786440 | tf_op jit(solution)/shard_map/ppermute | solution.py:281
  117.9 40.1 %copy-start.5 = (bf16[512,128]{1,0:T(8,128)(2,1)S(1)}, bf16[512,128]{1,0:T(8,128)(2,1)}, u32[]{:S(2)}) copy-start(bf16[512,128]{1,0:T(8,128)(2,1)} %param.19) | copy-start | bytes 393220
  117.9 10.9 %collective-permute-start.18 = (bf16[1024,128]{1,0:T(8,128)(2,1)S(1)}, bf16[1024,128]{1,0:T(8,128)(2,1)S(1)}, u32[]{:S(2)}, u32[]{:S(2)}) collective-permute-start(bf16[1024,128]{1,0:T(8,128)(2,1)S(1)} %add_convert_fusion.1), channel_id=1, source_target_pairs={{0,7},{1,0},{2,1},{3,2},{4,3},{5,4},{6,5},{7,6},{8,15},{9,8},{10,9... | collective-permute-start | bytes 786440 | tf_op jit(solution)/shard_map/ppermute | solution.py:281
  126.9 10.1 %collective-permute-start.15 = (bf16[1024,128]{1,0:T(8,128)(2,1)S(1)}, bf16[1024,128]{1,0:T(8,128)(2,1)S(1)}, u32[]{:S(2)}, u32[]{:S(2)}) collective-permute-start(bf16[1024,128]{1,0:T(8,128)(2,1)S(1)} %add_convert_fusion.3), channel_id=1, source_target_pairs={{0,1},{1,2},{2,3},{3,4},{4,5},{5,6},{6,7},{7,0},{8,9},{9,10},{10,1... | collective-permute-start | bytes 786440 | tf_op jit(solution)/shard_map/ppermute | solution.py:281
  128.9 10.1 %collective-permute-start.19 = (bf16[1024,128]{1,0:T(8,128)(2,1)S(1)}, bf16[1024,128]{1,0:T(8,128)(2,1)S(1)}, u32[]{:S(2)}, u32[]{:S(2)}) collective-permute-start(bf16[1024,128]{1,0:T(8,128)(2,1)S(1)} %add_convert_fusion), channel_id=1, source_target_pairs={{0,7},{1,0},{2,1},{3,2},{4,3},{5,4},{6,5},{7,6},{8,15},{9,8},{10,9... | collective-permute-start | bytes 786440 | tf_op jit(solution)/shard_map/ppermute | solution.py:281
  137.0 9.5 %collective-permute-start.16 = (bf16[1024,128]{1,0:T(8,128)(2,1)S(1)}, bf16[1024,128]{1,0:T(8,128)(2,1)S(1)}, u32[]{:S(2)}, u32[]{:S(2)}) collective-permute-start(bf16[1024,128]{1,0:T(8,128)(2,1)S(1)} %add_convert_fusion.2), channel_id=1, source_target_pairs={{0,1},{1,2},{2,3},{3,4},{4,5},{5,6},{6,7},{7,0},{8,9},{9,10},{10,1... | collective-permute-start | bytes 786440 | tf_op jit(solution)/shard_map/ppermute | solution.py:281
  146.6 11.4 %collective-permute-start.20 = (bf16[512,128]{1,0:T(8,128)(2,1)S(1)}, bf16[512,128]{1,0:T(8,128)(2,1)S(1)}, u32[]{:S(2)}, u32[]{:S(2)}) collective-permute-start(bf16[512,128]{1,0:T(8,128)(2,1)S(1)} %slice.86), channel_id=1, source_target_pairs={{0,8},{1,9},{2,10},{3,11},{4,12},{5,13},{6,14},{7,15},{8,0},{9,1},... | collective-permute-start | bytes 393224 | tf_op jit(solution)/shard_map/ppermute | solution.py:285
  (4 other events, 18.0 us)

commit v8 on v7

--- a/solution.py
+++ b/solution.py
@@ -85,6 +85,10 @@
     return tail[0:1] + tail[1:2]
 
 
+def distant(turn, k):
+    return lax.rem(turn + jnp.where(lax.rem(turn, 2) == 0, k, RING - k), RING)
+
+
 def square_sum(rows, *blocks):
     value = jnp.zeros((rows, blocks[0].shape[1]), f32)
     for block in blocks:
@@ -115,7 +119,7 @@
     def parts():
         for k in range(RING):
             for j in range(SIDE):
-                head = lax.rem(side + j, SIDE) * RING + lax.rem(turn + k, RING)
+                head = lax.rem(side + j, SIDE) * RING + distant(turn, k)
                 yield blocks[k], j * piece, head
 
     squares = early[...] + square_sum(rows, blocks[RING // 2])
@@ -228,7 +232,7 @@
 def share(ynorm, out_weight, place, k, out):
     rows, own = ynorm.shape[0], out.shape[1]
     for j in range(SIDE):
-        head = lax.rem(place[0] + j, SIDE) * RING + lax.rem(place[1] + k, RING)
+        head = lax.rem(place[0] + j, SIDE) * RING + distant(place[1], k)
         spot = pl.multiple_of(head * own, own)
         out[j * rows : (j + 1) * rows, :] = dot(ynorm, out_weight[:, pl.ds(spot, own)]).astype(bf16)
 
@@ -294,28 +298,40 @@
     return lax.ppermute(block, "section", [(i, i + ahead) for i in range(sections - ahead)])
 
 
+def swap_turn(block, odd):
+    route = []
+    for i in range(SIDE * RING):
+        ahead = 1 if i % 2 == odd else -1
+        route.append((i, i // RING * RING + (i + ahead) % RING))
+    return lax.ppermute(block, "head", route)
+
+
 def gather_ring(block):
+    far = RING // 2
     found = {0: block}
-    for k in range(1, RING // 2):
-        found[k] = to_turn(found[k - 1], -1)
-        found[RING - k] = to_turn(found[(RING - k + 1) % RING], 1)
-    found[RING // 2] = to_turn(found[RING // 2 - 1], -1)
+    for k in range(1, far):
+        found[k], found[RING - k] = swap_turn(found[(RING - k + 1) % RING], 0), swap_turn(found[k - 1], 1)
+    found[far] = swap_turn(found[far + 1], 0)
     return [found[k] for k in range(RING)]
 
 
-def add(a, b):
-    return (a.astype(f32) + b.astype(f32)).astype(bf16)
+def total(first, *others):
+    value = first.astype(f32)
+    for other in others:
+        value = value + other.astype(f32)
+    return value
 
 
 def reduce_ring(shares):
     far = RING // 2
-    up = to_turn(shares[far], 1)
-    down = None
+    one = swap_turn(shares[far], 0)
+    two = swap_turn(shares[far - 1], 0)
     for k in range(far - 1, 0, -1):
-        back = shares[RING - k]
-        up = to_turn(add(up, shares[k]), 1)
-        down = to_turn(back if down is None else add(down, back), -1)
-    return shares[0].astype(f32) + up.astype(f32) + down.astype(f32)
+        odd = (far - k) % 2
+        one = swap_turn(total(shares[RING - k if odd else k], one).astype(bf16), odd)
+        if k > 1:
+            two = swap_turn(total(shares[RING - k + 1 if odd else k - 1], two).astype(bf16), odd)
+    return total(shares[0], one, two)
 
 
 def local(

time: 160 us -> 155 us (0.969)
  the two profiles are of different devices: /device:TPU:40 before, /device:TPU:8 now
where the time goes in v8:
time: 155 us
  starting transfers between devices  69.6 us (45%)
  waiting for transfers between devices  53.4 us (34%)
  Pallas kernels  13.1 us (8%)
  blocking collectives  12.1 us (8%)
  local copies, waits for them, and re-layouts  3.92 us (3%)
  other arithmetic  2.1 us (1%)
    ppermute x14, starting transfers between devices, swap_turn(): return lax.ppermute(block, 'head', route)  43.4 us
    ppermute x14, waiting for transfers between devices, swap_turn(): return lax.ppermute(block, 'head', route)  38 us
    ppermute x2, starting transfers between devices, to_side(): lax.ppermute(block, 'head', [(i, (i + RING) % (SIDE * RING)) for i in ran...  13.5 us
    pallas_call x10, Pallas kernels, on_chip(): pl.pallas_call(kernel, out_shape=outs, in_specs=specs, out_specs=[pl.Bloc...  13.1 us
    ppermute x2, waiting for transfers between devices, to_side(): lax.ppermute(block, 'head', [(i, (i + RING) % (SIDE * RING)) for i in ran...  12.3 us
    all_to_all x1, blocking collectives, local(): lax.all_to_all(slots, 'section', 0, 0, axis_index_groups=by_row)  12.1 us
    ppermute x3, starting transfers between devices, to_row(): lax.ppermute(block, 'section', [(i, i + ahead) for i in range(sections -...  8.96 us
    ppermute x2, starting transfers between devices, to_core(): lax.ppermute(block, 'section', [(i, i ^ 1) for i in range(lax.axis_size('...  3.84 us
  transfers between devices with their start and end apart: 21, of which 17 were waited for; matrix products, arithmetic and copies ran while one was open for 2% of the time, Pallas kernels for 4%

profile of v8, /device:TPU:8, one launch (start us, length us, event | category | flops | bytes accessed | tf_op | source)
XLA Modules:
  0.0 154.7 jit_solution(354715198410713840)
XLA Ops:
  1.8 6.8 %collective-permute-start = (bf16[640,128]{1,0:T(8,128)(2,1)S(1)}, bf16[640,128]{1,0:T(8,128)(2,1)S(1)}, u32[]{:S(2)}, u32[]{:S(2)}) collective-permute-start(bf16[640,128]{1,0:T(8,128)(2,1)S(1)} %pad_maximum_fusion.one), channel_id=1, source_target_pairs={{0,8},{1,9},{2,10},{3,11},{4,12},{5,13},{6,14},{7,15},{8,0},{9,1},... | collective-permute-start | bytes 491528 | tf_op jit(solution)/shard_map/ppermute | solution.py:289
  8.6 7.6 %collective-permute-done.two = bf16[640,128]{1,0:T(8,128)(2,1)S(1)} collective-permute-done((bf16[640,128]{1,0:T(8,128)(2,1)S(1)}, bf16[640,128]{1,0:T(8,128)(2,1)S(1)}, u32[]{:S(2)}, u32[]{:S(2)}) %collective-permute-start) | collective-permute-done | bytes 163872 | tf_op jit(solution)/shard_map/ppermute | solution.py:289
  16.2 10.9 %collective-permute-start.2 = (bf16[1280,128]{1,0:T(8,128)(2,1)S(1)}, bf16[1280,128]{1,0:T(8,128)(2,1)S(1)}, u32[]{:S(2)}, u32[]{:S(2)}) collective-permute-start(bf16[1280,128]{1,0:T(8,128)(2,1)S(1)} %shard_map.109.refs_0_), channel_id=1, source_target_pairs={{0,7},{1,2},{2,1},{3,4},{4,3},{5,6},{6,5},{7,0},{8,15},{9,10},{10,... | collective-permute-start | bytes 983048 | tf_op jit(solution)/shard_map/ppermute | solution.py:306
  29.1 4.6 %collective-permute-done.2.refs_6_.refs_7_ = bf16[1280,128]{1,0:T(8,128)(2,1)S(1)} collective-permute-done((bf16[1280,128]{1,0:T(8,128)(2,1)S(1)}, bf16[1280,128]{1,0:T(8,128)(2,1)S(1)}, u32[]{:S(2)}, u32[]{:S(2)}) %collective-permute-start.2) | collective-permute-done | bytes 327712 | tf_op jit(solution)/shard_map/ppermute | solution.py:306
  35.7 2.2 %collective-permute-done.1.refs_1_ = bf16[1280,128]{1,0:T(8,128)(2,1)S(1)} collective-permute-done((bf16[1280,128]{1,0:T(8,128)(2,1)S(1)}, bf16[1280,128]{1,0:T(8,128)(2,1)S(1)}, u32[]{:S(2)}, u32[]{:S(2)}) %collective-permute-start.1) | collective-permute-done | bytes 327712 | tf_op jit(solution)/shard_map/ppermute | solution.py:306
  37.9 2.6 %collective-permute-start.4 = (bf16[1280,128]{1,0:T(8,128)(2,1)S(1)}, bf16[1280,128]{1,0:T(8,128)(2,1)S(1)}, u32[]{:S(2)}, u32[]{:S(2)}) collective-permute-start(bf16[1280,128]{1,0:T(8,128)(2,1)S(1)} %collective-permute-done.1.refs_1_), channel_id=1, source_target_pairs={{0,7},{1,2},{2,1},{3,4},{4,3},{5,6},{6,5},{7,0},{8,15},{9,10},{10,... | collective-permute-start | bytes 983048 | tf_op jit(solution)/shard_map/ppermute | solution.py:306
  40.5 3.6 %collective-permute-done.3.refs_2_ = bf16[1280,128]{1,0:T(8,128)(2,1)S(1)} collective-permute-done((bf16[1280,128]{1,0:T(8,128)(2,1)S(1)}, bf16[1280,128]{1,0:T(8,128)(2,1)S(1)}, u32[]{:S(2)}, u32[]{:S(2)}) %collective-permute-start.3) | collective-permute-done | bytes 327712 | tf_op jit(solution)/shard_map/ppermute | solution.py:306
  44.1 3.7 %collective-permute-start.6 = (bf16[1280,128]{1,0:T(8,128)(2,1)S(1)}, bf16[1280,128]{1,0:T(8,128)(2,1)S(1)}, u32[]{:S(2)}, u32[]{:S(2)}) collective-permute-start(bf16[1280,128]{1,0:T(8,128)(2,1)S(1)} %collective-permute-done.3.refs_2_), channel_id=1, source_target_pairs={{0,7},{1,2},{2,1},{3,4},{4,3},{5,6},{6,5},{7,0},{8,15},{9,10},{10,... | collective-permute-start | bytes 983048 | tf_op jit(solution)/shard_map/ppermute | solution.py:306
  50.2 4.9 %collective-permute-done.6.refs_4_.refs_5_ = bf16[1280,128]{1,0:T(8,128)(2,1)S(1)} collective-permute-done((bf16[1280,128]{1,0:T(8,128)(2,1)S(1)}, bf16[1280,128]{1,0:T(8,128)(2,1)S(1)}, u32[]{:S(2)}, u32[]{:S(2)}) %collective-permute-start.6) | collective-permute-done | bytes 327712 | tf_op jit(solution)/shard_map/ppermute | solution.py:306
  60.5 3.8 %collective-permute-done.7.refs_4_ = bf16[1280,128]{1,0:T(8,128)(2,1)S(1)} collective-permute-done((bf16[1280,128]{1,0:T(8,128)(2,1)S(1)}, bf16[1280,128]{1,0:T(8,128)(2,1)S(1)}, u32[]{:S(2)}, u32[]{:S(2)}) %collective-permute-start.7) | collective-permute-done | bytes 327712 | tf_op jit(solution)/shard_map/ppermute | solution.py:306
  68.0 2.8 %shard_map.112 = (f32[512,256]{1,0:T(8,128)S(1)}, f32[512,256]{1,0:T(8,128)S(1)}, f32[16,512]{1,0:T(8,128)S(1)}, f32[16,512]{1,0:T(8,128)S(1)}) custom-call(bf16[512,2048]{1,0:T(8,128)(2,1)S(1)} %get-tuple-element.79.normed, bf16[2048,256]{1,0:T(8,128)(2,1)S(1)} %copy-done.2, bf16[128,2048]{1,0:T(8,128)(2,1)S(1)} %pad.17.dt_weight, ...), custom_call_target="tpu_custom_call" | custom-call | flops 805306368 | bytes 4796416 | tf_op jit(solution)/shard_map/pallas_call | solution.py:268
  70.8 2.2 %shard_map.113 = (f32[512,256]{1,0:T(8,128)S(1)}, bf16[8,144,128]{2,1,0:T(8,128)(2,1)S(1)}) custom-call(s32[5]{0:T(128)S(1)} %stack.23.place, bf16[512,2048]{1,0:T(8,128)(2,1)S(1)} %get-tuple-element.79.normed, f32[512,256]{1,0:T(8,128)S(1)} %get-tuple-element.81.tailed, bf16[2048,128]{1,0:T(8,128)(2,1)S(1)} %get-tuple-element.82.bc_mine, ...), custom_call_target="tpu_custom_call" | custom-call | flops 536870912 | bytes 4522004 | tf_op jit(solution)/shard_map/pallas_call | solution.py:268
  73.0 12.1 %all_to_all.5.gathered = bf16[8,144,128]{2,1,0:T(8,128)(2,1)S(1)} all-to-all(bf16[8,144,128]{2,1,0:T(8,128)(2,1)S(1)} %get-tuple-element.86), channel_id=1, replica_groups={{0,16,32,48,64,80,96,112},{128,144,160,176,192,208,224,240},{256,272,28..., dimensions={0} | all-to-all | bytes 589824 | tf_op jit(solution)/shard_map/all_to_all | solution.py:401
  86.5 6.4 %collective-permute-start.10 = (bf16[144,128]{1,0:T(8,128)(2,1)S(1)}, bf16[144,128]{1,0:T(8,128)(2,1)S(1)}, u32[]{:S(2)}, u32[]{:S(2)}) collective-permute-start(bf16[144,128]{1,0:T(8,128)(2,1)S(1)} %get-tuple-element.93), channel_id=1, source_target_pairs={{0,256},{16,272},{32,288},{48,304},{64,320},{80,336},{96,352},{112... | collective-permute-start | bytes 110600 | tf_op jit(solution)/shard_map/ppermute | solution.py:298
  107.3 3.6 %collective-permute-start.17 = (bf16[1024,128]{1,0:T(8,128)(2,1)S(1)}, bf16[1024,128]{1,0:T(8,128)(2,1)S(1)}, u32[]{:S(2)}, u32[]{:S(2)}) collective-permute-start(bf16[1024,128]{1,0:T(8,128)(2,1)S(1)} %get-tuple-element.104), channel_id=1, source_target_pairs={{0,1},{1,0},{2,3},{3,2},{4,5},{5,4},{6,7},{7,6},{8,9},{9,8},{10,11... | collective-permute-start | bytes 786440 | tf_op jit(solution)/shard_map/ppermute | solution.py:306
  111.0 3.6 %collective-permute-done.13 = bf16[1024,128]{1,0:T(8,128)(2,1)S(1)} collective-permute-done((bf16[1024,128]{1,0:T(8,128)(2,1)S(1)}, bf16[1024,128]{1,0:T(8,128)(2,1)S(1)}, u32[]{:S(2)}, u32[]{:S(2)}) %collective-permute-start.13) | collective-permute-done | bytes 262176 | tf_op jit(solution)/shard_map/ppermute | solution.py:306
  114.7 2.8 %collective-permute-start.14 = (bf16[1024,128]{1,0:T(8,128)(2,1)S(1)}, bf16[1024,128]{1,0:T(8,128)(2,1)S(1)}, u32[]{:S(2)}, u32[]{:S(2)}) collective-permute-start(bf16[1024,128]{1,0:T(8,128)(2,1)S(1)} %add_convert_fusion.4), channel_id=1, source_target_pairs={{0,7},{1,2},{2,1},{3,4},{4,3},{5,6},{6,5},{7,0},{8,15},{9,10},{10,... | collective-permute-start | bytes 786440 | tf_op jit(solution)/shard_map/ppermute | solution.py:306
  119.5 2.9 %collective-permute-start.18 = (bf16[1024,128]{1,0:T(8,128)(2,1)S(1)}, bf16[1024,128]{1,0:T(8,128)(2,1)S(1)}, u32[]{:S(2)}, u32[]{:S(2)}) collective-permute-start(bf16[1024,128]{1,0:T(8,128)(2,1)S(1)} %add_convert_fusion.1), channel_id=1, source_target_pairs={{0,7},{1,2},{2,1},{3,4},{4,3},{5,6},{6,5},{7,0},{8,15},{9,10},{10,... | collective-permute-start | bytes 786440 | tf_op jit(solution)/shard_map/ppermute | solution.py:306
  126.6 3.8 %collective-permute-done.18 = bf16[1024,128]{1,0:T(8,128)(2,1)S(1)} collective-permute-done((bf16[1024,128]{1,0:T(8,128)(2,1)S(1)}, bf16[1024,128]{1,0:T(8,128)(2,1)S(1)}, u32[]{:S(2)}, u32[]{:S(2)}) %collective-permute-start.18) | collective-permute-done | bytes 262176 | tf_op jit(solution)/shard_map/ppermute | solution.py:306
  133.0 3.1 %collective-permute-start.16 = (bf16[1024,128]{1,0:T(8,128)(2,1)S(1)}, bf16[1024,128]{1,0:T(8,128)(2,1)S(1)}, u32[]{:S(2)}, u32[]{:S(2)}) collective-permute-start(bf16[1024,128]{1,0:T(8,128)(2,1)S(1)} %add_convert_fusion.2), channel_id=1, source_target_pairs={{0,7},{1,2},{2,1},{3,4},{4,3},{5,6},{6,5},{7,0},{8,15},{9,10},{10,... | collective-permute-start | bytes 786440 | tf_op jit(solution)/shard_map/ppermute | solution.py:306
  136.1 2.8 %collective-permute-done.19 = bf16[1024,128]{1,0:T(8,128)(2,1)S(1)} collective-permute-done((bf16[1024,128]{1,0:T(8,128)(2,1)S(1)}, bf16[1024,128]{1,0:T(8,128)(2,1)S(1)}, u32[]{:S(2)}, u32[]{:S(2)}) %collective-permute-start.19) | collective-permute-done | bytes 262176 | tf_op jit(solution)/shard_map/ppermute | solution.py:306
  138.9 3.5 %collective-permute-done.16 = bf16[1024,128]{1,0:T(8,128)(2,1)S(1)} collective-permute-done((bf16[1024,128]{1,0:T(8,128)(2,1)S(1)}, bf16[1024,128]{1,0:T(8,128)(2,1)S(1)}, u32[]{:S(2)}, u32[]{:S(2)}) %collective-permute-start.16) | collective-permute-done | bytes 262176 | tf_op jit(solution)/shard_map/ppermute | solution.py:306
  142.6 6.6 %collective-permute-start.20 = (bf16[512,128]{1,0:T(8,128)(2,1)S(1)}, bf16[512,128]{1,0:T(8,128)(2,1)S(1)}, u32[]{:S(2)}, u32[]{:S(2)}) collective-permute-start(bf16[512,128]{1,0:T(8,128)(2,1)S(1)} %slice.86), channel_id=1, source_target_pairs={{0,8},{1,9},{2,10},{3,11},{4,12},{5,13},{6,14},{7,15},{8,0},{9,1},... | collective-permute-start | bytes 393224 | tf_op jit(solution)/shard_map/ppermute | solution.py:289
  149.2 4.7 %collective-permute-done.20 = bf16[512,128]{1,0:T(8,128)(2,1)S(1)} collective-permute-done((bf16[512,128]{1,0:T(8,128)(2,1)S(1)}, bf16[512,128]{1,0:T(8,128)(2,1)S(1)}, u32[]{:S(2)}, u32[]{:S(2)}) %collective-permute-start.20) | collective-permute-done | bytes 131104 | tf_op jit(solution)/shard_map/ppermute | solution.py:289
  (59 shorter events, 42.4 us)
Async XLA Ops:
  1.8 14.5 %collective-permute-start = (bf16[640,128]{1,0:T(8,128)(2,1)S(1)}, bf16[640,128]{1,0:T(8,128)(2,1)S(1)}, u32[]{:S(2)}, u32[]{:S(2)}) collective-permute-start(bf16[640,128]{1,0:T(8,128)(2,1)S(1)} %pad_maximum_fusion.one), channel_id=1, source_target_pairs={{0,8},{1,9},{2,10},{3,11},{4,12},{5,13},{6,14},{7,15},{8,0},{9,1},... | collective-permute-start | bytes 491528 | tf_op jit(solution)/shard_map/ppermute | solution.py:289
  16.2 17.5 %collective-permute-start.2 = (bf16[1280,128]{1,0:T(8,128)(2,1)S(1)}, bf16[1280,128]{1,0:T(8,128)(2,1)S(1)}, u32[]{:S(2)}, u32[]{:S(2)}) collective-permute-start(bf16[1280,128]{1,0:T(8,128)(2,1)S(1)} %shard_map.109.refs_0_), channel_id=1, source_target_pairs={{0,7},{1,2},{2,1},{3,4},{4,3},{5,6},{6,5},{7,0},{8,15},{9,10},{10,... | collective-permute-start | bytes 983048 | tf_op jit(solution)/shard_map/ppermute | solution.py:306
  27.2 10.7 %collective-permute-start.1 = (bf16[1280,128]{1,0:T(8,128)(2,1)S(1)}, bf16[1280,128]{1,0:T(8,128)(2,1)S(1)}, u32[]{:S(2)}, u32[]{:S(2)}) collective-permute-start(bf16[1280,128]{1,0:T(8,128)(2,1)S(1)} %shard_map.109.refs_0_), channel_id=1, source_target_pairs={{0,1},{1,0},{2,3},{3,2},{4,5},{5,4},{6,7},{7,6},{8,9},{9,8},{10,11... | collective-permute-start | bytes 983048 | tf_op jit(solution)/shard_map/ppermute | solution.py:306
  33.8 10.4 %collective-permute-start.3 = (bf16[1280,128]{1,0:T(8,128)(2,1)S(1)}, bf16[1280,128]{1,0:T(8,128)(2,1)S(1)}, u32[]{:S(2)}, u32[]{:S(2)}) collective-permute-start(bf16[1280,128]{1,0:T(8,128)(2,1)S(1)} %collective-permute-done.2.refs_6_.refs_7_), channel_id=1, source_target_pairs={{0,1},{1,0},{2,3},{3,2},{4,5},{5,4},{6,7},{7,6},{8,9},{9,8},{10,11... | collective-permute-start | bytes 983048 | tf_op jit(solution)/shard_map/ppermute | solution.py:306
  37.9 10.4 %collective-permute-start.4 = (bf16[1280,128]{1,0:T(8,128)(2,1)S(1)}, bf16[1280,128]{1,0:T(8,128)(2,1)S(1)}, u32[]{:S(2)}, u32[]{:S(2)}) collective-permute-start(bf16[1280,128]{1,0:T(8,128)(2,1)S(1)} %collective-permute-done.1.refs_1_), channel_id=1, source_target_pairs={{0,7},{1,2},{2,1},{3,4},{4,3},{5,6},{6,5},{7,0},{8,15},{9,10},{10,... | collective-permute-start | bytes 983048 | tf_op jit(solution)/shard_map/ppermute | solution.py:306
  44.1 10.9 %collective-permute-start.6 = (bf16[1280,128]{1,0:T(8,128)(2,1)S(1)}, bf16[1280,128]{1,0:T(8,128)(2,1)S(1)}, u32[]{:S(2)}, u32[]{:S(2)}) collective-permute-start(bf16[1280,128]{1,0:T(8,128)(2,1)S(1)} %collective-permute-done.3.refs_2_), channel_id=1, source_target_pairs={{0,7},{1,2},{2,1},{3,4},{4,3},{5,6},{6,5},{7,0},{8,15},{9,10},{10,... | collective-permute-start | bytes 983048 | tf_op jit(solution)/shard_map/ppermute | solution.py:306
  48.3 11.8 %collective-permute-start.5 = (bf16[1280,128]{1,0:T(8,128)(2,1)S(1)}, bf16[1280,128]{1,0:T(8,128)(2,1)S(1)}, u32[]{:S(2)}, u32[]{:S(2)}) collective-permute-start(bf16[1280,128]{1,0:T(8,128)(2,1)S(1)} %collective-permute-done.4.refs_5_.refs_6_), channel_id=1, source_target_pairs={{0,1},{1,0},{2,3},{3,2},{4,5},{5,4},{6,7},{7,6},{8,9},{9,8},{10,11... | collective-permute-start | bytes 983048 | tf_op jit(solution)/shard_map/ppermute | solution.py:306
  55.1 9.1 %collective-permute-start.7 = (bf16[1280,128]{1,0:T(8,128)(2,1)S(1)}, bf16[1280,128]{1,0:T(8,128)(2,1)S(1)}, u32[]{:S(2)}, u32[]{:S(2)}) collective-permute-start(bf16[1280,128]{1,0:T(8,128)(2,1)S(1)} %collective-permute-done.6.refs_4_.refs_5_), channel_id=1, source_target_pairs={{0,1},{1,0},{2,3},{3,2},{4,5},{5,4},{6,7},{7,6},{8,9},{9,8},{10,11... | collective-permute-start | bytes 983048 | tf_op jit(solution)/shard_map/ppermute | solution.py:306
  60.0 7.9 %copy-start.6 = (bf16[2048,4]{0,1:T(4,128)(2,1)S(1)}, bf16[2048,4]{0,1:T(4,128)(2,1)}, u32[]{:S(2)}) copy-start(bf16[2048,4]{0,1:T(4,128)(2,1)} %param.23) | copy-start | bytes 49156
  66.0 4.8 %collective-permute-start.8 = (bf16[2048,128]{1,0:T(8,128)(2,1)S(1)}, bf16[2048,128]{1,0:T(8,128)(2,1)S(1)}, u32[]{:S(2)}, u32[]{:S(2)}) collective-permute-start(bf16[2048,128]{1,0:T(8,128)(2,1)S(1)} %get-tuple-element.82.bc_mine), channel_id=1, source_target_pairs={{0,16},{16,0},{32,48},{48,32},{64,80},{80,64},{96,112},{112,96},{1... | collective-permute-start | bytes 1572872 | tf_op jit(solution)/shard_map/ppermute | solution.py:293
  70.8 24.0 %copy-start.4 = (bf16[2048,256]{1,0:T(8,128)(2,1)S(1)}, bf16[2048,256]{1,0:T(8,128)(2,1)}, u32[]{:S(2)}) copy-start(bf16[2048,256]{1,0:T(8,128)(2,1)} %gate_weight.1) | copy-start | bytes 3145732
  85.8 11.0 %collective-permute-start.11 = (bf16[144,128]{1,0:T(8,128)(2,1)S(1)}, bf16[144,128]{1,0:T(8,128)(2,1)S(1)}, u32[]{:S(2)}, u32[]{:S(2)}) collective-permute-start(bf16[144,128]{1,0:T(8,128)(2,1)S(1)} %get-tuple-element.93), channel_id=1, source_target_pairs={{0,384},{16,400},{32,416},{48,432},{64,448},{80,464},{96,480},{112... | collective-permute-start | bytes 110600 | tf_op jit(solution)/shard_map/ppermute | solution.py:298
  86.5 10.3 %collective-permute-start.10 = (bf16[144,128]{1,0:T(8,128)(2,1)S(1)}, bf16[144,128]{1,0:T(8,128)(2,1)S(1)}, u32[]{:S(2)}, u32[]{:S(2)}) collective-permute-start(bf16[144,128]{1,0:T(8,128)(2,1)S(1)} %get-tuple-element.93), channel_id=1, source_target_pairs={{0,256},{16,272},{32,288},{48,304},{64,320},{80,336},{96,352},{112... | collective-permute-start | bytes 110600 | tf_op jit(solution)/shard_map/ppermute | solution.py:298
  92.9 5.9 %collective-permute-start.9 = (bf16[144,128]{1,0:T(8,128)(2,1)S(1)}, bf16[144,128]{1,0:T(8,128)(2,1)S(1)}, u32[]{:S(2)}, u32[]{:S(2)}) collective-permute-start(bf16[144,128]{1,0:T(8,128)(2,1)S(1)} %get-tuple-element.93), channel_id=1, source_target_pairs={{0,128},{16,144},{32,160},{48,176},{64,192},{80,208},{96,224},{112... | collective-permute-start | bytes 110600 | tf_op jit(solution)/shard_map/ppermute | solution.py:298
  98.8 3.1 %collective-permute-start.12 = (bf16[128,128]{1,0:T(8,128)(2,1)S(1)}, bf16[128,128]{1,0:T(8,128)(2,1)S(1)}, u32[]{:S(2)}, u32[]{:S(2)}) collective-permute-start(bf16[128,128]{1,0:T(8,128)(2,1)S(1)} %get-tuple-element.95), channel_id=1, source_target_pairs={{0,16},{16,0},{32,48},{48,32},{64,80},{80,64},{96,112},{112,96},{1... | collective-permute-start | bytes 98312 | tf_op jit(solution)/shard_map/ppermute | solution.py:293
  103.6 11.0 %collective-permute-start.13 = (bf16[1024,128]{1,0:T(8,128)(2,1)S(1)}, bf16[1024,128]{1,0:T(8,128)(2,1)S(1)}, u32[]{:S(2)}, u32[]{:S(2)}) collective-permute-start(bf16[1024,128]{1,0:T(8,128)(2,1)S(1)} %get-tuple-element.101), channel_id=1, source_target_pairs={{0,1},{1,0},{2,3},{3,2},{4,5},{5,4},{6,7},{7,6},{8,9},{9,8},{10,11... | collective-permute-start | bytes 786440 | tf_op jit(solution)/shard_map/ppermute | solution.py:306
  107.3 12.1 %collective-permute-start.17 = (bf16[1024,128]{1,0:T(8,128)(2,1)S(1)}, bf16[1024,128]{1,0:T(8,128)(2,1)S(1)}, u32[]{:S(2)}, u32[]{:S(2)}) collective-permute-start(bf16[1024,128]{1,0:T(8,128)(2,1)S(1)} %get-tuple-element.104), channel_id=1, source_target_pairs={{0,1},{1,0},{2,3},{3,2},{4,5},{5,4},{6,7},{7,6},{8,9},{9,8},{10,11... | collective-permute-start | bytes 786440 | tf_op jit(solution)/shard_map/ppermute | solution.py:306
  114.7 9.9 %collective-permute-start.14 = (bf16[1024,128]{1,0:T(8,128)(2,1)S(1)}, bf16[1024,128]{1,0:T(8,128)(2,1)S(1)}, u32[]{:S(2)}, u32[]{:S(2)}) collective-permute-start(bf16[1024,128]{1,0:T(8,128)(2,1)S(1)} %add_convert_fusion.4), channel_id=1, source_target_pairs={{0,7},{1,2},{2,1},{3,4},{4,3},{5,6},{6,5},{7,0},{8,15},{9,10},{10,... | collective-permute-start | bytes 786440 | tf_op jit(solution)/shard_map/ppermute | solution.py:306
  119.5 34.4 %copy-start.5 = (bf16[512,128]{1,0:T(8,128)(2,1)S(1)}, bf16[512,128]{1,0:T(8,128)(2,1)}, u32[]{:S(2)}) copy-start(bf16[512,128]{1,0:T(8,128)(2,1)} %param.19) | copy-start | bytes 393220
  119.5 10.8 %collective-permute-start.18 = (bf16[1024,128]{1,0:T(8,128)(2,1)S(1)}, bf16[1024,128]{1,0:T(8,128)(2,1)S(1)}, u32[]{:S(2)}, u32[]{:S(2)}) collective-permute-start(bf16[1024,128]{1,0:T(8,128)(2,1)S(1)} %add_convert_fusion.1), channel_id=1, source_target_pairs={{0,7},{1,2},{2,1},{3,4},{4,3},{5,6},{6,5},{7,0},{8,15},{9,10},{10,... | collective-permute-start | bytes 786440 | tf_op jit(solution)/shard_map/ppermute | solution.py:306
  124.6 8.3 %collective-permute-start.15 = (bf16[1024,128]{1,0:T(8,128)(2,1)S(1)}, bf16[1024,128]{1,0:T(8,128)(2,1)S(1)}, u32[]{:S(2)}, u32[]{:S(2)}) collective-permute-start(bf16[1024,128]{1,0:T(8,128)(2,1)S(1)} %add_convert_fusion.3), channel_id=1, source_target_pairs={{0,1},{1,0},{2,3},{3,2},{4,5},{5,4},{6,7},{7,6},{8,9},{9,8},{10,11... | collective-permute-start | bytes 786440 | tf_op jit(solution)/shard_map/ppermute | solution.py:306
  130.4 8.5 %collective-permute-start.19 = (bf16[1024,128]{1,0:T(8,128)(2,1)S(1)}, bf16[1024,128]{1,0:T(8,128)(2,1)S(1)}, u32[]{:S(2)}, u32[]{:S(2)}) collective-permute-start(bf16[1024,128]{1,0:T(8,128)(2,1)S(1)} %add_convert_fusion), channel_id=1, source_target_pairs={{0,1},{1,0},{2,3},{3,2},{4,5},{5,4},{6,7},{7,6},{8,9},{9,8},{10,11... | collective-permute-start | bytes 786440 | tf_op jit(solution)/shard_map/ppermute | solution.py:306
  133.0 9.5 %collective-permute-start.16 = (bf16[1024,128]{1,0:T(8,128)(2,1)S(1)}, bf16[1024,128]{1,0:T(8,128)(2,1)S(1)}, u32[]{:S(2)}, u32[]{:S(2)}) collective-permute-start(bf16[1024,128]{1,0:T(8,128)(2,1)S(1)} %add_convert_fusion.2), channel_id=1, source_target_pairs={{0,7},{1,2},{2,1},{3,4},{4,3},{5,6},{6,5},{7,0},{8,15},{9,10},{10,... | collective-permute-start | bytes 786440 | tf_op jit(solution)/shard_map/ppermute | solution.py:306
  142.6 11.4 %collective-permute-start.20 = (bf16[512,128]{1,0:T(8,128)(2,1)S(1)}, bf16[512,128]{1,0:T(8,128)(2,1)S(1)}, u32[]{:S(2)}, u32[]{:S(2)}) collective-permute-start(bf16[512,128]{1,0:T(8,128)(2,1)S(1)} %slice.86), channel_id=1, source_target_pairs={{0,8},{1,9},{2,10},{3,11},{4,12},{5,13},{6,14},{7,15},{8,0},{9,1},... | collective-permute-start | bytes 393224 | tf_op jit(solution)/shard_map/ppermute | solution.py:289
  (4 other events, 22.5 us)

commit v9 on v8

--- a/solution.py
+++ b/solution.py
@@ -359,7 +359,7 @@
     head, section = lax.axis_index("head"), lax.axis_index("section")
     place = jnp.stack([head // RING, head % RING, section % 2, section % ROW, section // ROW]).astype(jnp.int32)
 
-    piece = lax.dynamic_slice_in_dim(bc_weight, section % 2 * state_n, state_n, 1)
+    piece = jnp.where(section % 2 == 0, bc_weight[:, :state_n], bc_weight[:, state_n:])
     packed = jnp.concatenate([tokens, piece], 0)
     far = RING // 2
     joined = on_chip(join_kernel, [shape((SIDE * (rows + own), own), bf16)], [packed, to_side(packed)])[0]

time: 155 us -> 155 us (level)
  no operation moved by 1% of the time
where the time goes in v9:
time: 155 us
  starting transfers between devices  69.7 us (45%)
  waiting for transfers between devices  53.4 us (34%)
  Pallas kernels  13.1 us (8%)
  blocking collectives  12.1 us (8%)
  local copies, waits for them, and re-layouts  3.08 us (2%)
  other arithmetic  2.88 us (2%)
    ppermute x14, starting transfers between devices, swap_turn(): return lax.ppermute(block, 'head', route)  43.4 us
    ppermute x14, waiting for transfers between devices, swap_turn(): return lax.ppermute(block, 'head', route)  38 us
    ppermute x2, starting transfers between devices, to_side(): lax.ppermute(block, 'head', [(i, (i + RING) % (SIDE * RING)) for i in ran...  13.5 us
    pallas_call x10, Pallas kernels, on_chip(): pl.pallas_call(kernel, out_shape=outs, in_specs=specs, out_specs=[pl.Bloc...  13.1 us
    ppermute x2, waiting for transfers between devices, to_side(): lax.ppermute(block, 'head', [(i, (i + RING) % (SIDE * RING)) for i in ran...  12.3 us
    all_to_all x1, blocking collectives, local(): lax.all_to_all(slots, 'section', 0, 0, axis_index_groups=by_row)  12.1 us
    ppermute x3, starting transfers between devices, to_row(): lax.ppermute(block, 'section', [(i, i + ahead) for i in range(sections -...  8.97 us
    ppermute x2, starting transfers between devices, to_core(): lax.ppermute(block, 'section', [(i, i ^ 1) for i in range(lax.axis_size('...  3.84 us
  transfers between devices with their start and end apart: 21, of which 17 were waited for; matrix products, arithmetic and copies ran while one was open for 2% of the time, Pallas kernels for 4%

profile of v9, /device:TPU:8, one launch (start us, length us, event | category | flops | bytes accessed | tf_op | source)
XLA Modules:
  0.0 154.6 jit_solution(5766861386430662636)
XLA Ops:
  1.7 6.8 %collective-permute-start = (bf16[640,128]{1,0:T(8,128)(2,1)S(1)}, bf16[640,128]{1,0:T(8,128)(2,1)S(1)}, u32[]{:S(2)}, u32[]{:S(2)}) collective-permute-start(bf16[640,128]{1,0:T(8,128)(2,1)S(1)} %pad_maximum_fusion.one), channel_id=1, source_target_pairs={{0,8},{1,9},{2,10},{3,11},{4,12},{5,13},{6,14},{7,15},{8,0},{9,1},... | collective-permute-start | bytes 491528 | tf_op jit(solution)/shard_map/ppermute | solution.py:289
  8.5 7.6 %collective-permute-done.two = bf16[640,128]{1,0:T(8,128)(2,1)S(1)} collective-permute-done((bf16[640,128]{1,0:T(8,128)(2,1)S(1)}, bf16[640,128]{1,0:T(8,128)(2,1)S(1)}, u32[]{:S(2)}, u32[]{:S(2)}) %collective-permute-start) | collective-permute-done | bytes 163872 | tf_op jit(solution)/shard_map/ppermute | solution.py:289
  16.2 10.9 %collective-permute-start.2 = (bf16[1280,128]{1,0:T(8,128)(2,1)S(1)}, bf16[1280,128]{1,0:T(8,128)(2,1)S(1)}, u32[]{:S(2)}, u32[]{:S(2)}) collective-permute-start(bf16[1280,128]{1,0:T(8,128)(2,1)S(1)} %shard_map.109.refs_0_), channel_id=1, source_target_pairs={{0,7},{1,2},{2,1},{3,4},{4,3},{5,6},{6,5},{7,0},{8,15},{9,10},{10,... | collective-permute-start | bytes 983048 | tf_op jit(solution)/shard_map/ppermute | solution.py:306
  29.1 4.6 %collective-permute-done.2.refs_6_.refs_7_ = bf16[1280,128]{1,0:T(8,128)(2,1)S(1)} collective-permute-done((bf16[1280,128]{1,0:T(8,128)(2,1)S(1)}, bf16[1280,128]{1,0:T(8,128)(2,1)S(1)}, u32[]{:S(2)}, u32[]{:S(2)}) %collective-permute-start.2) | collective-permute-done | bytes 327712 | tf_op jit(solution)/shard_map/ppermute | solution.py:306
  35.6 2.2 %collective-permute-done.1.refs_1_ = bf16[1280,128]{1,0:T(8,128)(2,1)S(1)} collective-permute-done((bf16[1280,128]{1,0:T(8,128)(2,1)S(1)}, bf16[1280,128]{1,0:T(8,128)(2,1)S(1)}, u32[]{:S(2)}, u32[]{:S(2)}) %collective-permute-start.1) | collective-permute-done | bytes 327712 | tf_op jit(solution)/shard_map/ppermute | solution.py:306
  37.8 2.6 %collective-permute-start.4 = (bf16[1280,128]{1,0:T(8,128)(2,1)S(1)}, bf16[1280,128]{1,0:T(8,128)(2,1)S(1)}, u32[]{:S(2)}, u32[]{:S(2)}) collective-permute-start(bf16[1280,128]{1,0:T(8,128)(2,1)S(1)} %collective-permute-done.1.refs_1_), channel_id=1, source_target_pairs={{0,7},{1,2},{2,1},{3,4},{4,3},{5,6},{6,5},{7,0},{8,15},{9,10},{10,... | collective-permute-start | bytes 983048 | tf_op jit(solution)/shard_map/ppermute | solution.py:306
  40.5 3.6 %collective-permute-done.3.refs_2_ = bf16[1280,128]{1,0:T(8,128)(2,1)S(1)} collective-permute-done((bf16[1280,128]{1,0:T(8,128)(2,1)S(1)}, bf16[1280,128]{1,0:T(8,128)(2,1)S(1)}, u32[]{:S(2)}, u32[]{:S(2)}) %collective-permute-start.3) | collective-permute-done | bytes 327712 | tf_op jit(solution)/shard_map/ppermute | solution.py:306
  44.1 3.7 %collective-permute-start.6 = (bf16[1280,128]{1,0:T(8,128)(2,1)S(1)}, bf16[1280,128]{1,0:T(8,128)(2,1)S(1)}, u32[]{:S(2)}, u32[]{:S(2)}) collective-permute-start(bf16[1280,128]{1,0:T(8,128)(2,1)S(1)} %collective-permute-done.3.refs_2_), channel_id=1, source_target_pairs={{0,7},{1,2},{2,1},{3,4},{4,3},{5,6},{6,5},{7,0},{8,15},{9,10},{10,... | collective-permute-start | bytes 983048 | tf_op jit(solution)/shard_map/ppermute | solution.py:306
  50.1 4.9 %collective-permute-done.6.refs_4_.refs_5_ = bf16[1280,128]{1,0:T(8,128)(2,1)S(1)} collective-permute-done((bf16[1280,128]{1,0:T(8,128)(2,1)S(1)}, bf16[1280,128]{1,0:T(8,128)(2,1)S(1)}, u32[]{:S(2)}, u32[]{:S(2)}) %collective-permute-start.6) | collective-permute-done | bytes 327712 | tf_op jit(solution)/shard_map/ppermute | solution.py:306
  60.4 3.8 %collective-permute-done.7.refs_4_ = bf16[1280,128]{1,0:T(8,128)(2,1)S(1)} collective-permute-done((bf16[1280,128]{1,0:T(8,128)(2,1)S(1)}, bf16[1280,128]{1,0:T(8,128)(2,1)S(1)}, u32[]{:S(2)}, u32[]{:S(2)}) %collective-permute-start.7) | collective-permute-done | bytes 327712 | tf_op jit(solution)/shard_map/ppermute | solution.py:306
  67.9 2.8 %shard_map.112 = (f32[512,256]{1,0:T(8,128)S(1)}, f32[512,256]{1,0:T(8,128)S(1)}, f32[16,512]{1,0:T(8,128)S(1)}, f32[16,512]{1,0:T(8,128)S(1)}) custom-call(bf16[512,2048]{1,0:T(8,128)(2,1)S(1)} %get-tuple-element.79.normed, bf16[2048,256]{1,0:T(8,128)(2,1)S(1)} %copy-done.1, bf16[128,2048]{1,0:T(8,128)(2,1)S(1)} %pad.17.dt_weight, ...), custom_call_target="tpu_custom_call" | custom-call | flops 805306368 | bytes 4796416 | tf_op jit(solution)/shard_map/pallas_call | solution.py:268
  70.7 2.2 %shard_map.113 = (f32[512,256]{1,0:T(8,128)S(1)}, bf16[8,144,128]{2,1,0:T(8,128)(2,1)S(1)}) custom-call(s32[5]{0:T(128)S(1)} %stack.23.place, bf16[512,2048]{1,0:T(8,128)(2,1)S(1)} %get-tuple-element.79.normed, f32[512,256]{1,0:T(8,128)S(1)} %get-tuple-element.81.tailed, bf16[2048,128]{1,0:T(8,128)(2,1)S(1)} %get-tuple-element.82.bc_mine, ...), custom_call_target="tpu_custom_call" | custom-call | flops 536870912 | bytes 4522004 | tf_op jit(solution)/shard_map/pallas_call | solution.py:268
  73.0 12.1 %all_to_all.5.gathered = bf16[8,144,128]{2,1,0:T(8,128)(2,1)S(1)} all-to-all(bf16[8,144,128]{2,1,0:T(8,128)(2,1)S(1)} %get-tuple-element.86), channel_id=1, replica_groups={{0,16,32,48,64,80,96,112},{128,144,160,176,192,208,224,240},{256,272,28..., dimensions={0} | all-to-all | bytes 589824 | tf_op jit(solution)/shard_map/all_to_all | solution.py:401
  86.4 6.4 %collective-permute-start.10 = (bf16[144,128]{1,0:T(8,128)(2,1)S(1)}, bf16[144,128]{1,0:T(8,128)(2,1)S(1)}, u32[]{:S(2)}, u32[]{:S(2)}) collective-permute-start(bf16[144,128]{1,0:T(8,128)(2,1)S(1)} %get-tuple-element.93), channel_id=1, source_target_pairs={{0,256},{16,272},{32,288},{48,304},{64,320},{80,336},{96,352},{112... | collective-permute-start | bytes 110600 | tf_op jit(solution)/shard_map/ppermute | solution.py:298
  107.3 3.6 %collective-permute-start.17 = (bf16[1024,128]{1,0:T(8,128)(2,1)S(1)}, bf16[1024,128]{1,0:T(8,128)(2,1)S(1)}, u32[]{:S(2)}, u32[]{:S(2)}) collective-permute-start(bf16[1024,128]{1,0:T(8,128)(2,1)S(1)} %get-tuple-element.104), channel_id=1, source_target_pairs={{0,1},{1,0},{2,3},{3,2},{4,5},{5,4},{6,7},{7,6},{8,9},{9,8},{10,11... | collective-permute-start | bytes 786440 | tf_op jit(solution)/shard_map/ppermute | solution.py:306
  110.9 3.6 %collective-permute-done.13 = bf16[1024,128]{1,0:T(8,128)(2,1)S(1)} collective-permute-done((bf16[1024,128]{1,0:T(8,128)(2,1)S(1)}, bf16[1024,128]{1,0:T(8,128)(2,1)S(1)}, u32[]{:S(2)}, u32[]{:S(2)}) %collective-permute-start.13) | collective-permute-done | bytes 262176 | tf_op jit(solution)/shard_map/ppermute | solution.py:306
  114.6 2.8 %collective-permute-start.14 = (bf16[1024,128]{1,0:T(8,128)(2,1)S(1)}, bf16[1024,128]{1,0:T(8,128)(2,1)S(1)}, u32[]{:S(2)}, u32[]{:S(2)}) collective-permute-start(bf16[1024,128]{1,0:T(8,128)(2,1)S(1)} %add_convert_fusion.4), channel_id=1, source_target_pairs={{0,7},{1,2},{2,1},{3,4},{4,3},{5,6},{6,5},{7,0},{8,15},{9,10},{10,... | collective-permute-start | bytes 786440 | tf_op jit(solution)/shard_map/ppermute | solution.py:306
  119.5 2.9 %collective-permute-start.18 = (bf16[1024,128]{1,0:T(8,128)(2,1)S(1)}, bf16[1024,128]{1,0:T(8,128)(2,1)S(1)}, u32[]{:S(2)}, u32[]{:S(2)}) collective-permute-start(bf16[1024,128]{1,0:T(8,128)(2,1)S(1)} %add_convert_fusion.1), channel_id=1, source_target_pairs={{0,7},{1,2},{2,1},{3,4},{4,3},{5,6},{6,5},{7,0},{8,15},{9,10},{10,... | collective-permute-start | bytes 786440 | tf_op jit(solution)/shard_map/ppermute | solution.py:306
  126.5 3.8 %collective-permute-done.18 = bf16[1024,128]{1,0:T(8,128)(2,1)S(1)} collective-permute-done((bf16[1024,128]{1,0:T(8,128)(2,1)S(1)}, bf16[1024,128]{1,0:T(8,128)(2,1)S(1)}, u32[]{:S(2)}, u32[]{:S(2)}) %collective-permute-start.18) | collective-permute-done | bytes 262176 | tf_op jit(solution)/shard_map/ppermute | solution.py:306
  132.9 3.1 %collective-permute-start.16 = (bf16[1024,128]{1,0:T(8,128)(2,1)S(1)}, bf16[1024,128]{1,0:T(8,128)(2,1)S(1)}, u32[]{:S(2)}, u32[]{:S(2)}) collective-permute-start(bf16[1024,128]{1,0:T(8,128)(2,1)S(1)} %add_convert_fusion.2), channel_id=1, source_target_pairs={{0,7},{1,2},{2,1},{3,4},{4,3},{5,6},{6,5},{7,0},{8,15},{9,10},{10,... | collective-permute-start | bytes 786440 | tf_op jit(solution)/shard_map/ppermute | solution.py:306
  136.0 2.8 %collective-permute-done.19 = bf16[1024,128]{1,0:T(8,128)(2,1)S(1)} collective-permute-done((bf16[1024,128]{1,0:T(8,128)(2,1)S(1)}, bf16[1024,128]{1,0:T(8,128)(2,1)S(1)}, u32[]{:S(2)}, u32[]{:S(2)}) %collective-permute-start.19) | collective-permute-done | bytes 262176 | tf_op jit(solution)/shard_map/ppermute | solution.py:306
  138.8 3.5 %collective-permute-done.16 = bf16[1024,128]{1,0:T(8,128)(2,1)S(1)} collective-permute-done((bf16[1024,128]{1,0:T(8,128)(2,1)S(1)}, bf16[1024,128]{1,0:T(8,128)(2,1)S(1)}, u32[]{:S(2)}, u32[]{:S(2)}) %collective-permute-start.16) | collective-permute-done | bytes 262176 | tf_op jit(solution)/shard_map/ppermute | solution.py:306
  142.5 6.6 %collective-permute-start.20 = (bf16[512,128]{1,0:T(8,128)(2,1)S(1)}, bf16[512,128]{1,0:T(8,128)(2,1)S(1)}, u32[]{:S(2)}, u32[]{:S(2)}) collective-permute-start(bf16[512,128]{1,0:T(8,128)(2,1)S(1)} %slice.96), channel_id=1, source_target_pairs={{0,8},{1,9},{2,10},{3,11},{4,12},{5,13},{6,14},{7,15},{8,0},{9,1},... | collective-permute-start | bytes 393224 | tf_op jit(solution)/shard_map/ppermute | solution.py:289
  149.1 4.7 %collective-permute-done.20 = bf16[512,128]{1,0:T(8,128)(2,1)S(1)} collective-permute-done((bf16[512,128]{1,0:T(8,128)(2,1)S(1)}, bf16[512,128]{1,0:T(8,128)(2,1)S(1)}, u32[]{:S(2)}, u32[]{:S(2)}) %collective-permute-start.20) | collective-permute-done | bytes 131104 | tf_op jit(solution)/shard_map/ppermute | solution.py:289
  (57 shorter events, 42.3 us)
Async XLA Ops:
  1.7 14.5 %collective-permute-start = (bf16[640,128]{1,0:T(8,128)(2,1)S(1)}, bf16[640,128]{1,0:T(8,128)(2,1)S(1)}, u32[]{:S(2)}, u32[]{:S(2)}) collective-permute-start(bf16[640,128]{1,0:T(8,128)(2,1)S(1)} %pad_maximum_fusion.one), channel_id=1, source_target_pairs={{0,8},{1,9},{2,10},{3,11},{4,12},{5,13},{6,14},{7,15},{8,0},{9,1},... | collective-permute-start | bytes 491528 | tf_op jit(solution)/shard_map/ppermute | solution.py:289
  16.2 17.5 %collective-permute-start.2 = (bf16[1280,128]{1,0:T(8,128)(2,1)S(1)}, bf16[1280,128]{1,0:T(8,128)(2,1)S(1)}, u32[]{:S(2)}, u32[]{:S(2)}) collective-permute-start(bf16[1280,128]{1,0:T(8,128)(2,1)S(1)} %shard_map.109.refs_0_), channel_id=1, source_target_pairs={{0,7},{1,2},{2,1},{3,4},{4,3},{5,6},{6,5},{7,0},{8,15},{9,10},{10,... | collective-permute-start | bytes 983048 | tf_op jit(solution)/shard_map/ppermute | solution.py:306
  27.1 10.7 %collective-permute-start.1 = (bf16[1280,128]{1,0:T(8,128)(2,1)S(1)}, bf16[1280,128]{1,0:T(8,128)(2,1)S(1)}, u32[]{:S(2)}, u32[]{:S(2)}) collective-permute-start(bf16[1280,128]{1,0:T(8,128)(2,1)S(1)} %shard_map.109.refs_0_), channel_id=1, source_target_pairs={{0,1},{1,0},{2,3},{3,2},{4,5},{5,4},{6,7},{7,6},{8,9},{9,8},{10,11... | collective-permute-start | bytes 983048 | tf_op jit(solution)/shard_map/ppermute | solution.py:306
  33.7 10.4 %collective-permute-start.3 = (bf16[1280,128]{1,0:T(8,128)(2,1)S(1)}, bf16[1280,128]{1,0:T(8,128)(2,1)S(1)}, u32[]{:S(2)}, u32[]{:S(2)}) collective-permute-start(bf16[1280,128]{1,0:T(8,128)(2,1)S(1)} %collective-permute-done.2.refs_6_.refs_7_), channel_id=1, source_target_pairs={{0,1},{1,0},{2,3},{3,2},{4,5},{5,4},{6,7},{7,6},{8,9},{9,8},{10,11... | collective-permute-start | bytes 983048 | tf_op jit(solution)/shard_map/ppermute | solution.py:306
  37.8 10.4 %collective-permute-start.4 = (bf16[1280,128]{1,0:T(8,128)(2,1)S(1)}, bf16[1280,128]{1,0:T(8,128)(2,1)S(1)}, u32[]{:S(2)}, u32[]{:S(2)}) collective-permute-start(bf16[1280,128]{1,0:T(8,128)(2,1)S(1)} %collective-permute-done.1.refs_1_), channel_id=1, source_target_pairs={{0,7},{1,2},{2,1},{3,4},{4,3},{5,6},{6,5},{7,0},{8,15},{9,10},{10,... | collective-permute-start | bytes 983048 | tf_op jit(solution)/shard_map/ppermute | solution.py:306
  44.1 10.9 %collective-permute-start.6 = (bf16[1280,128]{1,0:T(8,128)(2,1)S(1)}, bf16[1280,128]{1,0:T(8,128)(2,1)S(1)}, u32[]{:S(2)}, u32[]{:S(2)}) collective-permute-start(bf16[1280,128]{1,0:T(8,128)(2,1)S(1)} %collective-permute-done.3.refs_2_), channel_id=1, source_target_pairs={{0,7},{1,2},{2,1},{3,4},{4,3},{5,6},{6,5},{7,0},{8,15},{9,10},{10,... | collective-permute-start | bytes 983048 | tf_op jit(solution)/shard_map/ppermute | solution.py:306
  48.2 11.8 %collective-permute-start.5 = (bf16[1280,128]{1,0:T(8,128)(2,1)S(1)}, bf16[1280,128]{1,0:T(8,128)(2,1)S(1)}, u32[]{:S(2)}, u32[]{:S(2)}) collective-permute-start(bf16[1280,128]{1,0:T(8,128)(2,1)S(1)} %collective-permute-done.4.refs_5_.refs_6_), channel_id=1, source_target_pairs={{0,1},{1,0},{2,3},{3,2},{4,5},{5,4},{6,7},{7,6},{8,9},{9,8},{10,11... | collective-permute-start | bytes 983048 | tf_op jit(solution)/shard_map/ppermute | solution.py:306
  55.0 9.1 %collective-permute-start.7 = (bf16[1280,128]{1,0:T(8,128)(2,1)S(1)}, bf16[1280,128]{1,0:T(8,128)(2,1)S(1)}, u32[]{:S(2)}, u32[]{:S(2)}) collective-permute-start(bf16[1280,128]{1,0:T(8,128)(2,1)S(1)} %collective-permute-done.6.refs_4_.refs_5_), channel_id=1, source_target_pairs={{0,1},{1,0},{2,3},{3,2},{4,5},{5,4},{6,7},{7,6},{8,9},{9,8},{10,11... | collective-permute-start | bytes 983048 | tf_op jit(solution)/shard_map/ppermute | solution.py:306
  60.0 7.9 %copy-start.5 = (bf16[2048,4]{0,1:T(4,128)(2,1)S(1)}, bf16[2048,4]{0,1:T(4,128)(2,1)}, u32[]{:S(2)}) copy-start(bf16[2048,4]{0,1:T(4,128)(2,1)} %param.23) | copy-start | bytes 49156
  65.9 4.8 %collective-permute-start.8 = (bf16[2048,128]{1,0:T(8,128)(2,1)S(1)}, bf16[2048,128]{1,0:T(8,128)(2,1)S(1)}, u32[]{:S(2)}, u32[]{:S(2)}) collective-permute-start(bf16[2048,128]{1,0:T(8,128)(2,1)S(1)} %get-tuple-element.82.bc_mine), channel_id=1, source_target_pairs={{0,16},{16,0},{32,48},{48,32},{64,80},{80,64},{96,112},{112,96},{1... | collective-permute-start | bytes 1572872 | tf_op jit(solution)/shard_map/ppermute | solution.py:293
  70.7 24.0 %copy-start.3 = (bf16[2048,256]{1,0:T(8,128)(2,1)S(1)}, bf16[2048,256]{1,0:T(8,128)(2,1)}, u32[]{:S(2)}) copy-start(bf16[2048,256]{1,0:T(8,128)(2,1)} %gate_weight.1) | copy-start | bytes 3145732
  85.7 11.0 %collective-permute-start.11 = (bf16[144,128]{1,0:T(8,128)(2,1)S(1)}, bf16[144,128]{1,0:T(8,128)(2,1)S(1)}, u32[]{:S(2)}, u32[]{:S(2)}) collective-permute-start(bf16[144,128]{1,0:T(8,128)(2,1)S(1)} %get-tuple-element.93), channel_id=1, source_target_pairs={{0,384},{16,400},{32,416},{48,432},{64,448},{80,464},{96,480},{112... | collective-permute-start | bytes 110600 | tf_op jit(solution)/shard_map/ppermute | solution.py:298
  86.4 10.4 %collective-permute-start.10 = (bf16[144,128]{1,0:T(8,128)(2,1)S(1)}, bf16[144,128]{1,0:T(8,128)(2,1)S(1)}, u32[]{:S(2)}, u32[]{:S(2)}) collective-permute-start(bf16[144,128]{1,0:T(8,128)(2,1)S(1)} %get-tuple-element.93), channel_id=1, source_target_pairs={{0,256},{16,272},{32,288},{48,304},{64,320},{80,336},{96,352},{112... | collective-permute-start | bytes 110600 | tf_op jit(solution)/shard_map/ppermute | solution.py:298
  92.8 5.9 %collective-permute-start.9 = (bf16[144,128]{1,0:T(8,128)(2,1)S(1)}, bf16[144,128]{1,0:T(8,128)(2,1)S(1)}, u32[]{:S(2)}, u32[]{:S(2)}) collective-permute-start(bf16[144,128]{1,0:T(8,128)(2,1)S(1)} %get-tuple-element.93), channel_id=1, source_target_pairs={{0,128},{16,144},{32,160},{48,176},{64,192},{80,208},{96,224},{112... | collective-permute-start | bytes 110600 | tf_op jit(solution)/shard_map/ppermute | solution.py:298
  98.7 3.1 %collective-permute-start.12 = (bf16[128,128]{1,0:T(8,128)(2,1)S(1)}, bf16[128,128]{1,0:T(8,128)(2,1)S(1)}, u32[]{:S(2)}, u32[]{:S(2)}) collective-permute-start(bf16[128,128]{1,0:T(8,128)(2,1)S(1)} %get-tuple-element.95), channel_id=1, source_target_pairs={{0,16},{16,0},{32,48},{48,32},{64,80},{80,64},{96,112},{112,96},{1... | collective-permute-start | bytes 98312 | tf_op jit(solution)/shard_map/ppermute | solution.py:293
  103.5 11.0 %collective-permute-start.13 = (bf16[1024,128]{1,0:T(8,128)(2,1)S(1)}, bf16[1024,128]{1,0:T(8,128)(2,1)S(1)}, u32[]{:S(2)}, u32[]{:S(2)}) collective-permute-start(bf16[1024,128]{1,0:T(8,128)(2,1)S(1)} %get-tuple-element.101), channel_id=1, source_target_pairs={{0,1},{1,0},{2,3},{3,2},{4,5},{5,4},{6,7},{7,6},{8,9},{9,8},{10,11... | collective-permute-start | bytes 786440 | tf_op jit(solution)/shard_map/ppermute | solution.py:306
  107.3 12.1 %collective-permute-start.17 = (bf16[1024,128]{1,0:T(8,128)(2,1)S(1)}, bf16[1024,128]{1,0:T(8,128)(2,1)S(1)}, u32[]{:S(2)}, u32[]{:S(2)}) collective-permute-start(bf16[1024,128]{1,0:T(8,128)(2,1)S(1)} %get-tuple-element.104), channel_id=1, source_target_pairs={{0,1},{1,0},{2,3},{3,2},{4,5},{5,4},{6,7},{7,6},{8,9},{9,8},{10,11... | collective-permute-start | bytes 786440 | tf_op jit(solution)/shard_map/ppermute | solution.py:306
  114.6 9.9 %collective-permute-start.14 = (bf16[1024,128]{1,0:T(8,128)(2,1)S(1)}, bf16[1024,128]{1,0:T(8,128)(2,1)S(1)}, u32[]{:S(2)}, u32[]{:S(2)}) collective-permute-start(bf16[1024,128]{1,0:T(8,128)(2,1)S(1)} %add_convert_fusion.4), channel_id=1, source_target_pairs={{0,7},{1,2},{2,1},{3,4},{4,3},{5,6},{6,5},{7,0},{8,15},{9,10},{10,... | collective-permute-start | bytes 786440 | tf_op jit(solution)/shard_map/ppermute | solution.py:306
  119.5 34.4 %copy-start.4 = (bf16[512,128]{1,0:T(8,128)(2,1)S(1)}, bf16[512,128]{1,0:T(8,128)(2,1)}, u32[]{:S(2)}) copy-start(bf16[512,128]{1,0:T(8,128)(2,1)} %param.19) | copy-start | bytes 393220
  119.5 10.8 %collective-permute-start.18 = (bf16[1024,128]{1,0:T(8,128)(2,1)S(1)}, bf16[1024,128]{1,0:T(8,128)(2,1)S(1)}, u32[]{:S(2)}, u32[]{:S(2)}) collective-permute-start(bf16[1024,128]{1,0:T(8,128)(2,1)S(1)} %add_convert_fusion.1), channel_id=1, source_target_pairs={{0,7},{1,2},{2,1},{3,4},{4,3},{5,6},{6,5},{7,0},{8,15},{9,10},{10,... | collective-permute-start | bytes 786440 | tf_op jit(solution)/shard_map/ppermute | solution.py:306
  124.6 8.3 %collective-permute-start.15 = (bf16[1024,128]{1,0:T(8,128)(2,1)S(1)}, bf16[1024,128]{1,0:T(8,128)(2,1)S(1)}, u32[]{:S(2)}, u32[]{:S(2)}) collective-permute-start(bf16[1024,128]{1,0:T(8,128)(2,1)S(1)} %add_convert_fusion.3), channel_id=1, source_target_pairs={{0,1},{1,0},{2,3},{3,2},{4,5},{5,4},{6,7},{7,6},{8,9},{9,8},{10,11... | collective-permute-start | bytes 786440 | tf_op jit(solution)/shard_map/ppermute | solution.py:306
  130.3 8.5 %collective-permute-start.19 = (bf16[1024,128]{1,0:T(8,128)(2,1)S(1)}, bf16[1024,128]{1,0:T(8,128)(2,1)S(1)}, u32[]{:S(2)}, u32[]{:S(2)}) collective-permute-start(bf16[1024,128]{1,0:T(8,128)(2,1)S(1)} %add_convert_fusion), channel_id=1, source_target_pairs={{0,1},{1,0},{2,3},{3,2},{4,5},{5,4},{6,7},{7,6},{8,9},{9,8},{10,11... | collective-permute-start | bytes 786440 | tf_op jit(solution)/shard_map/ppermute | solution.py:306
  132.9 9.5 %collective-permute-start.16 = (bf16[1024,128]{1,0:T(8,128)(2,1)S(1)}, bf16[1024,128]{1,0:T(8,128)(2,1)S(1)}, u32[]{:S(2)}, u32[]{:S(2)}) collective-permute-start(bf16[1024,128]{1,0:T(8,128)(2,1)S(1)} %add_convert_fusion.2), channel_id=1, source_target_pairs={{0,7},{1,2},{2,1},{3,4},{4,3},{5,6},{6,5},{7,0},{8,15},{9,10},{10,... | collective-permute-start | bytes 786440 | tf_op jit(solution)/shard_map/ppermute | solution.py:306
  142.5 11.4 %collective-permute-start.20 = (bf16[512,128]{1,0:T(8,128)(2,1)S(1)}, bf16[512,128]{1,0:T(8,128)(2,1)S(1)}, u32[]{:S(2)}, u32[]{:S(2)}) collective-permute-start(bf16[512,128]{1,0:T(8,128)(2,1)S(1)} %slice.96), channel_id=1, source_target_pairs={{0,8},{1,9},{2,10},{3,11},{4,12},{5,13},{6,14},{7,15},{8,0},{9,1},... | collective-permute-start | bytes 393224 | tf_op jit(solution)/shard_map/ppermute | solution.py:289
  (3 other events, 21.6 us)

commit v10 on v8

--- a/solution.py
+++ b/solution.py
@@ -324,10 +324,10 @@
 
 def reduce_ring(shares):
     far = RING // 2
-    one = swap_turn(shares[far], 0)
-    two = swap_turn(shares[far - 1], 0)
+    one = swap_turn(shares[far], 1)
+    two = swap_turn(shares[far + 1], 1)
     for k in range(far - 1, 0, -1):
-        odd = (far - k) % 2
+        odd = (far - k + 1) % 2
         one = swap_turn(total(shares[RING - k if odd else k], one).astype(bf16), odd)
         if k > 1:
             two = swap_turn(total(shares[RING - k + 1 if odd else k - 1], two).astype(bf16), odd)

time: 155 us -> 155 us (level)
  no operation moved by 1% of the time
where the time goes in v10:
time: 155 us
  starting transfers between devices  69.8 us (45%)
  waiting for transfers between devices  53.3 us (34%)
  Pallas kernels  13.1 us (8%)
  blocking collectives  12.1 us (8%)
  local copies, waits for them, and re-layouts  3.92 us (3%)
  other arithmetic  2.1 us (1%)
    ppermute x14, starting transfers between devices, swap_turn(): return lax.ppermute(block, 'head', route)  43.5 us
    ppermute x14, waiting for transfers between devices, swap_turn(): return lax.ppermute(block, 'head', route)  37.9 us
    ppermute x2, starting transfers between devices, to_side(): lax.ppermute(block, 'head', [(i, (i + RING) % (SIDE * RING)) for i in ran...  13.5 us
    pallas_call x10, Pallas kernels, on_chip(): pl.pallas_call(kernel, out_shape=outs, in_specs=specs, out_specs=[pl.Bloc...  13.1 us
    ppermute x2, waiting for transfers between devices, to_side(): lax.ppermute(block, 'head', [(i, (i + RING) % (SIDE * RING)) for i in ran...  12.3 us
    all_to_all x1, blocking collectives, local(): lax.all_to_all(slots, 'section', 0, 0, axis_index_groups=by_row)  12.1 us
    ppermute x3, starting transfers between devices, to_row(): lax.ppermute(block, 'section', [(i, i + ahead) for i in range(sections -...  8.98 us
    ppermute x2, starting transfers between devices, to_core(): lax.ppermute(block, 'section', [(i, i ^ 1) for i in range(lax.axis_size('...  3.84 us
  transfers between devices with their start and end apart: 21, of which 17 were waited for; matrix products, arithmetic and copies ran while one was open for 2% of the time, Pallas kernels for 4%

profile of v10, /device:TPU:8, one launch (start us, length us, event | category | flops | bytes accessed | tf_op | source)
XLA Modules:
  0.0 154.7 jit_solution(14376520024493543220)
XLA Ops:
  1.8 6.8 %collective-permute-start = (bf16[640,128]{1,0:T(8,128)(2,1)S(1)}, bf16[640,128]{1,0:T(8,128)(2,1)S(1)}, u32[]{:S(2)}, u32[]{:S(2)}) collective-permute-start(bf16[640,128]{1,0:T(8,128)(2,1)S(1)} %pad_maximum_fusion.one), channel_id=1, source_target_pairs={{0,8},{1,9},{2,10},{3,11},{4,12},{5,13},{6,14},{7,15},{8,0},{9,1},... | collective-permute-start | bytes 491528 | tf_op jit(solution)/shard_map/ppermute | solution.py:289
  8.6 7.6 %collective-permute-done.two = bf16[640,128]{1,0:T(8,128)(2,1)S(1)} collective-permute-done((bf16[640,128]{1,0:T(8,128)(2,1)S(1)}, bf16[640,128]{1,0:T(8,128)(2,1)S(1)}, u32[]{:S(2)}, u32[]{:S(2)}) %collective-permute-start) | collective-permute-done | bytes 163872 | tf_op jit(solution)/shard_map/ppermute | solution.py:289
  16.2 10.9 %collective-permute-start.2 = (bf16[1280,128]{1,0:T(8,128)(2,1)S(1)}, bf16[1280,128]{1,0:T(8,128)(2,1)S(1)}, u32[]{:S(2)}, u32[]{:S(2)}) collective-permute-start(bf16[1280,128]{1,0:T(8,128)(2,1)S(1)} %shard_map.109.refs_0_), channel_id=1, source_target_pairs={{0,7},{1,2},{2,1},{3,4},{4,3},{5,6},{6,5},{7,0},{8,15},{9,10},{10,... | collective-permute-start | bytes 983048 | tf_op jit(solution)/shard_map/ppermute | solution.py:306
  29.1 4.6 %collective-permute-done.2.refs_6_.refs_7_ = bf16[1280,128]{1,0:T(8,128)(2,1)S(1)} collective-permute-done((bf16[1280,128]{1,0:T(8,128)(2,1)S(1)}, bf16[1280,128]{1,0:T(8,128)(2,1)S(1)}, u32[]{:S(2)}, u32[]{:S(2)}) %collective-permute-start.2) | collective-permute-done | bytes 327712 | tf_op jit(solution)/shard_map/ppermute | solution.py:306
  37.9 2.6 %collective-permute-start.4 = (bf16[1280,128]{1,0:T(8,128)(2,1)S(1)}, bf16[1280,128]{1,0:T(8,128)(2,1)S(1)}, u32[]{:S(2)}, u32[]{:S(2)}) collective-permute-start(bf16[1280,128]{1,0:T(8,128)(2,1)S(1)} %collective-permute-done.1.refs_1_), channel_id=1, source_target_pairs={{0,7},{1,2},{2,1},{3,4},{4,3},{5,6},{6,5},{7,0},{8,15},{9,10},{10,... | collective-permute-start | bytes 983048 | tf_op jit(solution)/shard_map/ppermute | solution.py:306
  40.5 3.6 %collective-permute-done.3.refs_2_ = bf16[1280,128]{1,0:T(8,128)(2,1)S(1)} collective-permute-done((bf16[1280,128]{1,0:T(8,128)(2,1)S(1)}, bf16[1280,128]{1,0:T(8,128)(2,1)S(1)}, u32[]{:S(2)}, u32[]{:S(2)}) %collective-permute-start.3) | collective-permute-done | bytes 327712 | tf_op jit(solution)/shard_map/ppermute | solution.py:306
  44.1 3.7 %collective-permute-start.6 = (bf16[1280,128]{1,0:T(8,128)(2,1)S(1)}, bf16[1280,128]{1,0:T(8,128)(2,1)S(1)}, u32[]{:S(2)}, u32[]{:S(2)}) collective-permute-start(bf16[1280,128]{1,0:T(8,128)(2,1)S(1)} %collective-permute-done.3.refs_2_), channel_id=1, source_target_pairs={{0,7},{1,2},{2,1},{3,4},{4,3},{5,6},{6,5},{7,0},{8,15},{9,10},{10,... | collective-permute-start | bytes 983048 | tf_op jit(solution)/shard_map/ppermute | solution.py:306
  50.2 4.9 %collective-permute-done.6.refs_4_.refs_5_ = bf16[1280,128]{1,0:T(8,128)(2,1)S(1)} collective-permute-done((bf16[1280,128]{1,0:T(8,128)(2,1)S(1)}, bf16[1280,128]{1,0:T(8,128)(2,1)S(1)}, u32[]{:S(2)}, u32[]{:S(2)}) %collective-permute-start.6) | collective-permute-done | bytes 327712 | tf_op jit(solution)/shard_map/ppermute | solution.py:306
  60.5 3.8 %collective-permute-done.7.refs_4_ = bf16[1280,128]{1,0:T(8,128)(2,1)S(1)} collective-permute-done((bf16[1280,128]{1,0:T(8,128)(2,1)S(1)}, bf16[1280,128]{1,0:T(8,128)(2,1)S(1)}, u32[]{:S(2)}, u32[]{:S(2)}) %collective-permute-start.7) | collective-permute-done | bytes 327712 | tf_op jit(solution)/shard_map/ppermute | solution.py:306
  68.0 2.8 %shard_map.112 = (f32[512,256]{1,0:T(8,128)S(1)}, f32[512,256]{1,0:T(8,128)S(1)}, f32[16,512]{1,0:T(8,128)S(1)}, f32[16,512]{1,0:T(8,128)S(1)}) custom-call(bf16[512,2048]{1,0:T(8,128)(2,1)S(1)} %get-tuple-element.79.normed, bf16[2048,256]{1,0:T(8,128)(2,1)S(1)} %copy-done.2, bf16[128,2048]{1,0:T(8,128)(2,1)S(1)} %pad.17.dt_weight, ...), custom_call_target="tpu_custom_call" | custom-call | flops 805306368 | bytes 4796416 | tf_op jit(solution)/shard_map/pallas_call | solution.py:268
  70.8 2.2 %shard_map.113 = (f32[512,256]{1,0:T(8,128)S(1)}, bf16[8,144,128]{2,1,0:T(8,128)(2,1)S(1)}) custom-call(s32[5]{0:T(128)S(1)} %stack.23.place, bf16[512,2048]{1,0:T(8,128)(2,1)S(1)} %get-tuple-element.79.normed, f32[512,256]{1,0:T(8,128)S(1)} %get-tuple-element.81.tailed, bf16[2048,128]{1,0:T(8,128)(2,1)S(1)} %get-tuple-element.82.bc_mine, ...), custom_call_target="tpu_custom_call" | custom-call | flops 536870912 | bytes 4522004 | tf_op jit(solution)/shard_map/pallas_call | solution.py:268
  73.0 12.1 %all_to_all.5.gathered = bf16[8,144,128]{2,1,0:T(8,128)(2,1)S(1)} all-to-all(bf16[8,144,128]{2,1,0:T(8,128)(2,1)S(1)} %get-tuple-element.86), channel_id=1, replica_groups={{0,16,32,48,64,80,96,112},{128,144,160,176,192,208,224,240},{256,272,28..., dimensions={0} | all-to-all | bytes 589824 | tf_op jit(solution)/shard_map/all_to_all | solution.py:401
  86.5 6.4 %collective-permute-start.10 = (bf16[144,128]{1,0:T(8,128)(2,1)S(1)}, bf16[144,128]{1,0:T(8,128)(2,1)S(1)}, u32[]{:S(2)}, u32[]{:S(2)}) collective-permute-start(bf16[144,128]{1,0:T(8,128)(2,1)S(1)} %get-tuple-element.93), channel_id=1, source_target_pairs={{0,256},{16,272},{32,288},{48,304},{64,320},{80,336},{96,352},{112... | collective-permute-start | bytes 110600 | tf_op jit(solution)/shard_map/ppermute | solution.py:298
  103.6 2.8 %collective-permute-start.13 = (bf16[1024,128]{1,0:T(8,128)(2,1)S(1)}, bf16[1024,128]{1,0:T(8,128)(2,1)S(1)}, u32[]{:S(2)}, u32[]{:S(2)}) collective-permute-start(bf16[1024,128]{1,0:T(8,128)(2,1)S(1)} %get-tuple-element.101), channel_id=1, source_target_pairs={{0,7},{1,2},{2,1},{3,4},{4,3},{5,6},{6,5},{7,0},{8,15},{9,10},{10,... | collective-permute-start | bytes 786440 | tf_op jit(solution)/shard_map/ppermute | solution.py:306
  106.3 4.3 %collective-permute-start.17 = (bf16[1024,128]{1,0:T(8,128)(2,1)S(1)}, bf16[1024,128]{1,0:T(8,128)(2,1)S(1)}, u32[]{:S(2)}, u32[]{:S(2)}) collective-permute-start(bf16[1024,128]{1,0:T(8,128)(2,1)S(1)} %get-tuple-element.104), channel_id=1, source_target_pairs={{0,7},{1,2},{2,1},{3,4},{4,3},{5,6},{6,5},{7,0},{8,15},{9,10},{10,... | collective-permute-start | bytes 786440 | tf_op jit(solution)/shard_map/ppermute | solution.py:306
  112.2 3.6 %collective-permute-done.13 = bf16[1024,128]{1,0:T(8,128)(2,1)S(1)} collective-permute-done((bf16[1024,128]{1,0:T(8,128)(2,1)S(1)}, bf16[1024,128]{1,0:T(8,128)(2,1)S(1)}, u32[]{:S(2)}, u32[]{:S(2)}) %collective-permute-start.13) | collective-permute-done | bytes 262176 | tf_op jit(solution)/shard_map/ppermute | solution.py:306
  117.8 2.8 %collective-permute-done.17 = bf16[1024,128]{1,0:T(8,128)(2,1)S(1)} collective-permute-done((bf16[1024,128]{1,0:T(8,128)(2,1)S(1)}, bf16[1024,128]{1,0:T(8,128)(2,1)S(1)}, u32[]{:S(2)}, u32[]{:S(2)}) %collective-permute-start.17) | collective-permute-done | bytes 262176 | tf_op jit(solution)/shard_map/ppermute | solution.py:306
  124.6 2.8 %collective-permute-start.15 = (bf16[1024,128]{1,0:T(8,128)(2,1)S(1)}, bf16[1024,128]{1,0:T(8,128)(2,1)S(1)}, u32[]{:S(2)}, u32[]{:S(2)}) collective-permute-start(bf16[1024,128]{1,0:T(8,128)(2,1)S(1)} %add_convert_fusion.3), channel_id=1, source_target_pairs={{0,7},{1,2},{2,1},{3,4},{4,3},{5,6},{6,5},{7,0},{8,15},{9,10},{10,... | collective-permute-start | bytes 786440 | tf_op jit(solution)/shard_map/ppermute | solution.py:306
  127.4 2.9 %collective-permute-done.18 = bf16[1024,128]{1,0:T(8,128)(2,1)S(1)} collective-permute-done((bf16[1024,128]{1,0:T(8,128)(2,1)S(1)}, bf16[1024,128]{1,0:T(8,128)(2,1)S(1)}, u32[]{:S(2)}, u32[]{:S(2)}) %collective-permute-start.18) | collective-permute-done | bytes 262176 | tf_op jit(solution)/shard_map/ppermute | solution.py:306
  130.4 2.8 %collective-permute-start.19 = (bf16[1024,128]{1,0:T(8,128)(2,1)S(1)}, bf16[1024,128]{1,0:T(8,128)(2,1)S(1)}, u32[]{:S(2)}, u32[]{:S(2)}) collective-permute-start(bf16[1024,128]{1,0:T(8,128)(2,1)S(1)} %add_convert_fusion), channel_id=1, source_target_pairs={{0,7},{1,2},{2,1},{3,4},{4,3},{5,6},{6,5},{7,0},{8,15},{9,10},{10,... | collective-permute-start | bytes 786440 | tf_op jit(solution)/shard_map/ppermute | solution.py:306
  136.2 3.9 %collective-permute-done.19 = bf16[1024,128]{1,0:T(8,128)(2,1)S(1)} collective-permute-done((bf16[1024,128]{1,0:T(8,128)(2,1)S(1)}, bf16[1024,128]{1,0:T(8,128)(2,1)S(1)}, u32[]{:S(2)}, u32[]{:S(2)}) %collective-permute-start.19) | collective-permute-done | bytes 262176 | tf_op jit(solution)/shard_map/ppermute | solution.py:306
  140.1 2.3 %collective-permute-done.16 = bf16[1024,128]{1,0:T(8,128)(2,1)S(1)} collective-permute-done((bf16[1024,128]{1,0:T(8,128)(2,1)S(1)}, bf16[1024,128]{1,0:T(8,128)(2,1)S(1)}, u32[]{:S(2)}, u32[]{:S(2)}) %collective-permute-start.16) | collective-permute-done | bytes 262176 | tf_op jit(solution)/shard_map/ppermute | solution.py:306
  142.6 6.6 %collective-permute-start.20 = (bf16[512,128]{1,0:T(8,128)(2,1)S(1)}, bf16[512,128]{1,0:T(8,128)(2,1)S(1)}, u32[]{:S(2)}, u32[]{:S(2)}) collective-permute-start(bf16[512,128]{1,0:T(8,128)(2,1)S(1)} %slice.86), channel_id=1, source_target_pairs={{0,8},{1,9},{2,10},{3,11},{4,12},{5,13},{6,14},{7,15},{8,0},{9,1},... | collective-permute-start | bytes 393224 | tf_op jit(solution)/shard_map/ppermute | solution.py:289
  149.2 4.7 %collective-permute-done.20 = bf16[512,128]{1,0:T(8,128)(2,1)S(1)} collective-permute-done((bf16[512,128]{1,0:T(8,128)(2,1)S(1)}, bf16[512,128]{1,0:T(8,128)(2,1)S(1)}, u32[]{:S(2)}, u32[]{:S(2)}) %collective-permute-start.20) | collective-permute-done | bytes 131104 | tf_op jit(solution)/shard_map/ppermute | solution.py:289
  (59 shorter events, 42.5 us)
Async XLA Ops:
  1.8 14.5 %collective-permute-start = (bf16[640,128]{1,0:T(8,128)(2,1)S(1)}, bf16[640,128]{1,0:T(8,128)(2,1)S(1)}, u32[]{:S(2)}, u32[]{:S(2)}) collective-permute-start(bf16[640,128]{1,0:T(8,128)(2,1)S(1)} %pad_maximum_fusion.one), channel_id=1, source_target_pairs={{0,8},{1,9},{2,10},{3,11},{4,12},{5,13},{6,14},{7,15},{8,0},{9,1},... | collective-permute-start | bytes 491528 | tf_op jit(solution)/shard_map/ppermute | solution.py:289
  16.2 17.5 %collective-permute-start.2 = (bf16[1280,128]{1,0:T(8,128)(2,1)S(1)}, bf16[1280,128]{1,0:T(8,128)(2,1)S(1)}, u32[]{:S(2)}, u32[]{:S(2)}) collective-permute-start(bf16[1280,128]{1,0:T(8,128)(2,1)S(1)} %shard_map.109.refs_0_), channel_id=1, source_target_pairs={{0,7},{1,2},{2,1},{3,4},{4,3},{5,6},{6,5},{7,0},{8,15},{9,10},{10,... | collective-permute-start | bytes 983048 | tf_op jit(solution)/shard_map/ppermute | solution.py:306
  27.2 10.7 %collective-permute-start.1 = (bf16[1280,128]{1,0:T(8,128)(2,1)S(1)}, bf16[1280,128]{1,0:T(8,128)(2,1)S(1)}, u32[]{:S(2)}, u32[]{:S(2)}) collective-permute-start(bf16[1280,128]{1,0:T(8,128)(2,1)S(1)} %shard_map.109.refs_0_), channel_id=1, source_target_pairs={{0,1},{1,0},{2,3},{3,2},{4,5},{5,4},{6,7},{7,6},{8,9},{9,8},{10,11... | collective-permute-start | bytes 983048 | tf_op jit(solution)/shard_map/ppermute | solution.py:306
  33.8 10.4 %collective-permute-start.3 = (bf16[1280,128]{1,0:T(8,128)(2,1)S(1)}, bf16[1280,128]{1,0:T(8,128)(2,1)S(1)}, u32[]{:S(2)}, u32[]{:S(2)}) collective-permute-start(bf16[1280,128]{1,0:T(8,128)(2,1)S(1)} %collective-permute-done.2.refs_6_.refs_7_), channel_id=1, source_target_pairs={{0,1},{1,0},{2,3},{3,2},{4,5},{5,4},{6,7},{7,6},{8,9},{9,8},{10,11... | collective-permute-start | bytes 983048 | tf_op jit(solution)/shard_map/ppermute | solution.py:306
  37.9 10.4 %collective-permute-start.4 = (bf16[1280,128]{1,0:T(8,128)(2,1)S(1)}, bf16[1280,128]{1,0:T(8,128)(2,1)S(1)}, u32[]{:S(2)}, u32[]{:S(2)}) collective-permute-start(bf16[1280,128]{1,0:T(8,128)(2,1)S(1)} %collective-permute-done.1.refs_1_), channel_id=1, source_target_pairs={{0,7},{1,2},{2,1},{3,4},{4,3},{5,6},{6,5},{7,0},{8,15},{9,10},{10,... | collective-permute-start | bytes 983048 | tf_op jit(solution)/shard_map/ppermute | solution.py:306
  44.1 10.9 %collective-permute-start.6 = (bf16[1280,128]{1,0:T(8,128)(2,1)S(1)}, bf16[1280,128]{1,0:T(8,128)(2,1)S(1)}, u32[]{:S(2)}, u32[]{:S(2)}) collective-permute-start(bf16[1280,128]{1,0:T(8,128)(2,1)S(1)} %collective-permute-done.3.refs_2_), channel_id=1, source_target_pairs={{0,7},{1,2},{2,1},{3,4},{4,3},{5,6},{6,5},{7,0},{8,15},{9,10},{10,... | collective-permute-start | bytes 983048 | tf_op jit(solution)/shard_map/ppermute | solution.py:306
  48.3 11.8 %collective-permute-start.5 = (bf16[1280,128]{1,0:T(8,128)(2,1)S(1)}, bf16[1280,128]{1,0:T(8,128)(2,1)S(1)}, u32[]{:S(2)}, u32[]{:S(2)}) collective-permute-start(bf16[1280,128]{1,0:T(8,128)(2,1)S(1)} %collective-permute-done.4.refs_5_.refs_6_), channel_id=1, source_target_pairs={{0,1},{1,0},{2,3},{3,2},{4,5},{5,4},{6,7},{7,6},{8,9},{9,8},{10,11... | collective-permute-start | bytes 983048 | tf_op jit(solution)/shard_map/ppermute | solution.py:306
  55.1 9.1 %collective-permute-start.7 = (bf16[1280,128]{1,0:T(8,128)(2,1)S(1)}, bf16[1280,128]{1,0:T(8,128)(2,1)S(1)}, u32[]{:S(2)}, u32[]{:S(2)}) collective-permute-start(bf16[1280,128]{1,0:T(8,128)(2,1)S(1)} %collective-permute-done.6.refs_4_.refs_5_), channel_id=1, source_target_pairs={{0,1},{1,0},{2,3},{3,2},{4,5},{5,4},{6,7},{7,6},{8,9},{9,8},{10,11... | collective-permute-start | bytes 983048 | tf_op jit(solution)/shard_map/ppermute | solution.py:306
  60.0 7.9 %copy-start.6 = (bf16[2048,4]{0,1:T(4,128)(2,1)S(1)}, bf16[2048,4]{0,1:T(4,128)(2,1)}, u32[]{:S(2)}) copy-start(bf16[2048,4]{0,1:T(4,128)(2,1)} %param.23) | copy-start | bytes 49156
  66.0 4.8 %collective-permute-start.8 = (bf16[2048,128]{1,0:T(8,128)(2,1)S(1)}, bf16[2048,128]{1,0:T(8,128)(2,1)S(1)}, u32[]{:S(2)}, u32[]{:S(2)}) collective-permute-start(bf16[2048,128]{1,0:T(8,128)(2,1)S(1)} %get-tuple-element.82.bc_mine), channel_id=1, source_target_pairs={{0,16},{16,0},{32,48},{48,32},{64,80},{80,64},{96,112},{112,96},{1... | collective-permute-start | bytes 1572872 | tf_op jit(solution)/shard_map/ppermute | solution.py:293
  70.8 24.0 %copy-start.4 = (bf16[2048,256]{1,0:T(8,128)(2,1)S(1)}, bf16[2048,256]{1,0:T(8,128)(2,1)}, u32[]{:S(2)}) copy-start(bf16[2048,256]{1,0:T(8,128)(2,1)} %gate_weight.1) | copy-start | bytes 3145732
  85.8 11.0 %collective-permute-start.11 = (bf16[144,128]{1,0:T(8,128)(2,1)S(1)}, bf16[144,128]{1,0:T(8,128)(2,1)S(1)}, u32[]{:S(2)}, u32[]{:S(2)}) collective-permute-start(bf16[144,128]{1,0:T(8,128)(2,1)S(1)} %get-tuple-element.93), channel_id=1, source_target_pairs={{0,384},{16,400},{32,416},{48,432},{64,448},{80,464},{96,480},{112... | collective-permute-start | bytes 110600 | tf_op jit(solution)/shard_map/ppermute | solution.py:298
  86.5 10.4 %collective-permute-start.10 = (bf16[144,128]{1,0:T(8,128)(2,1)S(1)}, bf16[144,128]{1,0:T(8,128)(2,1)S(1)}, u32[]{:S(2)}, u32[]{:S(2)}) collective-permute-start(bf16[144,128]{1,0:T(8,128)(2,1)S(1)} %get-tuple-element.93), channel_id=1, source_target_pairs={{0,256},{16,272},{32,288},{48,304},{64,320},{80,336},{96,352},{112... | collective-permute-start | bytes 110600 | tf_op jit(solution)/shard_map/ppermute | solution.py:298
  92.9 5.9 %collective-permute-start.9 = (bf16[144,128]{1,0:T(8,128)(2,1)S(1)}, bf16[144,128]{1,0:T(8,128)(2,1)S(1)}, u32[]{:S(2)}, u32[]{:S(2)}) collective-permute-start(bf16[144,128]{1,0:T(8,128)(2,1)S(1)} %get-tuple-element.93), channel_id=1, source_target_pairs={{0,128},{16,144},{32,160},{48,176},{64,192},{80,208},{96,224},{112... | collective-permute-start | bytes 110600 | tf_op jit(solution)/shard_map/ppermute | solution.py:298
  98.8 3.1 %collective-permute-start.12 = (bf16[128,128]{1,0:T(8,128)(2,1)S(1)}, bf16[128,128]{1,0:T(8,128)(2,1)S(1)}, u32[]{:S(2)}, u32[]{:S(2)}) collective-permute-start(bf16[128,128]{1,0:T(8,128)(2,1)S(1)} %get-tuple-element.95), channel_id=1, source_target_pairs={{0,16},{16,0},{32,48},{48,32},{64,80},{80,64},{96,112},{112,96},{1... | collective-permute-start | bytes 98312 | tf_op jit(solution)/shard_map/ppermute | solution.py:293
  103.6 12.3 %collective-permute-start.13 = (bf16[1024,128]{1,0:T(8,128)(2,1)S(1)}, bf16[1024,128]{1,0:T(8,128)(2,1)S(1)}, u32[]{:S(2)}, u32[]{:S(2)}) collective-permute-start(bf16[1024,128]{1,0:T(8,128)(2,1)S(1)} %get-tuple-element.101), channel_id=1, source_target_pairs={{0,7},{1,2},{2,1},{3,4},{4,3},{5,6},{6,5},{7,0},{8,15},{9,10},{10,... | collective-permute-start | bytes 786440 | tf_op jit(solution)/shard_map/ppermute | solution.py:306
  106.3 14.3 %collective-permute-start.17 = (bf16[1024,128]{1,0:T(8,128)(2,1)S(1)}, bf16[1024,128]{1,0:T(8,128)(2,1)S(1)}, u32[]{:S(2)}, u32[]{:S(2)}) collective-permute-start(bf16[1024,128]{1,0:T(8,128)(2,1)S(1)} %get-tuple-element.104), channel_id=1, source_target_pairs={{0,7},{1,2},{2,1},{3,4},{4,3},{5,6},{6,5},{7,0},{8,15},{9,10},{10,... | collective-permute-start | bytes 786440 | tf_op jit(solution)/shard_map/ppermute | solution.py:306
  115.9 8.7 %collective-permute-start.14 = (bf16[1024,128]{1,0:T(8,128)(2,1)S(1)}, bf16[1024,128]{1,0:T(8,128)(2,1)S(1)}, u32[]{:S(2)}, u32[]{:S(2)}) collective-permute-start(bf16[1024,128]{1,0:T(8,128)(2,1)S(1)} %add_convert_fusion.4), channel_id=1, source_target_pairs={{0,1},{1,0},{2,3},{3,2},{4,5},{5,4},{6,7},{7,6},{8,9},{9,8},{10,11... | collective-permute-start | bytes 786440 | tf_op jit(solution)/shard_map/ppermute | solution.py:306
  120.7 33.2 %copy-start.5 = (bf16[512,128]{1,0:T(8,128)(2,1)S(1)}, bf16[512,128]{1,0:T(8,128)(2,1)}, u32[]{:S(2)}) copy-start(bf16[512,128]{1,0:T(8,128)(2,1)} %param.19) | copy-start | bytes 393220
  120.7 9.6 %collective-permute-start.18 = (bf16[1024,128]{1,0:T(8,128)(2,1)S(1)}, bf16[1024,128]{1,0:T(8,128)(2,1)S(1)}, u32[]{:S(2)}, u32[]{:S(2)}) collective-permute-start(bf16[1024,128]{1,0:T(8,128)(2,1)S(1)} %add_convert_fusion.1), channel_id=1, source_target_pairs={{0,1},{1,0},{2,3},{3,2},{4,5},{5,4},{6,7},{7,6},{8,9},{9,8},{10,11... | collective-permute-start | bytes 786440 | tf_op jit(solution)/shard_map/ppermute | solution.py:306
  124.6 9.5 %collective-permute-start.15 = (bf16[1024,128]{1,0:T(8,128)(2,1)S(1)}, bf16[1024,128]{1,0:T(8,128)(2,1)S(1)}, u32[]{:S(2)}, u32[]{:S(2)}) collective-permute-start(bf16[1024,128]{1,0:T(8,128)(2,1)S(1)} %add_convert_fusion.3), channel_id=1, source_target_pairs={{0,7},{1,2},{2,1},{3,4},{4,3},{5,6},{6,5},{7,0},{8,15},{9,10},{10,... | collective-permute-start | bytes 786440 | tf_op jit(solution)/shard_map/ppermute | solution.py:306
  130.4 9.7 %collective-permute-start.19 = (bf16[1024,128]{1,0:T(8,128)(2,1)S(1)}, bf16[1024,128]{1,0:T(8,128)(2,1)S(1)}, u32[]{:S(2)}, u32[]{:S(2)}) collective-permute-start(bf16[1024,128]{1,0:T(8,128)(2,1)S(1)} %add_convert_fusion), channel_id=1, source_target_pairs={{0,7},{1,2},{2,1},{3,4},{4,3},{5,6},{6,5},{7,0},{8,15},{9,10},{10,... | collective-permute-start | bytes 786440 | tf_op jit(solution)/shard_map/ppermute | solution.py:306
  134.2 8.3 %collective-permute-start.16 = (bf16[1024,128]{1,0:T(8,128)(2,1)S(1)}, bf16[1024,128]{1,0:T(8,128)(2,1)S(1)}, u32[]{:S(2)}, u32[]{:S(2)}) collective-permute-start(bf16[1024,128]{1,0:T(8,128)(2,1)S(1)} %add_convert_fusion.2), channel_id=1, source_target_pairs={{0,1},{1,0},{2,3},{3,2},{4,5},{5,4},{6,7},{7,6},{8,9},{9,8},{10,11... | collective-permute-start | bytes 786440 | tf_op jit(solution)/shard_map/ppermute | solution.py:306
  142.6 11.4 %collective-permute-start.20 = (bf16[512,128]{1,0:T(8,128)(2,1)S(1)}, bf16[512,128]{1,0:T(8,128)(2,1)S(1)}, u32[]{:S(2)}, u32[]{:S(2)}) collective-permute-start(bf16[512,128]{1,0:T(8,128)(2,1)S(1)} %slice.86), channel_id=1, source_target_pairs={{0,8},{1,9},{2,10},{3,11},{4,12},{5,13},{6,14},{7,15},{8,0},{9,1},... | collective-permute-start | bytes 393224 | tf_op jit(solution)/shard_map/ppermute | solution.py:289
  (4 other events, 22.5 us)

commit v11 on v8

--- a/solution.py
+++ b/solution.py
@@ -415,7 +415,7 @@
         [enter_own, enter_pair, logs, done, *above],
     )
     rest = to_core(send)
-    soon, later = (far, far + 1), tuple(k for k in range(RING) if k // 2 != RING // 4)
+    soon, later = (far, far - 1), tuple(k for k in range(RING) if k not in (far, far - 1))
     ynorm, *early = on_chip(
         functools.partial(finish_kernel, size_p, soon),
         [shape((rows, width), bf16)] + [shape((SIDE * rows, own), bf16)] * len(soon),

time: 155 us -> 155 us (level)
  no operation moved by 1% of the time
where the time goes in v11:
time: 155 us
  starting transfers between devices  69.7 us (45%)
  waiting for transfers between devices  53.4 us (34%)
  Pallas kernels  13.1 us (8%)
  blocking collectives  12.1 us (8%)
  local copies, waits for them, and re-layouts  3.92 us (3%)
  other arithmetic  2.1 us (1%)
    ppermute x14, starting transfers between devices, swap_turn(): return lax.ppermute(block, 'head', route)  43.4 us
    ppermute x14, waiting for transfers between devices, swap_turn(): return lax.ppermute(block, 'head', route)  38 us
    ppermute x2, starting transfers between devices, to_side(): lax.ppermute(block, 'head', [(i, (i + RING) % (SIDE * RING)) for i in ran...  13.5 us
    pallas_call x10, Pallas kernels, on_chip(): pl.pallas_call(kernel, out_shape=outs, in_specs=specs, out_specs=[pl.Bloc...  13.1 us
    ppermute x2, waiting for transfers between devices, to_side(): lax.ppermute(block, 'head', [(i, (i + RING) % (SIDE * RING)) for i in ran...  12.3 us
    all_to_all x1, blocking collectives, local(): lax.all_to_all(slots, 'section', 0, 0, axis_index_groups=by_row)  12.1 us
    ppermute x3, starting transfers between devices, to_row(): lax.ppermute(block, 'section', [(i, i + ahead) for i in range(sections -...  8.98 us
    ppermute x2, starting transfers between devices, to_core(): lax.ppermute(block, 'section', [(i, i ^ 1) for i in range(lax.axis_size('...  3.84 us
  transfers between devices with their start and end apart: 21, of which 17 were waited for; matrix products, arithmetic and copies ran while one was open for 2% of the time, Pallas kernels for 4%

profile of v11, /device:TPU:8, one launch (start us, length us, event | category | flops | bytes accessed | tf_op | source)
XLA Modules:
  0.0 154.7 jit_solution(2918951100199806286)
XLA Ops:
  1.8 6.8 %collective-permute-start = (bf16[640,128]{1,0:T(8,128)(2,1)S(1)}, bf16[640,128]{1,0:T(8,128)(2,1)S(1)}, u32[]{:S(2)}, u32[]{:S(2)}) collective-permute-start(bf16[640,128]{1,0:T(8,128)(2,1)S(1)} %pad_maximum_fusion.one), channel_id=1, source_target_pairs={{0,8},{1,9},{2,10},{3,11},{4,12},{5,13},{6,14},{7,15},{8,0},{9,1},... | collective-permute-start | bytes 491528 | tf_op jit(solution)/shard_map/ppermute | solution.py:289
  8.6 7.6 %collective-permute-done.two = bf16[640,128]{1,0:T(8,128)(2,1)S(1)} collective-permute-done((bf16[640,128]{1,0:T(8,128)(2,1)S(1)}, bf16[640,128]{1,0:T(8,128)(2,1)S(1)}, u32[]{:S(2)}, u32[]{:S(2)}) %collective-permute-start) | collective-permute-done | bytes 163872 | tf_op jit(solution)/shard_map/ppermute | solution.py:289
  16.2 10.9 %collective-permute-start.2 = (bf16[1280,128]{1,0:T(8,128)(2,1)S(1)}, bf16[1280,128]{1,0:T(8,128)(2,1)S(1)}, u32[]{:S(2)}, u32[]{:S(2)}) collective-permute-start(bf16[1280,128]{1,0:T(8,128)(2,1)S(1)} %shard_map.109.refs_0_), channel_id=1, source_target_pairs={{0,7},{1,2},{2,1},{3,4},{4,3},{5,6},{6,5},{7,0},{8,15},{9,10},{10,... | collective-permute-start | bytes 983048 | tf_op jit(solution)/shard_map/ppermute | solution.py:306
  29.1 4.6 %collective-permute-done.2.refs_6_.refs_7_ = bf16[1280,128]{1,0:T(8,128)(2,1)S(1)} collective-permute-done((bf16[1280,128]{1,0:T(8,128)(2,1)S(1)}, bf16[1280,128]{1,0:T(8,128)(2,1)S(1)}, u32[]{:S(2)}, u32[]{:S(2)}) %collective-permute-start.2) | collective-permute-done | bytes 327712 | tf_op jit(solution)/shard_map/ppermute | solution.py:306
  35.7 2.2 %collective-permute-done.1.refs_1_ = bf16[1280,128]{1,0:T(8,128)(2,1)S(1)} collective-permute-done((bf16[1280,128]{1,0:T(8,128)(2,1)S(1)}, bf16[1280,128]{1,0:T(8,128)(2,1)S(1)}, u32[]{:S(2)}, u32[]{:S(2)}) %collective-permute-start.1) | collective-permute-done | bytes 327712 | tf_op jit(solution)/shard_map/ppermute | solution.py:306
  37.9 2.6 %collective-permute-start.4 = (bf16[1280,128]{1,0:T(8,128)(2,1)S(1)}, bf16[1280,128]{1,0:T(8,128)(2,1)S(1)}, u32[]{:S(2)}, u32[]{:S(2)}) collective-permute-start(bf16[1280,128]{1,0:T(8,128)(2,1)S(1)} %collective-permute-done.1.refs_1_), channel_id=1, source_target_pairs={{0,7},{1,2},{2,1},{3,4},{4,3},{5,6},{6,5},{7,0},{8,15},{9,10},{10,... | collective-permute-start | bytes 983048 | tf_op jit(solution)/shard_map/ppermute | solution.py:306
  40.5 3.6 %collective-permute-done.3.refs_2_ = bf16[1280,128]{1,0:T(8,128)(2,1)S(1)} collective-permute-done((bf16[1280,128]{1,0:T(8,128)(2,1)S(1)}, bf16[1280,128]{1,0:T(8,128)(2,1)S(1)}, u32[]{:S(2)}, u32[]{:S(2)}) %collective-permute-start.3) | collective-permute-done | bytes 327712 | tf_op jit(solution)/shard_map/ppermute | solution.py:306
  44.1 3.7 %collective-permute-start.6 = (bf16[1280,128]{1,0:T(8,128)(2,1)S(1)}, bf16[1280,128]{1,0:T(8,128)(2,1)S(1)}, u32[]{:S(2)}, u32[]{:S(2)}) collective-permute-start(bf16[1280,128]{1,0:T(8,128)(2,1)S(1)} %collective-permute-done.3.refs_2_), channel_id=1, source_target_pairs={{0,7},{1,2},{2,1},{3,4},{4,3},{5,6},{6,5},{7,0},{8,15},{9,10},{10,... | collective-permute-start | bytes 983048 | tf_op jit(solution)/shard_map/ppermute | solution.py:306
  50.2 4.9 %collective-permute-done.6.refs_4_.refs_5_ = bf16[1280,128]{1,0:T(8,128)(2,1)S(1)} collective-permute-done((bf16[1280,128]{1,0:T(8,128)(2,1)S(1)}, bf16[1280,128]{1,0:T(8,128)(2,1)S(1)}, u32[]{:S(2)}, u32[]{:S(2)}) %collective-permute-start.6) | collective-permute-done | bytes 327712 | tf_op jit(solution)/shard_map/ppermute | solution.py:306
  60.5 3.8 %collective-permute-done.7.refs_4_ = bf16[1280,128]{1,0:T(8,128)(2,1)S(1)} collective-permute-done((bf16[1280,128]{1,0:T(8,128)(2,1)S(1)}, bf16[1280,128]{1,0:T(8,128)(2,1)S(1)}, u32[]{:S(2)}, u32[]{:S(2)}) %collective-permute-start.7) | collective-permute-done | bytes 327712 | tf_op jit(solution)/shard_map/ppermute | solution.py:306
  68.0 2.8 %shard_map.112 = (f32[512,256]{1,0:T(8,128)S(1)}, f32[512,256]{1,0:T(8,128)S(1)}, f32[16,512]{1,0:T(8,128)S(1)}, f32[16,512]{1,0:T(8,128)S(1)}) custom-call(bf16[512,2048]{1,0:T(8,128)(2,1)S(1)} %get-tuple-element.79.normed, bf16[2048,256]{1,0:T(8,128)(2,1)S(1)} %copy-done.2, bf16[128,2048]{1,0:T(8,128)(2,1)S(1)} %pad.17.dt_weight, ...), custom_call_target="tpu_custom_call" | custom-call | flops 805306368 | bytes 4796416 | tf_op jit(solution)/shard_map/pallas_call | solution.py:268
  70.8 2.2 %shard_map.113 = (f32[512,256]{1,0:T(8,128)S(1)}, bf16[8,144,128]{2,1,0:T(8,128)(2,1)S(1)}) custom-call(s32[5]{0:T(128)S(1)} %stack.23.place, bf16[512,2048]{1,0:T(8,128)(2,1)S(1)} %get-tuple-element.79.normed, f32[512,256]{1,0:T(8,128)S(1)} %get-tuple-element.81.tailed, bf16[2048,128]{1,0:T(8,128)(2,1)S(1)} %get-tuple-element.82.bc_mine, ...), custom_call_target="tpu_custom_call" | custom-call | flops 536870912 | bytes 4522004 | tf_op jit(solution)/shard_map/pallas_call | solution.py:268
  73.0 12.1 %all_to_all.5.gathered = bf16[8,144,128]{2,1,0:T(8,128)(2,1)S(1)} all-to-all(bf16[8,144,128]{2,1,0:T(8,128)(2,1)S(1)} %get-tuple-element.86), channel_id=1, replica_groups={{0,16,32,48,64,80,96,112},{128,144,160,176,192,208,224,240},{256,272,28..., dimensions={0} | all-to-all | bytes 589824 | tf_op jit(solution)/shard_map/all_to_all | solution.py:401
  86.5 6.4 %collective-permute-start.10 = (bf16[144,128]{1,0:T(8,128)(2,1)S(1)}, bf16[144,128]{1,0:T(8,128)(2,1)S(1)}, u32[]{:S(2)}, u32[]{:S(2)}) collective-permute-start(bf16[144,128]{1,0:T(8,128)(2,1)S(1)} %get-tuple-element.93), channel_id=1, source_target_pairs={{0,256},{16,272},{32,288},{48,304},{64,320},{80,336},{96,352},{112... | collective-permute-start | bytes 110600 | tf_op jit(solution)/shard_map/ppermute | solution.py:298
  105.8 3.6 %collective-permute-start.17 = (bf16[1024,128]{1,0:T(8,128)(2,1)S(1)}, bf16[1024,128]{1,0:T(8,128)(2,1)S(1)}, u32[]{:S(2)}, u32[]{:S(2)}) collective-permute-start(bf16[1024,128]{1,0:T(8,128)(2,1)S(1)} %get-tuple-element.104), channel_id=1, source_target_pairs={{0,1},{1,0},{2,3},{3,2},{4,5},{5,4},{6,7},{7,6},{8,9},{9,8},{10,11... | collective-permute-start | bytes 786440 | tf_op jit(solution)/shard_map/ppermute | solution.py:306
  111.0 3.6 %collective-permute-done.13 = bf16[1024,128]{1,0:T(8,128)(2,1)S(1)} collective-permute-done((bf16[1024,128]{1,0:T(8,128)(2,1)S(1)}, bf16[1024,128]{1,0:T(8,128)(2,1)S(1)}, u32[]{:S(2)}, u32[]{:S(2)}) %collective-permute-start.13) | collective-permute-done | bytes 262176 | tf_op jit(solution)/shard_map/ppermute | solution.py:306
  114.7 2.8 %collective-permute-start.14 = (bf16[1024,128]{1,0:T(8,128)(2,1)S(1)}, bf16[1024,128]{1,0:T(8,128)(2,1)S(1)}, u32[]{:S(2)}, u32[]{:S(2)}) collective-permute-start(bf16[1024,128]{1,0:T(8,128)(2,1)S(1)} %add_convert_fusion.4), channel_id=1, source_target_pairs={{0,7},{1,2},{2,1},{3,4},{4,3},{5,6},{6,5},{7,0},{8,15},{9,10},{10,... | collective-permute-start | bytes 786440 | tf_op jit(solution)/shard_map/ppermute | solution.py:306
  119.5 2.9 %collective-permute-start.18 = (bf16[1024,128]{1,0:T(8,128)(2,1)S(1)}, bf16[1024,128]{1,0:T(8,128)(2,1)S(1)}, u32[]{:S(2)}, u32[]{:S(2)}) collective-permute-start(bf16[1024,128]{1,0:T(8,128)(2,1)S(1)} %add_convert_fusion.1), channel_id=1, source_target_pairs={{0,7},{1,2},{2,1},{3,4},{4,3},{5,6},{6,5},{7,0},{8,15},{9,10},{10,... | collective-permute-start | bytes 786440 | tf_op jit(solution)/shard_map/ppermute | solution.py:306
  126.6 3.8 %collective-permute-done.18 = bf16[1024,128]{1,0:T(8,128)(2,1)S(1)} collective-permute-done((bf16[1024,128]{1,0:T(8,128)(2,1)S(1)}, bf16[1024,128]{1,0:T(8,128)(2,1)S(1)}, u32[]{:S(2)}, u32[]{:S(2)}) %collective-permute-start.18) | collective-permute-done | bytes 262176 | tf_op jit(solution)/shard_map/ppermute | solution.py:306
  133.0 3.1 %collective-permute-start.16 = (bf16[1024,128]{1,0:T(8,128)(2,1)S(1)}, bf16[1024,128]{1,0:T(8,128)(2,1)S(1)}, u32[]{:S(2)}, u32[]{:S(2)}) collective-permute-start(bf16[1024,128]{1,0:T(8,128)(2,1)S(1)} %add_convert_fusion.2), channel_id=1, source_target_pairs={{0,7},{1,2},{2,1},{3,4},{4,3},{5,6},{6,5},{7,0},{8,15},{9,10},{10,... | collective-permute-start | bytes 786440 | tf_op jit(solution)/shard_map/ppermute | solution.py:306
  136.1 2.8 %collective-permute-done.19 = bf16[1024,128]{1,0:T(8,128)(2,1)S(1)} collective-permute-done((bf16[1024,128]{1,0:T(8,128)(2,1)S(1)}, bf16[1024,128]{1,0:T(8,128)(2,1)S(1)}, u32[]{:S(2)}, u32[]{:S(2)}) %collective-permute-start.19) | collective-permute-done | bytes 262176 | tf_op jit(solution)/shard_map/ppermute | solution.py:306
  138.9 3.5 %collective-permute-done.16 = bf16[1024,128]{1,0:T(8,128)(2,1)S(1)} collective-permute-done((bf16[1024,128]{1,0:T(8,128)(2,1)S(1)}, bf16[1024,128]{1,0:T(8,128)(2,1)S(1)}, u32[]{:S(2)}, u32[]{:S(2)}) %collective-permute-start.16) | collective-permute-done | bytes 262176 | tf_op jit(solution)/shard_map/ppermute | solution.py:306
  142.6 6.6 %collective-permute-start.20 = (bf16[512,128]{1,0:T(8,128)(2,1)S(1)}, bf16[512,128]{1,0:T(8,128)(2,1)S(1)}, u32[]{:S(2)}, u32[]{:S(2)}) collective-permute-start(bf16[512,128]{1,0:T(8,128)(2,1)S(1)} %slice.86), channel_id=1, source_target_pairs={{0,8},{1,9},{2,10},{3,11},{4,12},{5,13},{6,14},{7,15},{8,0},{9,1},... | collective-permute-start | bytes 393224 | tf_op jit(solution)/shard_map/ppermute | solution.py:289
  149.2 4.7 %collective-permute-done.20 = bf16[512,128]{1,0:T(8,128)(2,1)S(1)} collective-permute-done((bf16[512,128]{1,0:T(8,128)(2,1)S(1)}, bf16[512,128]{1,0:T(8,128)(2,1)S(1)}, u32[]{:S(2)}, u32[]{:S(2)}) %collective-permute-start.20) | collective-permute-done | bytes 131104 | tf_op jit(solution)/shard_map/ppermute | solution.py:289
  (59 shorter events, 42.4 us)
Async XLA Ops:
  1.8 14.5 %collective-permute-start = (bf16[640,128]{1,0:T(8,128)(2,1)S(1)}, bf16[640,128]{1,0:T(8,128)(2,1)S(1)}, u32[]{:S(2)}, u32[]{:S(2)}) collective-permute-start(bf16[640,128]{1,0:T(8,128)(2,1)S(1)} %pad_maximum_fusion.one), channel_id=1, source_target_pairs={{0,8},{1,9},{2,10},{3,11},{4,12},{5,13},{6,14},{7,15},{8,0},{9,1},... | collective-permute-start | bytes 491528 | tf_op jit(solution)/shard_map/ppermute | solution.py:289
  16.2 17.5 %collective-permute-start.2 = (bf16[1280,128]{1,0:T(8,128)(2,1)S(1)}, bf16[1280,128]{1,0:T(8,128)(2,1)S(1)}, u32[]{:S(2)}, u32[]{:S(2)}) collective-permute-start(bf16[1280,128]{1,0:T(8,128)(2,1)S(1)} %shard_map.109.refs_0_), channel_id=1, source_target_pairs={{0,7},{1,2},{2,1},{3,4},{4,3},{5,6},{6,5},{7,0},{8,15},{9,10},{10,... | collective-permute-start | bytes 983048 | tf_op jit(solution)/shard_map/ppermute | solution.py:306
  27.2 10.7 %collective-permute-start.1 = (bf16[1280,128]{1,0:T(8,128)(2,1)S(1)}, bf16[1280,128]{1,0:T(8,128)(2,1)S(1)}, u32[]{:S(2)}, u32[]{:S(2)}) collective-permute-start(bf16[1280,128]{1,0:T(8,128)(2,1)S(1)} %shard_map.109.refs_0_), channel_id=1, source_target_pairs={{0,1},{1,0},{2,3},{3,2},{4,5},{5,4},{6,7},{7,6},{8,9},{9,8},{10,11... | collective-permute-start | bytes 983048 | tf_op jit(solution)/shard_map/ppermute | solution.py:306
  33.8 10.4 %collective-permute-start.3 = (bf16[1280,128]{1,0:T(8,128)(2,1)S(1)}, bf16[1280,128]{1,0:T(8,128)(2,1)S(1)}, u32[]{:S(2)}, u32[]{:S(2)}) collective-permute-start(bf16[1280,128]{1,0:T(8,128)(2,1)S(1)} %collective-permute-done.2.refs_6_.refs_7_), channel_id=1, source_target_pairs={{0,1},{1,0},{2,3},{3,2},{4,5},{5,4},{6,7},{7,6},{8,9},{9,8},{10,11... | collective-permute-start | bytes 983048 | tf_op jit(solution)/shard_map/ppermute | solution.py:306
  37.9 10.4 %collective-permute-start.4 = (bf16[1280,128]{1,0:T(8,128)(2,1)S(1)}, bf16[1280,128]{1,0:T(8,128)(2,1)S(1)}, u32[]{:S(2)}, u32[]{:S(2)}) collective-permute-start(bf16[1280,128]{1,0:T(8,128)(2,1)S(1)} %collective-permute-done.1.refs_1_), channel_id=1, source_target_pairs={{0,7},{1,2},{2,1},{3,4},{4,3},{5,6},{6,5},{7,0},{8,15},{9,10},{10,... | collective-permute-start | bytes 983048 | tf_op jit(solution)/shard_map/ppermute | solution.py:306
  44.1 10.9 %collective-permute-start.6 = (bf16[1280,128]{1,0:T(8,128)(2,1)S(1)}, bf16[1280,128]{1,0:T(8,128)(2,1)S(1)}, u32[]{:S(2)}, u32[]{:S(2)}) collective-permute-start(bf16[1280,128]{1,0:T(8,128)(2,1)S(1)} %collective-permute-done.3.refs_2_), channel_id=1, source_target_pairs={{0,7},{1,2},{2,1},{3,4},{4,3},{5,6},{6,5},{7,0},{8,15},{9,10},{10,... | collective-permute-start | bytes 983048 | tf_op jit(solution)/shard_map/ppermute | solution.py:306
  48.3 11.8 %collective-permute-start.5 = (bf16[1280,128]{1,0:T(8,128)(2,1)S(1)}, bf16[1280,128]{1,0:T(8,128)(2,1)S(1)}, u32[]{:S(2)}, u32[]{:S(2)}) collective-permute-start(bf16[1280,128]{1,0:T(8,128)(2,1)S(1)} %collective-permute-done.4.refs_5_.refs_6_), channel_id=1, source_target_pairs={{0,1},{1,0},{2,3},{3,2},{4,5},{5,4},{6,7},{7,6},{8,9},{9,8},{10,11... | collective-permute-start | bytes 983048 | tf_op jit(solution)/shard_map/ppermute | solution.py:306
  55.1 9.1 %collective-permute-start.7 = (bf16[1280,128]{1,0:T(8,128)(2,1)S(1)}, bf16[1280,128]{1,0:T(8,128)(2,1)S(1)}, u32[]{:S(2)}, u32[]{:S(2)}) collective-permute-start(bf16[1280,128]{1,0:T(8,128)(2,1)S(1)} %collective-permute-done.6.refs_4_.refs_5_), channel_id=1, source_target_pairs={{0,1},{1,0},{2,3},{3,2},{4,5},{5,4},{6,7},{7,6},{8,9},{9,8},{10,11... | collective-permute-start | bytes 983048 | tf_op jit(solution)/shard_map/ppermute | solution.py:306
  60.0 7.9 %copy-start.6 = (bf16[2048,4]{0,1:T(4,128)(2,1)S(1)}, bf16[2048,4]{0,1:T(4,128)(2,1)}, u32[]{:S(2)}) copy-start(bf16[2048,4]{0,1:T(4,128)(2,1)} %param.23) | copy-start | bytes 49156
  66.0 4.8 %collective-permute-start.8 = (bf16[2048,128]{1,0:T(8,128)(2,1)S(1)}, bf16[2048,128]{1,0:T(8,128)(2,1)S(1)}, u32[]{:S(2)}, u32[]{:S(2)}) collective-permute-start(bf16[2048,128]{1,0:T(8,128)(2,1)S(1)} %get-tuple-element.82.bc_mine), channel_id=1, source_target_pairs={{0,16},{16,0},{32,48},{48,32},{64,80},{80,64},{96,112},{112,96},{1... | collective-permute-start | bytes 1572872 | tf_op jit(solution)/shard_map/ppermute | solution.py:293
  70.8 24.0 %copy-start.4 = (bf16[2048,256]{1,0:T(8,128)(2,1)S(1)}, bf16[2048,256]{1,0:T(8,128)(2,1)}, u32[]{:S(2)}) copy-start(bf16[2048,256]{1,0:T(8,128)(2,1)} %gate_weight.1) | copy-start | bytes 3145732
  85.8 11.0 %collective-permute-start.11 = (bf16[144,128]{1,0:T(8,128)(2,1)S(1)}, bf16[144,128]{1,0:T(8,128)(2,1)S(1)}, u32[]{:S(2)}, u32[]{:S(2)}) collective-permute-start(bf16[144,128]{1,0:T(8,128)(2,1)S(1)} %get-tuple-element.93), channel_id=1, source_target_pairs={{0,384},{16,400},{32,416},{48,432},{64,448},{80,464},{96,480},{112... | collective-permute-start | bytes 110600 | tf_op jit(solution)/shard_map/ppermute | solution.py:298
  86.5 10.4 %collective-permute-start.10 = (bf16[144,128]{1,0:T(8,128)(2,1)S(1)}, bf16[144,128]{1,0:T(8,128)(2,1)S(1)}, u32[]{:S(2)}, u32[]{:S(2)}) collective-permute-start(bf16[144,128]{1,0:T(8,128)(2,1)S(1)} %get-tuple-element.93), channel_id=1, source_target_pairs={{0,256},{16,272},{32,288},{48,304},{64,320},{80,336},{96,352},{112... | collective-permute-start | bytes 110600 | tf_op jit(solution)/shard_map/ppermute | solution.py:298
  92.9 5.9 %collective-permute-start.9 = (bf16[144,128]{1,0:T(8,128)(2,1)S(1)}, bf16[144,128]{1,0:T(8,128)(2,1)S(1)}, u32[]{:S(2)}, u32[]{:S(2)}) collective-permute-start(bf16[144,128]{1,0:T(8,128)(2,1)S(1)} %get-tuple-element.93), channel_id=1, source_target_pairs={{0,128},{16,144},{32,160},{48,176},{64,192},{80,208},{96,224},{112... | collective-permute-start | bytes 110600 | tf_op jit(solution)/shard_map/ppermute | solution.py:298
  98.8 3.1 %collective-permute-start.12 = (bf16[128,128]{1,0:T(8,128)(2,1)S(1)}, bf16[128,128]{1,0:T(8,128)(2,1)S(1)}, u32[]{:S(2)}, u32[]{:S(2)}) collective-permute-start(bf16[128,128]{1,0:T(8,128)(2,1)S(1)} %get-tuple-element.95), channel_id=1, source_target_pairs={{0,16},{16,0},{32,48},{48,32},{64,80},{80,64},{96,112},{112,96},{1... | collective-permute-start | bytes 98312 | tf_op jit(solution)/shard_map/ppermute | solution.py:293
  103.6 11.0 %collective-permute-start.13 = (bf16[1024,128]{1,0:T(8,128)(2,1)S(1)}, bf16[1024,128]{1,0:T(8,128)(2,1)S(1)}, u32[]{:S(2)}, u32[]{:S(2)}) collective-permute-start(bf16[1024,128]{1,0:T(8,128)(2,1)S(1)} %get-tuple-element.101), channel_id=1, source_target_pairs={{0,1},{1,0},{2,3},{3,2},{4,5},{5,4},{6,7},{7,6},{8,9},{9,8},{10,11... | collective-permute-start | bytes 786440 | tf_op jit(solution)/shard_map/ppermute | solution.py:306
  105.8 13.7 %collective-permute-start.17 = (bf16[1024,128]{1,0:T(8,128)(2,1)S(1)}, bf16[1024,128]{1,0:T(8,128)(2,1)S(1)}, u32[]{:S(2)}, u32[]{:S(2)}) collective-permute-start(bf16[1024,128]{1,0:T(8,128)(2,1)S(1)} %get-tuple-element.104), channel_id=1, source_target_pairs={{0,1},{1,0},{2,3},{3,2},{4,5},{5,4},{6,7},{7,6},{8,9},{9,8},{10,11... | collective-permute-start | bytes 786440 | tf_op jit(solution)/shard_map/ppermute | solution.py:306
  114.7 9.9 %collective-permute-start.14 = (bf16[1024,128]{1,0:T(8,128)(2,1)S(1)}, bf16[1024,128]{1,0:T(8,128)(2,1)S(1)}, u32[]{:S(2)}, u32[]{:S(2)}) collective-permute-start(bf16[1024,128]{1,0:T(8,128)(2,1)S(1)} %add_convert_fusion.4), channel_id=1, source_target_pairs={{0,7},{1,2},{2,1},{3,4},{4,3},{5,6},{6,5},{7,0},{8,15},{9,10},{10,... | collective-permute-start | bytes 786440 | tf_op jit(solution)/shard_map/ppermute | solution.py:306
  119.5 34.4 %copy-start.5 = (bf16[512,128]{1,0:T(8,128)(2,1)S(1)}, bf16[512,128]{1,0:T(8,128)(2,1)}, u32[]{:S(2)}) copy-start(bf16[512,128]{1,0:T(8,128)(2,1)} %param.19) | copy-start | bytes 393220
  119.5 10.8 %collective-permute-start.18 = (bf16[1024,128]{1,0:T(8,128)(2,1)S(1)}, bf16[1024,128]{1,0:T(8,128)(2,1)S(1)}, u32[]{:S(2)}, u32[]{:S(2)}) collective-permute-start(bf16[1024,128]{1,0:T(8,128)(2,1)S(1)} %add_convert_fusion.1), channel_id=1, source_target_pairs={{0,7},{1,2},{2,1},{3,4},{4,3},{5,6},{6,5},{7,0},{8,15},{9,10},{10,... | collective-permute-start | bytes 786440 | tf_op jit(solution)/shard_map/ppermute | solution.py:306
  124.6 8.3 %collective-permute-start.15 = (bf16[1024,128]{1,0:T(8,128)(2,1)S(1)}, bf16[1024,128]{1,0:T(8,128)(2,1)S(1)}, u32[]{:S(2)}, u32[]{:S(2)}) collective-permute-start(bf16[1024,128]{1,0:T(8,128)(2,1)S(1)} %add_convert_fusion.3), channel_id=1, source_target_pairs={{0,1},{1,0},{2,3},{3,2},{4,5},{5,4},{6,7},{7,6},{8,9},{9,8},{10,11... | collective-permute-start | bytes 786440 | tf_op jit(solution)/shard_map/ppermute | solution.py:306
  130.4 8.5 %collective-permute-start.19 = (bf16[1024,128]{1,0:T(8,128)(2,1)S(1)}, bf16[1024,128]{1,0:T(8,128)(2,1)S(1)}, u32[]{:S(2)}, u32[]{:S(2)}) collective-permute-start(bf16[1024,128]{1,0:T(8,128)(2,1)S(1)} %add_convert_fusion), channel_id=1, source_target_pairs={{0,1},{1,0},{2,3},{3,2},{4,5},{5,4},{6,7},{7,6},{8,9},{9,8},{10,11... | collective-permute-start | bytes 786440 | tf_op jit(solution)/shard_map/ppermute | solution.py:306
  133.0 9.5 %collective-permute-start.16 = (bf16[1024,128]{1,0:T(8,128)(2,1)S(1)}, bf16[1024,128]{1,0:T(8,128)(2,1)S(1)}, u32[]{:S(2)}, u32[]{:S(2)}) collective-permute-start(bf16[1024,128]{1,0:T(8,128)(2,1)S(1)} %add_convert_fusion.2), channel_id=1, source_target_pairs={{0,7},{1,2},{2,1},{3,4},{4,3},{5,6},{6,5},{7,0},{8,15},{9,10},{10,... | collective-permute-start | bytes 786440 | tf_op jit(solution)/shard_map/ppermute | solution.py:306
  142.6 11.4 %collective-permute-start.20 = (bf16[512,128]{1,0:T(8,128)(2,1)S(1)}, bf16[512,128]{1,0:T(8,128)(2,1)S(1)}, u32[]{:S(2)}, u32[]{:S(2)}) collective-permute-start(bf16[512,128]{1,0:T(8,128)(2,1)S(1)} %slice.86), channel_id=1, source_target_pairs={{0,8},{1,9},{2,10},{3,11},{4,12},{5,13},{6,14},{7,15},{8,0},{9,1},... | collective-permute-start | bytes 393224 | tf_op jit(solution)/shard_map/ppermute | solution.py:289
  (4 other events, 22.5 us)
